TPU v7x, 32 devices: a whole 2x2x4 slice. The times are simulated.
32 devices in a mesh: ctx: 16 (over z, y, core), exp: 2 (over x).
Axes of the slice: x: 2, y: 2, z: 4, core: 2. Of those that a mesh axis runs over, the one named last changes fastest.
Arguments:
- query: bfloat16 [2, 2048, 2048], P('exp', 'ctx'), may hold values from -12 to 12
- key: bfloat16 [2, 2048, 2048], P('exp', 'ctx'), may hold values from -6 to 6
- value: bfloat16 [2, 2048, 2048], P('exp', 'ctx'), may hold values from -12 to 12
- cotangent: bfloat16 [2, 2048, 2048], P('exp', 'ctx'), may hold values from -6 to 6
- route_ids: int32 [2, 2048, 1], P('exp', 'ctx'), may hold values from 0 to 1; in each aligned block of 128 rows (0 to 127, 128 to 255, ..., all dimensions but the last counted through in order) at most 128 rows name the same one
- route_weights: float32 [2, 2048, 1], P('exp', 'ctx'), may hold values from 0.2 to 1
- block_mask: int32 [2, 16, 3], P('exp', 'ctx'), may hold values 0 or 1
- w_gate: bfloat16 [2, 2048, 512], P('exp'), may hold values from -0.125 to 0.125
- w_up: bfloat16 [2, 2048, 512], P('exp'), may hold values from -0.125 to 0.125
- w_down: bfloat16 [2, 512, 2048], P('exp'), may hold values from -0.25 to 0.25
Outputs:
- layer_out: bfloat16 [2, 2048, 2048], P('exp', 'ctx')
- grad_query: bfloat16 [2, 2048, 2048], P('exp', 'ctx')
- grad_key: bfloat16 [2, 2048, 2048], P('exp', 'ctx')
- grad_value: bfloat16 [2, 2048, 2048], P('exp', 'ctx')
- tangent_out: bfloat16 [2, 2048, 2048], P('exp', 'ctx')
Inputs may be any that keep to these rules, and one draw needn't show every extreme that they name: `route_ids`: among the 128 tokens of one block of a sequence, the routes of a token name distinct experts, no expert is named by more than 128 routes, and in every draw some block names some expert exactly 128 times.
All inputs are finite; a program needn't handle non-finite values. No bound on the sum of `block_mask` on one device may be relied on, other than what follows from the above.
Results may differ from a plain program's by a relative error of at most 0.035.
Values may be sent and summed in bfloat16 or wider, within the bound.
No kernel may reach another device: no remote copies, remote signals or barrier semaphores. Data moves between devices by JAX's collectives and lax.ppermute only.
A program may use at most 128 MiB of HBM per device.

v0:
```python
import jax
import jax.numpy as jnp
from jax import lax
from jax.sharding import PartitionSpec as P

HEADS = 16
WIN = 4


def passed_along(x, axis, by):
    devices = lax.axis_size(axis)
    pairs = [(i, i + by) for i in range(devices) if 0 <= i + by < devices]
    return lax.ppermute(x, axis, pairs)


def silu_parts(gate_pre):
    sigmoid_val = jax.nn.sigmoid(gate_pre)
    return (gate_pre * sigmoid_val, sigmoid_val * (1.0 + gate_pre * (1.0 - sigmoid_val)))


def heads_of(row_block):
    return row_block.reshape(row_block.shape[0], HEADS, row_block.shape[1] // HEADS)


def attend_probs(query_rows, key_window, allowed, score_scale):
    scores = (
        jnp.einsum(
            "qhd,khd->hqk",
            heads_of(query_rows),
            heads_of(key_window),
            preferred_element_type=jnp.float32,
        )
        * score_scale
    )
    scores = jnp.where(allowed[None], scores, -1e30)
    row_top = jnp.max(scores, axis=-1, keepdims=True)
    exp_scores = jnp.exp(scores - row_top)
    return exp_scores / jnp.sum(exp_scores, axis=-1, keepdims=True)


def routing_table(route_rows, experts, capacity):
    flat_ids = route_rows.reshape(-1)
    one_hot = (flat_ids[:, None] == jnp.arange(experts, dtype=jnp.int32)[None, :]).astype(jnp.int32)
    slot_rank = jnp.sum((jnp.cumsum(one_hot, axis=0) - one_hot) * one_hot, axis=1)
    target = flat_ids * capacity + slot_rank
    return (jnp.arange(experts * capacity, dtype=jnp.int32)[:, None] == target[None, :]).astype(
        jnp.bfloat16
    )


def dispatch(slot_table, row_block, routes, experts):
    pair_rows = jnp.repeat(row_block, routes, axis=0)
    sent = jnp.dot(slot_table, pair_rows, preferred_element_type=jnp.float32).astype(jnp.bfloat16)
    return sent.reshape(experts, -1, row_block.shape[1])


def combine(slot_table, returned, weights):
    rows_here, routes = weights.shape
    pair_vals = jnp.dot(
        slot_table.T, returned.reshape(-1, returned.shape[2]), preferred_element_type=jnp.float32
    )
    return jnp.sum(pair_vals.reshape(rows_here, routes, -1) * weights[:, :, None], axis=1)


def expert_forward(row_block, gate_matrix, up_matrix, down_matrix):
    gate_pre = jnp.dot(row_block, gate_matrix, preferred_element_type=jnp.float32)
    up_value = jnp.dot(row_block, up_matrix, preferred_element_type=jnp.float32)
    activated, slope_val = silu_parts(gate_pre)
    hidden = (activated * up_value).astype(jnp.bfloat16)
    return (
        jnp.dot(hidden, down_matrix, preferred_element_type=jnp.float32).astype(jnp.bfloat16),
        gate_pre,
        up_value,
    )


def expert_backward(cot_block, gate_pre, up_value, gate_matrix, up_matrix, down_matrix):
    hidden_grad = jnp.dot(cot_block, down_matrix.T, preferred_element_type=jnp.float32)
    activated, slope_val = silu_parts(gate_pre)
    gate_grad = (hidden_grad * up_value * slope_val).astype(jnp.bfloat16)
    up_grad = (hidden_grad * activated).astype(jnp.bfloat16)
    summed = jnp.dot(gate_grad, gate_matrix.T, preferred_element_type=jnp.float32) + jnp.dot(
        up_grad, up_matrix.T, preferred_element_type=jnp.float32
    )
    return summed.astype(jnp.bfloat16)


def expert_tangent(tan_block, gate_pre, up_value, gate_matrix, up_matrix, down_matrix):
    gate_tan = jnp.dot(tan_block, gate_matrix, preferred_element_type=jnp.float32)
    up_tan = jnp.dot(tan_block, up_matrix, preferred_element_type=jnp.float32)
    activated, slope_val = silu_parts(gate_pre)
    hidden_tan = (slope_val * gate_tan * up_value + activated * up_tan).astype(jnp.bfloat16)
    return jnp.dot(hidden_tan, down_matrix, preferred_element_type=jnp.float32).astype(jnp.bfloat16)


def local(query, key, value, cotangent, route_ids, route_weights, block_mask, w_gate, w_up, w_down):
    query_rows, key_rows, value_rows, upstream = (query[0], key[0], value[0], cotangent[0])
    rows_here, model_width = query_rows.shape
    score_scale = (model_width // HEADS) ** (-0.5)
    block_index = lax.axis_index("ctx")
    experts = lax.axis_size("exp") * w_gate.shape[0]
    routes = route_ids.shape[2]
    capacity = min(rows_here, 2 * rows_here * routes // experts)
    gate_matrix, up_matrix, down_matrix = (w_gate[0], w_up[0], w_down[0])
    moving = (key_rows, value_rows)
    windows = [moving]
    for offset in range(1, WIN):
        moving = passed_along((moving[0], moving[1]), "ctx", 1)
        windows.append(moving)
    key_window = jnp.concatenate([member[0] for member in windows], axis=0)
    value_window = jnp.concatenate([member[1] for member in windows], axis=0)
    rowpos = jnp.arange(rows_here, dtype=jnp.int32)
    pieces = [rowpos[:, None] >= rowpos[None, :]]
    for offset in range(1, WIN):
        visible = (block_index >= offset) & (block_mask[0, 0, offset - 1] == 1)
        pieces.append(jnp.broadcast_to(visible, (rows_here, rows_here)))
    allowed = jnp.concatenate(pieces, axis=1)
    attn_probs = attend_probs(query_rows, key_window, allowed, score_scale)
    probs_low = attn_probs.astype(jnp.bfloat16)
    attended = (
        jnp.einsum(
            "hqk,khd->qhd", probs_low, heads_of(value_window), preferred_element_type=jnp.float32
        )
        .reshape(rows_here, model_width)
        .astype(jnp.bfloat16)
    )
    slot_table = routing_table(route_ids[0], experts, capacity)
    weights = route_weights[0]
    send_rows = dispatch(slot_table, attended, routes, experts)
    send_cots = dispatch(slot_table, upstream, routes, experts)
    got_rows = lax.all_to_all(send_rows, "exp", split_axis=0, concat_axis=0, tiled=True)
    expert_out, gate_pre, up_value = expert_forward(
        got_rows.reshape(-1, model_width), gate_matrix, up_matrix, down_matrix
    )
    back_out = lax.all_to_all(
        expert_out.reshape(got_rows.shape), "exp", split_axis=0, concat_axis=0, tiled=True
    )
    got_cots = lax.all_to_all(send_cots, "exp", split_axis=0, concat_axis=0, tiled=True)
    route_grad = expert_backward(
        got_cots.reshape(-1, model_width), gate_pre, up_value, gate_matrix, up_matrix, down_matrix
    )
    back_grad = lax.all_to_all(
        route_grad.reshape(got_cots.shape), "exp", split_axis=0, concat_axis=0, tiled=True
    )
    layer_out = (attended.astype(jnp.float32) + combine(slot_table, back_out, weights)).astype(
        jnp.bfloat16
    )
    attn_cot = (upstream.astype(jnp.float32) + combine(slot_table, back_grad, weights)).astype(
        jnp.bfloat16
    )
    row_delta = jnp.einsum(
        "qhd,qhd->hq", heads_of(attn_cot), heads_of(attended), preferred_element_type=jnp.float32
    )
    prob_grad = jnp.einsum(
        "qhd,khd->hqk",
        heads_of(attn_cot),
        heads_of(value_window),
        preferred_element_type=jnp.float32,
    )
    score_grad = (attn_probs * (prob_grad - row_delta[:, :, None])).astype(jnp.bfloat16)
    grad_query = (
        (
            jnp.einsum(
                "hqk,khd->qhd", score_grad, heads_of(key_window), preferred_element_type=jnp.float32
            )
            * score_scale
        )
        .reshape(rows_here, model_width)
        .astype(jnp.bfloat16)
    )
    key_terms = (
        jnp.einsum(
            "hqk,qhd->khd", score_grad, heads_of(query_rows), preferred_element_type=jnp.float32
        )
        * score_scale
    ).reshape(WIN, rows_here, model_width)
    value_terms = jnp.einsum(
        "hqk,qhd->khd", probs_low, heads_of(attn_cot), preferred_element_type=jnp.float32
    ).reshape(WIN, rows_here, model_width)
    key_sum, value_sum = (key_terms[0], value_terms[0])
    for offset in range(1, WIN):
        arrived = (
            passed_along(key_terms[offset].astype(jnp.bfloat16), "ctx", -offset).astype(
                jnp.float32
            ),
            passed_along(value_terms[offset].astype(jnp.bfloat16), "ctx", -offset).astype(
                jnp.float32
            ),
        )
        key_sum = key_sum + arrived[0]
        value_sum = value_sum + arrived[1]
    grad_key = key_sum.astype(jnp.bfloat16)
    grad_value = value_sum.astype(jnp.bfloat16)
    moving = (grad_key, grad_value)
    tan_windows = [moving]
    for offset in range(1, WIN):
        moving = passed_along((moving[0], moving[1]), "ctx", 1)
        tan_windows.append(moving)
    tan_keys = jnp.concatenate([member[0] for member in tan_windows], axis=0)
    tan_values = jnp.concatenate([member[1] for member in tan_windows], axis=0)
    score_tan = (
        jnp.einsum(
            "qhd,khd->hqk",
            heads_of(grad_query),
            heads_of(key_window),
            preferred_element_type=jnp.float32,
        )
        + jnp.einsum(
            "qhd,khd->hqk",
            heads_of(query_rows),
            heads_of(tan_keys),
            preferred_element_type=jnp.float32,
        )
    ) * score_scale
    mean_tan = jnp.sum(attn_probs * score_tan, axis=-1, keepdims=True)
    prob_tan = (attn_probs * (score_tan - mean_tan)).astype(jnp.bfloat16)
    attn_tangent = (
        (
            jnp.einsum(
                "hqk,khd->qhd", prob_tan, heads_of(value_window), preferred_element_type=jnp.float32
            )
            + jnp.einsum(
                "hqk,khd->qhd", probs_low, heads_of(tan_values), preferred_element_type=jnp.float32
            )
        )
        .reshape(rows_here, model_width)
        .astype(jnp.bfloat16)
    )
    send_tans = dispatch(slot_table, attn_tangent, routes, experts)
    got_tans = lax.all_to_all(send_tans, "exp", split_axis=0, concat_axis=0, tiled=True)
    expert_tan = expert_tangent(
        got_tans.reshape(-1, model_width), gate_pre, up_value, gate_matrix, up_matrix, down_matrix
    )
    back_tan = lax.all_to_all(
        expert_tan.reshape(got_tans.shape), "exp", split_axis=0, concat_axis=0, tiled=True
    )
    tangent_out = (
        attn_tangent.astype(jnp.float32) + combine(slot_table, back_tan, weights)
    ).astype(jnp.bfloat16)
    return (layer_out[None], grad_query[None], grad_key[None], grad_value[None], tangent_out[None])


def solution(mesh):
    return jax.shard_map(
        local,
        mesh=mesh,
        in_specs=(
            P("exp", "ctx", None),
            P("exp", "ctx", None),
            P("exp", "ctx", None),
            P("exp", "ctx", None),
            P("exp", "ctx", None),
            P("exp", "ctx", None),
            P("exp", "ctx", None),
            P("exp", None, None),
            P("exp", None, None),
            P("exp", None, None),
        ),
        out_specs=(
            P("exp", "ctx", None),
            P("exp", "ctx", None),
            P("exp", "ctx", None),
            P("exp", "ctx", None),
            P("exp", "ctx", None),
        ),
        check_vma=False,
    )
```

profile of v0, /device:TPU:0, one launch (start us, length us, event | category | flops | bytes accessed | tf_op | source)
XLA Modules:
  0.0 290.3 jit_solution(16712628478666499899)
XLA Ops:
  2.1 3.2 %collective-permute-start.3 = (bf16[128,2048]{0,1:T(8,128)(2,1)S(1)}, bf16[128,2048]{0,1:T(8,128)(2,1)}, u32[]{:S(2)}, u32[]{:S(2)}) collective-permute-start(bf16[128,2048]{0,1:T(8,128)(2,1)S(1)} %bitcast.161), channel_id=1, source_target_pairs={{0,2},{2,4},{4,6},{6,8},{8,10},{10,12},{12,14},{14,16},{16,18},{18... | collective-permute-start | bytes 1572872 | tf_op jit(solution)/shard_map/ppermute | solution.py:13
  5.3 4.6 %collective-permute-start = (bf16[128,2048]{1,0:T(8,128)(2,1)}, bf16[128,2048]{1,0:T(8,128)(2,1)}, u32[]{:S(2)}, u32[]{:S(2)}) collective-permute-start(bf16[128,2048]{1,0:T(8,128)(2,1)} %bitcast.169), channel_id=1, source_target_pairs={{0,2},{2,4},{4,6},{6,8},{8,10},{10,12},{12,14},{14,16},{16,18},{18... | collective-permute-start | bytes 1572872 | tf_op jit(solution)/shard_map/ppermute | solution.py:13
  9.8 6.1 %collective-permute-start.4 = (bf16[128,2048]{0,1:T(8,128)(2,1)}, bf16[128,2048]{0,1:T(8,128)(2,1)}, u32[]{:S(2)}, u32[]{:S(2)}) collective-permute-start(bf16[128,2048]{0,1:T(8,128)(2,1)} %collective-permute-done.3), channel_id=1, source_target_pairs={{0,2},{2,4},{4,6},{6,8},{8,10},{10,12},{12,14},{14,16},{16,18},{18... | collective-permute-start | bytes 1572872 | tf_op jit(solution)/shard_map/ppermute | solution.py:13
  18.4 4.5 %collective-permute-start.1 = (bf16[128,2048]{1,0:T(8,128)(2,1)}, bf16[128,2048]{1,0:T(8,128)(2,1)}, u32[]{:S(2)}, u32[]{:S(2)}) collective-permute-start(bf16[128,2048]{1,0:T(8,128)(2,1)} %collective-permute-done), channel_id=1, source_target_pairs={{0,2},{2,4},{4,6},{6,8},{8,10},{10,12},{12,14},{14,16},{16,18},{18... | collective-permute-start | bytes 1572872 | tf_op jit(solution)/shard_map/ppermute | solution.py:13
  22.9 4.4 %collective-permute-start.5 = (bf16[128,2048]{0,1:T(8,128)(2,1)}, bf16[128,2048]{0,1:T(8,128)(2,1)}, u32[]{:S(2)}, u32[]{:S(2)}) collective-permute-start(bf16[128,2048]{0,1:T(8,128)(2,1)} %collective-permute-done.4), channel_id=1, source_target_pairs={{0,2},{2,4},{4,6},{6,8},{8,10},{10,12},{12,14},{14,16},{16,18},{18... | collective-permute-start | bytes 1572872 | tf_op jit(solution)/shard_map/ppermute | solution.py:13
  27.3 2.5 convolution_convert_fusion.2
  29.8 4.4 %all-to-all-start.2 = ((bf16[2,128,2048]{2,1,0:T(8,128)(2,1)}), bf16[2,128,2048]{2,1,0:T(8,128)(2,1)}, u32[]{:S(2)}, u32[]{:S(2)}) async-start(bf16[2,128,2048]{2,1,0:T(8,128)(2,1)} %bitcast.31), calls=%async_computation.2 | async-start | bytes 2097152 | tf_op jit(solution)/shard_map/all_to_all | solution.py:138
  40.3 2.1 copy.52
  42.4 2.0 copy.46
  44.4 2.0 copy.53
  46.5 4.4 %collective-permute-start.2 = (bf16[128,2048]{1,0:T(8,128)(2,1)}, bf16[128,2048]{1,0:T(8,128)(2,1)}, u32[]{:S(2)}, u32[]{:S(2)}) collective-permute-start(bf16[128,2048]{1,0:T(8,128)(2,1)} %collective-permute-done.1), channel_id=1, source_target_pairs={{0,2},{2,4},{4,6},{6,8},{8,10},{10,12},{12,14},{14,16},{16,18},{18... | collective-permute-start | bytes 1572872 | tf_op jit(solution)/shard_map/ppermute | solution.py:13
  50.9 2.0 copy.47
  52.9 2.0 copy.54
  55.0 2.1 fusion.60
  57.0 3.7 %fusion.81 = (f32[16,128]{1,0:T(8,128)S(1)}, f32[16,128,512]{1,2,0:T(8,128)}) fusion(f32[16,512,128]{2,1,0:T(8,128)S(1)} %fusion.60, pred[128,512]{0,1:T(8,128)(4,1)S(1)} %add_add_fusion), kind=kOutput, calls=%fused_computation.105 | output fusion | flops 6291967 | bytes 8462336 | tf_op jit(solution)/shard_map/sub | solution.py:37
  60.7 2.0 copy.48
  62.8 3.5 %convolution_convert_fusion.5 = bf16[16,128,128]{2,1,0:T(8,128)(2,1)S(1)} fusion(bf16[128,16,128]{0,2,1:T(8,128)(2,1)} %bitcast.180, bf16[128,16,128]{0,2,1:T(8,128)(2,1)} %bitcast.177, bf16[128,16,128]{0,2,1:T(8,128)(2,1)} %bitcast.174, bf16[128,16,128]{0,2,1:T(8,128)(2,1)} %bitcast.171, f32[16,128,512]{1,2,0:T(8,128)} %get-tuple-element.27, ...), kind=kOutput, calls=%fused_computation.56 | convolution fusion | flops 279183360 | bytes 6823936 | tf_op jit(solution)/shard_map/hqk,khd->qhd/dot_general | solution.py:121
  67.7 4.5 %all-to-all-start = ((bf16[2,128,2048]{2,1,0:T(8,128)(2,1)}), bf16[2,128,2048]{2,1,0:T(8,128)(2,1)}, u32[]{:S(2)}, u32[]{:S(2)}) async-start(bf16[2,128,2048]{2,1,0:T(8,128)(2,1)} %bitcast.154), calls=%async_computation | async-start | bytes 2097152 | tf_op jit(solution)/shard_map/all_to_all | solution.py:131
  72.2 2.8 fusion.12
  75.0 10.9 %all-to-all-done = bf16[2,128,2048]{2,1,0:T(8,128)(2,1)} async-done(((bf16[2,128,2048]{2,1,0:T(8,128)(2,1)}), bf16[2,128,2048]{2,1,0:T(8,128)(2,1)}, u32[]{:S(2)}, u32[]{:S(2)}) %all-to-all-start) | async-done | bytes 1048608 | tf_op jit(solution)/shard_map/all_to_all | solution.py:131
  85.9 2.8 fusion.18
  88.6 2.8 fusion.24
  94.1 4.6 %all-to-all-start.3 = ((bf16[2,128,2048]{2,1,0:T(8,128)(2,1)}), bf16[2,128,2048]{2,1,0:T(8,128)(2,1)}, u32[]{:S(2)}, u32[]{:S(2)}) async-start(bf16[2,128,2048]{2,1,0:T(8,128)(2,1)} %bitcast.157), calls=%async_computation.3 | async-start | bytes 2097152 | tf_op jit(solution)/shard_map/all_to_all | solution.py:142
  98.7 2.3 copy.107
  101.1 10.2 %all-to-all-done.3 = bf16[2,128,2048]{2,1,0:T(8,128)(2,1)} async-done(((bf16[2,128,2048]{2,1,0:T(8,128)(2,1)}), bf16[2,128,2048]{2,1,0:T(8,128)(2,1)}, u32[]{:S(2)}, u32[]{:S(2)}) %all-to-all-start.3) | async-done | bytes 1048608 | tf_op jit(solution)/shard_map/all_to_all | solution.py:142
  111.3 2.5 convolution_multiply_fusion.1
  113.8 2.5 copy.108
  116.4 1.8 fusion.51
  118.2 5.1 %fusion.83 = (bf16[512,16,128]{0,2,1:T(8,128)(2,1)S(1)}, f32[512,16,128]{0,2,1:T(8,128)}) fusion(bf16[128,16,128]{0,2,1:T(8,128)(2,1)S(1)} %get-tuple-element.16, f32[16,128,512]{1,2,0:T(8,128)} %get-tuple-element.27, f32[16,128]{1,0:T(8,128)S(1)} %get-tuple-element.26), kind=kOutput, calls=%fused_computation.107 | convolution fusion | flops 271581184 | bytes 11018240 | tf_op jit(solution)/shard_map/hqk,qhd->khd/dot_general | solution.py:177
  123.4 2.2 multiply_convert_fusion.1
  126.9 2.1 copy.76
  130.2 2.1 copy.75
  133.6 2.1 copy.73
  136.9 3.6 %fusion.82 = (bf16[512,16,128]{2,0,1:T(8,128)(2,1)}, f32[512,16,128]{2,0,1:T(8,128)S(1)}) fusion(bf16[16,128,512]{1,2,0:T(8,128)(2,1)} %multiply_convert_fusion.1, bf16[128,16,128]{2,1,0:T(8,128)(2,1)S(1)} %bitcast.149), kind=kOutput, calls=%fused_computation.106 | convolution fusion | flops 270532608 | bytes 8912896 | tf_op jit(solution)/shard_map/hqk,qhd->khd/dot_general | solution.py:172
  141.6 2.6 copy.68
  144.2 2.5 fusion.79
  146.7 2.1 copy.71
  150.0 2.0 copy.70
  153.4 2.0 copy.69
  155.4 2.3 slice.62
  157.7 2.5 copy.74
  161.9 2.0 add_convert_fusion
  163.9 3.7 %collective-permute-start.15 = (bf16[128,2048]{1,0:T(8,128)(2,1)S(1)}, bf16[128,2048]{1,0:T(8,128)(2,1)S(1)}, u32[]{:S(2)}, u32[]{:S(2)}) collective-permute-start(bf16[128,2048]{1,0:T(8,128)(2,1)S(1)} %add_convert_fusion), channel_id=1, source_target_pairs={{0,2},{2,4},{4,6},{6,8},{8,10},{10,12},{12,14},{14,16},{16,18},{18... | collective-permute-start | bytes 1572872 | tf_op jit(solution)/shard_map/ppermute | solution.py:13
  167.6 4.6 %collective-permute-done.7 = bf16[128,2048]{0,1:T(8,128)(2,1)} collective-permute-done((bf16[128,2048]{0,1:T(8,128)(2,1)}, bf16[128,2048]{0,1:T(8,128)(2,1)}, u32[]{:S(2)}, u32[]{:S(2)}) %collective-permute-start.7) | collective-permute-done | bytes 524320 | tf_op jit(solution)/shard_map/ppermute | solution.py:13
  172.2 1.8 fusion.50
  174.8 9.3 %collective-permute-start.12 = (bf16[128,2048]{0,1:T(8,128)(2,1)S(1)}, bf16[128,2048]{0,1:T(8,128)(2,1)S(1)}, u32[]{:S(2)}, u32[]{:S(2)}) collective-permute-start(bf16[128,2048]{0,1:T(8,128)(2,1)S(1)} %fusion.50), channel_id=1, source_target_pairs={{0,2},{2,4},{4,6},{6,8},{8,10},{10,12},{12,14},{14,16},{16,18},{18... | collective-permute-start | bytes 1572872 | tf_op jit(solution)/shard_map/ppermute | solution.py:13
  184.1 11.7 %collective-permute-start.16 = (bf16[128,2048]{1,0:T(8,128)(2,1)S(1)}, bf16[128,2048]{1,0:T(8,128)(2,1)S(1)}, u32[]{:S(2)}, u32[]{:S(2)}) collective-permute-start(bf16[128,2048]{1,0:T(8,128)(2,1)S(1)} %collective-permute-done.15), channel_id=1, source_target_pairs={{0,2},{2,4},{4,6},{6,8},{8,10},{10,12},{12,14},{14,16},{16,18},{18... | collective-permute-start | bytes 1572872 | tf_op jit(solution)/shard_map/ppermute | solution.py:13
  195.8 6.4 %collective-permute-start.13 = (bf16[128,2048]{0,1:T(8,128)(2,1)S(1)}, bf16[128,2048]{0,1:T(8,128)(2,1)}, u32[]{:S(2)}, u32[]{:S(2)}) collective-permute-start(bf16[128,2048]{0,1:T(8,128)(2,1)S(1)} %collective-permute-done.12), channel_id=1, source_target_pairs={{0,2},{2,4},{4,6},{6,8},{8,10},{10,12},{12,14},{14,16},{16,18},{18... | collective-permute-start | bytes 1572872 | tf_op jit(solution)/shard_map/ppermute | solution.py:13
  202.2 5.0 %collective-permute-start.17 = (bf16[128,2048]{1,0:T(8,128)(2,1)S(1)}, bf16[128,2048]{1,0:T(8,128)(2,1)S(1)}, u32[]{:S(2)}, u32[]{:S(2)}) collective-permute-start(bf16[128,2048]{1,0:T(8,128)(2,1)S(1)} %collective-permute-done.16), channel_id=1, source_target_pairs={{0,2},{2,4},{4,6},{6,8},{8,10},{10,12},{12,14},{14,16},{16,18},{18... | collective-permute-start | bytes 1572872 | tf_op jit(solution)/shard_map/ppermute | solution.py:13
  208.9 5.2 %collective-permute-start.14 = (bf16[128,2048]{0,1:T(8,128)(2,1)}, bf16[128,2048]{0,1:T(8,128)(2,1)}, u32[]{:S(2)}, u32[]{:S(2)}) collective-permute-start(bf16[128,2048]{0,1:T(8,128)(2,1)} %collective-permute-done.13), channel_id=1, source_target_pairs={{0,2},{2,4},{4,6},{6,8},{8,10},{10,12},{12,14},{14,16},{16,18},{18... | collective-permute-start | bytes 1572872 | tf_op jit(solution)/shard_map/ppermute | solution.py:13
  215.8 3.9 %copy.82 = bf16[512,2048]{0,1:T(8,128)(2,1)} copy(bf16[512,2048]{1,0:T(8,128)(2,1)} %pad_maximum_fusion.3) | data formatting | bytes 4194304 | tf_op jit(solution)/shard_map/concatenate | solution.py:200
  219.7 3.6 %fusion.69 = f32[16,128,128]{2,1,0:T(8,128)S(1)} fusion(bf16[512,16,128]{0,2,1:T(8,128)(2,1)} %bitcast.158, f32[16,128,512]{1,2,0:T(8,128)} %get-tuple-element.27, f32[16,128]{1,0:T(8,128)S(1)} %get-tuple-element.26), kind=kOutput, calls=%fused_computation.96 | convolution fusion | flops 270532608 | bytes 7348224 | tf_op jit(solution)/shard_map/hqk,khd->qhd/dot_general | solution.py:222
  231.9 4.6 %all-to-all-start.4 = ((bf16[2,128,2048]{2,1,0:T(8,128)(2,1)}), bf16[2,128,2048]{2,1,0:T(8,128)(2,1)}, u32[]{:S(2)}, u32[]{:S(2)}) async-start(bf16[2,128,2048]{2,1,0:T(8,128)(2,1)} %bitcast.155), calls=%async_computation.4 | async-start | bytes 2097152 | tf_op jit(solution)/shard_map/all_to_all | solution.py:230
  236.5 2.9 %convolution_convert_fusion.3 = bf16[256,2048]{1,0:T(8,128)(2,1)} fusion(bf16[1,512,2048]{2,1,0:T(8,128)(2,1)S(1)} %copy-done, f32[256,512]{1,0:T(8,128)} %copy-done.32, f32[256,512]{1,0:T(8,128)} %copy-done.9), kind=kOutput, calls=%fused_computation.15 | convolution fusion | flops 538181632 | bytes 4194304 | tf_op jit(solution)/shard_map/dot_general | solution.py:71
  239.4 10.5 %all-to-all-done.4 = bf16[2,128,2048]{2,1,0:T(8,128)(2,1)} async-done(((bf16[2,128,2048]{2,1,0:T(8,128)(2,1)}), bf16[2,128,2048]{2,1,0:T(8,128)(2,1)}, u32[]{:S(2)}, u32[]{:S(2)}) %all-to-all-start.4) | async-done | bytes 1048608 | tf_op jit(solution)/shard_map/all_to_all | solution.py:230
  249.9 4.5 %all-to-all-start.1 = ((bf16[2,128,2048]{2,1,0:T(8,128)(2,1)}), bf16[2,128,2048]{2,1,0:T(8,128)(2,1)}, u32[]{:S(2)}, u32[]{:S(2)}) async-start(bf16[2,128,2048]{2,1,0:T(8,128)(2,1)} %bitcast.168), calls=%async_computation.1 | async-start | bytes 2097152 | tf_op jit(solution)/shard_map/all_to_all | solution.py:135
  254.5 3.7 %fusion.36 = f32[256,512]{1,0:T(8,128)} fusion(f32[256,512]{1,0:T(8,128)} %copy-done.32, bf16[256,2048]{1,0:T(8,128)(2,1)} %bitcast.58, bf16[1,2048,512]{2,1,0:T(8,128)(2,1)} %param.17, f32[256,512]{1,0:T(8,128)} %copy-done.9), kind=kOutput, calls=%fused_computation.58 | convolution fusion | flops 538050560 | bytes 4718592 | tf_op jit(solution)/shard_map/dot_general | solution.py:89
  258.2 4.4 %convolution_convert_fusion = bf16[256,2048]{1,0:T(8,128)(2,1)} fusion(bf16[1,512,2048]{2,1,0:T(8,128)(2,1)S(1)} %copy-done, f32[256,512]{1,0:T(8,128)} %fusion.36, bf16[256,2048]{1,0:T(8,128)(2,1)} %bitcast.58, bf16[1,2048,512]{2,1,0:T(8,128)(2,1)} %param.18, f32[256,512]{1,0:T(8,128)S(1)} %copy-done.10), kind=kOutput, calls=%fused_computation.12 | convolution fusion | flops 1075183616 | bytes 7340032 | tf_op jit(solution)/shard_map/dot_general | solution.py:93
  262.6 6.7 %all-to-all-done.1 = bf16[2,128,2048]{2,1,0:T(8,128)(2,1)} async-done(((bf16[2,128,2048]{2,1,0:T(8,128)(2,1)}), bf16[2,128,2048]{2,1,0:T(8,128)(2,1)}, u32[]{:S(2)}, u32[]{:S(2)}) %all-to-all-start.1) | async-done | bytes 1048608 | tf_op jit(solution)/shard_map/all_to_all | solution.py:135
  269.2 4.4 %all-to-all-start.5 = ((bf16[2,128,2048]{2,1,0:T(8,128)(2,1)}), bf16[2,128,2048]{2,1,0:T(8,128)(2,1)}, u32[]{:S(2)}, u32[]{:S(2)}) async-start(bf16[2,128,2048]{2,1,0:T(8,128)(2,1)} %bitcast.167), calls=%async_computation.5 | async-start | bytes 2097152 | tf_op jit(solution)/shard_map/all_to_all | solution.py:234
  274.7 2.1 copy.85
  276.8 2.5 fusion.9
  280.5 7.4 %all-to-all-done.5 = bf16[2,128,2048]{2,1,0:T(8,128)(2,1)} async-done(((bf16[2,128,2048]{2,1,0:T(8,128)(2,1)}), bf16[2,128,2048]{2,1,0:T(8,128)(2,1)}, u32[]{:S(2)}, u32[]{:S(2)}) %all-to-all-start.5) | async-done | bytes 1048608 | tf_op jit(solution)/shard_map/all_to_all | solution.py:234
  287.9 2.4 fusion.8
  (134 shorter events, 37.2 us)
Async XLA Ops:
  0.6 71.6 %copy-start = (bf16[1,512,2048]{2,1,0:T(8,128)(2,1)S(1)}, bf16[1,512,2048]{2,1,0:T(8,128)(2,1)}, u32[]{:S(2)}) copy-start(bf16[1,512,2048]{2,1,0:T(8,128)(2,1)} %param.19) | copy-start | bytes 6291460
  0.6 33.6 %copy-start.13 = (bf16[1,128,2048]{2,1,0:T(8,128)(2,1)S(1)}, bf16[1,128,2048]{2,1,0:T(8,128)(2,1)}, u32[]{:S(2)}) copy-start(bf16[1,128,2048]{2,1,0:T(8,128)(2,1)} %param.12) | copy-start | bytes 1572868
  0.7 36.7 %copy-start.35 = (s32[1,1,3]{2,1,0:T(1,128)S(1)}, s32[1,1,3]{2,1,0:T(1,128)}, u32[]{:S(2)}) copy-start(s32[1,1,3]{2,1,0:T(1,128)} %param.16) | copy-start | bytes 40
  2.1 7.7 %collective-permute-start.3 = (bf16[128,2048]{0,1:T(8,128)(2,1)S(1)}, bf16[128,2048]{0,1:T(8,128)(2,1)}, u32[]{:S(2)}, u32[]{:S(2)}) collective-permute-start(bf16[128,2048]{0,1:T(8,128)(2,1)S(1)} %bitcast.161), channel_id=1, source_target_pairs={{0,2},{2,4},{4,6},{6,8},{8,10},{10,12},{12,14},{14,16},{16,18},{18... | collective-permute-start | bytes 1572872 | tf_op jit(solution)/shard_map/ppermute | solution.py:13
  5.3 13.1 %collective-permute-start = (bf16[128,2048]{1,0:T(8,128)(2,1)}, bf16[128,2048]{1,0:T(8,128)(2,1)}, u32[]{:S(2)}, u32[]{:S(2)}) collective-permute-start(bf16[128,2048]{1,0:T(8,128)(2,1)} %bitcast.169), channel_id=1, source_target_pairs={{0,2},{2,4},{4,6},{6,8},{8,10},{10,12},{12,14},{14,16},{16,18},{18... | collective-permute-start | bytes 1572872 | tf_op jit(solution)/shard_map/ppermute | solution.py:13
  9.8 13.0 %collective-permute-start.4 = (bf16[128,2048]{0,1:T(8,128)(2,1)}, bf16[128,2048]{0,1:T(8,128)(2,1)}, u32[]{:S(2)}, u32[]{:S(2)}) collective-permute-start(bf16[128,2048]{0,1:T(8,128)(2,1)} %collective-permute-done.3), channel_id=1, source_target_pairs={{0,2},{2,4},{4,6},{6,8},{8,10},{10,12},{12,14},{14,16},{16,18},{18... | collective-permute-start | bytes 1572872 | tf_op jit(solution)/shard_map/ppermute | solution.py:13
  18.4 28.1 %collective-permute-start.1 = (bf16[128,2048]{1,0:T(8,128)(2,1)}, bf16[128,2048]{1,0:T(8,128)(2,1)}, u32[]{:S(2)}, u32[]{:S(2)}) collective-permute-start(bf16[128,2048]{1,0:T(8,128)(2,1)} %collective-permute-done), channel_id=1, source_target_pairs={{0,2},{2,4},{4,6},{6,8},{8,10},{10,12},{12,14},{14,16},{16,18},{18... | collective-permute-start | bytes 1572872 | tf_op jit(solution)/shard_map/ppermute | solution.py:13
  22.9 30.0 %collective-permute-start.5 = (bf16[128,2048]{0,1:T(8,128)(2,1)}, bf16[128,2048]{0,1:T(8,128)(2,1)}, u32[]{:S(2)}, u32[]{:S(2)}) collective-permute-start(bf16[128,2048]{0,1:T(8,128)(2,1)} %collective-permute-done.4), channel_id=1, source_target_pairs={{0,2},{2,4},{4,6},{6,8},{8,10},{10,12},{12,14},{14,16},{16,18},{18... | collective-permute-start | bytes 1572872 | tf_op jit(solution)/shard_map/ppermute | solution.py:13
  29.8 37.9 %all-to-all-start.2 = ((bf16[2,128,2048]{2,1,0:T(8,128)(2,1)}), bf16[2,128,2048]{2,1,0:T(8,128)(2,1)}, u32[]{:S(2)}, u32[]{:S(2)}) async-start(bf16[2,128,2048]{2,1,0:T(8,128)(2,1)} %bitcast.31), calls=%async_computation.2 | async-start | bytes 2097152 | tf_op jit(solution)/shard_map/all_to_all | solution.py:138
  37.4 17.6 %copy-start.16 = (bf16[128,16,128]{2,0,1:T(8,128)(2,1)S(1)}, bf16[128,16,128]{2,0,1:T(8,128)(2,1)}, u32[]{:S(2)}) copy-start(bf16[128,16,128]{2,0,1:T(8,128)(2,1)} %copy.51) | copy-start | bytes 1572868
  46.5 14.3 %collective-permute-start.2 = (bf16[128,2048]{1,0:T(8,128)(2,1)}, bf16[128,2048]{1,0:T(8,128)(2,1)}, u32[]{:S(2)}, u32[]{:S(2)}) collective-permute-start(bf16[128,2048]{1,0:T(8,128)(2,1)} %collective-permute-done.1), channel_id=1, source_target_pairs={{0,2},{2,4},{4,6},{6,8},{8,10},{10,12},{12,14},{14,16},{16,18},{18... | collective-permute-start | bytes 1572872 | tf_op jit(solution)/shard_map/ppermute | solution.py:13
  67.7 18.1 %all-to-all-start = ((bf16[2,128,2048]{2,1,0:T(8,128)(2,1)}), bf16[2,128,2048]{2,1,0:T(8,128)(2,1)}, u32[]{:S(2)}, u32[]{:S(2)}) async-start(bf16[2,128,2048]{2,1,0:T(8,128)(2,1)} %bitcast.154), calls=%async_computation | async-start | bytes 2097152 | tf_op jit(solution)/shard_map/all_to_all | solution.py:131
  85.8 5.6 %copy-start.8 = (bf16[1,2048,512]{2,1,0:T(8,128)(2,1)S(1)}, bf16[1,2048,512]{2,1,0:T(8,128)(2,1)}, u32[]{:S(2)}) copy-start(bf16[1,2048,512]{2,1,0:T(8,128)(2,1)} %param.17) | copy-start | bytes 6291460
  85.9 5.6 %copy-start.11 = (f32[256,512]{1,0:T(8,128)S(1)}, f32[256,512]{1,0:T(8,128)}, u32[]{:S(2)}) copy-start(f32[256,512]{1,0:T(8,128)} %fusion.12) | copy-start | bytes 1572868
  88.6 2.9 copy-start.32
  88.6 3.8 %copy-start.4 = (bf16[1,2048,512]{2,1,0:T(8,128)(2,1)S(1)}, bf16[1,2048,512]{2,1,0:T(8,128)(2,1)}, u32[]{:S(2)}) copy-start(bf16[1,2048,512]{2,1,0:T(8,128)(2,1)} %param.18) | copy-start | bytes 6291460
  91.5 2.6 copy-start.9
  92.4 18.9 %copy-start.36 = (f32[1,128,1]{1,2,0:T(1,128)S(1)}, f32[1,128,1]{1,2,0:T(1,128)}, u32[]{:S(2)}) copy-start(f32[1,128,1]{1,2,0:T(1,128)} %param.15) | copy-start | bytes 1540
  94.1 17.1 %all-to-all-start.3 = ((bf16[2,128,2048]{2,1,0:T(8,128)(2,1)}), bf16[2,128,2048]{2,1,0:T(8,128)(2,1)}, u32[]{:S(2)}, u32[]{:S(2)}) async-start(bf16[2,128,2048]{2,1,0:T(8,128)(2,1)} %bitcast.157), calls=%async_computation.3 | async-start | bytes 2097152 | tf_op jit(solution)/shard_map/all_to_all | solution.py:142
  118.1 5.2 %copy-start.14 = (bf16[1,128,2048]{1,2,0:T(8,128)(2,1)S(1)}, bf16[1,128,2048]{1,2,0:T(8,128)(2,1)}, u32[]{:S(2)}) copy-start(bf16[1,128,2048]{1,2,0:T(8,128)(2,1)} %copy.45) | copy-start | bytes 1572868
  118.2 5.2 %copy-start.19 = (bf16[128,2048]{0,1:T(8,128)(2,1)S(1)}, bf16[128,2048]{0,1:T(8,128)(2,1)}, u32[]{:S(2)}) copy-start(bf16[128,2048]{0,1:T(8,128)(2,1)} %copy.46) | copy-start | bytes 1572868
  118.2 5.2 %copy-start.25 = (bf16[128,2048]{0,1:T(8,128)(2,1)S(1)}, bf16[128,2048]{0,1:T(8,128)(2,1)}, u32[]{:S(2)}) copy-start(bf16[128,2048]{0,1:T(8,128)(2,1)} %copy.47) | copy-start | bytes 1572868
  118.2 5.2 %copy-start.29 = (bf16[128,2048]{0,1:T(8,128)(2,1)S(1)}, bf16[128,2048]{0,1:T(8,128)(2,1)}, u32[]{:S(2)}) copy-start(bf16[128,2048]{0,1:T(8,128)(2,1)} %copy.48) | copy-start | bytes 1572868
  118.2 5.2 %copy-start.37 = (f32[16,128,512]{1,2,0:T(8,128)S(1)}, f32[16,128,512]{1,2,0:T(8,128)}, u32[]{:S(2)}) copy-start(f32[16,128,512]{1,2,0:T(8,128)} %get-tuple-element.27) | copy-start | bytes 12582916
  128.9 31.4 %collective-permute-start.11 = (bf16[128,2048]{1,0:T(8,128)(2,1)}, bf16[128,2048]{1,0:T(8,128)(2,1)}, u32[]{:S(2)}, u32[]{:S(2)}) collective-permute-start(bf16[128,2048]{1,0:T(8,128)(2,1)} %copy.76), channel_id=1, source_target_pairs={{6,0},{8,2},{10,4},{12,6},{14,8},{16,10},{18,12},{20,14},{22,16},{... | collective-permute-start | bytes 1572872 | tf_op jit(solution)/shard_map/ppermute | solution.py:13
  132.3 29.6 %collective-permute-start.10 = (bf16[128,2048]{1,0:T(8,128)(2,1)}, bf16[128,2048]{1,0:T(8,128)(2,1)}, u32[]{:S(2)}, u32[]{:S(2)}) collective-permute-start(bf16[128,2048]{1,0:T(8,128)(2,1)} %copy.75), channel_id=1, source_target_pairs={{4,0},{6,2},{8,4},{10,6},{12,8},{14,10},{16,12},{18,14},{20,16},{2... | collective-permute-start | bytes 1572872 | tf_op jit(solution)/shard_map/ppermute | solution.py:13
  135.6 26.2 %collective-permute-start.9 = (bf16[128,2048]{1,0:T(8,128)(2,1)}, bf16[128,2048]{1,0:T(8,128)(2,1)}, u32[]{:S(2)}, u32[]{:S(2)}) collective-permute-start(bf16[128,2048]{1,0:T(8,128)(2,1)} %copy.73), channel_id=1, source_target_pairs={{2,0},{4,2},{6,4},{8,6},{10,8},{12,10},{14,12},{16,14},{18,16},{20... | collective-permute-start | bytes 1572872 | tf_op jit(solution)/shard_map/ppermute | solution.py:13
  148.8 18.8 %collective-permute-start.8 = (bf16[128,2048]{0,1:T(8,128)(2,1)}, bf16[128,2048]{0,1:T(8,128)(2,1)}, u32[]{:S(2)}, u32[]{:S(2)}) collective-permute-start(bf16[128,2048]{0,1:T(8,128)(2,1)} %bitcast.184), channel_id=1, source_target_pairs={{6,0},{8,2},{10,4},{12,6},{14,8},{16,10},{18,12},{20,14},{22,16},{... | collective-permute-start | bytes 1572872 | tf_op jit(solution)/shard_map/ppermute | solution.py:13
  152.1 20.1 %collective-permute-start.7 = (bf16[128,2048]{0,1:T(8,128)(2,1)}, bf16[128,2048]{0,1:T(8,128)(2,1)}, u32[]{:S(2)}, u32[]{:S(2)}) collective-permute-start(bf16[128,2048]{0,1:T(8,128)(2,1)} %bitcast.185), channel_id=1, source_target_pairs={{4,0},{6,2},{8,4},{10,6},{12,8},{14,10},{16,12},{18,14},{20,16},{2... | collective-permute-start | bytes 1572872 | tf_op jit(solution)/shard_map/ppermute | solution.py:13
  160.3 46.9 %copy-start.5 = (bf16[16,128,512]{1,2,0:T(8,128)(2,1)S(1)}, bf16[16,128,512]{1,2,0:T(8,128)(2,1)}, u32[]{:S(2)}) copy-start(bf16[16,128,512]{1,2,0:T(8,128)(2,1)} %multiply_convert_fusion.1) | copy-start | bytes 6291460
  160.3 46.9 %copy-start.17 = (bf16[128,16,128]{2,0,1:T(8,128)(2,1)S(1)}, bf16[128,16,128]{2,0,1:T(8,128)(2,1)}, u32[]{:S(2)}) copy-start(bf16[128,16,128]{2,0,1:T(8,128)(2,1)} %copy.51) | copy-start | bytes 1572868
  160.3 46.9 %copy-start.21 = (bf16[128,16,128]{2,0,1:T(8,128)(2,1)S(1)}, bf16[128,16,128]{2,0,1:T(8,128)(2,1)}, u32[]{:S(2)}) copy-start(bf16[128,16,128]{2,0,1:T(8,128)(2,1)} %copy.52) | copy-start | bytes 1572868
  160.3 47.0 %copy-start.23 = (bf16[128,16,128]{2,0,1:T(8,128)(2,1)S(1)}, bf16[128,16,128]{2,0,1:T(8,128)(2,1)}, u32[]{:S(2)}) copy-start(bf16[128,16,128]{2,0,1:T(8,128)(2,1)} %copy.53) | copy-start | bytes 1572868
  160.3 47.0 %copy-start.27 = (bf16[128,16,128]{2,0,1:T(8,128)(2,1)S(1)}, bf16[128,16,128]{2,0,1:T(8,128)(2,1)}, u32[]{:S(2)}) copy-start(bf16[128,16,128]{2,0,1:T(8,128)(2,1)} %copy.54) | copy-start | bytes 1572868
  160.3 11.9 %collective-permute-start.6 = (bf16[128,2048]{0,1:T(8,128)(2,1)}, bf16[128,2048]{0,1:T(8,128)(2,1)S(1)}, u32[]{:S(2)}, u32[]{:S(2)}) collective-permute-start(bf16[128,2048]{0,1:T(8,128)(2,1)} %bitcast.186), channel_id=1, source_target_pairs={{2,0},{4,2},{6,4},{8,6},{10,8},{12,10},{14,12},{16,14},{18,16},{20... | collective-permute-start | bytes 1572872 | tf_op jit(solution)/shard_map/ppermute | solution.py:13
  163.9 50.3 %copy-start.12 = (bf16[128,2048]{1,0:T(8,128)(2,1)}, bf16[128,2048]{1,0:T(8,128)(2,1)S(1)}, u32[]{:S(2)}) copy-start(bf16[128,2048]{1,0:T(8,128)(2,1)S(1)} %add_convert_fusion) | copy-start | bytes 1572868
  163.9 20.2 %collective-permute-start.15 = (bf16[128,2048]{1,0:T(8,128)(2,1)S(1)}, bf16[128,2048]{1,0:T(8,128)(2,1)S(1)}, u32[]{:S(2)}, u32[]{:S(2)}) collective-permute-start(bf16[128,2048]{1,0:T(8,128)(2,1)S(1)} %add_convert_fusion), channel_id=1, source_target_pairs={{0,2},{2,4},{4,6},{6,8},{8,10},{10,12},{12,14},{14,16},{16,18},{18... | collective-permute-start | bytes 1572872 | tf_op jit(solution)/shard_map/ppermute | solution.py:13
  174.0 0.8 copy-start.1
  174.8 21.0 %collective-permute-start.12 = (bf16[128,2048]{0,1:T(8,128)(2,1)S(1)}, bf16[128,2048]{0,1:T(8,128)(2,1)S(1)}, u32[]{:S(2)}, u32[]{:S(2)}) collective-permute-start(bf16[128,2048]{0,1:T(8,128)(2,1)S(1)} %fusion.50), channel_id=1, source_target_pairs={{0,2},{2,4},{4,6},{6,8},{8,10},{10,12},{12,14},{14,16},{16,18},{18... | collective-permute-start | bytes 1572872 | tf_op jit(solution)/shard_map/ppermute | solution.py:13
  184.1 18.1 %collective-permute-start.16 = (bf16[128,2048]{1,0:T(8,128)(2,1)S(1)}, bf16[128,2048]{1,0:T(8,128)(2,1)S(1)}, u32[]{:S(2)}, u32[]{:S(2)}) collective-permute-start(bf16[128,2048]{1,0:T(8,128)(2,1)S(1)} %collective-permute-done.15), channel_id=1, source_target_pairs={{0,2},{2,4},{4,6},{6,8},{8,10},{10,12},{12,14},{14,16},{16,18},{18... | collective-permute-start | bytes 1572872 | tf_op jit(solution)/shard_map/ppermute | solution.py:13
  195.8 13.1 %copy-start.33 = (bf16[128,2048]{0,1:T(8,128)(2,1)}, bf16[128,2048]{0,1:T(8,128)(2,1)S(1)}, u32[]{:S(2)}) copy-start(bf16[128,2048]{0,1:T(8,128)(2,1)S(1)} %collective-permute-done.12) | copy-start | bytes 1572868
  195.8 13.1 %collective-permute-start.13 = (bf16[128,2048]{0,1:T(8,128)(2,1)S(1)}, bf16[128,2048]{0,1:T(8,128)(2,1)}, u32[]{:S(2)}, u32[]{:S(2)}) collective-permute-start(bf16[128,2048]{0,1:T(8,128)(2,1)S(1)} %collective-permute-done.12), channel_id=1, source_target_pairs={{0,2},{2,4},{4,6},{6,8},{8,10},{10,12},{12,14},{14,16},{16,18},{18... | collective-permute-start | bytes 1572872 | tf_op jit(solution)/shard_map/ppermute | solution.py:13
  202.2 11.9 %collective-permute-start.17 = (bf16[128,2048]{1,0:T(8,128)(2,1)S(1)}, bf16[128,2048]{1,0:T(8,128)(2,1)S(1)}, u32[]{:S(2)}, u32[]{:S(2)}) collective-permute-start(bf16[128,2048]{1,0:T(8,128)(2,1)S(1)} %collective-permute-done.16), channel_id=1, source_target_pairs={{0,2},{2,4},{4,6},{6,8},{8,10},{10,12},{12,14},{14,16},{16,18},{18... | collective-permute-start | bytes 1572872 | tf_op jit(solution)/shard_map/ppermute | solution.py:13
  208.9 14.5 %collective-permute-start.14 = (bf16[128,2048]{0,1:T(8,128)(2,1)}, bf16[128,2048]{0,1:T(8,128)(2,1)}, u32[]{:S(2)}, u32[]{:S(2)}) collective-permute-start(bf16[128,2048]{0,1:T(8,128)(2,1)} %collective-permute-done.13), channel_id=1, source_target_pairs={{0,2},{2,4},{4,6},{6,8},{8,10},{10,12},{12,14},{14,16},{16,18},{18... | collective-permute-start | bytes 1572872 | tf_op jit(solution)/shard_map/ppermute | solution.py:13
  219.7 3.6 %copy-start.2 = (bf16[128,2048]{0,1:T(8,128)(2,1)S(1)}, bf16[128,2048]{0,1:T(8,128)(2,1)}, u32[]{:S(2)}) copy-start(bf16[128,2048]{0,1:T(8,128)(2,1)} %copy-done.1) | copy-start | bytes 1572868
  219.7 3.6 %copy-start.34 = (bf16[128,2048]{0,1:T(8,128)(2,1)S(1)}, bf16[128,2048]{0,1:T(8,128)(2,1)}, u32[]{:S(2)}) copy-start(bf16[128,2048]{0,1:T(8,128)(2,1)} %copy-done.33) | copy-start | bytes 1572868
  224.8 1.0 copy-start.18
  224.8 1.2 copy-start.22
  224.8 1.3 copy-start.24
  224.9 1.5 copy-start.28
  224.9 1.6 copy-start.31
  224.9 3.0 %copy-start.38 = (f32[16,128,512]{1,2,0:T(8,128)S(1)}, f32[16,128,512]{1,2,0:T(8,128)}, u32[]{:S(2)}) copy-start(f32[16,128,512]{1,2,0:T(8,128)} %get-tuple-element.27) | copy-start | bytes 12582916
  227.8 1.4 copy-start.15
  227.8 1.5 copy-start.20
  227.8 1.5 copy-start.26
  227.9 1.5 copy-start.30
  230.4 9.0 %copy-start.6 = (bf16[16,128,128]{2,1,0:T(8,128)(2,1)}, bf16[16,128,128]{2,1,0:T(8,128)(2,1)S(1)}, u32[]{:S(2)}) copy-start(bf16[16,128,128]{2,1,0:T(8,128)(2,1)S(1)} %fusion.32) | copy-start | bytes 1572868
  231.9 18.0 %all-to-all-start.4 = ((bf16[2,128,2048]{2,1,0:T(8,128)(2,1)}), bf16[2,128,2048]{2,1,0:T(8,128)(2,1)}, u32[]{:S(2)}, u32[]{:S(2)}) async-start(bf16[2,128,2048]{2,1,0:T(8,128)(2,1)} %bitcast.155), calls=%async_computation.4 | async-start | bytes 2097152 | tf_op jit(solution)/shard_map/all_to_all | solution.py:230
  249.9 8.3 %copy-start.10 = (f32[256,512]{1,0:T(8,128)S(1)}, f32[256,512]{1,0:T(8,128)}, u32[]{:S(2)}) copy-start(f32[256,512]{1,0:T(8,128)} %copy-done.9) | copy-start | bytes 1572868
  249.9 19.3 %all-to-all-start.1 = ((bf16[2,128,2048]{2,1,0:T(8,128)(2,1)}), bf16[2,128,2048]{2,1,0:T(8,128)(2,1)}, u32[]{:S(2)}, u32[]{:S(2)}) async-start(bf16[2,128,2048]{2,1,0:T(8,128)(2,1)} %bitcast.168), calls=%async_computation.1 | async-start | bytes 2097152 | tf_op jit(solution)/shard_map/all_to_all | solution.py:135
  262.6 16.7 %copy-start.3 = (bf16[128,2048]{0,1:T(8,128)(2,1)S(1)}, bf16[128,2048]{0,1:T(8,128)(2,1)}, u32[]{:S(2)}) copy-start(bf16[128,2048]{0,1:T(8,128)(2,1)} %copy-done.1) | copy-start | bytes 1572868
  269.2 18.7 %all-to-all-start.5 = ((bf16[2,128,2048]{2,1,0:T(8,128)(2,1)}), bf16[2,128,2048]{2,1,0:T(8,128)(2,1)}, u32[]{:S(2)}, u32[]{:S(2)}) async-start(bf16[2,128,2048]{2,1,0:T(8,128)(2,1)} %bitcast.167), calls=%async_computation.5 | async-start | bytes 2097152 | tf_op jit(solution)/shard_map/all_to_all | solution.py:234
  274.7 5.6 %copy-start.7 = (bf16[16,128,128]{2,1,0:T(8,128)(2,1)S(1)}, bf16[16,128,128]{2,1,0:T(8,128)(2,1)}, u32[]{:S(2)}) copy-start(bf16[16,128,128]{2,1,0:T(8,128)(2,1)} %copy-done.6) | copy-start | bytes 1572868
where the time goes:
time: 294 us; the launch traced here: 290 us
  starting transfers between devices  103 us (35%)
  matrix products  59.9 us (20%)
  local copies, waits for them, and re-layouts  58.4 us (20%)
  waiting for transfers between devices  50.3 us (17%)
  other arithmetic  15 us (5%)
  between operations  3.33 us (1%)
    ppermute x18, starting transfers between devices, passed_along(): return lax.ppermute(x, axis, pairs)  76.3 us
    all_to_all x1, waiting for transfers between devices, local(): lax.all_to_all(send_rows, 'exp', split_axis=0, concat_axis=0, tiled=True)  10.9 us
    all_to_all x1, waiting for transfers between devices, local(): lax.all_to_all(send_tans, 'exp', split_axis=0, concat_axis=0, tiled=True)  10.5 us
    all_to_all x1, waiting for transfers between devices, local(): lax.all_to_all(route_grad.reshape(got_cots.shape), 'exp', split_axis=0, c...  10.2 us
    unnamed x83, local copies, waits for them, and re-layouts  9.88 us
    slice x4, local copies, waits for them, and re-layouts, local(): key_terms[offset].astype(jnp.bfloat16)  8.68 us
    dot_general x3, matrix products, combine(): jnp.dot(slot_table.T, returned.reshape(-1, returned.shape[2]), preferred_...  7.43 us
    all_to_all x1, waiting for transfers between devices, local(): lax.all_to_all(expert_tan.reshape(got_tans.shape), 'exp', split_axis=0, c...  7.41 us
  transfers between devices with their start and end apart: 24, of which 6 were waited for; matrix products, arithmetic and copies ran while one was open for 33% of the time, Pallas kernels for 0%

commit v1 on v0

v1 whole, which is shorter than its diff:
```python
import functools

import jax
import jax.numpy as jnp
from jax import lax
from jax.experimental import pallas as pl
from jax.experimental.pallas import tpu as pltpu
from jax.sharding import PartitionSpec as P

HEADS = 16
WIN = 4
PAIR = 2
SIDE = 128
FAR = 1e30
BF = jnp.bfloat16
F32 = jnp.float32
VMEM = pl.BlockSpec(memory_space=pltpu.VMEM)
SMEM = pl.BlockSpec(memory_space=pltpu.SMEM)
ANY = pl.BlockSpec(memory_space=pl.ANY)


def moved(x, by):
    devices = lax.axis_size("ctx")
    pairs = [(i, i + by) for i in range(devices) if 0 <= i + by < devices]
    return lax.ppermute(x, "ctx", pairs)


def swapped(x):
    return lax.ppermute(x, "ctx", [(i, i ^ 1) for i in range(lax.axis_size("ctx"))])


def crossed(x):
    return lax.ppermute(x, "exp", [(0, 1), (1, 0)])


def nn(a, b):
    return lax.dot_general(a, b, (((1,), (0,)), ((), ())), preferred_element_type=F32)


def nt(a, b):
    return lax.dot_general(a, b, (((1,), (1,)), ((), ())), preferred_element_type=F32)


def tn(a, b):
    return lax.dot_general(a, b, (((0,), (0,)), ((), ())), preferred_element_type=F32)


def silu_parts(gate_pre):
    sigmoid_val = jax.nn.sigmoid(gate_pre)
    return (gate_pre * sigmoid_val, sigmoid_val * (1.0 + gate_pre * (1.0 - sigmoid_val)))


def lanes_of(rows):
    return lax.broadcasted_iota(jnp.int32, (rows, SIDE), 1)


def put_side(side, lanes, head, column):
    first = column.astype(BF).astype(F32)
    second = (column - first).astype(BF).astype(F32)
    third = column - first - second
    for at, term in ((8, first), (16, second), (24, third)):
        side = jnp.where(lanes == at + head, term, side)
    return side


def get_side(side, lanes, head):
    mine = (lanes == 8 + head) | (lanes == 16 + head) | (lanes == 24 + head)
    return jnp.sum(jnp.where(mine, side, 0.0), axis=1, keepdims=True)


def hidden_by(flag):
    return (1.0 - flag) * FAR


def call(kernel, outs, scratch=(), limit=40, **kw):
    return pl.pallas_call(
        kernel,
        out_shape=outs,
        scratch_shapes=list(scratch),
        compiler_params=pltpu.CompilerParams(vmem_limit_bytes=limit * 1024 * 1024),
        **kw,
    )


def window_refs(far, near, own, rows, width):
    return {
        -3: (far, 0, 0, width),
        -2: (near, 0, 0, width),
        -1: (near, rows, 0, width),
        0: (own, 0, width, 2 * width),
        1: (own, rows, width, 2 * width),
    }


def stacked(window, js, rows, at, size, kind):
    return jnp.concatenate(
        [
            window[j][0][
                pl.ds(window[j][1], rows), pl.ds(pl.multiple_of(window[j][kind] + at, size), size)
            ]
            for j in js
        ],
        axis=0,
    )


def attend_kernel(size, far, near, own, me, keep, send, qx):
    rows, width = far.shape[0], far.shape[1] // 2
    heads = width // size
    scale = size ** (-0.5)
    core = me[0]
    window = window_refs(far, near, own, rows, width)
    lanes = lanes_of(rows)
    causal = lax.broadcasted_iota(jnp.int32, (rows, rows), 0) >= lax.broadcasted_iota(
        jnp.int32, (rows, rows), 1
    )
    qx[:, 0:width] = own[:, 0:width]
    for block in range(PAIR):
        flags = own[block * rows : (block + 1) * rows, 3 * width :].astype(F32)
        biases = [hidden_by(flags[:, w - 1 : w]) for w in range(1, WIN)]
        js = list(range(block - WIN + 1, block + 1))

        def one(head, side):
            at = head * size
            q = own[pl.ds(block * rows, rows), pl.ds(pl.multiple_of(at, size), size)]
            scores = nt(q, stacked(window, js, rows, at, size, 2)) * scale
            parts = [
                scores[:, n * rows : (n + 1) * rows] - biases[block - j - 1]
                if j < block
                else jnp.where(causal, scores[:, n * rows : (n + 1) * rows], -FAR)
                for n, j in enumerate(js)
            ]
            scores = jnp.concatenate(parts, axis=1)
            top = jnp.max(scores, axis=1, keepdims=True)
            weights = jnp.exp(scores - top)
            total = jnp.sum(weights, axis=1, keepdims=True)
            probs = (weights / total).astype(BF)
            out = nn(probs, stacked(window, js, rows, at, size, 3)).astype(BF)
            place = pl.ds(pl.multiple_of(at, size), size)

            @pl.when(core == block)
            def _():
                keep[:, place] = out

            @pl.when(core != block)
            def _():
                send[:, place] = out

            return put_side(side, lanes, head, top + jnp.log(total))

        side = lax.fori_loop(0, heads, one, jnp.where(lanes < WIN - 1, flags, 0.0))
        qx[block * rows : (block + 1) * rows, width:] = side.astype(BF)


def grads_kernel(size, far, near, own, qfb, qnb, qo, qna, qfa, cfb, cnb, co, cna, cfa, grads, tans):
    rows, width = far.shape[0], far.shape[1] // 2
    heads = width // size
    scale = size ** (-0.5)
    window = window_refs(far, near, own, rows, width)
    lanes = lanes_of(rows)
    causal = lax.broadcasted_iota(jnp.int32, (rows, rows), 0) >= lax.broadcasted_iota(
        jnp.int32, (rows, rows), 1
    )
    places = {-3: (0, 0), -2: (1, 0), -1: (1, 1), 0: (2, 0), 1: (2, 1), 2: (3, 0), 3: (3, 1), 4: (4, 0)}
    q_refs, c_refs = (qfb, qnb, qo, qna, qfa), (cfb, cnb, co, cna, cfa)

    def one(head, carry):
        at = pl.multiple_of(head * size, size)
        key_sums, value_sums = {}, {}
        kept = {}

        def added(sums, js, terms):
            for n, j in enumerate(js):
                term = terms[n * rows : (n + 1) * rows]
                sums[j] = sums[j] + term if j in sums else term

        for t in range(1 - WIN, WIN + 1):
            ref, half = places[t]
            here = pl.ds(half * rows, rows)
            q = q_refs[ref][here, pl.ds(at, size)]
            cot = c_refs[ref][here, pl.ds(at, size)]
            q_side = q_refs[ref][here, width:].astype(F32)
            c_side = c_refs[ref][here, width:].astype(F32)
            level = get_side(q_side, lanes, head)
            delta = get_side(c_side, lanes, head)
            js = list(range(max(1 - WIN, t - WIN + 1), min(1, t) + 1))
            keys = stacked(window, js, rows, head * size, size, 2)
            values = stacked(window, js, rows, head * size, size, 3)
            scores = nt(q, keys) * scale
            parts = []
            for n, j in enumerate(js):
                part = scores[:, n * rows : (n + 1) * rows]
                if j < t:
                    w = t - j
                    part = part - (level + hidden_by(q_side[:, w - 1 : w]))
                else:
                    part = jnp.where(causal, part - level, -FAR)
                parts.append(part)
            probs = jnp.exp(jnp.concatenate(parts, axis=1))
            probs_low = probs.astype(BF)
            score_grad = (probs * (nt(cot, values) - delta)).astype(BF)
            added(key_sums, js, tn(score_grad, q))
            added(value_sums, js, tn(probs_low, cot))
            if 0 <= t < PAIR:
                grad_q = (nn(score_grad, keys) * scale).astype(BF)
                grads[pl.ds(t * rows, rows), pl.ds(at, size)] = grad_q
                kept[t] = (js, q, keys, values, probs, probs_low, grad_q)
        key_grads = {j: (key_sums[j] * scale).astype(BF) for j in key_sums}
        value_grads = {j: value_sums[j].astype(BF) for j in value_sums}
        for t in range(PAIR):
            js, q, keys, values, probs, probs_low, grad_q = kept[t]
            here = pl.ds(t * rows, rows)
            grads[here, pl.ds(pl.multiple_of(width + at, size), size)] = key_grads[t]
            grads[here, pl.ds(pl.multiple_of(2 * width + at, size), size)] = value_grads[t]
            tan_keys = jnp.concatenate([key_grads[j] for j in js], axis=0)
            tan_values = jnp.concatenate([value_grads[j] for j in js], axis=0)
            score_tan = (nt(grad_q, keys) + nt(q, tan_keys)) * scale
            mean = jnp.sum(probs * score_tan, axis=1, keepdims=True)
            prob_tan = (probs * (score_tan - mean)).astype(BF)
            tans[here, pl.ds(at, size)] = (nn(prob_tan, values) + nn(probs_low, tan_values)).astype(BF)
        return carry

    lax.fori_loop(0, heads, one, 0)


def cot_sides(size, cot, attended, cx):
    rows, width = cot.shape[0], cot.shape[1] // PAIR
    lanes = lanes_of(rows)
    for half in range(PAIR):
        side = jnp.zeros((rows, SIDE), F32)
        for head in range(width // size):
            here = slice(half * width + head * size, half * width + (head + 1) * size)
            delta = jnp.sum(cot[:, here].astype(F32) * attended[:, here].astype(F32), axis=1, keepdims=True)
            side = put_side(side, lanes, head, delta)
        cx[half, :, 0:width] = cot[:, half * width : (half + 1) * width]
        cx[half, :, width:] = side.astype(BF)


def in_order(core, kept, got):
    return jnp.where(
        core == 0, jnp.concatenate([kept, got], axis=1), jnp.concatenate([got, kept], axis=1)
    )


def load_weights(core, whole, halves, buffer, sems):
    depth = halves[0].shape[0]
    copies = [
        pltpu.make_async_copy(whole, buffer.at[0], sems.at[0]),
        pltpu.make_async_copy(halves[0], buffer.at[1, pl.ds(core * depth, depth)], sems.at[1]),
        pltpu.make_async_copy(halves[1], buffer.at[1, pl.ds((1 - core) * depth, depth)], sems.at[2]),
    ]
    for copy in copies:
        copy.start()
    return [copies[:1], copies[1:]]


def ready(copies):
    for copy in copies:
        copy.wait()


def hidden_grad_kernel(me, cot, down, down_x, down_s, out, buffer, sems):
    loads = load_weights(me[0], down, (down_x, down_s), buffer, sems)
    units = down.shape[0]
    for e in range(2):
        ready(loads[e])
        out[:, e * units : (e + 1) * units] = nt(cot[...], buffer[e])


def expert_kernel(
    size, me, keep, got, cot, picks, hidden_grad, gate, gate_x, gate_s, up, up_x, up_s,
    cx, hidden, slope_up, active, gates, ups, sems,
):
    core = me[0]
    gate_loads = load_weights(core, gate, (gate_x, gate_s), gates, sems.at[0])
    up_loads = load_weights(core, up, (up_x, up_s), ups, sems.at[1])
    units = gate.shape[1]
    rows_in = in_order(core, keep[...], got[...])
    summed = None
    for e in range(2):
        here = slice(e * units, (e + 1) * units)
        chosen = picks[:, e : e + 1]
        ready(gate_loads[e])
        gate_pre = nn(rows_in, gates[e])
        ready(up_loads[e])
        up_value = nn(rows_in, ups[e])
        activated, slope = silu_parts(gate_pre)
        activated = activated * chosen
        slope = slope * up_value * chosen
        hidden[:, here] = (activated * up_value).astype(BF)
        slope_up[:, here] = slope
        active[:, here] = activated
        back = hidden_grad[:, here]
        term = nt((back * slope).astype(BF), gates[e]) + nt((back * activated).astype(BF), ups[e])
        summed = term if summed is None else summed + term
    weight = picks[:, 2:3]
    attn_cot = (cot[...].astype(F32) + summed.astype(BF).astype(F32) * weight).astype(BF)
    cot_sides(size, attn_cot, rows_in, cx)


def layer_kernel(me, keep, got, hidden, picks, down, down_x, down_s, out, buffer, sems):
    core = me[0]
    loads = load_weights(core, down, (down_x, down_s), buffer, sems)
    units = down.shape[0]
    rows_in = in_order(core, keep[...], got[...]).astype(F32)
    ready(loads[0])
    summed = nn(hidden[:, 0:units], buffer[0])
    ready(loads[1])
    summed = summed + nn(hidden[:, units:], buffer[1])
    out[...] = (rows_in + summed.astype(BF).astype(F32) * picks[:, 2:3]).astype(BF)


def tangent_kernel(
    me, keep, got, slope_up, active, picks, gate, gate_x, gate_s, up, up_x, up_s, down, down_x, down_s,
    out, gates, ups, downs, sems,
):
    core = me[0]
    gate_loads = load_weights(core, gate, (gate_x, gate_s), gates, sems.at[0])
    up_loads = load_weights(core, up, (up_x, up_s), ups, sems.at[1])
    down_loads = load_weights(core, down, (down_x, down_s), downs, sems.at[2])
    units = gate.shape[1]
    rows_in = in_order(core, keep[...], got[...])
    summed = None
    for e in range(2):
        here = slice(e * units, (e + 1) * units)
        ready(gate_loads[e])
        gate_tan = nn(rows_in, gates[e])
        ready(up_loads[e])
        up_tan = nn(rows_in, ups[e])
        hidden = (slope_up[:, here] * gate_tan + active[:, here] * up_tan).astype(BF)
        ready(down_loads[e])
        term = nn(hidden, downs[e])
        summed = term if summed is None else summed + term
    out[...] = (rows_in.astype(F32) + summed.astype(BF).astype(F32) * picks[:, 2:3]).astype(BF)


def exchanged_weights(core, w_gate, w_up, w_down):
    halves = []
    for matrix in (w_down, w_gate, w_up):
        depth = matrix.shape[0] // 2
        over = crossed(lax.dynamic_slice_in_dim(matrix, core * depth, depth, 0))
        halves.append((over, swapped(over)))
    return halves


def like(*shape, kind=BF):
    return jax.ShapeDtypeStruct(shape, kind)


class PairExperts:
    def __init__(self, core, upstream, route_ids, route_weights, w_gate, w_up, w_down):
        own = lax.axis_index("exp")
        self.me = core.reshape(1)
        self.upstream = upstream
        mine = (route_ids == own).astype(F32)
        self.picks = jnp.concatenate([mine, 1.0 - mine, route_weights], axis=1)
        down, gate, up = exchanged_weights(core, w_gate, w_up, w_down)
        self.gate, self.up, self.down = ((w_gate,) + gate, (w_up,) + up, (w_down,) + down)
        rows, wide = upstream.shape
        units = w_gate.shape[1]
        self.rows, self.wide, self.units = rows, wide, units
        self.tall = pltpu.VMEM((2, wide, units), BF)
        self.flat = pltpu.VMEM((2, units, wide), BF)
        self.hidden_grad = call(
            hidden_grad_kernel,
            like(rows, 2 * units, kind=F32),
            [self.flat, pltpu.SemaphoreType.DMA((3,))],
            in_specs=[SMEM, VMEM, ANY, ANY, ANY],
            out_specs=VMEM,
        )(self.me, upstream, *self.down)

    def forward(self, size, keep, got):
        rows, wide, units = self.rows, self.wide, self.units
        cx, hidden, self.slope_up, self.active = call(
            functools.partial(expert_kernel, size),
            (
                like(PAIR, rows, wide // PAIR + SIDE),
                like(rows, 2 * units),
                like(rows, 2 * units, kind=F32),
                like(rows, 2 * units, kind=F32),
            ),
            [self.tall, self.tall, pltpu.SemaphoreType.DMA((2, 3))],
            in_specs=[SMEM] + [VMEM] * 5 + [ANY] * 6,
            out_specs=(VMEM,) * 4,
        )(self.me, keep, got, self.upstream, self.picks, self.hidden_grad, *self.gate, *self.up)
        layer_out = call(
            layer_kernel,
            like(rows, wide),
            [self.flat, pltpu.SemaphoreType.DMA((3,))],
            in_specs=[SMEM] + [VMEM] * 4 + [ANY] * 3,
            out_specs=VMEM,
        )(self.me, keep, got, hidden, self.picks, *self.down)
        return cx, layer_out

    def tangent(self, keep, got):
        return call(
            tangent_kernel,
            like(self.rows, self.wide),
            [self.tall, self.tall, self.flat, pltpu.SemaphoreType.DMA((3, 3))],
            in_specs=[SMEM] + [VMEM] * 5 + [ANY] * 9,
            out_specs=VMEM,
        )(self.me, keep, got, self.slope_up, self.active, self.picks, *self.gate, *self.up, *self.down)


def routing_table(route_rows, experts, capacity):
    flat_ids = route_rows.reshape(-1)
    one_hot = (flat_ids[:, None] == jnp.arange(experts, dtype=jnp.int32)[None, :]).astype(jnp.int32)
    slot_rank = jnp.sum((jnp.cumsum(one_hot, axis=0) - one_hot) * one_hot, axis=1)
    target = flat_ids * capacity + slot_rank
    return (jnp.arange(experts * capacity, dtype=jnp.int32)[:, None] == target[None, :]).astype(
        jnp.bfloat16
    )


def dispatch(slot_table, row_block, routes, experts):
    pair_rows = jnp.repeat(row_block, routes, axis=0)
    sent = jnp.dot(slot_table, pair_rows, preferred_element_type=jnp.float32).astype(jnp.bfloat16)
    return sent.reshape(experts, -1, row_block.shape[1])


def combine(slot_table, returned, weights):
    rows_here, routes = weights.shape
    pair_vals = jnp.dot(
        slot_table.T, returned.reshape(-1, returned.shape[2]), preferred_element_type=jnp.float32
    )
    return jnp.sum(pair_vals.reshape(rows_here, routes, -1) * weights[:, :, None], axis=1)


def expert_forward(row_block, gate_matrix, up_matrix, down_matrix):
    gate_pre = jnp.dot(row_block, gate_matrix, preferred_element_type=jnp.float32)
    up_value = jnp.dot(row_block, up_matrix, preferred_element_type=jnp.float32)
    activated, slope_val = silu_parts(gate_pre)
    hidden = (activated * up_value).astype(jnp.bfloat16)
    return (
        jnp.dot(hidden, down_matrix, preferred_element_type=jnp.float32).astype(jnp.bfloat16),
        gate_pre,
        up_value,
    )


def expert_backward(cot_block, gate_pre, up_value, gate_matrix, up_matrix, down_matrix):
    hidden_grad = jnp.dot(cot_block, down_matrix.T, preferred_element_type=jnp.float32)
    activated, slope_val = silu_parts(gate_pre)
    gate_grad = (hidden_grad * up_value * slope_val).astype(jnp.bfloat16)
    up_grad = (hidden_grad * activated).astype(jnp.bfloat16)
    summed = jnp.dot(gate_grad, gate_matrix.T, preferred_element_type=jnp.float32) + jnp.dot(
        up_grad, up_matrix.T, preferred_element_type=jnp.float32
    )
    return summed.astype(jnp.bfloat16)


def expert_tangent(tan_block, gate_pre, up_value, gate_matrix, up_matrix, down_matrix):
    gate_tan = jnp.dot(tan_block, gate_matrix, preferred_element_type=jnp.float32)
    up_tan = jnp.dot(tan_block, up_matrix, preferred_element_type=jnp.float32)
    activated, slope_val = silu_parts(gate_pre)
    hidden_tan = (slope_val * gate_tan * up_value + activated * up_tan).astype(jnp.bfloat16)
    return jnp.dot(hidden_tan, down_matrix, preferred_element_type=jnp.float32).astype(jnp.bfloat16)


class RoutedExperts:
    def __init__(self, core, upstream, route_ids, route_weights, w_gate, w_up, w_down):
        rows, routes = route_ids.shape
        self.experts = lax.axis_size("exp")
        self.routes = routes
        capacity = min(rows, 2 * rows * routes // self.experts)
        self.core, self.upstream, self.weights = core, upstream, route_weights
        self.matrices = (w_gate, w_up, w_down)
        self.table = routing_table(route_ids, self.experts, capacity)
        self.got_cots = self.sent(upstream)

    def across(self, x):
        return lax.all_to_all(x, "exp", split_axis=0, concat_axis=0, tiled=True)

    def sent(self, x):
        return self.across(dispatch(self.table, x, self.routes, self.experts))

    def returned(self, x):
        back = self.across(x.reshape(self.got_cots.shape))
        return combine(self.table, back, self.weights)

    def forward(self, size, keep, got):
        attended = in_order(self.core, keep, got)
        rows, wide = attended.shape
        got_rows = self.sent(attended).reshape(-1, wide)
        expert_out, self.gate_pre, self.up_value = expert_forward(got_rows, *self.matrices)
        route_grad = expert_backward(
            self.got_cots.reshape(-1, wide), self.gate_pre, self.up_value, *self.matrices
        )
        attn_cot = (self.upstream.astype(F32) + self.returned(route_grad)).astype(BF)
        layer_out = (attended.astype(F32) + self.returned(expert_out)).astype(BF)
        cx = call(
            functools.partial(cot_sides, size),
            like(PAIR, rows, wide // PAIR + SIDE),
            in_specs=[VMEM, VMEM],
            out_specs=VMEM,
        )(attn_cot, attended)
        return cx, layer_out

    def tangent(self, keep, got):
        rows = in_order(self.core, keep, got)
        got_rows = self.sent(rows).reshape(-1, rows.shape[1])
        out = expert_tangent(got_rows, self.gate_pre, self.up_value, *self.matrices)
        return (rows.astype(F32) + self.returned(out)).astype(BF)


def paired(core, kept, got):
    return jnp.where(
        core == 0, jnp.concatenate([kept, got], axis=0), jnp.concatenate([got, kept], axis=0)
    )


def of_core(parts, core):
    return jnp.where(core == 0, parts[0], parts[1])


def neighbours(x, rows):
    return (
        moved(x[rows:], 2 * PAIR),
        moved(x, PAIR),
        moved(x, -PAIR),
        moved(x[:rows], -2 * PAIR),
    )


def local(query, key, value, cotangent, route_ids, route_weights, block_mask, w_gate, w_up, w_down):
    rows, wide = query.shape[1:]
    width = wide // PAIR
    size = wide // HEADS
    index = lax.axis_index("ctx")
    core = index % PAIR
    me = core.reshape(1)

    seen = (block_mask[0, 0] == 1) & (index >= jnp.arange(1, WIN, dtype=jnp.int32))
    flags = jnp.pad(seen.astype(BF), (0, SIDE - WIN + 1))
    flags = jnp.broadcast_to(flags[None], (rows, SIDE))

    def half(at):
        return [x[0][:, at * width : (at + 1) * width] for x in (query, key, value)] + [flags]

    first, second = (jnp.concatenate(half(at), axis=1) for at in range(PAIR))
    own = paired(core, of_core((first, second), core), swapped(of_core((second, first), core)))
    sent = own[:, width : 3 * width]
    near, far = moved(sent, PAIR), moved(sent[rows:], 2 * PAIR)

    pair = lax.axis_size("exp") == 2 and route_ids.shape[2] == 1
    experts = (PairExperts if pair else RoutedExperts)(
        core, cotangent[0], route_ids[0], route_weights[0], w_gate[0], w_up[0], w_down[0]
    )

    keep, send, qx = call(
        functools.partial(attend_kernel, size),
        (like(rows, width), like(rows, width), like(PAIR * rows, width + SIDE)),
        in_specs=[VMEM, VMEM, VMEM, SMEM],
        out_specs=(VMEM,) * 3,
    )(far, near, own, me)
    got = swapped(send)
    qfb, qnb, qna, qfa = neighbours(qx, rows)

    cx, layer_out = experts.forward(size, keep, got)
    co = paired(core, of_core((cx[0], cx[1]), core), swapped(of_core((cx[1], cx[0]), core)))
    cfb, cnb, cna, cfa = neighbours(co, rows)

    grads, tans = call(
        functools.partial(grads_kernel, size),
        (like(PAIR * rows, 3 * width), like(PAIR * rows, width)),
        in_specs=[VMEM] * 13,
        out_specs=(VMEM,) * 2,
    )(far, near, own, qfb, qnb, qx, qna, qfa, cfb, cnb, co, cna, cfa)

    def mine(x):
        return of_core((x[:rows], x[rows:]), core)

    def others(x):
        return of_core((x[rows:], x[:rows]), core)

    tangent_out = experts.tangent(mine(tans), swapped(others(tans)))
    kept, got = mine(grads), swapped(others(grads))
    outs = [
        in_order(core, kept[:, at : at + width], got[:, at : at + width])
        for at in range(0, 3 * width, width)
    ]
    return (layer_out[None], *(x[None] for x in outs), tangent_out[None])


def solution(mesh):
    return jax.shard_map(
        local,
        mesh=mesh,
        in_specs=(
            P("exp", "ctx", None),
            P("exp", "ctx", None),
            P("exp", "ctx", None),
            P("exp", "ctx", None),
            P("exp", "ctx", None),
            P("exp", "ctx", None),
            P("exp", "ctx", None),
            P("exp", None, None),
            P("exp", None, None),
            P("exp", None, None),
        ),
        out_specs=(
            P("exp", "ctx", None),
            P("exp", "ctx", None),
            P("exp", "ctx", None),
            P("exp", "ctx", None),
            P("exp", "ctx", None),
        ),
        check_vma=False,
    )
```

time: 294 us -> 219 us (0.74)
  matrix products: 59.9 us -> 0 us
  Pallas kernels: 0 us -> 52.7 us
  local copies, waits for them, and re-layouts: 58.4 us -> 14.6 us
  starting transfers between devices: 103 us -> 63.3 us
  waiting for transfers between devices: 50.3 us -> 78.7 us
  other arithmetic: 15 us -> 6.39 us
    ppermute x18 -> x21, waiting for transfers between devices: 4.66 us -> 78.7 us  [the longest x3 58.8 us: crossed(): return lax.ppermute(x, 'exp', [(0, 1), (1, 0)])]
    dot_general x24 -> x0, matrix products: 59.9 us -> none  [the longest x3 7.43 us: combine(): jnp.dot(slot_table.T, returned.reshape(-1, returned.shape[2]), preferred_...]
    pallas_call x0 -> x6, Pallas kernels: none -> 52.7 us  [the longest x1 25.2 us: local(): call(functools.partial(grads_kernel, size), (like(PAIR * rows, 3 * width)...]
    all_to_all x6 -> x0, waiting for transfers between devices: 45.7 us -> none  [the longest x1 10.9 us: local(): lax.all_to_all(send_rows, 'exp', split_axis=0, concat_axis=0, tiled=True)]
    all_to_all x6 -> x0, starting transfers between devices: 27 us -> none  [the longest x1 4.62 us: local(): lax.all_to_all(send_tans, 'exp', split_axis=0, concat_axis=0, tiled=True)]
    ppermute x18 -> x21, starting transfers between devices: 76.3 us -> 63.3 us  [the longest x10 57.9 us: moved(): return lax.ppermute(x, 'ctx', pairs)]
    slice x9 -> x7, local copies, waits for them, and re-layouts: 16.5 us -> 4.21 us  [the longest x3 2.17 us: half(): x[0][:, at * width:(at + 1) * width]]
    concatenate x8 -> x4, local copies, waits for them, and re-layouts: 11.1 us -> 0.23 us  [the longest x1 0.11 us: __init__(): self.picks = jnp.concatenate([mine, 1.0 - mine, route_weights], axis=1)]
  transfers between devices with their start and end apart: 24 -> 21, of which waited for: 6 -> 5; matrix products, arithmetic and copies ran while one was open for 33% -> 3% of each run, Pallas kernels for 0% -> 10%
where the time goes in v1:
time: 219 us; the launch traced here: 217 us
  waiting for transfers between devices  78.7 us (36%)
  starting transfers between devices  63.3 us (29%)
  Pallas kernels  52.7 us (24%)
  local copies, waits for them, and re-layouts  14.6 us (7%)
  other arithmetic  6.39 us (3%)
    ppermute x3, waiting for transfers between devices, crossed(): return lax.ppermute(x, 'exp', [(0, 1), (1, 0)])  58.8 us
    ppermute x10, starting transfers between devices, moved(): return lax.ppermute(x, 'ctx', pairs)  57.9 us
    pallas_call x1, Pallas kernels, local(): call(functools.partial(grads_kernel, size), (like(PAIR * rows, 3 * width)...  25.2 us
    ppermute x10, waiting for transfers between devices, moved(): return lax.ppermute(x, 'ctx', pairs)  19.9 us
    pallas_call x1, Pallas kernels, local(): call(functools.partial(attend_kernel, size), (like(rows, width), like(row...  10.6 us
    unnamed x32, local copies, waits for them, and re-layouts  7.56 us
    pallas_call x1, Pallas kernels, forward(): call(functools.partial(expert_kernel, size), (like(PAIR, rows, wide // PA...  6.04 us
    pallas_call x1, Pallas kernels, tangent(): call(tangent_kernel, like(self.rows, self.wide), [self.tall, self.tall, s...  4.44 us
  transfers between devices with their start and end apart: 21, of which 5 were waited for; matrix products, arithmetic and copies ran while one was open for 3% of the time, Pallas kernels for 10%

profile of v1, /device:TPU:0, one launch (start us, length us, event | category | flops | bytes accessed | tf_op | source)
XLA Modules:
  0.0 216.7 jit_solution(10922427003750386924)
XLA Ops:
  0.7 0.7 bitcast_and_fusion
  1.4 1.1 fusion.4
  2.4 1.1 fusion.5
  3.6 1.3 broadcast_select_fusion.1
  4.9 0.5 collective-permute-start
  5.3 2.4 %dynamic-slice_bitcast_fusion = bf16[1024,512]{1,0:T(8,128)(2,1)} fusion(bf16[1,2048,512]{2,1,0:T(8,128)(2,1)} %param.18, s32[]{:T(128)S(6)} %select_n.128), kind=kLoop, calls=%fused_computation.1 | loop fusion | bytes 2097156 | tf_op jit(solution)/shard_map/dynamic_slice | solution.py:341
  7.8 2.5 %collective-permute-start.8 = (bf16[1024,512]{1,0:T(8,128)(2,1)}, bf16[1024,512]{1,0:T(8,128)(2,1)}, u32[]{:S(2)}, u32[]{:S(2)}) collective-permute-start(bf16[1024,512]{1,0:T(8,128)(2,1)} %dynamic-slice_bitcast_fusion), channel_id=1, source_target_pairs={{0,1},{1,0},{2,3},{3,2},{4,5},{5,4},{6,7},{7,6},{8,9},{9,8},{10,11... | collective-permute-start | bytes 3145736 | tf_op jit(solution)/shard_map/ppermute | solution.py:33
  10.2 0.1 dynamic-slice_bitcast_fusion.2
  10.3 0.1 collective-permute-start.4
  10.4 1.4 copy-done.3
  11.8 0.1 dynamic-slice_bitcast_fusion.1
  11.9 0.7 collective-permute-start.6
  12.6 0.0 collective-permute-done
  12.6 1.8 maximum_select_fusion.own
  14.3 1.1 slice.110
  15.5 4.4 %collective-permute-start.2 = (bf16[256,2048]{1,0:T(8,128)(2,1)}, bf16[256,2048]{1,0:T(8,128)(2,1)}, u32[]{:S(2)}, u32[]{:S(2)}) collective-permute-start(bf16[256,2048]{1,0:T(8,128)(2,1)} %slice.110), channel_id=1, source_target_pairs={{0,4},{2,6},{4,8},{6,10},{8,12},{10,14},{12,16},{14,18},{16,20},{1... | collective-permute-start | bytes 3145736 | tf_op jit(solution)/shard_map/ppermute | solution.py:25
  19.9 37.0 %collective-permute-done.4.down_x = bf16[256,2048]{1,0:T(8,128)(2,1)S(1)} collective-permute-done((bf16[256,2048]{1,0:T(8,128)(2,1)S(1)}, bf16[256,2048]{1,0:T(8,128)(2,1)S(1)}, u32[]{:S(2)}, u32[]{:S(2)}) %collective-permute-start.4) | collective-permute-done | bytes 1048608 | tf_op jit(solution)/shard_map/ppermute | solution.py:33
  56.9 0.0 collective-permute-start.5
  56.9 0.0 collective-permute-done.8.up_x
  56.9 0.5 collective-permute-start.9
  57.4 21.7 %collective-permute-done.6.gate_x = bf16[1024,512]{1,0:T(8,128)(2,1)} collective-permute-done((bf16[1024,512]{1,0:T(8,128)(2,1)S(1)}, bf16[1024,512]{1,0:T(8,128)(2,1)}, u32[]{:S(2)}, u32[]{:S(2)}) %collective-permute-start.6) | collective-permute-done | bytes 1048608 | tf_op jit(solution)/shard_map/ppermute | solution.py:33
  79.2 0.0 collective-permute-start.7
  79.2 0.8 slice.109
  80.0 3.9 %collective-permute-start.1 = (bf16[128,2048]{1,0:T(8,128)(2,1)}, bf16[128,2048]{1,0:T(8,128)(2,1)S(1)}, u32[]{:S(2)}, u32[]{:S(2)}) collective-permute-start(bf16[128,2048]{1,0:T(8,128)(2,1)} %slice.109), channel_id=1, source_target_pairs={{0,8},{2,10},{4,12},{6,14},{8,16},{10,18},{12,20},{14,22},{16,24},... | collective-permute-start | bytes 1572872 | tf_op jit(solution)/shard_map/ppermute | solution.py:25
  83.9 12.1 %collective-permute-done.1.far = bf16[128,2048]{1,0:T(8,128)(2,1)S(1)} collective-permute-done((bf16[128,2048]{1,0:T(8,128)(2,1)}, bf16[128,2048]{1,0:T(8,128)(2,1)S(1)}, u32[]{:S(2)}, u32[]{:S(2)}) %collective-permute-start.1) | collective-permute-done | bytes 524320 | tf_op jit(solution)/shard_map/ppermute | solution.py:25
  96.0 0.8 copy-done.8
  96.8 1.0 copy-done.9
  97.9 10.6 %shard_map.137 = (bf16[128,1024]{1,0:T(8,128)(2,1)S(1)}, bf16[128,1024]{1,0:T(8,128)(2,1)}, bf16[256,1152]{1,0:T(8,128)(2,1)S(1)}) custom-call(bf16[128,2048]{1,0:T(8,128)(2,1)S(1)} %copy-done.9, bf16[256,2048]{1,0:T(8,128)(2,1)} %collective-permute-done.2.near, bf16[256,3200]{1,0:T(8,128)(2,1)S(1)} %maximum_select_fusion.own, s32[1]{0:T(128)} %bitcast.me), custom_call_target="tpu_custom_call" | custom-call | tf_op jit(solution)/shard_map/pallas_call | solution.py:550
  108.4 0.7 copy-done.11
  109.2 0.1 copy.18.picks
  109.3 0.0 collective-permute-done.5.down_s
  109.3 0.0 copy-start.1
  109.3 1.6 copy-done.1
  110.9 1.0 copy-done.6
  111.9 2.4 %shard_map.138.hidden_grad = f32[128,1024]{1,0:T(8,128)S(1)} custom-call(s32[1]{0:T(128)} %bitcast.me, bf16[128,2048]{1,0:T(8,128)(2,1)S(1)} %bitcast.45, bf16[512,2048]{1,0:T(8,128)(2,1)S(1)} %bitcast.38, bf16[256,2048]{1,0:T(8,128)(2,1)S(1)} %collective-permute-done.4.down_x, bf16[256,2048]{1,0:T(8,128)(2,1)} %collective-permute-done.5.down_s), custom_call_target="tpu_custom_call" | custom-call | tf_op jit(solution)/shard_map/pallas_call | solution.py:364
  114.4 0.0 copy-done.5
  114.5 0.1 copy-done.7
  114.5 0.1 copy-done.12
  114.6 6.0 %shard_map.139 = (bf16[2,128,1152]{2,1,0:T(8,128)(2,1)S(1)}, bf16[128,1024]{1,0:T(8,128)(2,1)S(1)}, f32[128,1024]{1,0:T(8,128)S(1)}, f32[128,1024]{1,0:T(8,128)S(1)}) custom-call(s32[1]{0:T(128)} %bitcast.me, bf16[128,1024]{1,0:T(8,128)(2,1)S(1)} %copy-done.12, bf16[128,1024]{1,0:T(8,128)(2,1)} %collective-permute-done.3.got, ...), custom_call_target="tpu_custom_call" | custom-call | tf_op jit(solution)/shard_map/pallas_call | solution.py:374
  120.7 0.1 select_bitcast_fusion.1
  120.7 0.6 collective-permute-start.14
  121.4 1.4 collective-permute-start.13
  122.8 1.3 collective-permute-start.12
  124.1 4.6 %collective-permute-start.11 = (bf16[256,1152]{1,0:T(8,128)(2,1)S(1)}, bf16[256,1152]{1,0:T(8,128)(2,1)S(1)}, u32[]{:S(2)}, u32[]{:S(2)}) collective-permute-start(bf16[256,1152]{1,0:T(8,128)(2,1)S(1)} %get-tuple-element.17.qo), channel_id=1, source_target_pairs={{0,4},{2,6},{4,8},{6,10},{8,12},{10,14},{12,16},{14,18},{16,20},{1... | collective-permute-start | bytes 1769480 | tf_op jit(solution)/shard_map/ppermute | solution.py:25
  128.7 4.9 %collective-permute-start.10 = (bf16[128,1152]{1,0:T(8,128)(2,1)S(1)}, bf16[128,1152]{1,0:T(8,128)(2,1)S(1)}, u32[]{:S(2)}, u32[]{:S(2)}) collective-permute-start(bf16[128,1152]{1,0:T(8,128)(2,1)S(1)} %get-tuple-element.40), channel_id=1, source_target_pairs={{0,8},{2,10},{4,12},{6,14},{8,16},{10,18},{12,20},{14,22},{16,24},... | collective-permute-start | bytes 884744 | tf_op jit(solution)/shard_map/ppermute | solution.py:25
  133.6 0.1 maximum_select_fusion.1.co
  133.7 1.3 collective-permute-start.17
  135.0 5.0 %collective-permute-start.16 = (bf16[256,1152]{1,0:T(8,128)(2,1)S(1)}, bf16[256,1152]{1,0:T(8,128)(2,1)S(1)}, u32[]{:S(2)}, u32[]{:S(2)}) collective-permute-start(bf16[256,1152]{1,0:T(8,128)(2,1)S(1)} %maximum_select_fusion.1.co), channel_id=1, source_target_pairs={{0,4},{2,6},{4,8},{6,10},{8,12},{10,14},{12,16},{14,18},{16,20},{1... | collective-permute-start | bytes 1769480 | tf_op jit(solution)/shard_map/ppermute | solution.py:25
  140.1 1.3 collective-permute-start.18
  141.4 29.9 %collective-permute-start.15 = (bf16[128,1152]{1,0:T(8,128)(2,1)S(1)}, bf16[128,1152]{1,0:T(8,128)(2,1)S(1)}, u32[]{:S(2)}, u32[]{:S(2)}) collective-permute-start(bf16[128,1152]{1,0:T(8,128)(2,1)S(1)} %get-tuple-element.36), channel_id=1, source_target_pairs={{0,8},{2,10},{4,12},{6,14},{8,16},{10,18},{12,20},{14,22},{16,24},... | collective-permute-start | bytes 884744 | tf_op jit(solution)/shard_map/ppermute | solution.py:25
  171.3 4.4 %collective-permute-done.15.cfb = bf16[128,1152]{1,0:T(8,128)(2,1)S(1)} collective-permute-done((bf16[128,1152]{1,0:T(8,128)(2,1)S(1)}, bf16[128,1152]{1,0:T(8,128)(2,1)S(1)}, u32[]{:S(2)}, u32[]{:S(2)}) %collective-permute-start.15) | collective-permute-done | bytes 294944 | tf_op jit(solution)/shard_map/ppermute | solution.py:25
  175.7 3.3 %collective-permute-done.16.cnb = bf16[256,1152]{1,0:T(8,128)(2,1)S(1)} collective-permute-done((bf16[256,1152]{1,0:T(8,128)(2,1)S(1)}, bf16[256,1152]{1,0:T(8,128)(2,1)S(1)}, u32[]{:S(2)}, u32[]{:S(2)}) %collective-permute-start.16) | collective-permute-done | bytes 589856 | tf_op jit(solution)/shard_map/ppermute | solution.py:25
  179.1 25.2 %shard_map.141 = (bf16[256,3072]{1,0:T(8,128)(2,1)S(1)}, bf16[256,1024]{1,0:T(8,128)(2,1)S(1)}) custom-call(bf16[128,2048]{1,0:T(8,128)(2,1)S(1)} %copy-done.10, bf16[256,2048]{1,0:T(8,128)(2,1)} %collective-permute-done.2.near, bf16[256,3200]{1,0:T(8,128)(2,1)S(1)} %maximum_select_fusion.own, bf16[128,1152]{1,0:T(8,128)(2,1)S(1)} %collective-permute-done.10.qfb, ...), custom_call_target="tpu_custom_call" | custom-call | tf_op jit(solution)/shard_map/pallas_call | solution.py:563
  204.3 0.0 copy-start.2
  204.3 0.1 broadcast_select_fusion.3
  204.4 0.1 collective-permute-start.19
  204.5 0.6 collective-permute-start.20
  205.1 0.8 copy-done.2
  205.9 4.0 %shard_map.140 = bf16[128,2048]{1,0:T(8,128)(2,1)} custom-call(s32[1]{0:T(128)} %bitcast.me, bf16[128,1024]{1,0:T(8,128)(2,1)S(1)} %copy-done.12, bf16[128,1024]{1,0:T(8,128)(2,1)} %collective-permute-done.3.got, bf16[128,1024]{1,0:T(8,128)(2,1)S(1)} %get-tuple-element.16.hidden, f32[128,3]{1,0:T(8,128)S(1)} %copy.18.picks, bf16[512,2048]{1,0:T(8,128)(2,1)S(1)} %bitcast.39, ...), custom_call_target="tpu_custom_call" | custom-call | tf_op jit(solution)/shard_map/pallas_call | solution.py:386
  209.9 0.1 slice_bitcast_fusion.1
  209.9 4.4 %shard_map.142 = bf16[128,2048]{1,0:T(8,128)(2,1)} custom-call(s32[1]{0:T(128)} %bitcast.me, bf16[128,1024]{1,0:T(8,128)(2,1)S(1)} %get-tuple-element.42.keep, bf16[128,1024]{1,0:T(8,128)(2,1)S(1)} %collective-permute-done.20.got, f32[128,1024]{1,0:T(8,128)S(1)} %get-tuple-element.21.slope_up, f32[128,1024]{1,0:T(8,128)S(1)} %get-tuple-element.22.active, ...), custom_call_target="tpu_custom_call" | custom-call | tf_op jit(solution)/shard_map/pallas_call | solution.py:396
  214.4 0.1 slice_bitcast_fusion
  214.4 0.9 maximum_select_fusion.4
  215.4 1.4 maximum_select_fusion.2
  (42 shorter events, 0.3 us)
Async XLA Ops:
  0.6 2.9 %copy-start.13 = (bf16[1,128,2048]{2,1,0:T(8,128)(2,1)S(1)}, bf16[1,128,2048]{2,1,0:T(8,128)(2,1)}, u32[]{:S(2)}) copy-start(bf16[1,128,2048]{2,1,0:T(8,128)(2,1)} %param.12) | copy-start | bytes 1572868
  4.9 5.4 %copy-start = (bf16[1,512,2048]{2,1,0:T(8,128)(2,1)S(1)}, bf16[1,512,2048]{2,1,0:T(8,128)(2,1)}, u32[]{:S(2)}) copy-start(bf16[1,512,2048]{2,1,0:T(8,128)(2,1)} %param.19) | copy-start | bytes 6291460
  4.9 7.7 %collective-permute-start = (bf16[128,3200]{1,0:T(8,128)(2,1)}, bf16[128,3200]{1,0:T(8,128)(2,1)}, u32[]{:S(2)}, u32[]{:S(2)}) collective-permute-start(bf16[128,3200]{1,0:T(8,128)(2,1)} %get-tuple-element.26), channel_id=1, source_target_pairs={{0,2},{2,0},{4,6},{6,4},{8,10},{10,8},{12,14},{14,12},{16,18},{18,... | collective-permute-start | bytes 2457608 | tf_op jit(solution)/shard_map/ppermute | solution.py:29
  7.8 49.2 %collective-permute-start.8 = (bf16[1024,512]{1,0:T(8,128)(2,1)}, bf16[1024,512]{1,0:T(8,128)(2,1)}, u32[]{:S(2)}, u32[]{:S(2)}) collective-permute-start(bf16[1024,512]{1,0:T(8,128)(2,1)} %dynamic-slice_bitcast_fusion), channel_id=1, source_target_pairs={{0,1},{1,0},{2,3},{3,2},{4,5},{5,4},{6,7},{7,6},{8,9},{9,8},{10,11... | collective-permute-start | bytes 3145736 | tf_op jit(solution)/shard_map/ppermute | solution.py:33
  10.2 1.6 copy-start.3
  10.3 46.6 %collective-permute-start.4 = (bf16[256,2048]{1,0:T(8,128)(2,1)S(1)}, bf16[256,2048]{1,0:T(8,128)(2,1)S(1)}, u32[]{:S(2)}, u32[]{:S(2)}) collective-permute-start(bf16[256,2048]{1,0:T(8,128)(2,1)S(1)} %dynamic-slice_bitcast_fusion.2), channel_id=1, source_target_pairs={{0,1},{1,0},{2,3},{3,2},{4,5},{5,4},{6,7},{7,6},{8,9},{9,8},{10,11... | collective-permute-start | bytes 3145736 | tf_op jit(solution)/shard_map/ppermute | solution.py:33
  11.9 67.3 %collective-permute-start.6 = (bf16[1024,512]{1,0:T(8,128)(2,1)S(1)}, bf16[1024,512]{1,0:T(8,128)(2,1)}, u32[]{:S(2)}, u32[]{:S(2)}) collective-permute-start(bf16[1024,512]{1,0:T(8,128)(2,1)S(1)} %dynamic-slice_bitcast_fusion.1), channel_id=1, source_target_pairs={{0,1},{1,0},{2,3},{3,2},{4,5},{5,4},{6,7},{7,6},{8,9},{9,8},{10,11... | collective-permute-start | bytes 3145736 | tf_op jit(solution)/shard_map/ppermute | solution.py:33
  15.5 81.4 %collective-permute-start.2 = (bf16[256,2048]{1,0:T(8,128)(2,1)}, bf16[256,2048]{1,0:T(8,128)(2,1)}, u32[]{:S(2)}, u32[]{:S(2)}) collective-permute-start(bf16[256,2048]{1,0:T(8,128)(2,1)} %slice.110), channel_id=1, source_target_pairs={{0,4},{2,6},{4,8},{6,10},{8,12},{10,14},{12,16},{14,18},{16,20},{1... | collective-permute-start | bytes 3145736 | tf_op jit(solution)/shard_map/ppermute | solution.py:25
  56.9 52.4 %collective-permute-start.5 = (bf16[256,2048]{1,0:T(8,128)(2,1)S(1)}, bf16[256,2048]{1,0:T(8,128)(2,1)}, u32[]{:S(2)}, u32[]{:S(2)}) collective-permute-start(bf16[256,2048]{1,0:T(8,128)(2,1)S(1)} %collective-permute-done.4.down_x), channel_id=1, source_target_pairs={{0,2},{2,0},{4,6},{6,4},{8,10},{10,8},{12,14},{14,12},{16,18},{18,... | collective-permute-start | bytes 3145736 | tf_op jit(solution)/shard_map/ppermute | solution.py:29
  56.9 57.5 %collective-permute-start.9 = (bf16[1024,512]{1,0:T(8,128)(2,1)}, bf16[1024,512]{1,0:T(8,128)(2,1)}, u32[]{:S(2)}, u32[]{:S(2)}) collective-permute-start(bf16[1024,512]{1,0:T(8,128)(2,1)} %collective-permute-done.8.up_x), channel_id=1, source_target_pairs={{0,2},{2,0},{4,6},{6,4},{8,10},{10,8},{12,14},{14,12},{16,18},{18,... | collective-permute-start | bytes 3145736 | tf_op jit(solution)/shard_map/ppermute | solution.py:29
  79.2 35.3 %collective-permute-start.7 = (bf16[1024,512]{1,0:T(8,128)(2,1)}, bf16[1024,512]{1,0:T(8,128)(2,1)}, u32[]{:S(2)}, u32[]{:S(2)}) collective-permute-start(bf16[1024,512]{1,0:T(8,128)(2,1)} %collective-permute-done.6.gate_x), channel_id=1, source_target_pairs={{0,2},{2,0},{4,6},{6,4},{8,10},{10,8},{12,14},{14,12},{16,18},{18,... | collective-permute-start | bytes 3145736 | tf_op jit(solution)/shard_map/ppermute | solution.py:29
  80.0 29.1 %copy-start.15 = (s32[1,128,1]{1,2,0:T(1,128)S(1)}, s32[1,128,1]{1,2,0:T(1,128)}, u32[]{:S(2)}) copy-start(s32[1,128,1]{1,2,0:T(1,128)} %param.14) | copy-start | bytes 1540
  80.0 29.1 %copy-start.14 = (f32[1,128,1]{1,2,0:T(1,128)S(1)}, f32[1,128,1]{1,2,0:T(1,128)}, u32[]{:S(2)}) copy-start(f32[1,128,1]{1,2,0:T(1,128)} %param.15) | copy-start | bytes 1540
  80.0 16.0 %collective-permute-start.1 = (bf16[128,2048]{1,0:T(8,128)(2,1)}, bf16[128,2048]{1,0:T(8,128)(2,1)S(1)}, u32[]{:S(2)}, u32[]{:S(2)}) collective-permute-start(bf16[128,2048]{1,0:T(8,128)(2,1)} %slice.109), channel_id=1, source_target_pairs={{0,8},{2,10},{4,12},{6,14},{8,16},{10,18},{12,20},{14,22},{16,24},... | collective-permute-start | bytes 1572872 | tf_op jit(solution)/shard_map/ppermute | solution.py:25
  96.0 0.8 copy-start.8
  96.8 1.0 copy-start.9
  108.4 0.7 copy-start.11
  109.1 5.3 %collective-permute-start.3 = (bf16[128,1024]{1,0:T(8,128)(2,1)}, bf16[128,1024]{1,0:T(8,128)(2,1)}, u32[]{:S(2)}, u32[]{:S(2)}) collective-permute-start(bf16[128,1024]{1,0:T(8,128)(2,1)} %get-tuple-element.15), channel_id=1, source_target_pairs={{0,2},{2,0},{4,6},{6,4},{8,10},{10,8},{12,14},{14,12},{16,18},{18,... | collective-permute-start | bytes 786440 | tf_op jit(solution)/shard_map/ppermute | solution.py:29
  109.3 1.6 copy-start.1
  110.9 1.0 copy-start.6
  111.9 2.5 %copy-start.4 = (bf16[1,2048,512]{2,1,0:T(8,128)(2,1)S(1)}, bf16[1,2048,512]{2,1,0:T(8,128)(2,1)}, u32[]{:S(2)}) copy-start(bf16[1,2048,512]{2,1,0:T(8,128)(2,1)} %param.17) | copy-start | bytes 6291460
  111.9 2.5 %copy-start.5 = (bf16[1,2048,512]{2,1,0:T(8,128)(2,1)S(1)}, bf16[1,2048,512]{2,1,0:T(8,128)(2,1)}, u32[]{:S(2)}) copy-start(bf16[1,2048,512]{2,1,0:T(8,128)(2,1)} %param.18) | copy-start | bytes 6291460
  111.9 2.6 %copy-start.7 = (bf16[1,128,2048]{2,1,0:T(8,128)(2,1)S(1)}, bf16[1,128,2048]{2,1,0:T(8,128)(2,1)}, u32[]{:S(2)}) copy-start(bf16[1,128,2048]{2,1,0:T(8,128)(2,1)} %param.13) | copy-start | bytes 1572868
  111.9 2.7 %copy-start.12 = (bf16[128,1024]{1,0:T(8,128)(2,1)S(1)}, bf16[128,1024]{1,0:T(8,128)(2,1)}, u32[]{:S(2)}) copy-start(bf16[128,1024]{1,0:T(8,128)(2,1)} %copy-done.11) | copy-start | bytes 786436
  120.7 12.9 %collective-permute-start.14 = (bf16[128,1152]{1,0:T(8,128)(2,1)S(1)}, bf16[128,1152]{1,0:T(8,128)(2,1)S(1)}, u32[]{:S(2)}, u32[]{:S(2)}) collective-permute-start(bf16[128,1152]{1,0:T(8,128)(2,1)S(1)} %get-tuple-element.38), channel_id=1, source_target_pairs={{0,2},{2,0},{4,6},{6,4},{8,10},{10,8},{12,14},{14,12},{16,18},{18,... | collective-permute-start | bytes 884744 | tf_op jit(solution)/shard_map/ppermute | solution.py:29
  121.3 57.7 %copy-start.10 = (bf16[128,2048]{1,0:T(8,128)(2,1)S(1)}, bf16[128,2048]{1,0:T(8,128)(2,1)}, u32[]{:S(2)}) copy-start(bf16[128,2048]{1,0:T(8,128)(2,1)} %copy-done.8) | copy-start | bytes 1572868
  121.4 13.7 %collective-permute-start.13 = (bf16[128,1152]{1,0:T(8,128)(2,1)S(1)}, bf16[128,1152]{1,0:T(8,128)(2,1)S(1)}, u32[]{:S(2)}, u32[]{:S(2)}) collective-permute-start(bf16[128,1152]{1,0:T(8,128)(2,1)S(1)} %get-tuple-element.39), channel_id=1, source_target_pairs={{8,0},{10,2},{12,4},{14,6},{16,8},{18,10},{20,12},{22,14},{24,16},... | collective-permute-start | bytes 884744 | tf_op jit(solution)/shard_map/ppermute | solution.py:25
  122.8 18.6 %collective-permute-start.12 = (bf16[256,1152]{1,0:T(8,128)(2,1)S(1)}, bf16[256,1152]{1,0:T(8,128)(2,1)S(1)}, u32[]{:S(2)}, u32[]{:S(2)}) collective-permute-start(bf16[256,1152]{1,0:T(8,128)(2,1)S(1)} %get-tuple-element.17.qo), channel_id=1, source_target_pairs={{4,0},{6,2},{8,4},{10,6},{12,8},{14,10},{16,12},{18,14},{20,16},{2... | collective-permute-start | bytes 1769480 | tf_op jit(solution)/shard_map/ppermute | solution.py:25
  124.1 47.2 %collective-permute-start.11 = (bf16[256,1152]{1,0:T(8,128)(2,1)S(1)}, bf16[256,1152]{1,0:T(8,128)(2,1)S(1)}, u32[]{:S(2)}, u32[]{:S(2)}) collective-permute-start(bf16[256,1152]{1,0:T(8,128)(2,1)S(1)} %get-tuple-element.17.qo), channel_id=1, source_target_pairs={{0,4},{2,6},{4,8},{6,10},{8,12},{10,14},{12,16},{14,18},{16,20},{1... | collective-permute-start | bytes 1769480 | tf_op jit(solution)/shard_map/ppermute | solution.py:25
  128.7 11.4 %collective-permute-start.10 = (bf16[128,1152]{1,0:T(8,128)(2,1)S(1)}, bf16[128,1152]{1,0:T(8,128)(2,1)S(1)}, u32[]{:S(2)}, u32[]{:S(2)}) collective-permute-start(bf16[128,1152]{1,0:T(8,128)(2,1)S(1)} %get-tuple-element.40), channel_id=1, source_target_pairs={{0,8},{2,10},{4,12},{6,14},{8,16},{10,18},{12,20},{14,22},{16,24},... | collective-permute-start | bytes 884744 | tf_op jit(solution)/shard_map/ppermute | solution.py:25
  133.7 42.0 %collective-permute-start.17 = (bf16[256,1152]{1,0:T(8,128)(2,1)S(1)}, bf16[256,1152]{1,0:T(8,128)(2,1)S(1)}, u32[]{:S(2)}, u32[]{:S(2)}) collective-permute-start(bf16[256,1152]{1,0:T(8,128)(2,1)S(1)} %maximum_select_fusion.1.co), channel_id=1, source_target_pairs={{4,0},{6,2},{8,4},{10,6},{12,8},{14,10},{16,12},{18,14},{20,16},{2... | collective-permute-start | bytes 1769480 | tf_op jit(solution)/shard_map/ppermute | solution.py:25
  135.0 44.0 %collective-permute-start.16 = (bf16[256,1152]{1,0:T(8,128)(2,1)S(1)}, bf16[256,1152]{1,0:T(8,128)(2,1)S(1)}, u32[]{:S(2)}, u32[]{:S(2)}) collective-permute-start(bf16[256,1152]{1,0:T(8,128)(2,1)S(1)} %maximum_select_fusion.1.co), channel_id=1, source_target_pairs={{0,4},{2,6},{4,8},{6,10},{8,12},{10,14},{12,16},{14,18},{16,20},{1... | collective-permute-start | bytes 1769480 | tf_op jit(solution)/shard_map/ppermute | solution.py:25
  140.1 31.2 %collective-permute-start.18 = (bf16[128,1152]{1,0:T(8,128)(2,1)S(1)}, bf16[128,1152]{1,0:T(8,128)(2,1)S(1)}, u32[]{:S(2)}, u32[]{:S(2)}) collective-permute-start(bf16[128,1152]{1,0:T(8,128)(2,1)S(1)} %get-tuple-element.35), channel_id=1, source_target_pairs={{8,0},{10,2},{12,4},{14,6},{16,8},{18,10},{20,12},{22,14},{24,16},... | collective-permute-start | bytes 884744 | tf_op jit(solution)/shard_map/ppermute | solution.py:25
  141.4 34.3 %collective-permute-start.15 = (bf16[128,1152]{1,0:T(8,128)(2,1)S(1)}, bf16[128,1152]{1,0:T(8,128)(2,1)S(1)}, u32[]{:S(2)}, u32[]{:S(2)}) collective-permute-start(bf16[128,1152]{1,0:T(8,128)(2,1)S(1)} %get-tuple-element.36), channel_id=1, source_target_pairs={{0,8},{2,10},{4,12},{6,14},{8,16},{10,18},{12,20},{14,22},{16,24},... | collective-permute-start | bytes 884744 | tf_op jit(solution)/shard_map/ppermute | solution.py:25
  204.3 1.6 copy-start.2
  204.4 10.0 %collective-permute-start.19 = (bf16[128,3072]{1,0:T(8,128)(2,1)S(1)}, bf16[128,3072]{1,0:T(8,128)(2,1)S(1)}, u32[]{:S(2)}, u32[]{:S(2)}) collective-permute-start(bf16[128,3072]{1,0:T(8,128)(2,1)S(1)} %get-tuple-element.28), channel_id=1, source_target_pairs={{0,2},{2,0},{4,6},{6,4},{8,10},{10,8},{12,14},{14,12},{16,18},{18,... | collective-permute-start | bytes 2359304 | tf_op jit(solution)/shard_map/ppermute | solution.py:29
  204.5 5.4 %collective-permute-start.20 = (bf16[128,1024]{1,0:T(8,128)(2,1)S(1)}, bf16[128,1024]{1,0:T(8,128)(2,1)S(1)}, u32[]{:S(2)}, u32[]{:S(2)}) collective-permute-start(bf16[128,1024]{1,0:T(8,128)(2,1)S(1)} %get-tuple-element.41), channel_id=1, source_target_pairs={{0,2},{2,0},{4,6},{6,4},{8,10},{10,8},{12,14},{14,12},{16,18},{18,... | collective-permute-start | bytes 786440 | tf_op jit(solution)/shard_map/ppermute | solution.py:29

commit v2 on v1

v2 whole, which is shorter than its diff:
```python
import functools

import jax
import jax.numpy as jnp
from jax import lax
from jax.experimental import pallas as pl
from jax.experimental.pallas import tpu as pltpu
from jax.sharding import PartitionSpec as P

HEADS = 16
WIN = 4
PAIR = 2
SIDE = 128
FAR = 1e30
BF = jnp.bfloat16
F32 = jnp.float32
VMEM = pl.BlockSpec(memory_space=pltpu.VMEM)
SMEM = pl.BlockSpec(memory_space=pltpu.SMEM)
ANY = pl.BlockSpec(memory_space=pl.ANY)


def moved(x, by):
    devices = lax.axis_size("ctx")
    pairs = [(i, i + by) for i in range(devices) if 0 <= i + by < devices]
    return lax.ppermute(x, "ctx", pairs)


def swapped(x, bit=1):
    return lax.ppermute(x, "ctx", [(i, i ^ bit) for i in range(lax.axis_size("ctx"))])


def crossed(x):
    return lax.ppermute(x, "exp", [(0, 1), (1, 0)])


def nn(a, b):
    return lax.dot_general(a, b, (((1,), (0,)), ((), ())), preferred_element_type=F32)


def nt(a, b):
    return lax.dot_general(a, b, (((1,), (1,)), ((), ())), preferred_element_type=F32)


def tn(a, b):
    return lax.dot_general(a, b, (((0,), (0,)), ((), ())), preferred_element_type=F32)


def silu_parts(gate_pre):
    sigmoid_val = jax.nn.sigmoid(gate_pre)
    return (gate_pre * sigmoid_val, sigmoid_val * (1.0 + gate_pre * (1.0 - sigmoid_val)))


LEVEL, DELTA = 8, 32


def terms_of(x):
    first = x.astype(BF).astype(F32)
    second = (x - first).astype(BF).astype(F32)
    return jnp.concatenate([first, second, x - first - second], axis=0)


def rows_of(side, at, heads):
    return sum(side[at + n * heads : at + (n + 1) * heads].astype(F32) for n in range(3))


def hidden_by(flag):
    return (1.0 - flag) * FAR


def causal_of(rows):
    return lax.broadcasted_iota(jnp.int32, (rows, rows), 1) >= lax.broadcasted_iota(
        jnp.int32, (rows, rows), 0
    )


def like(*shape, kind=BF):
    return jax.ShapeDtypeStruct(shape, kind)


def call(kernel, outs, args, scratch=(), time=1, limit=8, alias=None, spaces=None):
    return pl.pallas_call(
        kernel,
        out_shape=outs,
        in_specs=[space for _, space in args],
        out_specs=jax.tree.map(lambda _: VMEM, outs) if spaces is None else spaces,
        input_output_aliases=alias or {},
        scratch_shapes=list(scratch),
        compiler_params=pltpu.CompilerParams(vmem_limit_bytes=limit * 1024 * 1024),
        cost_estimate=pl.CostEstimate(flops=int(time * 1.1e9), bytes_accessed=0, transcendentals=0),
    )(*(array for array, _ in args))


def vmem(*arrays):
    return [(array, VMEM) for array in arrays]


def anywhere(*arrays):
    return [(array, ANY) for array in arrays]


def tied(x, after):
    return call(lambda *refs: None, like(*x.shape), anywhere(x, after), alias={0: 0}, spaces=ANY, limit=1)


def fetch(copies):
    for copy in copies:
        copy.start()
    return copies


def ready(copies):
    for copy in copies:
        copy.wait()


def split_kernel(me, query, key, value, flags, keep, send, sems):
    core = me[0]
    rows, wide = query.shape[1:]
    width = wide // PAIR
    copies = []
    for m, (ref, owner) in enumerate(((keep, core), (send, 1 - core))):
        columns = pl.ds(pl.multiple_of(owner * width, width), width)
        for n, x in enumerate((query, key, value)):
            copies.append(
                pltpu.make_async_copy(x.at[0, :, columns], ref.at[:, pl.ds(n * width, width)], sems.at[m, n])
            )
    fetch(copies)
    seen = jnp.where(lax.broadcasted_iota(jnp.int32, (SIDE, rows), 0) < WIN - 1, flags[...], 0.0)
    for ref in (keep, send):
        ref[:, 3 * width :] = seen.astype(BF)
    ready(copies)


def join_kernel(me, keep, got, after, q2, kv2, odd, side, sems):
    core = me[0]
    rows, width = odd.shape[0], q2.shape[1]
    copies = []
    for n, (ref, block) in enumerate(((keep, core), (got, 1 - core))):
        here = pl.ds(pl.multiple_of(block * rows, rows), rows)
        for m, (target, at) in enumerate(((q2, 0), (kv2, width), (side, 3 * width))):
            source = ref.at[:, pl.ds(at, target.shape[1])]
            copies.append(pltpu.make_async_copy(source, target.at[here, :], sems.at[n, m]))
    fetch(copies)

    @pl.when(core == 1)
    def _():
        fetch([pltpu.make_async_copy(keep.at[:, pl.ds(width, 2 * width)], odd, sems.at[2, 0])])

    @pl.when(core != 1)
    def _():
        fetch([pltpu.make_async_copy(got.at[:, pl.ds(width, 2 * width)], odd, sems.at[2, 0])])

    ready(copies)
    ready([pltpu.make_async_copy(keep.at[:, pl.ds(width, 2 * width)], odd, sems.at[2, 0])])


def cut_kernel(x, after, whole, even, odd):
    rows = even.shape[0]
    whole[...] = x[...]
    even[...] = x[:rows]
    odd[...] = x[rows:]


def weights_kernel(me, gate, up, down, after, first, over, sems):
    core, lane = me[0], me[1]

    def half(ref, out, at):
        depth = out.shape[0]
        return pltpu.make_async_copy(ref.at[pl.ds(core * depth, depth)], out, sems.at[at])

    @pl.when(lane == 0)
    def _():
        half(gate, first, 0).start()

    @pl.when(lane != 0)
    def _():
        half(up, first, 0).start()

    half(down, over, 1).start()
    half(gate, first, 0).wait()
    half(down, over, 1).wait()


def cots_kernel(me, keep, got, side, whole, even, odd):
    core = me[0]
    rows, width = keep.shape[0], keep.shape[1] - SIDE
    for ref, block in ((keep, core), (got, 1 - core)):
        here = pl.ds(pl.multiple_of(block * rows, rows), rows)
        filled = (ref[:, width:].astype(F32) + side[here, :].astype(F32)).astype(BF)
        whole[here, 0:width] = ref[:, 0:width]
        whole[here, width:] = filled

        @pl.when(block == 0)
        def _():
            even[:, 0:width] = ref[:, 0:width]
            even[:, width:] = filled

        @pl.when(block == 1)
        def _():
            odd[:, 0:width] = ref[:, 0:width]
            odd[:, width:] = filled


def window_refs(far, near, own, rows):
    return {-3: (far, 0), -2: (near, 0), -1: (near, rows), 0: (own, 0), 1: (own, rows)}


def stacked(window, js, rows, at, size):
    return jnp.concatenate(
        [window[j][0][pl.ds(window[j][1], rows), pl.ds(pl.multiple_of(at, size), size)] for j in js],
        axis=0,
    )


def each_head(heads, one, step=2):
    def some(n, carry):
        for at in range(step):
            one(step * n + at)
        return carry

    lax.fori_loop(0, heads // step, some, 0)


def attend_kernel(size, me, far, near, own, q2, flags, after, cut, keep, send, side, levels):
    rows, width = far.shape[0], far.shape[1] // 2
    heads = width // size
    scale = size ** (-0.5)
    core = me[0]
    window = window_refs(far, near, own, rows)
    causal = causal_of(rows)
    for block in range(PAIR):
        seen = flags[block * rows : (block + 1) * rows, :].astype(F32)
        biases = [hidden_by(seen[w - 1 : w]) for w in range(1, WIN)]
        js = list(range(block - WIN + 1, block + 1))

        def one(head):
            at = pl.multiple_of(head * size, size)
            q = q2[pl.ds(block * rows, rows), pl.ds(at, size)]
            scores = nt(stacked(window, js, rows, at, size), q) * scale
            parts = [
                scores[n * rows : (n + 1) * rows] - biases[block - j - 1]
                if j < block
                else jnp.where(causal, scores[n * rows : (n + 1) * rows], -FAR)
                for n, j in enumerate(js)
            ]
            scores = jnp.concatenate(parts, axis=0)
            top = jnp.max(scores, axis=0, keepdims=True)
            weights = jnp.exp(scores - top)
            total = jnp.sum(weights, axis=0, keepdims=True)
            probs = (weights * (1.0 / total)).astype(BF)
            out = tn(probs, stacked(window, js, rows, width + at, size)).astype(BF)

            @pl.when(core == block)
            def _():
                keep[:, pl.ds(at, size)] = out

            @pl.when(core != block)
            def _():
                send[:, pl.ds(at, size)] = out

            levels[pl.ds(head, 1), :] = top + jnp.log(total)

        each_head(heads, one)
        filled = jnp.concatenate(
            [seen[:LEVEL], terms_of(levels[...]), jnp.zeros((SIDE - LEVEL - 3 * heads, rows), F32)], axis=0
        )
        side[block * rows : (block + 1) * rows, :] = filled.astype(BF)


def scores_back(q, cot, level, delta, seen, keys, values, js, t, causal, scale):
    rows = q.shape[0]
    scores = nt(keys, q) * scale
    parts = []
    for n, j in enumerate(js):
        part = scores[n * rows : (n + 1) * rows]
        if j < t:
            part = part - (level + hidden_by(seen[t - j - 1 : t - j]))
        else:
            part = jnp.where(causal, part - level, -FAR)
        parts.append(part)
    probs = jnp.exp(jnp.concatenate(parts, axis=0))
    return probs, (probs * (nt(values, cot) - delta)).astype(BF)


def add_blocks(sums, js, terms, rows):
    for n, j in enumerate(js):
        term = terms[n * rows : (n + 1) * rows]
        sums[j] = sums[j] + term if j in sums else term


def own_grads_kernel(
    size, me, far, near, own, q2, co, probs_out, probs_low_out, grads_q, q_keep, q_send, key_sums, value_sums,
    levels, deltas,
):
    rows, width = far.shape[0], far.shape[1] // 2
    heads = width // size
    scale = size ** (-0.5)
    core = me[0]
    window = window_refs(far, near, own, rows)
    causal = causal_of(rows)
    sides = [co[t * rows : (t + 1) * rows, width:].astype(F32) for t in range(PAIR)]
    for t in range(PAIR):
        levels[t] = rows_of(sides[t], LEVEL, heads)
        deltas[t] = rows_of(sides[t], DELTA, heads)

    def one(head):
        at = pl.multiple_of(head * size, size)
        here = pl.ds(at, size)
        keys_at, values_at = {}, {}
        for t in range(PAIR):
            place = pl.ds(t * rows, rows)
            js = list(range(t - WIN + 1, t + 1))
            q, cot = q2[place, here], co[place, here]
            keys = stacked(window, js, rows, at, size)
            values = stacked(window, js, rows, width + at, size)
            probs, score_grad = scores_back(
                q, cot, levels[t, pl.ds(head, 1), :], deltas[t, pl.ds(head, 1), :], sides[t][0:8],
                keys, values, js, t, causal, scale,
            )
            probs_low = probs.astype(BF)
            probs_out[head, t] = probs
            probs_low_out[head, t] = probs_low.T
            add_blocks(keys_at, js, nn(score_grad, q), rows)
            add_blocks(values_at, js, nn(probs_low, cot), rows)
            grad_q = (tn(score_grad, keys) * scale).astype(BF)
            grads_q[place, here] = grad_q

            @pl.when(core == t)
            def _():
                q_keep[:, here] = grad_q

            @pl.when(core != t)
            def _():
                q_send[:, here] = grad_q

        for j in keys_at:
            place = pl.ds((j + WIN - 1) * rows, rows)
            key_sums[place, here] = keys_at[j]
            value_sums[place, here] = values_at[j]

    each_head(heads, one)


def grads_kernel(
    size, me, far, near, own, q2, qfb, qnb, qna, qfa, cfb, cnb, cna, cfa, probs_in, probs_low_in, grads_q,
    key_sums, value_sums, after, keep, send, tans_keep, tans_send, levels, deltas,
):
    rows, width = far.shape[0], far.shape[1] // 2
    heads = width // size
    scale = size ** (-0.5)
    core = me[0]
    window = window_refs(far, near, own, rows)
    causal = causal_of(rows)
    others = (
        (-3, qfb, cfb, 0), (-2, qnb, cnb, 0), (-1, qnb, cnb, 1),
        (2, qna, cna, 0), (3, qna, cna, 1), (4, qfa, cfa, 0),
    )
    sides = [c_ref[half * rows : (half + 1) * rows, width:].astype(F32) for _, _, c_ref, half in others]
    for n, side in enumerate(sides):
        levels[n] = rows_of(side, LEVEL, heads)
        deltas[n] = rows_of(side, DELTA, heads)

    def one(head):
        at = pl.multiple_of(head * size, size)
        here = pl.ds(at, size)
        blocks = range(1 - WIN, PAIR)
        keys_at = {j: key_sums[pl.ds((j + WIN - 1) * rows, rows), here] for j in blocks}
        values_at = {j: value_sums[pl.ds((j + WIN - 1) * rows, rows), here] for j in blocks}
        for n, (t, q_ref, c_ref, half) in enumerate(others):
            place = pl.ds(half * rows, rows)
            js = list(range(max(1 - WIN, t - WIN + 1), min(1, t) + 1))
            q, cot = q_ref[place, here], c_ref[place, here]
            keys = stacked(window, js, rows, at, size)
            values = stacked(window, js, rows, width + at, size)
            probs, score_grad = scores_back(
                q, cot, levels[n, pl.ds(head, 1), :], deltas[n, pl.ds(head, 1), :], sides[n][0:8],
                keys, values, js, t, causal, scale,
            )
            add_blocks(keys_at, js, nn(score_grad, q), rows)
            add_blocks(values_at, js, nn(probs.astype(BF), cot), rows)
        key_grads = {j: (keys_at[j] * scale).astype(BF) for j in blocks}
        value_grads = {j: values_at[j].astype(BF) for j in blocks}
        for t in range(PAIR):
            place = pl.ds(t * rows, rows)
            js = list(range(t - WIN + 1, t + 1))
            keys = stacked(window, js, rows, at, size)
            values = stacked(window, js, rows, width + at, size)
            probs = probs_in[head, t]
            both_keys = jnp.concatenate([keys, jnp.concatenate([key_grads[j] for j in js], axis=0)], axis=1)
            both_rows = jnp.concatenate([grads_q[place, here], q2[place, here]], axis=1)
            tan_values = jnp.concatenate([value_grads[j] for j in js], axis=0)
            score_tan = nt(both_keys, both_rows) * scale
            mean = jnp.sum(probs * score_tan, axis=0, keepdims=True)
            prob_tan = (probs * (score_tan - mean)).astype(BF)
            tan = (tn(prob_tan, values) + nn(probs_low_in[head, t], tan_values)).astype(BF)

            def put(grads, tans):
                grads[:, here] = key_grads[t]
                grads[:, pl.ds(pl.multiple_of(width + at, size), size)] = value_grads[t]
                tans[:, here] = tan

            pl.when(core == t)(lambda: put(keep, tans_keep))
            pl.when(core != t)(lambda: put(send, tans_send))

    each_head(heads, one)


def gather_kernel(me, q_keep, q_got, keep, got, out_q, out_k, out_v):
    core = me[0]
    width = q_keep.shape[1]
    for owner, q, kv in ((core, q_keep, keep), (1 - core, q_got, got)):
        columns = pl.ds(pl.multiple_of(owner * width, width), width)
        out_q[:, columns] = q[...]
        out_k[:, columns] = kv[:, 0:width]
        out_v[:, columns] = kv[:, width:]


def cot_sides(size, cot, attended, put):
    rows, width = cot.shape[0], cot.shape[1] // PAIR
    heads = width // size
    lanes = lax.broadcasted_iota(jnp.int32, (rows, SIDE), 1)
    for half in range(PAIR):
        sums = jnp.zeros((rows, SIDE), F32)
        for head in range(heads):
            here = slice(half * width + head * size, half * width + (head + 1) * size)
            delta = jnp.sum(cot[:, here].astype(F32) * attended[:, here].astype(F32), axis=1, keepdims=True)
            sums = jnp.where(lanes == head, delta, sums)
        blank = jnp.zeros((DELTA, rows), F32)
        rest = jnp.zeros((SIDE - DELTA - 3 * heads, rows), F32)
        side = jnp.concatenate([blank, terms_of(sums.T[0:heads]), rest], axis=0)
        put(half, jnp.concatenate([cot[:, half * width : (half + 1) * width], side.astype(BF)], axis=1))


def cots_out(core, keep, send):
    def put(half, payload):
        @pl.when(core == half)
        def _():
            keep[...] = payload

        @pl.when(core != half)
        def _():
            send[...] = payload

    return put


def in_order(core, kept, got):
    return jnp.where(
        core == 0, jnp.concatenate([kept, got], axis=1), jnp.concatenate([got, kept], axis=1)
    )


def load_down(core, down, over, over_s, buffer, sems):
    depth = over.shape[0]
    return (
        fetch([pltpu.make_async_copy(down, buffer.at[0], sems.at[0])]),
        fetch(
            [
                pltpu.make_async_copy(over, buffer.at[1, pl.ds(core * depth, depth)], sems.at[1]),
                pltpu.make_async_copy(over_s, buffer.at[1, pl.ds((1 - core) * depth, depth)], sems.at[2]),
            ]
        ),
    )


def load_inner(core, lane, gate, up, first, second, first_s, second_s, buffer, sems):
    depth = first.shape[0]
    copies = []
    for n, (ref, which, half) in enumerate(
        ((first, lane, core), (second, 1 - lane, core), (first_s, lane, 1 - core), (second_s, 1 - lane, 1 - core))
    ):
        target = buffer.at[1, which, pl.ds(half * depth, depth)]
        copies.append(pltpu.make_async_copy(ref, target, sems.at[2 + n]))
    own = [
        pltpu.make_async_copy(gate, buffer.at[0, 0], sems.at[0]),
        pltpu.make_async_copy(up, buffer.at[0, 1], sems.at[1]),
    ]
    return fetch(own), fetch(copies)


def hidden_grad_kernel(me, cot, down, over, over_s, out, buffer, sems):
    loads = load_down(me[0], down, over, over_s, buffer, sems)
    units = down.shape[0]
    for e in range(2):
        ready(loads[e])
        out[:, e * units : (e + 1) * units] = nt(cot[0], buffer[e])


def expert_kernel(
    size, me, keep, got, cot, picks, hidden_grad, gate, up, first, second, first_s, second_s,
    cot_keep, cot_send, hidden, slope_up, active, inner, sems,
):
    core = me[0]
    loads = load_inner(core, me[1], gate, up, first, second, first_s, second_s, inner, sems)
    units = gate.shape[1]
    rows_in = in_order(core, keep[...], got[...])
    summed = None
    for e in range(2):
        here = slice(e * units, (e + 1) * units)
        chosen = picks[:, e : e + 1]
        ready(loads[e])
        gate_pre = nn(rows_in, inner[e, 0])
        up_value = nn(rows_in, inner[e, 1])
        activated, slope = silu_parts(gate_pre)
        activated = activated * chosen
        slope = slope * up_value * chosen
        hidden[:, here] = (activated * up_value).astype(BF)
        slope_up[:, here] = slope
        active[:, here] = activated
        back = hidden_grad[:, here]
        term = nt((back * slope).astype(BF), inner[e, 0]) + nt((back * activated).astype(BF), inner[e, 1])
        summed = term if summed is None else summed + term
    weight = picks[:, 2:3]
    attn_cot = (cot[0].astype(F32) + summed.astype(BF).astype(F32) * weight).astype(BF)
    cot_sides(size, attn_cot, rows_in, cots_out(core, cot_keep, cot_send))


def layer_kernel(me, keep, got, hidden, picks, down, over, over_s, out, buffer, sems):
    core = me[0]
    loads = load_down(core, down, over, over_s, buffer, sems)
    units = down.shape[0]
    rows_in = in_order(core, keep[...], got[...]).astype(F32)
    ready(loads[0])
    summed = nn(hidden[:, 0:units], buffer[0])
    ready(loads[1])
    summed = summed + nn(hidden[:, units:], buffer[1])
    out[...] = (rows_in + summed.astype(BF).astype(F32) * picks[:, 2:3]).astype(BF)


def tangent_kernel(
    me, keep, got, slope_up, active, picks, gate, up, first, second, first_s, second_s, down, over, over_s,
    out, inner, buffer, inner_sems, sems,
):
    core = me[0]
    loads = load_inner(core, me[1], gate, up, first, second, first_s, second_s, inner, inner_sems)
    down_loads = load_down(core, down, over, over_s, buffer, sems)
    units = gate.shape[1]
    rows_in = in_order(core, keep[...], got[...])
    summed = None
    for e in range(2):
        here = slice(e * units, (e + 1) * units)
        ready(loads[e])
        gate_tan = nn(rows_in, inner[e, 0])
        up_tan = nn(rows_in, inner[e, 1])
        hidden = (slope_up[:, here] * gate_tan + active[:, here] * up_tan).astype(BF)
        ready(down_loads[e])
        term = nn(hidden, buffer[e])
        summed = term if summed is None else summed + term
    out[...] = (rows_in.astype(F32) + summed.astype(BF).astype(F32) * picks[:, 2:3]).astype(BF)


class PairExperts:
    def __init__(self, index, after, upstream, route_ids, route_weights, w_gate, w_up, w_down):
        core, lane = index % 2, index // 2 % 2
        own = lax.axis_index("exp")
        self.me = jnp.stack([core, lane])
        self.upstream = upstream
        mine = (route_ids == own).astype(F32)
        self.picks = jnp.concatenate([mine, 1.0 - mine, route_weights], axis=1)
        rows, wide = upstream.shape[1:]
        units = w_gate.shape[1]
        self.cut = call(
            weights_kernel,
            (like(wide // 2, units), like(units // 2, wide)),
            [(self.me, SMEM)] + anywhere(w_gate, w_up, w_down, after),
            [pltpu.SemaphoreType.DMA((2,))],
        )
        first, self.over = crossed(self.cut[0]), crossed(self.cut[1])
        self.first = (first, swapped(first), swapped(first, 2))
        self.whole = (w_gate, w_up, w_down)
        self.rows, self.wide, self.units = rows, wide, units
        self.inner_buffer = pltpu.VMEM((2, 2, wide, units), BF)
        self.buffer = pltpu.VMEM((2, units, wide), BF)

    def begun(self):
        return self.cut[0]

    def before(self):
        return self.first[0]

    def forward(self, size, keep, got):
        rows, wide, units = self.rows, self.wide, self.units
        first, first_s, second = self.first
        w_gate, w_up, w_down = self.whole
        over, second = tied(self.over, keep), tied(second, keep)
        self.down = (w_down, over, swapped(over))
        self.inner = (w_gate, w_up, first, second, first_s, swapped(second))
        hidden_grad = call(
            hidden_grad_kernel,
            like(rows, 2 * units, kind=F32),
            [(self.me, SMEM)] + vmem(self.upstream) + anywhere(*self.down),
            [self.buffer, pltpu.SemaphoreType.DMA((3,))],
            time=2.5,
            limit=10,
        )
        half = like(rows, wide // PAIR + SIDE)
        cot_keep, cot_send, hidden, self.slope_up, self.active = call(
            functools.partial(expert_kernel, size),
            (half, half, like(rows, 2 * units), like(rows, 2 * units, kind=F32), like(rows, 2 * units, kind=F32)),
            [(self.me, SMEM)] + vmem(keep, got, self.upstream, self.picks, hidden_grad) + anywhere(*self.inner),
            [self.inner_buffer, pltpu.SemaphoreType.DMA((6,))],
            time=6,
            limit=18,
        )
        layer_out = call(
            layer_kernel,
            like(rows, wide),
            [(self.me, SMEM)] + vmem(keep, got, hidden, self.picks) + anywhere(*self.down),
            [self.buffer, pltpu.SemaphoreType.DMA((3,))],
            time=4,
            limit=10,
        )
        return cot_keep, cot_send, layer_out

    def tangent(self, keep, got):
        return call(
            tangent_kernel,
            like(self.rows, self.wide),
            [(self.me, SMEM)]
            + vmem(keep, got, self.slope_up, self.active, self.picks)
            + anywhere(*self.inner, *self.down),
            [self.inner_buffer, self.buffer, pltpu.SemaphoreType.DMA((6,)), pltpu.SemaphoreType.DMA((3,))],
            time=4.5,
            limit=22,
        )


def routing_table(route_rows, experts, capacity):
    flat_ids = route_rows.reshape(-1)
    one_hot = (flat_ids[:, None] == jnp.arange(experts, dtype=jnp.int32)[None, :]).astype(jnp.int32)
    slot_rank = jnp.sum((jnp.cumsum(one_hot, axis=0) - one_hot) * one_hot, axis=1)
    target = flat_ids * capacity + slot_rank
    return (jnp.arange(experts * capacity, dtype=jnp.int32)[:, None] == target[None, :]).astype(
        jnp.bfloat16
    )


def dispatch(slot_table, row_block, routes, experts):
    pair_rows = jnp.repeat(row_block, routes, axis=0)
    sent = jnp.dot(slot_table, pair_rows, preferred_element_type=jnp.float32).astype(jnp.bfloat16)
    return sent.reshape(experts, -1, row_block.shape[1])


def combine(slot_table, returned, weights):
    rows_here, routes = weights.shape
    pair_vals = jnp.dot(
        slot_table.T, returned.reshape(-1, returned.shape[2]), preferred_element_type=jnp.float32
    )
    return jnp.sum(pair_vals.reshape(rows_here, routes, -1) * weights[:, :, None], axis=1)


def expert_forward(row_block, gate_matrix, up_matrix, down_matrix):
    gate_pre = jnp.dot(row_block, gate_matrix, preferred_element_type=jnp.float32)
    up_value = jnp.dot(row_block, up_matrix, preferred_element_type=jnp.float32)
    activated, slope_val = silu_parts(gate_pre)
    hidden = (activated * up_value).astype(jnp.bfloat16)
    return (
        jnp.dot(hidden, down_matrix, preferred_element_type=jnp.float32).astype(jnp.bfloat16),
        gate_pre,
        up_value,
    )


def expert_backward(cot_block, gate_pre, up_value, gate_matrix, up_matrix, down_matrix):
    hidden_grad = jnp.dot(cot_block, down_matrix.T, preferred_element_type=jnp.float32)
    activated, slope_val = silu_parts(gate_pre)
    gate_grad = (hidden_grad * up_value * slope_val).astype(jnp.bfloat16)
    up_grad = (hidden_grad * activated).astype(jnp.bfloat16)
    summed = jnp.dot(gate_grad, gate_matrix.T, preferred_element_type=jnp.float32) + jnp.dot(
        up_grad, up_matrix.T, preferred_element_type=jnp.float32
    )
    return summed.astype(jnp.bfloat16)


def expert_tangent(tan_block, gate_pre, up_value, gate_matrix, up_matrix, down_matrix):
    gate_tan = jnp.dot(tan_block, gate_matrix, preferred_element_type=jnp.float32)
    up_tan = jnp.dot(tan_block, up_matrix, preferred_element_type=jnp.float32)
    activated, slope_val = silu_parts(gate_pre)
    hidden_tan = (slope_val * gate_tan * up_value + activated * up_tan).astype(jnp.bfloat16)
    return jnp.dot(hidden_tan, down_matrix, preferred_element_type=jnp.float32).astype(jnp.bfloat16)


class RoutedExperts:
    def __init__(self, index, after, upstream, route_ids, route_weights, w_gate, w_up, w_down):
        rows, routes = route_ids.shape
        self.experts = lax.axis_size("exp")
        self.routes = routes
        capacity = min(rows, 2 * rows * routes // self.experts)
        self.core, self.upstream, self.weights = index % 2, upstream[0], route_weights
        self.matrices = (w_gate, w_up, w_down)
        self.table = routing_table(route_ids, self.experts, capacity)
        self.got_cots = self.sent(self.upstream)

    def begun(self):
        return self.got_cots

    def before(self):
        return self.got_cots

    def across(self, x):
        return lax.all_to_all(x, "exp", split_axis=0, concat_axis=0, tiled=True)

    def sent(self, x):
        return self.across(dispatch(self.table, x, self.routes, self.experts))

    def returned(self, x):
        back = self.across(x.reshape(self.got_cots.shape))
        return combine(self.table, back, self.weights)

    def forward(self, size, keep, got):
        attended = in_order(self.core, keep, got)
        rows, wide = attended.shape
        got_rows = self.sent(attended).reshape(-1, wide)
        expert_out, self.gate_pre, self.up_value = expert_forward(got_rows, *self.matrices)
        route_grad = expert_backward(
            self.got_cots.reshape(-1, wide), self.gate_pre, self.up_value, *self.matrices
        )
        attn_cot = (self.upstream.astype(F32) + self.returned(route_grad)).astype(BF)
        layer_out = (attended.astype(F32) + self.returned(expert_out)).astype(BF)

        def kernel(me, cot, rows_in, cot_keep, cot_send):
            cot_sides(size, cot, rows_in, cots_out(me[0], cot_keep, cot_send))

        half = like(rows, wide // PAIR + SIDE)
        cot_keep, cot_send = call(
            kernel, (half, half), [(self.core.reshape(1), SMEM)] + vmem(attn_cot, attended)
        )
        return cot_keep, cot_send, layer_out

    def tangent(self, keep, got):
        rows = in_order(self.core, keep, got)
        got_rows = self.sent(rows).reshape(-1, rows.shape[1])
        out = expert_tangent(got_rows, self.gate_pre, self.up_value, *self.matrices)
        return (rows.astype(F32) + self.returned(out)).astype(BF)


def neighbours(whole, even, odd):
    return (
        moved(odd, 2 * PAIR),
        moved(whole, PAIR),
        moved(whole, -PAIR),
        moved(even, -2 * PAIR),
    )


def local(query, key, value, cotangent, route_ids, route_weights, block_mask, w_gate, w_up, w_down):
    rows, wide = query.shape[1:]
    width = wide // PAIR
    size = wide // HEADS
    heads = width // size
    index = lax.axis_index("ctx")
    core = index % PAIR
    me = [(core.reshape(1), SMEM)]

    seen = (block_mask[0] == 1) & (index >= jnp.arange(1, WIN, dtype=jnp.int32))
    flags = jnp.pad(seen.astype(F32).T, ((0, SIDE - WIN + 1), (0, 0)))
    packed = like(rows, 3 * width + SIDE)
    own_part, mate_part = call(
        split_kernel,
        (packed, packed),
        me + anywhere(query, key, value) + vmem(flags),
        [pltpu.SemaphoreType.DMA((2, 3))],
    )
    got_part = swapped(mate_part)
    pair = lax.axis_size("exp") == 2 and route_ids.shape[2] == 1
    experts = (PairExperts if pair else RoutedExperts)(
        index, mate_part, cotangent, route_ids[0], route_weights[0], w_gate[0], w_up[0], w_down[0]
    )
    q2, kv2, kv_odd, side = call(
        join_kernel,
        (like(2 * rows, width), like(2 * rows, 2 * width), like(rows, 2 * width), like(2 * rows, SIDE)),
        me + anywhere(own_part, got_part, experts.begun()),
        [pltpu.SemaphoreType.DMA((3, 3))],
    )
    near, far = moved(kv2, PAIR), moved(kv_odd, 2 * PAIR)
    blocks = (like(2 * rows, width), like(rows, width), like(rows, width))
    q_parts = call(cut_kernel, blocks, vmem(q2) + anywhere(near))

    keep, send, side = call(
        functools.partial(attend_kernel, size),
        (like(rows, width), like(rows, width), like(2 * rows, SIDE)),
        me + vmem(far, near, kv2, q2, side) + anywhere(experts.before(), q_parts[0]),
        [pltpu.VMEM((heads, rows), F32)],
        time=9,
    )
    got = swapped(send)
    qfb, qnb, qna, qfa = neighbours(*q_parts)

    cot_keep, cot_send, layer_out = experts.forward(size, keep, got)
    payload = wide // PAIR + SIDE
    co, co_even, co_odd = call(
        cots_kernel,
        (like(2 * rows, payload), like(rows, payload), like(rows, payload)),
        me + vmem(cot_keep, swapped(cot_send), side),
    )
    cfb, cnb, cna, cfa = neighbours(co, co_even, co_odd)

    sums = like((WIN + 1) * rows, width, kind=F32)
    probs, probs_low, grads_q, q_keep, q_send, key_sums, value_sums = call(
        functools.partial(own_grads_kernel, size),
        (
            like(heads, 2, WIN * rows, rows, kind=F32),
            like(heads, 2, rows, WIN * rows),
            like(2 * rows, width), like(rows, width), like(rows, width),
            sums, sums,
        ),
        me + vmem(far, near, kv2, q2, co),
        [pltpu.VMEM((2, heads, rows), F32)] * 2,
        time=12,
    )
    q_got = swapped(q_send)
    kv_half, half = like(rows, 2 * width), like(rows, width)
    kv_keep, kv_send, tan_keep, tan_send = call(
        functools.partial(grads_kernel, size),
        (kv_half, kv_half, half, half),
        me
        + vmem(far, near, kv2, q2, qfb, qnb, qna, qfa, cfb, cnb, cna, cfa)
        + vmem(probs, probs_low, grads_q, key_sums, value_sums)
        + anywhere(layer_out),
        [pltpu.VMEM((6, heads, rows), F32)] * 2,
        time=16,
    )
    tan_got = swapped(tan_send)
    kv_got = swapped(kv_send)
    tangent_out = experts.tangent(tan_keep, tan_got)
    out = like(rows, wide)
    outs = call(gather_kernel, (out, out, out), me + vmem(q_keep, q_got, kv_keep, kv_got))
    return (layer_out[None], *(x[None] for x in outs), tangent_out[None])


def solution(mesh):
    return jax.shard_map(
        local,
        mesh=mesh,
        in_specs=(
            P("exp", "ctx", None),
            P("exp", "ctx", None),
            P("exp", "ctx", None),
            P("exp", "ctx", None),
            P("exp", "ctx", None),
            P("exp", "ctx", None),
            P("exp", "ctx", None),
            P("exp", None, None),
            P("exp", None, None),
            P("exp", None, None),
        ),
        out_specs=(
            P("exp", "ctx", None),
            P("exp", "ctx", None),
            P("exp", "ctx", None),
            P("exp", "ctx", None),
            P("exp", "ctx", None),
        ),
        check_vma=False,
    )
```

time: 219 us -> 150 us (0.68)
  waiting for transfers between devices: 78.7 us -> 39.3 us
  starting transfers between devices: 63.3 us -> 39.2 us
  other arithmetic: 6.39 us -> 0.77 us
  Pallas kernels: 52.7 us -> 57.8 us
  local copies, waits for them, and re-layouts: 14.6 us -> 10 us
    ppermute x3 -> x2, waiting for transfers between devices: 58.8 us -> 23.1 us  [crossed(): return lax.ppermute(x, 'exp', [(0, 1), (1, 0)])]
    ppermute x10, starting transfers between devices: 57.9 us -> 31.8 us  [moved(): return lax.ppermute(x, 'ctx', pairs)]
    ppermute x10, waiting for transfers between devices: 19.9 us -> 12.1 us  [moved(): return lax.ppermute(x, 'ctx', pairs)]
    select_n x8 -> x0, other arithmetic: 5.65 us -> none  [the longest x2 2.28 us: in_order(): jnp.where(core == 0, jnp.concatenate([kept, got], axis=1), jnp.concatenat...]
    pallas_call x6 -> x15, Pallas kernels: 52.7 us -> 57.8 us  [call(): pl.pallas_call(kernel, out_shape=outs, in_specs=[space for _, space in ar...]
    slice x7 -> x0, local copies, waits for them, and re-layouts: 4.21 us -> none  [the longest x3 2.17 us: half(): x[0][:, at * width:(at + 1) * width]]
    ppermute x8 -> x10, waiting for transfers between devices: 0.02 us -> 4.08 us  [swapped(): lax.ppermute(x, 'ctx', [(i, i ^ bit) for i in range(lax.axis_size('ctx'))])]
    dynamic_slice x3 -> x0, local copies, waits for them, and re-layouts: 2.6 us -> none  [exchanged_weights(): over = crossed(lax.dynamic_slice_in_dim(matrix, core * depth, depth, 0))]
  transfers between devices with their start and end apart: 21 -> 22, of which waited for: 5 -> 7; matrix products, arithmetic and copies ran while one was open for 3% -> 0% of each run, Pallas kernels for 10% -> 26%
where the time goes in v2:
time: 150 us; the launch traced here: 148 us
  Pallas kernels  57.8 us (39%)
  waiting for transfers between devices  39.3 us (26%)
  starting transfers between devices  39.2 us (26%)
  local copies, waits for them, and re-layouts  10 us (7%)
    pallas_call x15, Pallas kernels, call(): pl.pallas_call(kernel, out_shape=outs, in_specs=[space for _, space in ar...  57.8 us
    ppermute x10, starting transfers between devices, moved(): return lax.ppermute(x, 'ctx', pairs)  31.8 us
    ppermute x2, waiting for transfers between devices, crossed(): return lax.ppermute(x, 'exp', [(0, 1), (1, 0)])  23.1 us
    ppermute x10, waiting for transfers between devices, moved(): return lax.ppermute(x, 'ctx', pairs)  12.1 us
    unnamed x54, local copies, waits for them, and re-layouts  9.82 us
    ppermute x10, starting transfers between devices, swapped(): lax.ppermute(x, 'ctx', [(i, i ^ bit) for i in range(lax.axis_size('ctx'))])  4.2 us
    ppermute x10, waiting for transfers between devices, swapped(): lax.ppermute(x, 'ctx', [(i, i ^ bit) for i in range(lax.axis_size('ctx'))])  4.08 us
    ppermute x2, starting transfers between devices, crossed(): return lax.ppermute(x, 'exp', [(0, 1), (1, 0)])  3.15 us
  transfers between devices with their start and end apart: 22, of which 7 were waited for; matrix products, arithmetic and copies ran while one was open for 0% of the time, Pallas kernels for 26%

profile of v2, /device:TPU:0, one launch (start us, length us, event | category | flops | bytes accessed | tf_op | source)
XLA Modules:
  0.0 148.3 jit_solution(1999787971190549189)
XLA Ops:
  0.6 0.7 compare_bitcast_fusion
  1.3 0.1 copy.21
  1.4 0.0 copy-start.10
  1.5 1.2 copy-done.10
  2.6 1.0 copy-done.11
  3.7 1.0 copy-done.12
  4.7 0.2 shard_map.137
  5.0 0.9 copy-done.19
  5.9 0.5 collective-permute-start
  6.3 0.1 pad_add_fusion.me
  6.4 1.6 %copy-done.1 = bf16[1,2048,512]{2,1,0:T(8,128)(2,1)S(1)} copy-done((bf16[1,2048,512]{2,1,0:T(8,128)(2,1)S(1)}, bf16[1,2048,512]{2,1,0:T(8,128)(2,1)}, u32[]{:S(2)}) %copy-start.1) | copy-done | bytes 2097176
  8.0 1.6 %copy-done.3 = bf16[1,512,2048]{2,1,0:T(8,128)(2,1)S(1)} copy-done((bf16[1,512,2048]{2,1,0:T(8,128)(2,1)S(1)}, bf16[1,512,2048]{2,1,0:T(8,128)(2,1)}, u32[]{:S(2)}) %copy-start.3) | copy-done | bytes 2097176
  9.6 0.7 shard_map.138
  10.3 2.6 %collective-permute-start.3 = (bf16[1024,512]{1,0:T(8,128)(2,1)S(1)}, bf16[1024,512]{1,0:T(8,128)(2,1)}, u32[]{:S(2)}, u32[]{:S(2)}) collective-permute-start(bf16[1024,512]{1,0:T(8,128)(2,1)S(1)} %get-tuple-element.43.after), channel_id=1, source_target_pairs={{0,1},{1,0},{2,3},{3,2},{4,5},{5,4},{6,7},{7,6},{8,9},{9,8},{10,11... | collective-permute-start | bytes 3145736 | tf_op jit(solution)/shard_map/ppermute | solution.py:33
  12.9 0.0 collective-permute-done.got
  12.9 1.4 shard_map.139
  14.3 0.0 copy-start.21
  14.3 3.5 %collective-permute-start.2 = (bf16[256,2048]{1,0:T(8,128)(2,1)S(1)}, bf16[256,2048]{1,0:T(8,128)(2,1)S(1)}, u32[]{:S(2)}, u32[]{:S(2)}) collective-permute-start(bf16[256,2048]{1,0:T(8,128)(2,1)S(1)} %get-tuple-element.45.own), channel_id=1, source_target_pairs={{0,4},{2,6},{4,8},{6,10},{8,12},{10,14},{12,16},{14,18},{16,20},{1... | collective-permute-start | bytes 3145736 | tf_op jit(solution)/shard_map/ppermute | solution.py:25
  17.8 3.5 %collective-permute-start.1 = (bf16[128,2048]{1,0:T(8,128)(2,1)S(1)}, bf16[128,2048]{1,0:T(8,128)(2,1)S(1)}, u32[]{:S(2)}, u32[]{:S(2)}) collective-permute-start(bf16[128,2048]{1,0:T(8,128)(2,1)S(1)} %get-tuple-element.44), channel_id=1, source_target_pairs={{0,8},{2,10},{4,12},{6,14},{8,16},{10,18},{12,20},{14,22},{16,24},... | collective-permute-start | bytes 1572872 | tf_op jit(solution)/shard_map/ppermute | solution.py:25
  21.3 0.6 collective-permute-start.5
  21.9 15.1 %collective-permute-done.3.after.first = bf16[1024,512]{1,0:T(8,128)(2,1)} collective-permute-done((bf16[1024,512]{1,0:T(8,128)(2,1)S(1)}, bf16[1024,512]{1,0:T(8,128)(2,1)}, u32[]{:S(2)}, u32[]{:S(2)}) %collective-permute-start.3) | collective-permute-done | bytes 1048608 | tf_op jit(solution)/shard_map/ppermute | solution.py:33
  37.0 2.0 %collective-permute-start.7 = (bf16[1024,512]{1,0:T(8,128)(2,1)}, bf16[1024,512]{1,0:T(8,128)(2,1)}, u32[]{:S(2)}, u32[]{:S(2)}) collective-permute-start(bf16[1024,512]{1,0:T(8,128)(2,1)} %collective-permute-done.3.after.first), channel_id=1, source_target_pairs={{0,4},{2,6},{4,0},{6,2},{8,12},{10,14},{12,8},{14,10},{16,20},{18,... | collective-permute-start | bytes 3145736 | tf_op jit(solution)/shard_map/ppermute | solution.py:29
  39.0 2.3 %collective-permute-done.2.after.near = bf16[256,2048]{1,0:T(8,128)(2,1)S(1)} collective-permute-done((bf16[256,2048]{1,0:T(8,128)(2,1)S(1)}, bf16[256,2048]{1,0:T(8,128)(2,1)S(1)}, u32[]{:S(2)}, u32[]{:S(2)}) %collective-permute-start.2) | collective-permute-done | bytes 1048608 | tf_op jit(solution)/shard_map/ppermute | solution.py:25
  41.3 0.1 shard_map.140
  41.4 0.0 copy-start.15
  41.4 0.8 copy-done.15
  42.2 9.0 %shard_map.141 = (bf16[128,1024]{1,0:T(8,128)(2,1)S(1)}, bf16[128,1024]{1,0:T(8,128)(2,1)S(1)}, bf16[256,128]{1,0:T(8,128)(2,1)S(1)}) custom-call(s32[1]{0:T(128)} %bitcast.me, bf16[128,2048]{1,0:T(8,128)(2,1)S(1)} %collective-permute-done.1.far, bf16[256,2048]{1,0:T(8,128)(2,1)S(1)} %collective-permute-done.2.after.near, ...), custom_call_target="tpu_custom_call" | custom-call | flops 9900000256 | tf_op jit(solution)/shard_map/pallas_call | solution.py:81
  51.2 0.0 copy-start.17
  51.2 0.0 copy-start.23
  51.3 8.0 %collective-permute-done.5.refs_0_ = bf16[256,2048]{1,0:T(8,128)(2,1)} collective-permute-done((bf16[256,2048]{1,0:T(8,128)(2,1)S(1)}, bf16[256,2048]{1,0:T(8,128)(2,1)}, u32[]{:S(2)}, u32[]{:S(2)}) %collective-permute-start.5) | collective-permute-done | bytes 1048608 | tf_op jit(solution)/shard_map/ppermute | solution.py:33
  59.3 0.1 collective-permute-start.6
  59.4 0.5 collective-permute-start.8
  59.9 3.1 %collective-permute-done.7.refs_0_ = bf16[1024,512]{1,0:T(8,128)(2,1)} collective-permute-done((bf16[1024,512]{1,0:T(8,128)(2,1)}, bf16[1024,512]{1,0:T(8,128)(2,1)}, u32[]{:S(2)}, u32[]{:S(2)}) %collective-permute-start.7) | collective-permute-done | bytes 1048608 | tf_op jit(solution)/shard_map/ppermute | solution.py:29
  63.0 0.0 collective-permute-start.9
  63.0 0.5 collective-permute-start.4
  63.5 0.1 copy.22.picks
  63.6 1.4 collective-permute-start.14
  65.1 5.0 %collective-permute-start.13 = (bf16[256,1024]{1,0:T(8,128)(2,1)}, bf16[256,1024]{1,0:T(8,128)(2,1)S(1)}, u32[]{:S(2)}, u32[]{:S(2)}) collective-permute-start(bf16[256,1024]{1,0:T(8,128)(2,1)} %copy-done.14), channel_id=1, source_target_pairs={{0,4},{2,6},{4,8},{6,10},{8,12},{10,14},{12,16},{14,18},{16,20},{1... | collective-permute-start | bytes 1572872 | tf_op jit(solution)/shard_map/ppermute | solution.py:25
  70.1 0.0 copy-start.4
  70.2 1.6 %copy-done.4 = bf16[1,512,2048]{2,1,0:T(8,128)(2,1)S(1)} copy-done((bf16[1,512,2048]{2,1,0:T(8,128)(2,1)S(1)}, bf16[1,512,2048]{2,1,0:T(8,128)(2,1)}, u32[]{:S(2)}) %copy-start.4) | copy-done | bytes 2097176
  71.7 3.1 %shard_map.143.hidden_grad = f32[128,1024]{1,0:T(8,128)S(1)} custom-call(s32[2]{0:T(128)S(1)} %pad_add_fusion.me, bf16[1,128,2048]{2,1,0:T(8,128)(2,1)S(1)} %copy-done.13, bf16[512,2048]{1,0:T(8,128)(2,1)S(1)} %bitcast.23, bf16[256,2048]{1,0:T(8,128)(2,1)} %shard_map.142.over, bf16[256,2048]{1,0:T(8,128)(2,1)} %collective-permute-done.6.over_s), custom_call_target="tpu_custom_call" | custom-call | flops 2750000128 | tf_op jit(solution)/shard_map/pallas_call | solution.py:81
  74.9 4.9 %collective-permute-start.12 = (bf16[128,1024]{1,0:T(8,128)(2,1)S(1)}, bf16[128,1024]{1,0:T(8,128)(2,1)S(1)}, u32[]{:S(2)}, u32[]{:S(2)}) collective-permute-start(bf16[128,1024]{1,0:T(8,128)(2,1)S(1)} %copy-done.16), channel_id=1, source_target_pairs={{0,8},{2,10},{4,12},{6,14},{8,16},{10,18},{12,20},{14,22},{16,24},... | collective-permute-start | bytes 786440 | tf_op jit(solution)/shard_map/ppermute | solution.py:25
  79.7 0.0 copy-start.5
  79.7 1.4 collective-permute-start.15
  81.2 5.9 %shard_map.145 = (bf16[128,1152]{1,0:T(8,128)(2,1)S(1)}, bf16[128,1152]{1,0:T(8,128)(2,1)S(1)}, bf16[128,1024]{1,0:T(8,128)(2,1)S(1)}, f32[128,1024]{1,0:T(8,128)S(1)}, f32[128,1024]{1,0:T(8,128)S(1)}) custom-call(s32[2]{0:T(128)S(1)} %pad_add_fusion.me, bf16[128,1024]{1,0:T(8,128)(2,1)S(1)} %copy-done.24, bf16[128,1024]{1,0:T(8,128)(2,1)} %collective-permute-done.4.got, ...), custom_call_target="tpu_custom_call" | custom-call | flops 6600000000 | tf_op jit(solution)/shard_map/pallas_call | solution.py:81
  87.2 0.1 collective-permute-start.10
  87.2 4.2 %shard_map.146.after = bf16[128,2048]{1,0:T(8,128)(2,1)} custom-call(s32[2]{0:T(128)S(1)} %pad_add_fusion.me, bf16[128,1024]{1,0:T(8,128)(2,1)S(1)} %copy-done.24, bf16[128,1024]{1,0:T(8,128)(2,1)} %collective-permute-done.4.got, bf16[128,1024]{1,0:T(8,128)(2,1)S(1)} %get-tuple-element.52.hidden, f32[128,3]{1,0:T(8,128)S(1)} %copy.22.picks, ...), custom_call_target="tpu_custom_call" | custom-call | flops 4400000000 | tf_op jit(solution)/shard_map/pallas_call | solution.py:81
  91.5 0.0 copy-start.22
  91.5 0.1 shard_map.147
  91.6 1.4 collective-permute-start.18
  93.1 4.6 %collective-permute-start.17 = (bf16[256,1152]{1,0:T(8,128)(2,1)S(1)}, bf16[256,1152]{1,0:T(8,128)(2,1)S(1)}, u32[]{:S(2)}, u32[]{:S(2)}) collective-permute-start(bf16[256,1152]{1,0:T(8,128)(2,1)S(1)} %get-tuple-element.56.co), channel_id=1, source_target_pairs={{0,4},{2,6},{4,8},{6,10},{8,12},{10,14},{12,16},{14,18},{16,20},{1... | collective-permute-start | bytes 1769480 | tf_op jit(solution)/shard_map/ppermute | solution.py:25
  97.7 4.5 %collective-permute-start.16 = (bf16[128,1152]{1,0:T(8,128)(2,1)S(1)}, bf16[128,1152]{1,0:T(8,128)(2,1)S(1)}, u32[]{:S(2)}, u32[]{:S(2)}) collective-permute-start(bf16[128,1152]{1,0:T(8,128)(2,1)S(1)} %get-tuple-element.61), channel_id=1, source_target_pairs={{0,8},{2,10},{4,12},{6,14},{8,16},{10,18},{12,20},{14,22},{16,24},... | collective-permute-start | bytes 884744 | tf_op jit(solution)/shard_map/ppermute | solution.py:25
  102.2 0.0 copy-start.18
  102.3 1.6 %collective-permute-start.19 = (bf16[128,1152]{1,0:T(8,128)(2,1)S(1)}, bf16[128,1152]{1,0:T(8,128)(2,1)S(1)}, u32[]{:S(2)}, u32[]{:S(2)}) collective-permute-start(bf16[128,1152]{1,0:T(8,128)(2,1)S(1)} %get-tuple-element.62), channel_id=1, source_target_pairs={{8,0},{10,2},{12,4},{14,6},{16,8},{18,10},{20,12},{22,14},{24,16},... | collective-permute-start | bytes 884744 | tf_op jit(solution)/shard_map/ppermute | solution.py:25
  103.9 8.3 %shard_map.148 = (f32[8,2,512,128]{3,2,1,0:T(8,128)S(1)}, bf16[8,2,128,512]{3,2,1,0:T(8,128)(2,1)S(1)}, bf16[256,1024]{1,0:T(8,128)(2,1)S(1)}, bf16[128,1024]{1,...) custom-call(s32[1]{0:T(128)} %bitcast.me, ...), custom_call_target="tpu_custom_call" | custom-call | flops 13200000000 | tf_op jit(solution)/shard_map/pallas_call | solution.py:81
  112.2 4.5 %collective-permute-done.19.cfa = bf16[128,1152]{1,0:T(8,128)(2,1)S(1)} collective-permute-done((bf16[128,1152]{1,0:T(8,128)(2,1)S(1)}, bf16[128,1152]{1,0:T(8,128)(2,1)S(1)}, u32[]{:S(2)}, u32[]{:S(2)}) %collective-permute-start.19) | collective-permute-done | bytes 294944 | tf_op jit(solution)/shard_map/ppermute | solution.py:25
  116.7 5.3 %collective-permute-done.17.cnb = bf16[256,1152]{1,0:T(8,128)(2,1)S(1)} collective-permute-done((bf16[256,1152]{1,0:T(8,128)(2,1)S(1)}, bf16[256,1152]{1,0:T(8,128)(2,1)S(1)}, u32[]{:S(2)}, u32[]{:S(2)}) %collective-permute-start.17) | collective-permute-done | bytes 589856 | tf_op jit(solution)/shard_map/ppermute | solution.py:25
  122.0 18.1 %shard_map.149 = (bf16[128,2048]{1,0:T(8,128)(2,1)S(1)}, bf16[128,2048]{1,0:T(8,128)(2,1)S(1)}, bf16[128,1024]{1,0:T(8,128)(2,1)S(1)}, bf16[128,1024]{1,0:T(8,128)(2,1)S(1)}) custom-call(s32[1]{0:T(128)} %bitcast.me, bf16[128,2048]{1,0:T(8,128)(2,1)S(1)} %collective-permute-done.1.far, bf16[256,2048]{1,0:T(8,128)(2,1)S(1)} %copy-done.9, ...), custom_call_target="tpu_custom_call" | custom-call | flops 17600000000 | tf_op jit(solution)/shard_map/pallas_call | solution.py:81
  140.1 0.1 collective-permute-start.21
  140.2 0.4 collective-permute-start.20
  140.6 0.1 collective-permute-start.11
  140.7 0.9 collective-permute-done.21.got
  141.7 5.4 %shard_map.151 = bf16[128,2048]{1,0:T(8,128)(2,1)} custom-call(s32[2]{0:T(128)S(1)} %pad_add_fusion.me, bf16[128,1024]{1,0:T(8,128)(2,1)S(1)} %get-tuple-element.73.keep, bf16[128,1024]{1,0:T(8,128)(2,1)S(1)} %collective-permute-done.21.got, f32[128,1024]{1,0:T(8,128)S(1)} %get-tuple-element.75.slope_up, f32[128,1024]{1,0:T(8,128)S(1)} %get-tuple-element.76.active, ...), custom_call_target="tpu_custom_call" | custom-call | flops 4950000128 | tf_op jit(solution)/shard_map/pallas_call | solution.py:81
  147.0 1.2 shard_map.150
  (57 shorter events, 0.1 us)
Async XLA Ops:
  1.4 5.0 %copy-start = (bf16[1,2048,512]{2,1,0:T(8,128)(2,1)S(1)}, bf16[1,2048,512]{2,1,0:T(8,128)(2,1)}, u32[]{:S(2)}) copy-start(bf16[1,2048,512]{2,1,0:T(8,128)(2,1)} %param.17) | copy-start | bytes 6291460
  1.4 1.2 copy-start.10
  2.6 1.0 copy-start.11
  3.7 1.0 copy-start.12
  5.0 0.9 copy-start.19
  5.9 7.0 %collective-permute-start = (bf16[128,3200]{1,0:T(8,128)(2,1)S(1)}, bf16[128,3200]{1,0:T(8,128)(2,1)}, u32[]{:S(2)}, u32[]{:S(2)}) collective-permute-start(bf16[128,3200]{1,0:T(8,128)(2,1)S(1)} %get-tuple-element.42.after), channel_id=1, source_target_pairs={{0,2},{2,0},{4,6},{6,4},{8,10},{10,8},{12,14},{14,12},{16,18},{18,... | collective-permute-start | bytes 2457608 | tf_op jit(solution)/shard_map/ppermute | solution.py:29
  6.4 1.6 %copy-start.1 = (bf16[1,2048,512]{2,1,0:T(8,128)(2,1)S(1)}, bf16[1,2048,512]{2,1,0:T(8,128)(2,1)}, u32[]{:S(2)}) copy-start(bf16[1,2048,512]{2,1,0:T(8,128)(2,1)} %param.18) | copy-start | bytes 6291460
  8.0 1.6 %copy-start.3 = (bf16[1,512,2048]{2,1,0:T(8,128)(2,1)S(1)}, bf16[1,512,2048]{2,1,0:T(8,128)(2,1)}, u32[]{:S(2)}) copy-start(bf16[1,512,2048]{2,1,0:T(8,128)(2,1)} %param.19) | copy-start | bytes 6291460
  9.6 3.3 %copy-start.20 = (bf16[128,3200]{1,0:T(8,128)(2,1)S(1)}, bf16[128,3200]{1,0:T(8,128)(2,1)}, u32[]{:S(2)}) copy-start(bf16[128,3200]{1,0:T(8,128)(2,1)} %copy-done.19) | copy-start | bytes 2457604
  10.3 26.7 %collective-permute-start.3 = (bf16[1024,512]{1,0:T(8,128)(2,1)S(1)}, bf16[1024,512]{1,0:T(8,128)(2,1)}, u32[]{:S(2)}, u32[]{:S(2)}) collective-permute-start(bf16[1024,512]{1,0:T(8,128)(2,1)S(1)} %get-tuple-element.43.after), channel_id=1, source_target_pairs={{0,1},{1,0},{2,3},{3,2},{4,5},{5,4},{6,7},{7,6},{8,9},{9,8},{10,11... | collective-permute-start | bytes 3145736 | tf_op jit(solution)/shard_map/ppermute | solution.py:33
  14.3 36.9 %copy-start.6 = (bf16[256,2048]{1,0:T(8,128)(2,1)}, bf16[256,2048]{1,0:T(8,128)(2,1)S(1)}, u32[]{:S(2)}) copy-start(bf16[256,2048]{1,0:T(8,128)(2,1)S(1)} %get-tuple-element.45.own) | copy-start | bytes 3145732
  14.3 36.9 %copy-start.21 = (bf16[256,1024]{1,0:T(8,128)(2,1)}, bf16[256,1024]{1,0:T(8,128)(2,1)S(1)}, u32[]{:S(2)}) copy-start(bf16[256,1024]{1,0:T(8,128)(2,1)S(1)} %get-tuple-element.46.x.q2) | copy-start | bytes 1572868
  14.3 26.9 %collective-permute-start.2 = (bf16[256,2048]{1,0:T(8,128)(2,1)S(1)}, bf16[256,2048]{1,0:T(8,128)(2,1)S(1)}, u32[]{:S(2)}, u32[]{:S(2)}) collective-permute-start(bf16[256,2048]{1,0:T(8,128)(2,1)S(1)} %get-tuple-element.45.own), channel_id=1, source_target_pairs={{0,4},{2,6},{4,8},{6,10},{8,12},{10,14},{12,16},{14,18},{16,20},{1... | collective-permute-start | bytes 3145736 | tf_op jit(solution)/shard_map/ppermute | solution.py:25
  17.8 24.3 %collective-permute-start.1 = (bf16[128,2048]{1,0:T(8,128)(2,1)S(1)}, bf16[128,2048]{1,0:T(8,128)(2,1)S(1)}, u32[]{:S(2)}, u32[]{:S(2)}) collective-permute-start(bf16[128,2048]{1,0:T(8,128)(2,1)S(1)} %get-tuple-element.44), channel_id=1, source_target_pairs={{0,8},{2,10},{4,12},{6,14},{8,16},{10,18},{12,20},{14,22},{16,24},... | collective-permute-start | bytes 1572872 | tf_op jit(solution)/shard_map/ppermute | solution.py:25
  21.3 38.0 %collective-permute-start.5 = (bf16[256,2048]{1,0:T(8,128)(2,1)S(1)}, bf16[256,2048]{1,0:T(8,128)(2,1)}, u32[]{:S(2)}, u32[]{:S(2)}) collective-permute-start(bf16[256,2048]{1,0:T(8,128)(2,1)S(1)} %get-tuple-element.51), channel_id=1, source_target_pairs={{0,1},{1,0},{2,3},{3,2},{4,5},{5,4},{6,7},{7,6},{8,9},{9,8},{10,11... | collective-permute-start | bytes 3145736 | tf_op jit(solution)/shard_map/ppermute | solution.py:33
  37.0 26.0 %collective-permute-start.7 = (bf16[1024,512]{1,0:T(8,128)(2,1)}, bf16[1024,512]{1,0:T(8,128)(2,1)}, u32[]{:S(2)}, u32[]{:S(2)}) collective-permute-start(bf16[1024,512]{1,0:T(8,128)(2,1)} %collective-permute-done.3.after.first), channel_id=1, source_target_pairs={{0,4},{2,6},{4,0},{6,2},{8,12},{10,14},{12,8},{14,10},{16,20},{18,... | collective-permute-start | bytes 3145736 | tf_op jit(solution)/shard_map/ppermute | solution.py:29
  41.3 9.9 %copy-start.8 = (bf16[256,2048]{1,0:T(8,128)(2,1)}, bf16[256,2048]{1,0:T(8,128)(2,1)S(1)}, u32[]{:S(2)}) copy-start(bf16[256,2048]{1,0:T(8,128)(2,1)S(1)} %collective-permute-done.2.after.near) | copy-start | bytes 3145732
  41.4 0.8 copy-start.15
  42.2 9.1 %copy-start.14 = (bf16[256,1024]{1,0:T(8,128)(2,1)}, bf16[256,1024]{1,0:T(8,128)(2,1)S(1)}, u32[]{:S(2)}) copy-start(bf16[256,1024]{1,0:T(8,128)(2,1)S(1)} %get-tuple-element.48.cut) | copy-start | bytes 1572868
  51.2 11.7 %copy-start.17 = (bf16[128,1024]{1,0:T(8,128)(2,1)}, bf16[128,1024]{1,0:T(8,128)(2,1)S(1)}, u32[]{:S(2)}) copy-start(bf16[128,1024]{1,0:T(8,128)(2,1)S(1)} %get-tuple-element.50) | copy-start | bytes 786436
  51.2 11.7 %copy-start.23 = (bf16[128,1024]{1,0:T(8,128)(2,1)}, bf16[128,1024]{1,0:T(8,128)(2,1)S(1)}, u32[]{:S(2)}) copy-start(bf16[128,1024]{1,0:T(8,128)(2,1)S(1)} %get-tuple-element.49.refs_1_.keep) | copy-start | bytes 786436
  59.3 3.7 %copy-start.26 = (s32[1,128,1]{1,2,0:T(1,128)S(1)}, s32[1,128,1]{1,2,0:T(1,128)}, u32[]{:S(2)}) copy-start(s32[1,128,1]{1,2,0:T(1,128)} %param.14) | copy-start | bytes 1540
  59.3 4.2 %copy-start.25 = (f32[1,128,1]{1,2,0:T(1,128)S(1)}, f32[1,128,1]{1,2,0:T(1,128)}, u32[]{:S(2)}) copy-start(f32[1,128,1]{1,2,0:T(1,128)} %param.15) | copy-start | bytes 1540
  59.3 10.8 %copy-start.13 = (bf16[1,128,2048]{2,1,0:T(8,128)(2,1)S(1)}, bf16[1,128,2048]{2,1,0:T(8,128)(2,1)}, u32[]{:S(2)}) copy-start(bf16[1,128,2048]{2,1,0:T(8,128)(2,1)} %cot.3) | copy-start | bytes 1572868
  59.3 5.8 %collective-permute-start.6 = (bf16[256,2048]{1,0:T(8,128)(2,1)}, bf16[256,2048]{1,0:T(8,128)(2,1)}, u32[]{:S(2)}, u32[]{:S(2)}) collective-permute-start(bf16[256,2048]{1,0:T(8,128)(2,1)} %shard_map.142.over), channel_id=1, source_target_pairs={{0,2},{2,0},{4,6},{6,4},{8,10},{10,8},{12,14},{14,12},{16,18},{18,... | collective-permute-start | bytes 3145736 | tf_op jit(solution)/shard_map/ppermute | solution.py:29
  59.4 15.5 %collective-permute-start.8 = (bf16[1024,512]{1,0:T(8,128)(2,1)}, bf16[1024,512]{1,0:T(8,128)(2,1)}, u32[]{:S(2)}, u32[]{:S(2)}) collective-permute-start(bf16[1024,512]{1,0:T(8,128)(2,1)} %collective-permute-done.3.after.first), channel_id=1, source_target_pairs={{0,2},{2,0},{4,6},{6,4},{8,10},{10,8},{12,14},{14,12},{16,18},{18,... | collective-permute-start | bytes 3145736 | tf_op jit(solution)/shard_map/ppermute | solution.py:29
  63.0 18.2 %collective-permute-start.9 = (bf16[1024,512]{1,0:T(8,128)(2,1)}, bf16[1024,512]{1,0:T(8,128)(2,1)}, u32[]{:S(2)}, u32[]{:S(2)}) collective-permute-start(bf16[1024,512]{1,0:T(8,128)(2,1)} %shard_map.144.second), channel_id=1, source_target_pairs={{0,2},{2,0},{4,6},{6,4},{8,10},{10,8},{12,14},{14,12},{16,18},{18,... | collective-permute-start | bytes 3145736 | tf_op jit(solution)/shard_map/ppermute | solution.py:29
  63.0 16.7 %collective-permute-start.4 = (bf16[128,1024]{1,0:T(8,128)(2,1)}, bf16[128,1024]{1,0:T(8,128)(2,1)}, u32[]{:S(2)}, u32[]{:S(2)}) collective-permute-start(bf16[128,1024]{1,0:T(8,128)(2,1)} %copy-done.17), channel_id=1, source_target_pairs={{0,2},{2,0},{4,6},{6,4},{8,10},{10,8},{12,14},{14,12},{16,18},{18,... | collective-permute-start | bytes 786440 | tf_op jit(solution)/shard_map/ppermute | solution.py:29
  63.6 17.6 %copy-start.2 = (bf16[1,2048,512]{2,1,0:T(8,128)(2,1)S(1)}, bf16[1,2048,512]{2,1,0:T(8,128)(2,1)}, u32[]{:S(2)}) copy-start(bf16[1,2048,512]{2,1,0:T(8,128)(2,1)} %param.18) | copy-start | bytes 6291460
  63.6 38.6 %collective-permute-start.14 = (bf16[256,1024]{1,0:T(8,128)(2,1)}, bf16[256,1024]{1,0:T(8,128)(2,1)S(1)}, u32[]{:S(2)}, u32[]{:S(2)}) collective-permute-start(bf16[256,1024]{1,0:T(8,128)(2,1)} %copy-done.14), channel_id=1, source_target_pairs={{4,0},{6,2},{8,4},{10,6},{12,8},{14,10},{16,12},{18,14},{20,16},{2... | collective-permute-start | bytes 1572872 | tf_op jit(solution)/shard_map/ppermute | solution.py:25
  65.1 47.1 %collective-permute-start.13 = (bf16[256,1024]{1,0:T(8,128)(2,1)}, bf16[256,1024]{1,0:T(8,128)(2,1)S(1)}, u32[]{:S(2)}, u32[]{:S(2)}) collective-permute-start(bf16[256,1024]{1,0:T(8,128)(2,1)} %copy-done.14), channel_id=1, source_target_pairs={{0,4},{2,6},{4,8},{6,10},{8,12},{10,14},{12,16},{14,18},{16,20},{1... | collective-permute-start | bytes 1572872 | tf_op jit(solution)/shard_map/ppermute | solution.py:25
  70.1 1.6 %copy-start.4 = (bf16[1,512,2048]{2,1,0:T(8,128)(2,1)S(1)}, bf16[1,512,2048]{2,1,0:T(8,128)(2,1)}, u32[]{:S(2)}) copy-start(bf16[1,512,2048]{2,1,0:T(8,128)(2,1)} %param.19) | copy-start | bytes 6291460
  71.7 3.1 %copy-start.16 = (bf16[128,1024]{1,0:T(8,128)(2,1)S(1)}, bf16[128,1024]{1,0:T(8,128)(2,1)}, u32[]{:S(2)}) copy-start(bf16[128,1024]{1,0:T(8,128)(2,1)} %copy-done.15) | copy-start | bytes 786436
  71.7 9.5 %copy-start.24 = (bf16[128,1024]{1,0:T(8,128)(2,1)S(1)}, bf16[128,1024]{1,0:T(8,128)(2,1)}, u32[]{:S(2)}) copy-start(bf16[128,1024]{1,0:T(8,128)(2,1)} %copy-done.23) | copy-start | bytes 786436
  74.9 18.2 %collective-permute-start.12 = (bf16[128,1024]{1,0:T(8,128)(2,1)S(1)}, bf16[128,1024]{1,0:T(8,128)(2,1)S(1)}, u32[]{:S(2)}, u32[]{:S(2)}) collective-permute-start(bf16[128,1024]{1,0:T(8,128)(2,1)S(1)} %copy-done.16), channel_id=1, source_target_pairs={{0,8},{2,10},{4,12},{6,14},{8,16},{10,18},{12,20},{14,22},{16,24},... | collective-permute-start | bytes 786440 | tf_op jit(solution)/shard_map/ppermute | solution.py:25
  79.7 7.5 %copy-start.5 = (bf16[1,512,2048]{2,1,0:T(8,128)(2,1)S(1)}, bf16[1,512,2048]{2,1,0:T(8,128)(2,1)}, u32[]{:S(2)}) copy-start(bf16[1,512,2048]{2,1,0:T(8,128)(2,1)} %param.19) | copy-start | bytes 6291460
  79.7 17.9 %collective-permute-start.15 = (bf16[128,1024]{1,0:T(8,128)(2,1)S(1)}, bf16[128,1024]{1,0:T(8,128)(2,1)S(1)}, u32[]{:S(2)}, u32[]{:S(2)}) collective-permute-start(bf16[128,1024]{1,0:T(8,128)(2,1)S(1)} %get-tuple-element.60), channel_id=1, source_target_pairs={{8,0},{10,2},{12,4},{14,6},{16,8},{18,10},{20,12},{22,14},{24,16},... | collective-permute-start | bytes 786440 | tf_op jit(solution)/shard_map/ppermute | solution.py:25
  87.2 4.4 %collective-permute-start.10 = (bf16[128,1152]{1,0:T(8,128)(2,1)S(1)}, bf16[128,1152]{1,0:T(8,128)(2,1)S(1)}, u32[]{:S(2)}, u32[]{:S(2)}) collective-permute-start(bf16[128,1152]{1,0:T(8,128)(2,1)S(1)} %get-tuple-element.54), channel_id=1, source_target_pairs={{0,2},{2,0},{4,6},{6,4},{8,10},{10,8},{12,14},{14,12},{16,18},{18,... | collective-permute-start | bytes 884744 | tf_op jit(solution)/shard_map/ppermute | solution.py:29
  91.5 12.4 %copy-start.7 = (bf16[256,2048]{1,0:T(8,128)(2,1)S(1)}, bf16[256,2048]{1,0:T(8,128)(2,1)}, u32[]{:S(2)}) copy-start(bf16[256,2048]{1,0:T(8,128)(2,1)} %copy-done.6) | copy-start | bytes 3145732
  91.5 12.4 %copy-start.9 = (bf16[256,2048]{1,0:T(8,128)(2,1)S(1)}, bf16[256,2048]{1,0:T(8,128)(2,1)}, u32[]{:S(2)}) copy-start(bf16[256,2048]{1,0:T(8,128)(2,1)} %copy-done.8) | copy-start | bytes 3145732
  91.5 12.4 %copy-start.22 = (bf16[256,1024]{1,0:T(8,128)(2,1)S(1)}, bf16[256,1024]{1,0:T(8,128)(2,1)}, u32[]{:S(2)}) copy-start(bf16[256,1024]{1,0:T(8,128)(2,1)} %copy-done.21) | copy-start | bytes 1572868
  91.6 25.1 %collective-permute-start.18 = (bf16[256,1152]{1,0:T(8,128)(2,1)S(1)}, bf16[256,1152]{1,0:T(8,128)(2,1)S(1)}, u32[]{:S(2)}, u32[]{:S(2)}) collective-permute-start(bf16[256,1152]{1,0:T(8,128)(2,1)S(1)} %get-tuple-element.56.co), channel_id=1, source_target_pairs={{4,0},{6,2},{8,4},{10,6},{12,8},{14,10},{16,12},{18,14},{20,16},{2... | collective-permute-start | bytes 1769480 | tf_op jit(solution)/shard_map/ppermute | solution.py:25
  93.1 28.9 %collective-permute-start.17 = (bf16[256,1152]{1,0:T(8,128)(2,1)S(1)}, bf16[256,1152]{1,0:T(8,128)(2,1)S(1)}, u32[]{:S(2)}, u32[]{:S(2)}) collective-permute-start(bf16[256,1152]{1,0:T(8,128)(2,1)S(1)} %get-tuple-element.56.co), channel_id=1, source_target_pairs={{0,4},{2,6},{4,8},{6,10},{8,12},{10,14},{12,16},{14,18},{16,20},{1... | collective-permute-start | bytes 1769480 | tf_op jit(solution)/shard_map/ppermute | solution.py:25
  97.7 14.5 %collective-permute-start.16 = (bf16[128,1152]{1,0:T(8,128)(2,1)S(1)}, bf16[128,1152]{1,0:T(8,128)(2,1)S(1)}, u32[]{:S(2)}, u32[]{:S(2)}) collective-permute-start(bf16[128,1152]{1,0:T(8,128)(2,1)S(1)} %get-tuple-element.61), channel_id=1, source_target_pairs={{0,8},{2,10},{4,12},{6,14},{8,16},{10,18},{12,20},{14,22},{16,24},... | collective-permute-start | bytes 884744 | tf_op jit(solution)/shard_map/ppermute | solution.py:25
  102.2 19.7 %copy-start.18 = (bf16[128,2048]{1,0:T(8,128)(2,1)S(1)}, bf16[128,2048]{1,0:T(8,128)(2,1)}, u32[]{:S(2)}) copy-start(bf16[128,2048]{1,0:T(8,128)(2,1)} %shard_map.146.after) | copy-start | bytes 1572868
  102.3 14.4 %collective-permute-start.19 = (bf16[128,1152]{1,0:T(8,128)(2,1)S(1)}, bf16[128,1152]{1,0:T(8,128)(2,1)S(1)}, u32[]{:S(2)}, u32[]{:S(2)}) collective-permute-start(bf16[128,1152]{1,0:T(8,128)(2,1)S(1)} %get-tuple-element.62), channel_id=1, source_target_pairs={{8,0},{10,2},{12,4},{14,6},{16,8},{18,10},{20,12},{22,14},{24,16},... | collective-permute-start | bytes 884744 | tf_op jit(solution)/shard_map/ppermute | solution.py:25
  140.1 1.6 %collective-permute-start.21 = (bf16[128,1024]{1,0:T(8,128)(2,1)S(1)}, bf16[128,1024]{1,0:T(8,128)(2,1)S(1)}, u32[]{:S(2)}, u32[]{:S(2)}) collective-permute-start(bf16[128,1024]{1,0:T(8,128)(2,1)S(1)} %get-tuple-element.74), channel_id=1, source_target_pairs={{0,2},{2,0},{4,6},{6,4},{8,10},{10,8},{12,14},{14,12},{16,18},{18,... | collective-permute-start | bytes 786440 | tf_op jit(solution)/shard_map/ppermute | solution.py:29
  140.2 6.8 %collective-permute-start.20 = (bf16[128,2048]{1,0:T(8,128)(2,1)S(1)}, bf16[128,2048]{1,0:T(8,128)(2,1)S(1)}, u32[]{:S(2)}, u32[]{:S(2)}) collective-permute-start(bf16[128,2048]{1,0:T(8,128)(2,1)S(1)} %get-tuple-element.69), channel_id=1, source_target_pairs={{0,2},{2,0},{4,6},{6,4},{8,10},{10,8},{12,14},{14,12},{16,18},{18,... | collective-permute-start | bytes 1572872 | tf_op jit(solution)/shard_map/ppermute | solution.py:29
  140.6 6.4 %collective-permute-start.11 = (bf16[128,1024]{1,0:T(8,128)(2,1)S(1)}, bf16[128,1024]{1,0:T(8,128)(2,1)S(1)}, u32[]{:S(2)}, u32[]{:S(2)}) collective-permute-start(bf16[128,1024]{1,0:T(8,128)(2,1)S(1)} %get-tuple-element.58), channel_id=1, source_target_pairs={{0,2},{2,0},{4,6},{6,4},{8,10},{10,8},{12,14},{14,12},{16,18},{18,... | collective-permute-start | bytes 786440 | tf_op jit(solution)/shard_map/ppermute | solution.py:29

commit v3 on v2

v3 whole, which is shorter than its diff:
```python
import functools

import jax
import jax.numpy as jnp
from jax import lax
from jax.experimental import pallas as pl
from jax.experimental.pallas import tpu as pltpu
from jax.sharding import PartitionSpec as P

HEADS = 16
WIN = 4
PAIR = 2
SIDE = 128
FAR = 1e30
BF = jnp.bfloat16
F32 = jnp.float32
VMEM = pl.BlockSpec(memory_space=pltpu.VMEM)
SMEM = pl.BlockSpec(memory_space=pltpu.SMEM)
ANY = pl.BlockSpec(memory_space=pl.ANY)
HBM = pl.BlockSpec(memory_space=pltpu.HBM)


def moved(x, by):
    devices = lax.axis_size("ctx")
    pairs = [(i, i + by) for i in range(devices) if 0 <= i + by < devices]
    return lax.ppermute(x, "ctx", pairs)


def swapped(x, bit=1):
    return lax.ppermute(x, "ctx", [(i, i ^ bit) for i in range(lax.axis_size("ctx"))])


def this_core():
    return lax.axis_index("ctx") % PAIR


def this_lane():
    return lax.axis_index("ctx") // PAIR % 2


def crossed(x):
    return lax.ppermute(x, "exp", [(0, 1), (1, 0)])


def nn(a, b):
    return lax.dot_general(a, b, (((1,), (0,)), ((), ())), preferred_element_type=F32)


def nt(a, b):
    return lax.dot_general(a, b, (((1,), (1,)), ((), ())), preferred_element_type=F32)


def tn(a, b):
    return lax.dot_general(a, b, (((0,), (0,)), ((), ())), preferred_element_type=F32)


def silu_parts(gate_pre):
    sigmoid_val = jax.nn.sigmoid(gate_pre)
    return (gate_pre * sigmoid_val, sigmoid_val * (1.0 + gate_pre * (1.0 - sigmoid_val)))


LEVEL, DELTA = 8, 32


def terms_of(x):
    first = x.astype(BF).astype(F32)
    second = (x - first).astype(BF).astype(F32)
    return jnp.concatenate([first, second, x - first - second], axis=0)


def rows_of(side, at, heads):
    return sum(side[at + n * heads : at + (n + 1) * heads].astype(F32) for n in range(3))


def hidden_by(flag):
    return (1.0 - flag) * FAR


def causal_of(rows):
    return lax.broadcasted_iota(jnp.int32, (rows, rows), 1) >= lax.broadcasted_iota(
        jnp.int32, (rows, rows), 0
    )


def like(*shape, kind=BF):
    return jax.ShapeDtypeStruct(shape, kind)


def call(kernel, outs, args, scratch=(), time=1, limit=8, alias=None, spaces=None):
    return pl.pallas_call(
        kernel,
        out_shape=outs,
        in_specs=[space for _, space in args],
        out_specs=jax.tree.map(lambda _: VMEM, outs) if spaces is None else spaces,
        input_output_aliases=alias or {},
        scratch_shapes=list(scratch),
        compiler_params=pltpu.CompilerParams(vmem_limit_bytes=limit * 1024 * 1024),
        cost_estimate=pl.CostEstimate(flops=int(time * 1.1e9), bytes_accessed=0, transcendentals=0),
    )(*(array for array, _ in args))


def vmem(*arrays):
    return [(array, VMEM) for array in arrays]


def hbm(*arrays):
    return [(array, HBM) for array in arrays]


def anywhere(*arrays):
    return [(array, ANY) for array in arrays]


def tied(x, *after):
    return call(lambda *refs: None, like(*x.shape), anywhere(x, *after), alias={0: 0}, spaces=ANY, limit=1, time=0.01)


def fetch(copies):
    for copy in copies:
        copy.start()
    return copies


def ready(copies):
    for copy in copies:
        copy.wait()


def through(moves, sems):
    ins = [pltpu.make_async_copy(source, buffer, sems.at[0, n]) for n, (source, buffer, _) in enumerate(moves)]
    outs = [pltpu.make_async_copy(buffer, target, sems.at[1, n]) for n, (_, buffer, target) in enumerate(moves)]
    fetch(ins)
    for first, second in zip(ins, outs):
        first.wait()
        second.start()
    ready(outs)


def columns_of(core, width):
    return [pl.ds(pl.multiple_of(n * width, width), width) for n in (core, 1 - core)]


def join_kernel(query, key, value, mask, got, q2, kv2, odd, side):
    core = this_core()
    rows, width = got.shape[0], q2.shape[1]
    mine, _ = columns_of(core, width)
    here, there = (pl.ds(pl.multiple_of(n * rows, rows), rows) for n in (core, 1 - core))
    q2[here, :] = query[0, :, mine]
    q2[there, :] = got[:, 0:width]
    kept = jnp.concatenate([key[0, :, mine], value[0, :, mine]], axis=1)
    sent = got[:, width : 3 * width]
    kv2[here, :] = kept
    kv2[there, :] = sent
    odd[...] = jnp.where(core == 1, kept, sent)
    side[here, :] = seen_by(mask, rows)
    side[there, :] = got[:, 3 * width :]


def seen_by(mask, rows):
    at = lax.broadcasted_iota(jnp.int32, (SIDE, rows), 0)
    sees = jnp.zeros((SIDE, rows), F32)
    for w in range(1, WIN):
        flag = jnp.where((mask[0, 0, w - 1] == 1) & (lax.axis_index("ctx") >= w), 1.0, 0.0)
        sees = jnp.where(at == w - 1, flag, sees)
    return sees.astype(BF)


def shift_kernel(own, other, up, down):
    lane = this_lane()
    rows = own.shape[0] // 2

    def put(first, last):
        up[0:rows] = first[rows : 2 * rows]
        up[rows : 3 * rows] = last[...]
        down[0 : 2 * rows] = first[...]
        down[2 * rows : 3 * rows] = last[0:rows]

    pl.when(lane == 0)(lambda: put(own, other))
    pl.when(lane != 0)(lambda: put(other, own))


def around_kernel(other, below, above, before, after):
    lane = this_lane()
    rows = other.shape[0] // 2

    @pl.when(lane == 0)
    def _():
        before[...] = below[...]
        after[0 : 2 * rows] = other[...]
        after[2 * rows :] = above[0:rows]

    @pl.when(lane != 0)
    def _():
        before[0:rows] = below[2 * rows :]
        before[rows:] = other[...]
        after[...] = above[...]


def split_moves(query, key, value, blocks, sent):
    width = query.shape[2] // 2
    _, others = columns_of(this_core(), width)
    return [
        (ref.at[0, :, others], blocks.at[n], sent.at[:, pl.ds(n * width, width)])
        for n, ref in enumerate((query, key, value))
    ]


def split_kernel(mask, query, key, value, sent, blocks, seen, sems, seen_sem):
    through(split_moves(query, key, value, blocks, sent), sems)
    send_seen(mask, seen, sent, seen_sem)


def send_seen(mask, seen, sent, sem):
    rows = seen.shape[1]
    seen[...] = seen_by(mask, rows)
    copy = pltpu.make_async_copy(seen, sent.at[:, pl.ds(sent.shape[1] - rows, rows)], sem)
    copy.start()
    copy.wait()


def cut_kernel(
    mask, gate, up, down, query, key, value, inner, down_half, sent, parts, down_parts, blocks, seen, sems, seen_sem
):
    def moves(matrix, buffers, out):
        pieces, size = buffers.shape[:2]
        start = this_core() * pieces * size
        return [
            (matrix.at[pl.ds(start + n * size, size)], buffers.at[n], out.at[pl.ds(n * size, size)])
            for n in range(pieces)
        ]

    through(
        split_moves(query, key, value, blocks, sent)
        + moves(gate, parts.at[0], inner.at[0])
        + moves(up, parts.at[1], inner.at[1])
        + moves(down, down_parts, down_half),
        sems,
    )
    send_seen(mask, seen, sent, seen_sem)


def cots_kernel(keep, got, side, whole, even, odd):
    core = this_core()
    rows, width = keep.shape[0], keep.shape[1] - SIDE
    for ref, block in ((keep, core), (got, 1 - core)):
        here = pl.ds(pl.multiple_of(block * rows, rows), rows)
        filled = (ref[:, width:].astype(F32) + side[here, :].astype(F32)).astype(BF)
        whole[here, 0:width] = ref[:, 0:width]
        whole[here, width:] = filled

        @pl.when(block == 0)
        def _():
            even[:, 0:width] = ref[:, 0:width]
            even[:, width:] = filled

        @pl.when(block == 1)
        def _():
            odd[:, 0:width] = ref[:, 0:width]
            odd[:, width:] = filled


def window_refs(far, near, own, rows):
    return {-3: (far, 0), -2: (near, 0), -1: (near, rows), 0: (own, 0), 1: (own, rows)}


def stacked(window, js, rows, here):
    return jnp.concatenate([window[j][0][pl.ds(window[j][1], rows), here] for j in js], axis=0)


def each_head(heads, one, step=2):
    def some(n, carry):
        for at in range(step):
            one(step * n + at)
        return carry

    lax.fori_loop(0, heads // step, some, 0)


def attend_kernel(size, far, near, own, q2, flags, *rest):
    side, keep, send, levels = rest[-4:]
    rows, width = far.shape[0], far.shape[1] // 2
    heads = width // size
    scale = size ** (-0.5)
    core = this_core()
    window = window_refs(far, near, own, rows)
    causal = causal_of(rows)
    seen = [flags[block * rows : block * rows + LEVEL, :].astype(F32) for block in range(PAIR)]

    def one(head):
        here = pl.ds(pl.multiple_of(head * size, size), size)
        there = pl.ds(pl.multiple_of(width + head * size, size), size)
        outs = []
        for block in range(PAIR):
            js = list(range(block - WIN + 1, block + 1))
            q = q2[pl.ds(block * rows, rows), here]
            scores = nt(stacked(window, js, rows, here), q) * scale
            parts = [
                scores[n * rows : (n + 1) * rows] - hidden_by(seen[block][block - j - 1 : block - j])
                if j < block
                else jnp.where(causal, scores[n * rows : (n + 1) * rows], -FAR)
                for n, j in enumerate(js)
            ]
            scores = jnp.concatenate(parts, axis=0)
            top = jnp.max(scores, axis=0, keepdims=True)
            weights = jnp.exp(scores - top)
            total = jnp.sum(weights, axis=0, keepdims=True)
            probs = weights * (1.0 / total)
            levels[block, pl.ds(head, 1), :] = top + jnp.log(total)
            outs.append(tn(probs.astype(BF), stacked(window, js, rows, there)).astype(BF))
        keep[:, here] = jnp.where(core == 0, outs[0], outs[1])
        send[:, here] = jnp.where(core == 0, outs[1], outs[0])

    each_head(heads, one)
    for block in range(PAIR):
        filled = jnp.concatenate(
            [seen[block], terms_of(levels[block]), jnp.zeros((SIDE - LEVEL - 3 * heads, rows), F32)], axis=0
        )
        side[block * rows : (block + 1) * rows, :] = filled.astype(BF)


def scores_back(q, cot, level, delta, seen, keys, values, js, t, causal, scale):
    rows = q.shape[0]
    scores = nt(keys, q) * scale
    parts = []
    for n, j in enumerate(js):
        part = scores[n * rows : (n + 1) * rows]
        if j < t:
            part = part - (level + hidden_by(seen[t - j - 1 : t - j]))
        else:
            part = jnp.where(causal, part - level, -FAR)
        parts.append(part)
    probs = jnp.exp(jnp.concatenate(parts, axis=0))
    return probs, (probs * (nt(values, cot) - delta)).astype(BF)


def add_blocks(sums, js, terms, rows):
    for n, j in enumerate(js):
        term = terms[n * rows : (n + 1) * rows]
        sums[j] = sums[j] + term if j in sums else term


def own_grads_kernel(
    size, far, near, own, q2, co, probs_out, probs_low_out, grads_q, q_keep, q_send, key_sums, value_sums, levels, deltas,
):
    rows, width = far.shape[0], far.shape[1] // 2
    heads = width // size
    scale = size ** (-0.5)
    core = this_core()
    window = window_refs(far, near, own, rows)
    causal = causal_of(rows)
    sides = [co[t * rows : (t + 1) * rows, width:].astype(F32) for t in range(PAIR)]
    for t in range(PAIR):
        levels[t] = rows_of(sides[t], LEVEL, heads)
        deltas[t] = rows_of(sides[t], DELTA, heads)

    def one(head):
        here = pl.ds(pl.multiple_of(head * size, size), size)
        there = pl.ds(pl.multiple_of(width + head * size, size), size)
        keys_at, values_at, grads = {}, {}, []
        for t in range(PAIR):
            place = pl.ds(t * rows, rows)
            js = list(range(t - WIN + 1, t + 1))
            q, cot = q2[place, here], co[place, here]
            keys = stacked(window, js, rows, here)
            probs, score_grad = scores_back(
                q, cot, levels[t, pl.ds(head, 1), :], deltas[t, pl.ds(head, 1), :], sides[t][0:LEVEL],
                keys, stacked(window, js, rows, there), js, t, causal, scale,
            )
            probs_low = probs.astype(BF)
            probs_out[head, t] = probs_low
            probs_low_out[head, t] = probs_low.T
            add_blocks(keys_at, js, nn(score_grad, q), rows)
            add_blocks(values_at, js, nn(probs_low, cot), rows)
            grads.append((tn(score_grad, keys) * scale).astype(BF))
            grads_q[place, here] = grads[t]
        q_keep[:, here] = jnp.where(core == 0, grads[0], grads[1])
        q_send[:, here] = jnp.where(core == 0, grads[1], grads[0])
        for j in keys_at:
            place = pl.ds((j + WIN - 1) * rows, rows)
            key_sums[place, here] = keys_at[j]
            value_sums[place, here] = values_at[j]

    each_head(heads, one)


def grads_kernel(
    size, far, near, own, q2, q_before, q_after, cfb, cnb, cna, cfa, probs_in, probs_low_in, grads_q,
    key_sums, value_sums, after, keep, send, tans_keep, tans_send, levels, deltas,
):
    rows, width = far.shape[0], far.shape[1] // 2
    heads = width // size
    scale = size ** (-0.5)
    core = this_core()
    window = window_refs(far, near, own, rows)
    causal = causal_of(rows)
    others = (
        (-3, q_before, 0, cfb, 0), (-2, q_before, 1, cnb, 0), (-1, q_before, 2, cnb, 1),
        (2, q_after, 0, cna, 0), (3, q_after, 1, cna, 1), (4, q_after, 2, cfa, 0),
    )
    sides = [c_ref[half * rows : (half + 1) * rows, width:].astype(F32) for _, _, _, c_ref, half in others]
    for n, side in enumerate(sides):
        levels[n] = rows_of(side, LEVEL, heads)
        deltas[n] = rows_of(side, DELTA, heads)

    def one(head):
        at = pl.multiple_of(head * size, size)
        here = pl.ds(at, size)
        there = pl.ds(pl.multiple_of(width + at, size), size)
        blocks = range(1 - WIN, PAIR)
        keys_at = {j: key_sums[pl.ds((j + WIN - 1) * rows, rows), here] for j in blocks}
        values_at = {j: value_sums[pl.ds((j + WIN - 1) * rows, rows), here] for j in blocks}
        for n, (t, q_ref, q_half, c_ref, half) in enumerate(others):
            js = list(range(max(1 - WIN, t - WIN + 1), min(1, t) + 1))
            q, cot = q_ref[pl.ds(q_half * rows, rows), here], c_ref[pl.ds(half * rows, rows), here]
            keys = stacked(window, js, rows, here)
            values = stacked(window, js, rows, there)
            probs, score_grad = scores_back(
                q, cot, levels[n, pl.ds(head, 1), :], deltas[n, pl.ds(head, 1), :], sides[n][0:8],
                keys, values, js, t, causal, scale,
            )
            add_blocks(keys_at, js, nn(score_grad, q), rows)
            add_blocks(values_at, js, nn(probs.astype(BF), cot), rows)
        key_grads = {j: (keys_at[j] * scale).astype(BF) for j in blocks}
        value_grads = {j: values_at[j].astype(BF) for j in blocks}
        tans = []
        for t in range(PAIR):
            place = pl.ds(t * rows, rows)
            js = list(range(t - WIN + 1, t + 1))
            keys = stacked(window, js, rows, here)
            probs = probs_in[head, t].astype(F32)
            both_keys = jnp.concatenate([keys, jnp.concatenate([key_grads[j] for j in js], axis=0)], axis=1)
            both_rows = jnp.concatenate([grads_q[place, here], q2[place, here]], axis=1)
            tan_values = jnp.concatenate([value_grads[j] for j in js], axis=0)
            score_tan = nt(both_keys, both_rows) * scale
            mean = jnp.sum(probs * score_tan, axis=0, keepdims=True)
            prob_tan = (probs * (score_tan - mean)).astype(BF)
            tan = tn(prob_tan, stacked(window, js, rows, there)) + nn(probs_low_in[head, t], tan_values)
            tans.append(tan.astype(BF))
        for grads, tans_out, mine, other in ((keep, tans_keep, 0, 1), (send, tans_send, 1, 0)):
            grads[:, here] = jnp.where(core == 0, key_grads[mine], key_grads[other])
            grads[:, there] = jnp.where(core == 0, value_grads[mine], value_grads[other])
            tans_out[:, here] = jnp.where(core == 0, tans[mine], tans[other])

    each_head(heads, one)


def gather_kernel(q_keep, q_got, keep, got, out_q, out_k, out_v):
    core = this_core()
    width = q_keep.shape[1]
    for owner, q, kv in ((core, q_keep, keep), (1 - core, q_got, got)):
        columns = pl.ds(pl.multiple_of(owner * width, width), width)
        out_q[:, columns] = q[...]
        out_k[:, columns] = kv[:, 0:width]
        out_v[:, columns] = kv[:, width:]


def cot_payload(size, cot, attended):
    rows, width = cot.shape
    heads = width // size
    lanes = lax.broadcasted_iota(jnp.int32, (rows, SIDE), 1)
    sums = jnp.zeros((rows, SIDE), F32)
    for head in range(heads):
        here = slice(head * size, (head + 1) * size)
        delta = jnp.sum(cot[:, here].astype(F32) * attended[:, here].astype(F32), axis=1, keepdims=True)
        sums = jnp.where(lanes == head, delta, sums)
    blank = jnp.zeros((DELTA, rows), F32)
    rest = jnp.zeros((SIDE - DELTA - 3 * heads, rows), F32)
    side = jnp.concatenate([blank, terms_of(sums.T[0:heads]), rest], axis=0)
    return jnp.concatenate([cot, side.astype(BF)], axis=1)


def in_order(core, kept, got):
    return jnp.where(
        core == 0, jnp.concatenate([kept, got], axis=1), jnp.concatenate([got, kept], axis=1)
    )


def pair_of(a, b, bit):
    return jnp.where(bit == 0, a, b), jnp.where(bit == 0, b, a)


def down_of_other(hidden, core, over, over_s):
    half = hidden.shape[1] // 2
    mine, others = pair_of(hidden[:, :half], hidden[:, half:], core)
    return nn(mine, over[...]) + nn(others, over_s[...])


def hidden_grad_kernel(cot, down, out):
    out[...] = nt(cot[0], down[...])


def middle_of(chosen, gate_pre, up_value, back, hidden, slope_up, active):
    activated, slope = silu_parts(gate_pre)
    activated = activated * chosen
    slope = slope * up_value * chosen
    hidden[...] = (activated * up_value).astype(BF)
    slope_up[...] = slope
    active[...] = activated
    return (back * slope).astype(BF), (back * activated).astype(BF)


def own_expert_kernel(keep, got, picks, back, gate, up, sum_keep, sum_got, hidden, slope_up, active):
    mine, others = columns_of(this_core(), keep.shape[1])
    rows_keep, rows_got = keep[...], got[...]

    def inner(ref):
        return nn(rows_keep, ref[mine, :]) + nn(rows_got, ref[others, :])

    gate_grad, up_grad = middle_of(picks[:, 0:1], inner(gate), inner(up), back[...], hidden, slope_up, active)
    for here, out in ((mine, sum_keep), (others, sum_got)):
        out[...] = nt(gate_grad, gate[here, :]) + nt(up_grad, up[here, :])


def other_expert_kernel(
    size, keep, got, cot, picks, sum_keep, sum_got, inner, inner_s, over, over_s,
    cot_keep, cot_send, hidden, slope_up, active,
):
    core = this_core()
    mine, others = columns_of(core, keep.shape[1])
    rows_keep, rows_got = keep[...], got[...]
    cots = cot[0]
    back = jnp.concatenate(pair_of(nt(cots, over[...]), nt(cots, over_s[...]), core), axis=1)
    gate_pre, up_value = (nn(rows_keep, inner[n]) + nn(rows_got, inner_s[n]) for n in range(2))
    gate_grad, up_grad = middle_of(picks[:, 1:2], gate_pre, up_value, back, hidden, slope_up, active)
    weight = picks[:, 2:3]
    for here, attended, so_far, ref, out in (
        (others, rows_got, sum_got, inner_s, cot_send),
        (mine, rows_keep, sum_keep, inner, cot_keep),
    ):
        summed = so_far[...] + nt(gate_grad, ref[0]) + nt(up_grad, ref[1])
        attn_cot = (cot[0, :, here].astype(F32) + summed.astype(BF).astype(F32) * weight).astype(BF)
        out[...] = cot_payload(size, attn_cot, attended)


def layer_kernel(keep, got, hidden_own, hidden, picks, down, over, over_s, after, out):
    core = this_core()
    rows_in = in_order(core, keep[...], got[...]).astype(F32)
    summed = nn(hidden_own[...], down[...]) + down_of_other(hidden[...], core, over, over_s)
    out[...] = (rows_in + summed.astype(BF).astype(F32) * picks[:, 2:3]).astype(BF)


def tangent_kernel(
    keep, got, slope_up_own, active_own, slope_up, active, picks, gate, up, inner, inner_s, down, over, over_s, out
):
    core = this_core()
    rows_keep, rows_got = keep[...], got[...]
    rows_in = in_order(core, rows_keep, rows_got)
    hidden = slope_up_own[...] * nn(rows_in, gate[...]) + active_own[...] * nn(rows_in, up[...])
    summed = nn(hidden.astype(BF), down[...])
    gate_tan, up_tan = (nn(rows_keep, inner[n]) + nn(rows_got, inner_s[n]) for n in range(2))
    hidden = slope_up[...] * gate_tan + active[...] * up_tan
    summed = summed + down_of_other(hidden.astype(BF), core, over, over_s)
    out[...] = (rows_in.astype(F32) + summed.astype(BF).astype(F32) * picks[:, 2:3]).astype(BF)


class PairExperts:
    def __init__(self, index, own_rows, mask, upstream, route_ids, route_weights, w_gate, w_up, w_down):
        own = lax.axis_index("exp")
        self.upstream = upstream
        mine = (route_ids == own).astype(F32)
        self.picks = jnp.concatenate([mine, 1.0 - mine, route_weights], axis=1)
        rows, wide = upstream.shape[1:]
        units = w_gate.shape[1]
        pieces = 4
        inner, down_half, self.mates = call(
            cut_kernel,
            (like(2, wide // 2, units), like(units // 2, wide), like(rows, 3 * wide // 2 + SIDE)),
            [(mask, SMEM)] + hbm(w_gate, w_up, w_down, *own_rows),
            [
                pltpu.VMEM((2, pieces, wide // 2 // pieces, units), BF),
                pltpu.VMEM((pieces, units // 2 // pieces, wide), BF),
                pltpu.VMEM((3, rows, wide // 2), BF),
                pltpu.VMEM((SIDE, rows), BF),
                pltpu.SemaphoreType.DMA((2, 3 * pieces + 3)),
                pltpu.SemaphoreType.DMA(()),
            ],
            limit=60,
            spaces=(HBM, HBM, HBM),
        )
        self.inner, self.over = crossed(inner), crossed(down_half)
        self.whole = (w_gate, w_up, w_down)
        self.rows, self.wide, self.units = rows, wide, units
        self.back_own = call(
            hidden_grad_kernel, like(rows, units, kind=F32), vmem(upstream, w_down), time=1.5
        )

    def before(self):
        return [self.back_own]

    def forward(self, size, keep, got, after):
        rows, wide, units = self.rows, self.wide, self.units
        w_gate, w_up, w_down = self.whole
        half, inner = like(rows, wide // PAIR + SIDE), like(rows, units, kind=F32)
        sums = like(rows, wide // PAIR, kind=F32)
        sum_keep, sum_got, hidden_own, *own_slopes = call(
            own_expert_kernel,
            (sums, sums, like(rows, units), inner, inner),
            vmem(keep, got, self.picks, self.back_own, w_gate, w_up),
            time=0.1,
        )
        inner_o, over = tied(self.inner, keep), tied(self.over, sum_keep, after)
        self.down = (w_down, over, swapped(over))
        self.inner = (inner_o, swapped(inner_o))
        cot_keep, cot_send, hidden, *slopes = call(
            functools.partial(other_expert_kernel, size),
            (half, half, like(rows, units), inner, inner),
            vmem(keep, got, self.upstream, self.picks, sum_keep, sum_got, *self.inner, *self.down[1:]),
            time=4.5,
        )
        self.slopes = own_slopes + slopes

        def layer(after):
            return call(
                layer_kernel,
                like(rows, wide),
                vmem(keep, got, hidden_own, hidden, self.picks, *self.down) + anywhere(after),
                time=3,
            )

        return cot_keep, cot_send, layer

    def tangent(self, keep, got):
        return call(
            tangent_kernel,
            like(self.rows, self.wide),
            vmem(keep, got, *self.slopes, self.picks, *self.whole[:2], *self.inner, *self.down),
            time=4.5,
        )


def routing_table(route_rows, experts, capacity):
    flat_ids = route_rows.reshape(-1)
    one_hot = (flat_ids[:, None] == jnp.arange(experts, dtype=jnp.int32)[None, :]).astype(jnp.int32)
    slot_rank = jnp.sum((jnp.cumsum(one_hot, axis=0) - one_hot) * one_hot, axis=1)
    target = flat_ids * capacity + slot_rank
    return (jnp.arange(experts * capacity, dtype=jnp.int32)[:, None] == target[None, :]).astype(
        jnp.bfloat16
    )


def dispatch(slot_table, row_block, routes, experts):
    pair_rows = jnp.repeat(row_block, routes, axis=0)
    sent = jnp.dot(slot_table, pair_rows, preferred_element_type=jnp.float32).astype(jnp.bfloat16)
    return sent.reshape(experts, -1, row_block.shape[1])


def combine(slot_table, returned, weights):
    rows_here, routes = weights.shape
    pair_vals = jnp.dot(
        slot_table.T, returned.reshape(-1, returned.shape[2]), preferred_element_type=jnp.float32
    )
    return jnp.sum(pair_vals.reshape(rows_here, routes, -1) * weights[:, :, None], axis=1)


def expert_forward(row_block, gate_matrix, up_matrix, down_matrix):
    gate_pre = jnp.dot(row_block, gate_matrix, preferred_element_type=jnp.float32)
    up_value = jnp.dot(row_block, up_matrix, preferred_element_type=jnp.float32)
    activated, slope_val = silu_parts(gate_pre)
    hidden = (activated * up_value).astype(jnp.bfloat16)
    return (
        jnp.dot(hidden, down_matrix, preferred_element_type=jnp.float32).astype(jnp.bfloat16),
        gate_pre,
        up_value,
    )


def expert_backward(cot_block, gate_pre, up_value, gate_matrix, up_matrix, down_matrix):
    hidden_grad = jnp.dot(cot_block, down_matrix.T, preferred_element_type=jnp.float32)
    activated, slope_val = silu_parts(gate_pre)
    gate_grad = (hidden_grad * up_value * slope_val).astype(jnp.bfloat16)
    up_grad = (hidden_grad * activated).astype(jnp.bfloat16)
    summed = jnp.dot(gate_grad, gate_matrix.T, preferred_element_type=jnp.float32) + jnp.dot(
        up_grad, up_matrix.T, preferred_element_type=jnp.float32
    )
    return summed.astype(jnp.bfloat16)


def expert_tangent(tan_block, gate_pre, up_value, gate_matrix, up_matrix, down_matrix):
    gate_tan = jnp.dot(tan_block, gate_matrix, preferred_element_type=jnp.float32)
    up_tan = jnp.dot(tan_block, up_matrix, preferred_element_type=jnp.float32)
    activated, slope_val = silu_parts(gate_pre)
    hidden_tan = (slope_val * gate_tan * up_value + activated * up_tan).astype(jnp.bfloat16)
    return jnp.dot(hidden_tan, down_matrix, preferred_element_type=jnp.float32).astype(jnp.bfloat16)


class RoutedExperts:
    def __init__(self, index, own_rows, mask, upstream, route_ids, route_weights, w_gate, w_up, w_down):
        rows, routes = route_ids.shape
        self.experts = lax.axis_size("exp")
        self.routes = routes
        capacity = min(rows, 2 * rows * routes // self.experts)
        self.core, self.upstream, self.weights = index % 2, upstream[0], route_weights
        self.matrices = (w_gate, w_up, w_down)
        self.table = routing_table(route_ids, self.experts, capacity)
        self.got_cots = self.sent(self.upstream)
        wide = self.upstream.shape[1]
        self.mates = call(
            split_kernel,
            like(rows, 3 * wide // 2 + SIDE),
            [(mask, SMEM)] + hbm(*own_rows),
            [
                pltpu.VMEM((3, rows, wide // 2), BF),
                pltpu.VMEM((SIDE, rows), BF),
                pltpu.SemaphoreType.DMA((2, 3)),
                pltpu.SemaphoreType.DMA(()),
            ],
            limit=20,
            spaces=HBM,
        )

    def before(self):
        return [self.got_cots]

    def across(self, x):
        return lax.all_to_all(x, "exp", split_axis=0, concat_axis=0, tiled=True)

    def sent(self, x):
        return self.across(dispatch(self.table, x, self.routes, self.experts))

    def returned(self, x):
        back = self.across(x.reshape(self.got_cots.shape))
        return combine(self.table, back, self.weights)

    def forward(self, size, keep, got, after):
        attended = in_order(self.core, keep, got)
        rows, wide = attended.shape
        got_rows = self.sent(attended).reshape(-1, wide)
        expert_out, self.gate_pre, self.up_value = expert_forward(got_rows, *self.matrices)
        route_grad = expert_backward(
            self.got_cots.reshape(-1, wide), self.gate_pre, self.up_value, *self.matrices
        )
        attn_cot = (self.upstream.astype(F32) + self.returned(route_grad)).astype(BF)
        layer_out = (attended.astype(F32) + self.returned(expert_out)).astype(BF)

        def kernel(cot, kept, got, cot_keep, cot_send):
            width = kept.shape[1]
            for part, attended, out in ((this_core(), kept, cot_keep), (1 - this_core(), got, cot_send)):
                here = pl.ds(pl.multiple_of(part * width, width), width)
                out[...] = cot_payload(size, cot[:, here], attended[...])

        half = like(rows, wide // PAIR + SIDE)
        cot_keep, cot_send = call(
            kernel, (half, half), vmem(attn_cot, keep, got)
        )
        return cot_keep, cot_send, lambda after: layer_out

    def tangent(self, keep, got):
        rows = in_order(self.core, keep, got)
        got_rows = self.sent(rows).reshape(-1, rows.shape[1])
        out = expert_tangent(got_rows, self.gate_pre, self.up_value, *self.matrices)
        return (rows.astype(F32) + self.returned(out)).astype(BF)


def neighbours(whole, even, odd):
    return (
        moved(odd, 2 * PAIR),
        moved(whole, PAIR),
        moved(whole, -PAIR),
        moved(even, -2 * PAIR),
    )


def local(query, key, value, cotangent, route_ids, route_weights, block_mask, w_gate, w_up, w_down):
    rows, wide = query.shape[1:]
    width = wide // PAIR
    size = wide // HEADS
    heads = width // size
    index = lax.axis_index("ctx")
    core = index % PAIR

    pair = lax.axis_size("exp") == 2 and route_ids.shape[2] == 1
    experts = (PairExperts if pair else RoutedExperts)(
        index, (query, key, value), block_mask, cotangent, route_ids[0], route_weights[0], w_gate[0], w_up[0], w_down[0]
    )
    half, pairs = like(rows, width), like(2 * rows, width)
    q2, own, odd, side = call(
        join_kernel,
        (pairs, like(2 * rows, wide), like(rows, wide), like(2 * rows, SIDE)),
        vmem(query, key, value) + [(block_mask, SMEM)] + vmem(swapped(experts.mates)),
    )
    near, far = moved(own, PAIR), moved(odd, 2 * PAIR)
    three = like(3 * rows, width)
    q_other = swapped(q2, 2)
    q_up, q_down = call(shift_kernel, (three, three), vmem(q2, q_other))
    side, keep, send = call(
        functools.partial(attend_kernel, size),
        (
            like(2 * rows, SIDE),
            half,
            half,
        ),
        vmem(far, near, own, q2, side) + anywhere(q_up, *experts.before()),
        [pltpu.VMEM((PAIR, heads, rows), F32)],
        time=0.1,
    )
    got = swapped(send)
    q_below, q_above = moved(q_up, 2 * PAIR), moved(q_down, -2 * PAIR)
    q_before, q_after = call(around_kernel, (three, three), vmem(q_other, q_below, q_above))

    cot_keep, cot_send, layer = experts.forward(size, keep, got, q_before)
    payload = wide // PAIR + SIDE
    co, co_even, co_odd = call(
        cots_kernel,
        (like(2 * rows, payload), like(rows, payload), like(rows, payload)),
        vmem(cot_keep, swapped(cot_send), side),
    )
    cfb, cnb, cna, cfa = neighbours(co, co_even, co_odd)

    layer_out = layer(co)
    sums = like((WIN + 1) * rows, width, kind=F32)
    probs, probs_low, grads_q, q_keep, q_send, key_sums, value_sums = call(
        functools.partial(own_grads_kernel, size),
        (
            like(heads, PAIR, WIN * rows, rows),
            like(heads, PAIR, rows, WIN * rows),
            pairs, half, half, sums, sums,
        ),
        vmem(far, near, own, q2, co),
        [pltpu.VMEM((2, heads, rows), F32)] * 2,
        time=7,
    )
    q_got = swapped(q_send)
    kv_half = like(rows, 2 * width)
    kv_keep, kv_send, tan_keep, tan_send = call(
        functools.partial(grads_kernel, size),
        (kv_half, kv_half, half, half),
        vmem(far, near, own, q2, q_before, q_after, cfb, cnb, cna, cfa)
        + vmem(probs, probs_low, grads_q, key_sums, value_sums)
        + anywhere(layer_out),
        [pltpu.VMEM((6, heads, rows), F32)] * 2,
        time=16,
    )
    tan_got = swapped(tan_send)
    kv_got = swapped(kv_send)
    tangent_out = experts.tangent(tan_keep, tan_got)
    out = like(rows, wide)
    outs = call(gather_kernel, (out, out, out), vmem(q_keep, q_got, kv_keep, kv_got))
    return (layer_out[None], *(x[None] for x in outs), tangent_out[None])


def solution(mesh):
    return jax.shard_map(
        local,
        mesh=mesh,
        in_specs=(
            P("exp", "ctx", None),
            P("exp", "ctx", None),
            P("exp", "ctx", None),
            P("exp", "ctx", None),
            P("exp", "ctx", None),
            P("exp", "ctx", None),
            P("exp", "ctx", None),
            P("exp", None, None),
            P("exp", None, None),
            P("exp", None, None),
        ),
        out_specs=(
            P("exp", "ctx", None),
            P("exp", "ctx", None),
            P("exp", "ctx", None),
            P("exp", "ctx", None),
            P("exp", "ctx", None),
        ),
        check_vma=False,
    )
```

time: 150 us -> 149 us (level)
  waiting for transfers between devices: 39.3 us -> 56.6 us
  local copies, waits for them, and re-layouts: 10 us -> 3.21 us
  starting transfers between devices: 39.2 us -> 33.4 us
  Pallas kernels: 57.8 us -> 53.1 us
    ppermute x10 -> x9, waiting for transfers between devices: 4.08 us -> 36.8 us  [swapped(): lax.ppermute(x, 'ctx', [(i, i ^ bit) for i in range(lax.axis_size('ctx'))])]
    ppermute x2, waiting for transfers between devices: 23.1 us -> 0.33 us  [crossed(): return lax.ppermute(x, 'exp', [(0, 1), (1, 0)])]
    ppermute x10 -> x8, waiting for transfers between devices: 12.1 us -> 19.4 us  [moved(): return lax.ppermute(x, 'ctx', pairs)]
    unnamed x54 -> x50, local copies, waits for them, and re-layouts: 9.82 us -> 3.1 us
    pallas_call x15 -> x16, Pallas kernels: 57.8 us -> 53.1 us  [call(): pl.pallas_call(kernel, out_shape=outs, in_specs=[space for _, space in ar...]
    ppermute x10 -> x8, starting transfers between devices: 31.8 us -> 27.3 us  [moved(): return lax.ppermute(x, 'ctx', pairs)]
    ppermute x10 -> x9, starting transfers between devices: 4.2 us -> 2.52 us  [swapped(): lax.ppermute(x, 'ctx', [(i, i ^ bit) for i in range(lax.axis_size('ctx'))])]
  transfers between devices with their start and end apart: 22 -> 19, of which waited for: 7 -> 11; matrix products, arithmetic and copies ran while one was open for 0% -> 0% of each run, Pallas kernels for 26% -> 17%
where the time goes in v3:
time: 149 us; the launch traced here: 147 us
  waiting for transfers between devices  56.6 us (38%)
  Pallas kernels  53.1 us (36%)
  starting transfers between devices  33.4 us (22%)
  local copies, waits for them, and re-layouts  3.21 us (2%)
    pallas_call x16, Pallas kernels, call(): pl.pallas_call(kernel, out_shape=outs, in_specs=[space for _, space in ar...  53.1 us
    ppermute x9, waiting for transfers between devices, swapped(): lax.ppermute(x, 'ctx', [(i, i ^ bit) for i in range(lax.axis_size('ctx'))])  36.8 us
    ppermute x8, starting transfers between devices, moved(): return lax.ppermute(x, 'ctx', pairs)  27.3 us
    ppermute x8, waiting for transfers between devices, moved(): return lax.ppermute(x, 'ctx', pairs)  19.4 us
    ppermute x2, starting transfers between devices, crossed(): return lax.ppermute(x, 'exp', [(0, 1), (1, 0)])  3.6 us
    unnamed x50, local copies, waits for them, and re-layouts  3.1 us
  transfers between devices with their start and end apart: 19, of which 11 were waited for; matrix products, arithmetic and copies ran while one was open for 0% of the time, Pallas kernels for 17%

profile of v3, /device:TPU:0, one launch (start us, length us, event | category | flops | bytes accessed | tf_op | source)
XLA Modules:
  0.0 147.3 jit_solution(7700724846348876055)
XLA Ops:
  0.7 5.0 %shard_map.137 = (bf16[2,1024,512]{2,1,0:T(8,128)(2,1)}, bf16[256,2048]{1,0:T(8,128)(2,1)}, bf16[128,3200]{1,0:T(8,128)(2,1)}) custom-call(s32[1,1,3]{2,1,0:T(1,128)} %mask.3, bf16[2048,512]{1,0:T(8,128)(2,1)} %bitcast.12, bf16[2048,512]{1,0:T(8,128)(2,1)} %bitcast.15, bf16[512,2048]{1,0:T(8,128)(2,1)} %bitcast.18, bf16[1,128,2048]{2,1,0:T(8,128)(2,1)} %query.3, ...), custom_call_target="tpu_custom_call" | custom-call | flops 1100000000 | tf_op jit(solution)/shard_map/pallas_call | solution.py:90
  5.7 0.0 copy-start.3
  5.7 0.0 copy-start.17
  5.7 3.0 %collective-permute-start.5 = (bf16[2,1024,512]{2,1,0:T(8,128)(2,1)}, bf16[2,1024,512]{2,1,0:T(8,128)(2,1)}, u32[]{:S(2)}, u32[]{:S(2)}) collective-permute-start(bf16[2,1024,512]{2,1,0:T(8,128)(2,1)} %get-tuple-element.57), channel_id=1, source_target_pairs={{0,1},{1,0},{2,3},{3,2},{4,5},{5,4},{6,7},{7,6},{8,9},{9,8},{10,11... | collective-permute-start | bytes 6291464 | tf_op jit(solution)/shard_map/ppermute | solution.py:42
  8.7 0.0 collective-permute-start
  8.7 2.5 %collective-permute-done.got = bf16[128,3200]{1,0:T(8,128)(2,1)S(1)} collective-permute-done((bf16[128,3200]{1,0:T(8,128)(2,1)}, bf16[128,3200]{1,0:T(8,128)(2,1)S(1)}, u32[]{:S(2)}, u32[]{:S(2)}) %collective-permute-start) | collective-permute-done | bytes 819232 | tf_op jit(solution)/shard_map/ppermute | solution.py:30
  11.2 0.8 shard_map.138
  12.0 0.0 copy-start.12
  12.1 3.5 %collective-permute-start.2 = (bf16[256,2048]{1,0:T(8,128)(2,1)S(1)}, bf16[256,2048]{1,0:T(8,128)(2,1)S(1)}, u32[]{:S(2)}, u32[]{:S(2)}) collective-permute-start(bf16[256,2048]{1,0:T(8,128)(2,1)S(1)} %get-tuple-element.48.own), channel_id=1, source_target_pairs={{0,4},{2,6},{4,8},{6,10},{8,12},{10,14},{12,16},{14,18},{16,20},{1... | collective-permute-start | bytes 3145736 | tf_op jit(solution)/shard_map/ppermute | solution.py:26
  15.6 1.5 %collective-permute-start.3 = (bf16[256,1024]{1,0:T(8,128)(2,1)S(1)}, bf16[256,1024]{1,0:T(8,128)(2,1)S(1)}, u32[]{:S(2)}, u32[]{:S(2)}) collective-permute-start(bf16[256,1024]{1,0:T(8,128)(2,1)S(1)} %get-tuple-element.49.own.q2), channel_id=1, source_target_pairs={{0,4},{2,6},{4,0},{6,2},{8,12},{10,14},{12,8},{14,10},{16,20},{18,... | collective-permute-start | bytes 1572872 | tf_op jit(solution)/shard_map/ppermute | solution.py:30
  17.1 3.5 %collective-permute-start.1 = (bf16[128,2048]{1,0:T(8,128)(2,1)S(1)}, bf16[128,2048]{1,0:T(8,128)(2,1)S(1)}, u32[]{:S(2)}, u32[]{:S(2)}) collective-permute-start(bf16[128,2048]{1,0:T(8,128)(2,1)S(1)} %get-tuple-element.47), channel_id=1, source_target_pairs={{0,8},{2,10},{4,12},{6,14},{8,16},{10,18},{12,20},{14,22},{16,24},... | collective-permute-start | bytes 1572872 | tf_op jit(solution)/shard_map/ppermute | solution.py:26
  20.6 0.6 collective-permute-start.7
  21.2 0.8 shard_map.140.rest_1_.back
  22.0 27.4 %collective-permute-done.3.other = bf16[256,1024]{1,0:T(8,128)(2,1)S(1)} collective-permute-done((bf16[256,1024]{1,0:T(8,128)(2,1)S(1)}, bf16[256,1024]{1,0:T(8,128)(2,1)S(1)}, u32[]{:S(2)}, u32[]{:S(2)}) %collective-permute-start.3) | collective-permute-done | bytes 524320 | tf_op jit(solution)/shard_map/ppermute | solution.py:30
  49.4 1.0 shard_map.139
  50.5 0.0 collective-permute-done.1.far
  50.5 0.0 collective-permute-done.2.near
  50.5 4.6 %shard_map.141 = (bf16[256,128]{1,0:T(8,128)(2,1)S(1)}, bf16[128,1024]{1,0:T(8,128)(2,1)S(1)}, bf16[128,1024]{1,0:T(8,128)(2,1)S(1)}) custom-call(bf16[128,2048]{1,0:T(8,128)(2,1)S(1)} %collective-permute-done.1.far, bf16[256,2048]{1,0:T(8,128)(2,1)S(1)} %collective-permute-done.2.near, bf16[256,2048]{1,0:T(8,128)(2,1)S(1)} %get-tuple-element.48.own, ...), custom_call_target="tpu_custom_call" | custom-call | flops 110000000 | tf_op jit(solution)/shard_map/pallas_call | solution.py:90
  55.1 0.0 copy-start.21
  55.1 0.3 collective-permute-done.5.refs_0_
  55.5 0.4 copy-done.21
  55.8 0.0 collective-permute-start.6
  55.8 1.4 collective-permute-start.9
  57.2 6.9 %collective-permute-start.8 = (bf16[384,1024]{1,0:T(8,128)(2,1)S(1)}, bf16[384,1024]{1,0:T(8,128)(2,1)}, u32[]{:S(2)}, u32[]{:S(2)}) collective-permute-start(bf16[384,1024]{1,0:T(8,128)(2,1)S(1)} %get-tuple-element.51.rest_0_), channel_id=1, source_target_pairs={{0,8},{2,10},{4,12},{6,14},{8,16},{10,18},{12,20},{14,22},{16,24},... | collective-permute-start | bytes 2359304 | tf_op jit(solution)/shard_map/ppermute | solution.py:26
  64.1 0.1 collective-permute-start.4
  64.3 0.1 copy.20.picks
  64.4 1.7 %collective-permute-done.4.got = bf16[128,1024]{1,0:T(8,128)(2,1)} collective-permute-done((bf16[128,1024]{1,0:T(8,128)(2,1)}, bf16[128,1024]{1,0:T(8,128)(2,1)}, u32[]{:S(2)}, u32[]{:S(2)}) %collective-permute-start.4) | collective-permute-done | bytes 262176 | tf_op jit(solution)/shard_map/ppermute | solution.py:30
  66.0 1.6 %copy-done.1 = bf16[1,2048,512]{2,1,0:T(8,128)(2,1)S(1)} copy-done((bf16[1,2048,512]{2,1,0:T(8,128)(2,1)S(1)}, bf16[1,2048,512]{2,1,0:T(8,128)(2,1)}, u32[]{:S(2)}) %copy-start.1) | copy-done | bytes 2097176
  67.6 3.1 %shard_map.142 = (f32[128,1024]{1,0:T(8,128)S(1)}, f32[128,1024]{1,0:T(8,128)S(1)}, bf16[128,512]{1,0:T(8,128)(2,1)S(1)}, f32[128,512]{1,0:T(8,128)S(1)}, f32[128,512]{1,0:T(8,128)S(1)}) custom-call(bf16[128,1024]{1,0:T(8,128)(2,1)S(1)} %get-tuple-element.52.keep.refs_1_, bf16[128,1024]{1,0:T(8,128)(2,1)} %collective-permute-done.4.got, ...), custom_call_target="tpu_custom_call" | custom-call | flops 110000000 | tf_op jit(solution)/shard_map/pallas_call | solution.py:90
  70.7 8.9 %collective-permute-done.9.above = bf16[384,1024]{1,0:T(8,128)(2,1)} collective-permute-done((bf16[384,1024]{1,0:T(8,128)(2,1)}, bf16[384,1024]{1,0:T(8,128)(2,1)}, u32[]{:S(2)}, u32[]{:S(2)}) %collective-permute-start.9) | collective-permute-done | bytes 786464 | tf_op jit(solution)/shard_map/ppermute | solution.py:26
  79.7 0.9 collective-permute-done.8.below
  80.6 1.5 shard_map.144
  82.0 0.0 copy-start.18
  82.0 0.0 collective-permute-done.7.refs_0_
  82.1 0.1 collective-permute-start.10
  82.1 2.9 %collective-permute-done.10.over_s = bf16[256,2048]{1,0:T(8,128)(2,1)S(1)} collective-permute-done((bf16[256,2048]{1,0:T(8,128)(2,1)}, bf16[256,2048]{1,0:T(8,128)(2,1)S(1)}, u32[]{:S(2)}, u32[]{:S(2)}) %collective-permute-start.10) | collective-permute-done | bytes 1048608 | tf_op jit(solution)/shard_map/ppermute | solution.py:30
  85.0 0.0 collective-permute-done.6.inner_s
  85.0 5.6 %shard_map.146 = (bf16[128,1152]{1,0:T(8,128)(2,1)S(1)}, bf16[128,1152]{1,0:T(8,128)(2,1)S(1)}, bf16[128,512]{1,0:T(8,128)(2,1)S(1)}, f32[128,512]{1,0:T(8,128)S(1)}, f32[128,512]{1,0:T(8,128)S(1)}) custom-call(bf16[128,1024]{1,0:T(8,128)(2,1)S(1)} %get-tuple-element.52.keep.refs_1_, bf16[128,1024]{1,0:T(8,128)(2,1)} %collective-permute-done.4.got, ...), custom_call_target="tpu_custom_call" | custom-call | flops 4950000128 | tf_op jit(solution)/shard_map/pallas_call | solution.py:90
  90.6 0.0 copy-start.13
  90.6 0.0 copy-start.15
  90.6 0.2 collective-permute-start.11
  90.8 1.5 collective-permute-done.11.got
  92.3 0.1 shard_map.147
  92.4 1.3 collective-permute-start.15
  93.7 4.6 %collective-permute-start.14 = (bf16[256,1152]{1,0:T(8,128)(2,1)S(1)}, bf16[256,1152]{1,0:T(8,128)(2,1)S(1)}, u32[]{:S(2)}, u32[]{:S(2)}) collective-permute-start(bf16[256,1152]{1,0:T(8,128)(2,1)S(1)} %get-tuple-element.65.after.co), channel_id=1, source_target_pairs={{0,4},{2,6},{4,8},{6,10},{8,12},{10,14},{12,16},{14,18},{16,20},{1... | collective-permute-start | bytes 1769480 | tf_op jit(solution)/shard_map/ppermute | solution.py:26
  98.3 4.5 %collective-permute-start.13 = (bf16[128,1152]{1,0:T(8,128)(2,1)S(1)}, bf16[128,1152]{1,0:T(8,128)(2,1)S(1)}, u32[]{:S(2)}, u32[]{:S(2)}) collective-permute-start(bf16[128,1152]{1,0:T(8,128)(2,1)S(1)} %get-tuple-element.69), channel_id=1, source_target_pairs={{0,8},{2,10},{4,12},{6,14},{8,16},{10,18},{12,20},{14,22},{16,24},... | collective-permute-start | bytes 884744 | tf_op jit(solution)/shard_map/ppermute | solution.py:26
  102.8 0.0 copy-start.4
  102.8 1.6 %collective-permute-start.16 = (bf16[128,1152]{1,0:T(8,128)(2,1)S(1)}, bf16[128,1152]{1,0:T(8,128)(2,1)S(1)}, u32[]{:S(2)}, u32[]{:S(2)}) collective-permute-start(bf16[128,1152]{1,0:T(8,128)(2,1)S(1)} %get-tuple-element.70), channel_id=1, source_target_pairs={{8,0},{10,2},{12,4},{14,6},{16,8},{18,10},{20,12},{22,14},{24,16},... | collective-permute-start | bytes 884744 | tf_op jit(solution)/shard_map/ppermute | solution.py:26
  104.4 5.2 %shard_map.149 = (bf16[8,2,512,128]{3,2,1,0:T(8,128)(2,1)S(1)}, bf16[8,2,128,512]{3,2,1,0:T(8,128)(2,1)S(1)}, bf16[256,1024]{1,0:T(8,128)(2,1)S(1)}, bf16[128,10...) custom-call(bf16[128,2048]{1,0:T(8,128)(2,1)S(1)} %copy-done.15, ...), custom_call_target="tpu_custom_call" | custom-call | flops 7699999744 | tf_op jit(solution)/shard_map/pallas_call | solution.py:90
  109.7 2.9 %shard_map.148.after = bf16[128,2048]{1,0:T(8,128)(2,1)} custom-call(bf16[128,1024]{1,0:T(8,128)(2,1)S(1)} %get-tuple-element.52.keep.refs_1_, bf16[128,1024]{1,0:T(8,128)(2,1)} %collective-permute-done.4.got, bf16[128,512]{1,0:T(8,128)(2,1)S(1)} %get-tuple-element.54.hidden_own, bf16[128,512]{1,0:T(8,128)(2,1)S(1)} %get-tuple-element.61.hidden, ...), custom_call_target="tpu_custom_call" | custom-call | flops 3300000000 | tf_op jit(solution)/shard_map/pallas_call | solution.py:90
  112.6 0.0 collective-permute-done.13.cfb
  112.6 4.3 %collective-permute-done.16.cfa = bf16[128,1152]{1,0:T(8,128)(2,1)S(1)} collective-permute-done((bf16[128,1152]{1,0:T(8,128)(2,1)S(1)}, bf16[128,1152]{1,0:T(8,128)(2,1)S(1)}, u32[]{:S(2)}, u32[]{:S(2)}) %collective-permute-start.16) | collective-permute-done | bytes 294944 | tf_op jit(solution)/shard_map/ppermute | solution.py:26
  116.9 0.0 collective-permute-done.15.cna
  116.9 5.3 %collective-permute-done.14.cnb = bf16[256,1152]{1,0:T(8,128)(2,1)S(1)} collective-permute-done((bf16[256,1152]{1,0:T(8,128)(2,1)S(1)}, bf16[256,1152]{1,0:T(8,128)(2,1)S(1)}, u32[]{:S(2)}, u32[]{:S(2)}) %collective-permute-start.14) | collective-permute-done | bytes 589856 | tf_op jit(solution)/shard_map/ppermute | solution.py:26
  122.1 1.0 copy-done.22
  123.2 15.9 %shard_map.150 = (bf16[128,2048]{1,0:T(8,128)(2,1)S(1)}, bf16[128,2048]{1,0:T(8,128)(2,1)S(1)}, bf16[128,1024]{1,0:T(8,128)(2,1)S(1)}, bf16[128,1024]{1,0:T(8,128)(2,1)S(1)}) custom-call(bf16[128,2048]{1,0:T(8,128)(2,1)S(1)} %copy-done.15, bf16[256,2048]{1,0:T(8,128)(2,1)S(1)} %copy-done.8, bf16[256,2048]{1,0:T(8,128)(2,1)S(1)} %copy-done.6, ...), custom_call_target="tpu_custom_call" | custom-call | flops 17600000000 | tf_op jit(solution)/shard_map/pallas_call | solution.py:90
  139.1 0.1 collective-permute-start.18
  139.2 0.5 collective-permute-start.17
  139.7 0.1 collective-permute-start.12
  139.8 0.9 collective-permute-done.18.got
  140.7 5.3 %shard_map.152 = bf16[128,2048]{1,0:T(8,128)(2,1)} custom-call(bf16[128,1024]{1,0:T(8,128)(2,1)S(1)} %get-tuple-element.81.keep, bf16[128,1024]{1,0:T(8,128)(2,1)S(1)} %collective-permute-done.18.got, f32[128,512]{1,0:T(8,128)S(1)} %get-tuple-element.83.slope_up_own, f32[128,512]{1,0:T(8,128)S(1)} %get-tuple-element.84.active_own, ...), custom_call_target="tpu_custom_call" | custom-call | flops 4950000128 | tf_op jit(solution)/shard_map/pallas_call | solution.py:90
  146.0 0.0 collective-permute-done.12.q_got
  146.0 0.0 collective-permute-done.17.got
  146.0 1.3 shard_map.151
  (43 shorter events, 0.1 us)
Async XLA Ops:
  0.6 10.6 %copy-start.9 = (bf16[1,128,2048]{2,1,0:T(8,128)(2,1)S(1)}, bf16[1,128,2048]{2,1,0:T(8,128)(2,1)}, u32[]{:S(2)}) copy-start(bf16[1,128,2048]{2,1,0:T(8,128)(2,1)} %query.3) | copy-start | bytes 1572868
  0.6 10.6 %copy-start.10 = (bf16[1,128,2048]{2,1,0:T(8,128)(2,1)S(1)}, bf16[1,128,2048]{2,1,0:T(8,128)(2,1)}, u32[]{:S(2)}) copy-start(bf16[1,128,2048]{2,1,0:T(8,128)(2,1)} %key.3) | copy-start | bytes 1572868
  0.7 10.6 %copy-start.11 = (bf16[1,128,2048]{2,1,0:T(8,128)(2,1)S(1)}, bf16[1,128,2048]{2,1,0:T(8,128)(2,1)}, u32[]{:S(2)}) copy-start(bf16[1,128,2048]{2,1,0:T(8,128)(2,1)} %value.3) | copy-start | bytes 1572868
  0.7 10.6 %copy-start.16 = (s32[1,1,3]{2,1,0:T(1,128)S(1)}, s32[1,1,3]{2,1,0:T(1,128)}, u32[]{:S(2)}) copy-start(s32[1,1,3]{2,1,0:T(1,128)} %mask.3) | copy-start | bytes 40
  5.7 15.5 %copy-start.3 = (bf16[1,512,2048]{2,1,0:T(8,128)(2,1)S(1)}, bf16[1,512,2048]{2,1,0:T(8,128)(2,1)}, u32[]{:S(2)}) copy-start(bf16[1,512,2048]{2,1,0:T(8,128)(2,1)} %param.19) | copy-start | bytes 6291460
  5.7 15.5 %copy-start.17 = (bf16[1,128,2048]{2,1,0:T(8,128)(2,1)S(1)}, bf16[1,128,2048]{2,1,0:T(8,128)(2,1)}, u32[]{:S(2)}) copy-start(bf16[1,128,2048]{2,1,0:T(8,128)(2,1)} %cot.3) | copy-start | bytes 1572868
  5.7 49.8 %collective-permute-start.5 = (bf16[2,1024,512]{2,1,0:T(8,128)(2,1)}, bf16[2,1024,512]{2,1,0:T(8,128)(2,1)}, u32[]{:S(2)}, u32[]{:S(2)}) collective-permute-start(bf16[2,1024,512]{2,1,0:T(8,128)(2,1)} %get-tuple-element.57), channel_id=1, source_target_pairs={{0,1},{1,0},{2,3},{3,2},{4,5},{5,4},{6,7},{7,6},{8,9},{9,8},{10,11... | collective-permute-start | bytes 6291464 | tf_op jit(solution)/shard_map/ppermute | solution.py:42
  8.7 2.5 %collective-permute-start = (bf16[128,3200]{1,0:T(8,128)(2,1)}, bf16[128,3200]{1,0:T(8,128)(2,1)S(1)}, u32[]{:S(2)}, u32[]{:S(2)}) collective-permute-start(bf16[128,3200]{1,0:T(8,128)(2,1)} %get-tuple-element.46), channel_id=1, source_target_pairs={{0,2},{2,0},{4,6},{6,4},{8,10},{10,8},{12,14},{14,12},{16,18},{18,... | collective-permute-start | bytes 2457608 | tf_op jit(solution)/shard_map/ppermute | solution.py:30
  12.0 38.4 %copy-start.5 = (bf16[256,2048]{1,0:T(8,128)(2,1)}, bf16[256,2048]{1,0:T(8,128)(2,1)S(1)}, u32[]{:S(2)}) copy-start(bf16[256,2048]{1,0:T(8,128)(2,1)S(1)} %get-tuple-element.48.own) | copy-start | bytes 3145732
  12.0 38.4 %copy-start.12 = (bf16[256,1024]{1,0:T(8,128)(2,1)}, bf16[256,1024]{1,0:T(8,128)(2,1)S(1)}, u32[]{:S(2)}) copy-start(bf16[256,1024]{1,0:T(8,128)(2,1)S(1)} %get-tuple-element.49.own.q2) | copy-start | bytes 1572868
  12.1 38.4 %collective-permute-start.2 = (bf16[256,2048]{1,0:T(8,128)(2,1)S(1)}, bf16[256,2048]{1,0:T(8,128)(2,1)S(1)}, u32[]{:S(2)}, u32[]{:S(2)}) collective-permute-start(bf16[256,2048]{1,0:T(8,128)(2,1)S(1)} %get-tuple-element.48.own), channel_id=1, source_target_pairs={{0,4},{2,6},{4,8},{6,10},{8,12},{10,14},{12,16},{14,18},{16,20},{1... | collective-permute-start | bytes 3145736 | tf_op jit(solution)/shard_map/ppermute | solution.py:26
  15.6 33.9 %collective-permute-start.3 = (bf16[256,1024]{1,0:T(8,128)(2,1)S(1)}, bf16[256,1024]{1,0:T(8,128)(2,1)S(1)}, u32[]{:S(2)}, u32[]{:S(2)}) collective-permute-start(bf16[256,1024]{1,0:T(8,128)(2,1)S(1)} %get-tuple-element.49.own.q2), channel_id=1, source_target_pairs={{0,4},{2,6},{4,0},{6,2},{8,12},{10,14},{12,8},{14,10},{16,20},{18,... | collective-permute-start | bytes 1572872 | tf_op jit(solution)/shard_map/ppermute | solution.py:30
  17.1 33.4 %collective-permute-start.1 = (bf16[128,2048]{1,0:T(8,128)(2,1)S(1)}, bf16[128,2048]{1,0:T(8,128)(2,1)S(1)}, u32[]{:S(2)}, u32[]{:S(2)}) collective-permute-start(bf16[128,2048]{1,0:T(8,128)(2,1)S(1)} %get-tuple-element.47), channel_id=1, source_target_pairs={{0,8},{2,10},{4,12},{6,14},{8,16},{10,18},{12,20},{14,22},{16,24},... | collective-permute-start | bytes 1572872 | tf_op jit(solution)/shard_map/ppermute | solution.py:26
  20.6 61.5 %collective-permute-start.7 = (bf16[256,2048]{1,0:T(8,128)(2,1)}, bf16[256,2048]{1,0:T(8,128)(2,1)}, u32[]{:S(2)}, u32[]{:S(2)}) collective-permute-start(bf16[256,2048]{1,0:T(8,128)(2,1)} %get-tuple-element.58), channel_id=1, source_target_pairs={{0,1},{1,0},{2,3},{3,2},{4,5},{5,4},{6,7},{7,6},{8,9},{9,8},{10,11... | collective-permute-start | bytes 3145736 | tf_op jit(solution)/shard_map/ppermute | solution.py:42
  49.4 5.7 %copy-start.19 = (bf16[256,1024]{1,0:T(8,128)(2,1)}, bf16[256,1024]{1,0:T(8,128)(2,1)S(1)}, u32[]{:S(2)}) copy-start(bf16[256,1024]{1,0:T(8,128)(2,1)S(1)} %collective-permute-done.3.other) | copy-start | bytes 1572868
  50.5 4.6 %copy-start.14 = (bf16[128,2048]{1,0:T(8,128)(2,1)}, bf16[128,2048]{1,0:T(8,128)(2,1)S(1)}, u32[]{:S(2)}) copy-start(bf16[128,2048]{1,0:T(8,128)(2,1)S(1)} %collective-permute-done.1.far) | copy-start | bytes 1572868
  50.5 4.6 %copy-start.7 = (bf16[256,2048]{1,0:T(8,128)(2,1)}, bf16[256,2048]{1,0:T(8,128)(2,1)S(1)}, u32[]{:S(2)}) copy-start(bf16[256,2048]{1,0:T(8,128)(2,1)S(1)} %collective-permute-done.2.near) | copy-start | bytes 3145732
  55.1 0.7 copy-start.21
  55.5 8.8 %copy-start.24 = (s32[1,128,1]{1,2,0:T(1,128)S(1)}, s32[1,128,1]{1,2,0:T(1,128)}, u32[]{:S(2)}) copy-start(s32[1,128,1]{1,2,0:T(1,128)} %param.14) | copy-start | bytes 1540
  55.5 8.8 %copy-start.23 = (f32[1,128,1]{1,2,0:T(1,128)S(1)}, f32[1,128,1]{1,2,0:T(1,128)}, u32[]{:S(2)}) copy-start(f32[1,128,1]{1,2,0:T(1,128)} %param.15) | copy-start | bytes 1540
  55.5 10.6 %copy-start = (bf16[1,2048,512]{2,1,0:T(8,128)(2,1)S(1)}, bf16[1,2048,512]{2,1,0:T(8,128)(2,1)}, u32[]{:S(2)}) copy-start(bf16[1,2048,512]{2,1,0:T(8,128)(2,1)} %param.17) | copy-start | bytes 6291460
  55.8 29.2 %collective-permute-start.6 = (bf16[2,1024,512]{2,1,0:T(8,128)(2,1)}, bf16[2,1024,512]{2,1,0:T(8,128)(2,1)}, u32[]{:S(2)}, u32[]{:S(2)}) collective-permute-start(bf16[2,1024,512]{2,1,0:T(8,128)(2,1)} %shard_map.143.inner), channel_id=1, source_target_pairs={{0,2},{2,0},{4,6},{6,4},{8,10},{10,8},{12,14},{14,12},{16,18},{18,... | collective-permute-start | bytes 6291464 | tf_op jit(solution)/shard_map/ppermute | solution.py:30
  55.8 23.9 %collective-permute-start.9 = (bf16[384,1024]{1,0:T(8,128)(2,1)}, bf16[384,1024]{1,0:T(8,128)(2,1)}, u32[]{:S(2)}, u32[]{:S(2)}) collective-permute-start(bf16[384,1024]{1,0:T(8,128)(2,1)} %get-tuple-element.59), channel_id=1, source_target_pairs={{8,0},{10,2},{12,4},{14,6},{16,8},{18,10},{20,12},{22,14},{24,16},... | collective-permute-start | bytes 2359304 | tf_op jit(solution)/shard_map/ppermute | solution.py:26
  57.2 23.3 %collective-permute-start.8 = (bf16[384,1024]{1,0:T(8,128)(2,1)S(1)}, bf16[384,1024]{1,0:T(8,128)(2,1)}, u32[]{:S(2)}, u32[]{:S(2)}) collective-permute-start(bf16[384,1024]{1,0:T(8,128)(2,1)S(1)} %get-tuple-element.51.rest_0_), channel_id=1, source_target_pairs={{0,8},{2,10},{4,12},{6,14},{8,16},{10,18},{12,20},{14,22},{16,24},... | collective-permute-start | bytes 2359304 | tf_op jit(solution)/shard_map/ppermute | solution.py:26
  64.1 1.9 %collective-permute-start.4 = (bf16[128,1024]{1,0:T(8,128)(2,1)}, bf16[128,1024]{1,0:T(8,128)(2,1)}, u32[]{:S(2)}, u32[]{:S(2)}) collective-permute-start(bf16[128,1024]{1,0:T(8,128)(2,1)} %copy-done.21), channel_id=1, source_target_pairs={{0,2},{2,0},{4,6},{6,4},{8,10},{10,8},{12,14},{14,12},{16,18},{18,... | collective-permute-start | bytes 786440 | tf_op jit(solution)/shard_map/ppermute | solution.py:30
  66.0 1.6 %copy-start.1 = (bf16[1,2048,512]{2,1,0:T(8,128)(2,1)S(1)}, bf16[1,2048,512]{2,1,0:T(8,128)(2,1)}, u32[]{:S(2)}) copy-start(bf16[1,2048,512]{2,1,0:T(8,128)(2,1)} %param.18) | copy-start | bytes 6291460
  67.6 12.9 %copy-start.20 = (bf16[256,1024]{1,0:T(8,128)(2,1)S(1)}, bf16[256,1024]{1,0:T(8,128)(2,1)}, u32[]{:S(2)}) copy-start(bf16[256,1024]{1,0:T(8,128)(2,1)} %copy-done.19) | copy-start | bytes 1572868
  82.0 3.0 %copy-start.18 = (bf16[1,128,2048]{2,1,0:T(8,128)(2,1)S(1)}, bf16[1,128,2048]{2,1,0:T(8,128)(2,1)}, u32[]{:S(2)}) copy-start(bf16[1,128,2048]{2,1,0:T(8,128)(2,1)} %cot.3) | copy-start | bytes 1572868
  82.1 2.9 %collective-permute-start.10 = (bf16[256,2048]{1,0:T(8,128)(2,1)}, bf16[256,2048]{1,0:T(8,128)(2,1)S(1)}, u32[]{:S(2)}, u32[]{:S(2)}) collective-permute-start(bf16[256,2048]{1,0:T(8,128)(2,1)} %shard_map.145.over), channel_id=1, source_target_pairs={{0,2},{2,0},{4,6},{6,4},{8,10},{10,8},{12,14},{14,12},{16,18},{18,... | collective-permute-start | bytes 3145736 | tf_op jit(solution)/shard_map/ppermute | solution.py:30
  90.6 13.8 %copy-start.6 = (bf16[256,2048]{1,0:T(8,128)(2,1)S(1)}, bf16[256,2048]{1,0:T(8,128)(2,1)}, u32[]{:S(2)}) copy-start(bf16[256,2048]{1,0:T(8,128)(2,1)} %copy-done.5) | copy-start | bytes 3145732
  90.6 13.8 %copy-start.8 = (bf16[256,2048]{1,0:T(8,128)(2,1)S(1)}, bf16[256,2048]{1,0:T(8,128)(2,1)}, u32[]{:S(2)}) copy-start(bf16[256,2048]{1,0:T(8,128)(2,1)} %copy-done.7) | copy-start | bytes 3145732
  90.6 13.8 %copy-start.13 = (bf16[256,1024]{1,0:T(8,128)(2,1)S(1)}, bf16[256,1024]{1,0:T(8,128)(2,1)}, u32[]{:S(2)}) copy-start(bf16[256,1024]{1,0:T(8,128)(2,1)} %copy-done.12) | copy-start | bytes 1572868
  90.6 13.8 %copy-start.15 = (bf16[128,2048]{1,0:T(8,128)(2,1)S(1)}, bf16[128,2048]{1,0:T(8,128)(2,1)}, u32[]{:S(2)}) copy-start(bf16[128,2048]{1,0:T(8,128)(2,1)} %copy-done.14) | copy-start | bytes 1572868
  90.6 1.6 %collective-permute-start.11 = (bf16[128,1152]{1,0:T(8,128)(2,1)S(1)}, bf16[128,1152]{1,0:T(8,128)(2,1)S(1)}, u32[]{:S(2)}, u32[]{:S(2)}) collective-permute-start(bf16[128,1152]{1,0:T(8,128)(2,1)S(1)} %get-tuple-element.63), channel_id=1, source_target_pairs={{0,2},{2,0},{4,6},{6,4},{8,10},{10,8},{12,14},{14,12},{16,18},{18,... | collective-permute-start | bytes 884744 | tf_op jit(solution)/shard_map/ppermute | solution.py:30
  92.4 24.5 %collective-permute-start.15 = (bf16[256,1152]{1,0:T(8,128)(2,1)S(1)}, bf16[256,1152]{1,0:T(8,128)(2,1)S(1)}, u32[]{:S(2)}, u32[]{:S(2)}) collective-permute-start(bf16[256,1152]{1,0:T(8,128)(2,1)S(1)} %get-tuple-element.65.after.co), channel_id=1, source_target_pairs={{4,0},{6,2},{8,4},{10,6},{12,8},{14,10},{16,12},{18,14},{20,16},{2... | collective-permute-start | bytes 1769480 | tf_op jit(solution)/shard_map/ppermute | solution.py:26
  93.7 28.4 %collective-permute-start.14 = (bf16[256,1152]{1,0:T(8,128)(2,1)S(1)}, bf16[256,1152]{1,0:T(8,128)(2,1)S(1)}, u32[]{:S(2)}, u32[]{:S(2)}) collective-permute-start(bf16[256,1152]{1,0:T(8,128)(2,1)S(1)} %get-tuple-element.65.after.co), channel_id=1, source_target_pairs={{0,4},{2,6},{4,8},{6,10},{8,12},{10,14},{12,16},{14,18},{16,20},{1... | collective-permute-start | bytes 1769480 | tf_op jit(solution)/shard_map/ppermute | solution.py:26
  98.3 14.3 %collective-permute-start.13 = (bf16[128,1152]{1,0:T(8,128)(2,1)S(1)}, bf16[128,1152]{1,0:T(8,128)(2,1)S(1)}, u32[]{:S(2)}, u32[]{:S(2)}) collective-permute-start(bf16[128,1152]{1,0:T(8,128)(2,1)S(1)} %get-tuple-element.69), channel_id=1, source_target_pairs={{0,8},{2,10},{4,12},{6,14},{8,16},{10,18},{12,20},{14,22},{16,24},... | collective-permute-start | bytes 884744 | tf_op jit(solution)/shard_map/ppermute | solution.py:26
  102.8 6.9 %copy-start.4 = (bf16[1,512,2048]{2,1,0:T(8,128)(2,1)S(1)}, bf16[1,512,2048]{2,1,0:T(8,128)(2,1)}, u32[]{:S(2)}) copy-start(bf16[1,512,2048]{2,1,0:T(8,128)(2,1)} %param.19) | copy-start | bytes 6291460
  102.8 14.1 %collective-permute-start.16 = (bf16[128,1152]{1,0:T(8,128)(2,1)S(1)}, bf16[128,1152]{1,0:T(8,128)(2,1)S(1)}, u32[]{:S(2)}, u32[]{:S(2)}) collective-permute-start(bf16[128,1152]{1,0:T(8,128)(2,1)S(1)} %get-tuple-element.70), channel_id=1, source_target_pairs={{8,0},{10,2},{12,4},{14,6},{16,8},{18,10},{20,12},{22,14},{24,16},... | collective-permute-start | bytes 884744 | tf_op jit(solution)/shard_map/ppermute | solution.py:26
  122.1 1.0 copy-start.22
  123.2 17.5 %copy-start.2 = (bf16[1,2048,512]{2,1,0:T(8,128)(2,1)S(1)}, bf16[1,2048,512]{2,1,0:T(8,128)(2,1)}, u32[]{:S(2)}) copy-start(bf16[1,2048,512]{2,1,0:T(8,128)(2,1)} %param.18) | copy-start | bytes 6291460
  139.1 1.6 %collective-permute-start.18 = (bf16[128,1024]{1,0:T(8,128)(2,1)S(1)}, bf16[128,1024]{1,0:T(8,128)(2,1)S(1)}, u32[]{:S(2)}, u32[]{:S(2)}) collective-permute-start(bf16[128,1024]{1,0:T(8,128)(2,1)S(1)} %get-tuple-element.82), channel_id=1, source_target_pairs={{0,2},{2,0},{4,6},{6,4},{8,10},{10,8},{12,14},{14,12},{16,18},{18,... | collective-permute-start | bytes 786440 | tf_op jit(solution)/shard_map/ppermute | solution.py:30
  139.2 6.8 %collective-permute-start.17 = (bf16[128,2048]{1,0:T(8,128)(2,1)S(1)}, bf16[128,2048]{1,0:T(8,128)(2,1)S(1)}, u32[]{:S(2)}, u32[]{:S(2)}) collective-permute-start(bf16[128,2048]{1,0:T(8,128)(2,1)S(1)} %get-tuple-element.77), channel_id=1, source_target_pairs={{0,2},{2,0},{4,6},{6,4},{8,10},{10,8},{12,14},{14,12},{16,18},{18,... | collective-permute-start | bytes 1572872 | tf_op jit(solution)/shard_map/ppermute | solution.py:30
  139.7 6.3 %collective-permute-start.12 = (bf16[128,1024]{1,0:T(8,128)(2,1)S(1)}, bf16[128,1024]{1,0:T(8,128)(2,1)S(1)}, u32[]{:S(2)}, u32[]{:S(2)}) collective-permute-start(bf16[128,1024]{1,0:T(8,128)(2,1)S(1)} %get-tuple-element.67), channel_id=1, source_target_pairs={{0,2},{2,0},{4,6},{6,4},{8,10},{10,8},{12,14},{14,12},{16,18},{18,... | collective-permute-start | bytes 786440 | tf_op jit(solution)/shard_map/ppermute | solution.py:30

commit v4 on v3

--- a/solution.py
+++ b/solution.py
@@ -111,8 +111,9 @@
     return [(array, ANY) for array in arrays]
 
 
-def tied(x, *after):
-    return call(lambda *refs: None, like(*x.shape), anywhere(x, *after), alias={0: 0}, spaces=ANY, limit=1, time=0.01)
+def tied(x, *after, time=0.01):
+    out = like(*x.shape, kind=x.dtype)
+    return call(lambda *refs: None, out, anywhere(x, *after), alias={0: 0}, spaces=ANY, limit=1, time=time)
 
 
 def fetch(copies):
@@ -409,6 +410,7 @@
         blocks = range(1 - WIN, PAIR)
         keys_at = {j: key_sums[pl.ds((j + WIN - 1) * rows, rows), here] for j in blocks}
         values_at = {j: value_sums[pl.ds((j + WIN - 1) * rows, rows), here] for j in blocks}
+        score_grads, probs_at, qs, cots = {}, {}, {}, {}
         for n, (t, q_ref, q_half, c_ref, half) in enumerate(others):
             js = list(range(max(1 - WIN, t - WIN + 1), min(1, t) + 1))
             q, cot = q_ref[pl.ds(q_half * rows, rows), here], c_ref[pl.ds(half * rows, rows), here]
@@ -418,8 +420,19 @@
                 q, cot, levels[n, pl.ds(head, 1), :], deltas[n, pl.ds(head, 1), :], sides[n][0:8],
                 keys, values, js, t, causal, scale,
             )
-            add_blocks(keys_at, js, nn(score_grad, q), rows)
-            add_blocks(values_at, js, nn(probs.astype(BF), cot), rows)
+            probs = probs.astype(BF)
+            qs[t], cots[t] = q, cot
+            for m, j in enumerate(js):
+                score_grads[j, t] = score_grad[m * rows : (m + 1) * rows]
+                probs_at[j, t] = probs[m * rows : (m + 1) * rows]
+        for j in blocks:
+            ts = [t for t in qs if (j, t) in probs_at]
+            keys_at[j] = keys_at[j] + nn(
+                jnp.concatenate([score_grads[j, t] for t in ts], axis=1), jnp.concatenate([qs[t] for t in ts], axis=0)
+            )
+            values_at[j] = values_at[j] + nn(
+                jnp.concatenate([probs_at[j, t] for t in ts], axis=1), jnp.concatenate([cots[t] for t in ts], axis=0)
+            )
         key_grads = {j: (keys_at[j] * scale).astype(BF) for j in blocks}
         value_grads = {j: values_at[j].astype(BF) for j in blocks}
         tans = []
@@ -441,7 +454,7 @@
             grads[:, there] = jnp.where(core == 0, value_grads[mine], value_grads[other])
             tans_out[:, here] = jnp.where(core == 0, tans[mine], tans[other])
 
-    each_head(heads, one)
+    each_head(heads, one, 4)
 
 
 def gather_kernel(q_keep, q_got, keep, got, out_q, out_k, out_v):
@@ -509,6 +522,19 @@
     gate_grad, up_grad = middle_of(picks[:, 0:1], inner(gate), inner(up), back[...], hidden, slope_up, active)
     for here, out in ((mine, sum_keep), (others, sum_got)):
         out[...] = nt(gate_grad, gate[here, :]) + nt(up_grad, up[here, :])
+
+
+def stream(pairs, sems):
+    copies = fetch([pltpu.make_async_copy(source, buffer, sems.at[n]) for n, (source, buffer) in enumerate(pairs)])
+
+    def waiting(n):
+        def get():
+            copies[n].wait()
+            return pairs[n][1][...]
+
+        return get
+
+    return [waiting(n) for n in range(len(pairs))]
 
 
 def other_expert_kernel(
@@ -532,7 +558,8 @@
         out[...] = cot_payload(size, attn_cot, attended)
 
 
-def layer_kernel(keep, got, hidden_own, hidden, picks, down, over, over_s, after, out):
+def layer_kernel(keep, got, hidden_own, hidden, picks, down, over, over_s, *rest):
+    out = rest[-1]
     core = this_core()
     rows_in = in_order(core, keep[...], got[...]).astype(F32)
     summed = nn(hidden_own[...], down[...]) + down_of_other(hidden[...], core, over, over_s)
@@ -540,16 +567,23 @@
 
 
 def tangent_kernel(
-    keep, got, slope_up_own, active_own, slope_up, active, picks, gate, up, inner, inner_s, down, over, over_s, out
+    keep, got, slope_up_own, active_own, slope_up, active, picks, gate, up, inner, inner_s, down, over, over_s, out,
+    inners, overs, sems,
 ):
     core = this_core()
+    gate_o, gate_s, up_o, up_s, over, over_s = stream(
+        [(ref.at[n], inners.at[m, n]) for n in range(2) for m, ref in enumerate((inner, inner_s))]
+        + [(over, overs.at[0]), (over_s, overs.at[1])],
+        sems,
+    )
     rows_keep, rows_got = keep[...], got[...]
     rows_in = in_order(core, rows_keep, rows_got)
     hidden = slope_up_own[...] * nn(rows_in, gate[...]) + active_own[...] * nn(rows_in, up[...])
     summed = nn(hidden.astype(BF), down[...])
-    gate_tan, up_tan = (nn(rows_keep, inner[n]) + nn(rows_got, inner_s[n]) for n in range(2))
+    gate_tan = nn(rows_keep, gate_o()) + nn(rows_got, gate_s())
+    up_tan = nn(rows_keep, up_o()) + nn(rows_got, up_s())
     hidden = slope_up[...] * gate_tan + active[...] * up_tan
-    summed = summed + down_of_other(hidden.astype(BF), core, over, over_s)
+    summed = summed + down_of_other(hidden.astype(BF), core, over(), over_s())
     out[...] = (rows_in.astype(F32) + summed.astype(BF).astype(F32) * picks[:, 2:3]).astype(BF)
 
 
@@ -598,7 +632,8 @@
             vmem(keep, got, self.picks, self.back_own, w_gate, w_up),
             time=0.1,
         )
-        inner_o, over = tied(self.inner, keep), tied(self.over, sum_keep, after)
+        inner_o, over = tied(self.inner, keep), tied(self.over, sum_keep)
+        sum_got = tied(sum_got, *after, time=6)
         self.down = (w_down, over, swapped(over))
         self.inner = (inner_o, swapped(inner_o))
         cot_keep, cot_send, hidden, *slopes = call(
@@ -609,11 +644,11 @@
         )
         self.slopes = own_slopes + slopes
 
-        def layer(after):
+        def layer(*after):
             return call(
                 layer_kernel,
                 like(rows, wide),
-                vmem(keep, got, hidden_own, hidden, self.picks, *self.down) + anywhere(after),
+                vmem(keep, got, hidden_own, hidden, self.picks, *self.down) + anywhere(*after),
                 time=3,
             )
 
@@ -623,8 +658,17 @@
         return call(
             tangent_kernel,
             like(self.rows, self.wide),
-            vmem(keep, got, *self.slopes, self.picks, *self.whole[:2], *self.inner, *self.down),
+            vmem(keep, got, *self.slopes, self.picks, *self.whole[:2])
+            + anywhere(*self.inner)
+            + vmem(self.down[0])
+            + anywhere(*self.down[1:]),
+            [
+                pltpu.VMEM((2, 2, self.wide // 2, self.units), BF),
+                pltpu.VMEM((2, self.units // 2, self.wide), BF),
+                pltpu.SemaphoreType.DMA((6,)),
+            ],
             time=4.5,
+            limit=16,
         )
 
 
@@ -742,7 +786,7 @@
         cot_keep, cot_send = call(
             kernel, (half, half), vmem(attn_cot, keep, got)
         )
-        return cot_keep, cot_send, lambda after: layer_out
+        return cot_keep, cot_send, lambda *after: layer_out
 
     def tangent(self, keep, got):
         rows = in_order(self.core, keep, got)
@@ -797,7 +841,7 @@
     q_below, q_above = moved(q_up, 2 * PAIR), moved(q_down, -2 * PAIR)
     q_before, q_after = call(around_kernel, (three, three), vmem(q_other, q_below, q_above))
 
-    cot_keep, cot_send, layer = experts.forward(size, keep, got, q_before)
+    cot_keep, cot_send, layer = experts.forward(size, keep, got, (q_below, q_above))
     payload = wide // PAIR + SIDE
     co, co_even, co_odd = call(
         cots_kernel,
@@ -806,7 +850,7 @@
     )
     cfb, cnb, cna, cfa = neighbours(co, co_even, co_odd)
 
-    layer_out = layer(co)
+    layer_out = layer(co, q_before)
     sums = like((WIN + 1) * rows, width, kind=F32)
     probs, probs_low, grads_q, q_keep, q_send, key_sums, value_sums = call(
         functools.partial(own_grads_kernel, size),

time: 149 us -> 139 us (0.933)
  Pallas kernels: 53.1 us -> 46.6 us
  waiting for transfers between devices: 56.6 us -> 52.7 us
    ppermute x2, waiting for transfers between devices: 0.33 us -> 7.18 us  [crossed(): return lax.ppermute(x, 'exp', [(0, 1), (1, 0)])]
    ppermute x8, waiting for transfers between devices: 19.4 us -> 12.9 us  [moved(): return lax.ppermute(x, 'ctx', pairs)]
    pallas_call x16 -> x17, Pallas kernels: 53.1 us -> 46.6 us  [call(): pl.pallas_call(kernel, out_shape=outs, in_specs=[space for _, space in ar...]
    ppermute x9, waiting for transfers between devices: 36.8 us -> 32.6 us  [swapped(): lax.ppermute(x, 'ctx', [(i, i ^ bit) for i in range(lax.axis_size('ctx'))])]
  transfers between devices with their start and end apart: 19 -> 19, of which waited for: 11 -> 10; matrix products, arithmetic and copies ran while one was open for 0% -> 0% of each run, Pallas kernels for 17% -> 18%
where the time goes in v4:
time: 139 us; the launch traced here: 137 us
  waiting for transfers between devices  52.7 us (38%)
  Pallas kernels  46.6 us (34%)
  starting transfers between devices  33.2 us (24%)
  local copies, waits for them, and re-layouts  3.88 us (3%)
    pallas_call x17, Pallas kernels, call(): pl.pallas_call(kernel, out_shape=outs, in_specs=[space for _, space in ar...  46.6 us
    ppermute x9, waiting for transfers between devices, swapped(): lax.ppermute(x, 'ctx', [(i, i ^ bit) for i in range(lax.axis_size('ctx'))])  32.6 us
    ppermute x8, starting transfers between devices, moved(): return lax.ppermute(x, 'ctx', pairs)  27.2 us
    ppermute x8, waiting for transfers between devices, moved(): return lax.ppermute(x, 'ctx', pairs)  12.9 us
    ppermute x2, waiting for transfers between devices, crossed(): return lax.ppermute(x, 'exp', [(0, 1), (1, 0)])  7.18 us
    unnamed x50, local copies, waits for them, and re-layouts  3.77 us
    ppermute x2, starting transfers between devices, crossed(): return lax.ppermute(x, 'exp', [(0, 1), (1, 0)])  3.6 us
  transfers between devices with their start and end apart: 19, of which 10 were waited for; matrix products, arithmetic and copies ran while one was open for 0% of the time, Pallas kernels for 18%

profile of v4, /device:TPU:0, one launch (start us, length us, event | category | flops | bytes accessed | tf_op | source)
XLA Modules:
  0.0 137.5 jit_solution(14136390950613956117)
XLA Ops:
  0.7 5.0 %shard_map.137 = (bf16[2,1024,512]{2,1,0:T(8,128)(2,1)}, bf16[256,2048]{1,0:T(8,128)(2,1)}, bf16[128,3200]{1,0:T(8,128)(2,1)}) custom-call(s32[1,1,3]{2,1,0:T(1,128)} %mask.3, bf16[2048,512]{1,0:T(8,128)(2,1)} %bitcast.12, bf16[2048,512]{1,0:T(8,128)(2,1)} %bitcast.15, bf16[512,2048]{1,0:T(8,128)(2,1)} %bitcast.18, bf16[1,128,2048]{2,1,0:T(8,128)(2,1)} %query.3, ...), custom_call_target="tpu_custom_call" | custom-call | flops 1100000000 | tf_op jit(solution)/shard_map/pallas_call | solution.py:90
  5.7 0.0 copy-start.3
  5.7 0.0 copy-start.17
  5.7 3.0 %collective-permute-start.7 = (bf16[2,1024,512]{2,1,0:T(8,128)(2,1)}, bf16[2,1024,512]{2,1,0:T(8,128)(2,1)}, u32[]{:S(2)}, u32[]{:S(2)}) collective-permute-start(bf16[2,1024,512]{2,1,0:T(8,128)(2,1)} %get-tuple-element.58), channel_id=1, source_target_pairs={{0,1},{1,0},{2,3},{3,2},{4,5},{5,4},{6,7},{7,6},{8,9},{9,8},{10,11... | collective-permute-start | bytes 6291464 | tf_op jit(solution)/shard_map/ppermute | solution.py:42
  8.7 0.0 collective-permute-start
  8.7 2.5 %collective-permute-done.got = bf16[128,3200]{1,0:T(8,128)(2,1)S(1)} collective-permute-done((bf16[128,3200]{1,0:T(8,128)(2,1)}, bf16[128,3200]{1,0:T(8,128)(2,1)S(1)}, u32[]{:S(2)}, u32[]{:S(2)}) %collective-permute-start) | collective-permute-done | bytes 819232 | tf_op jit(solution)/shard_map/ppermute | solution.py:30
  11.2 0.0 copy-done.9
  11.3 0.8 shard_map.138
  12.1 0.0 copy-start.12
  12.1 3.5 %collective-permute-start.2 = (bf16[256,2048]{1,0:T(8,128)(2,1)S(1)}, bf16[256,2048]{1,0:T(8,128)(2,1)S(1)}, u32[]{:S(2)}, u32[]{:S(2)}) collective-permute-start(bf16[256,2048]{1,0:T(8,128)(2,1)S(1)} %get-tuple-element.48.own), channel_id=1, source_target_pairs={{0,4},{2,6},{4,8},{6,10},{8,12},{10,14},{12,16},{14,18},{16,20},{1... | collective-permute-start | bytes 3145736 | tf_op jit(solution)/shard_map/ppermute | solution.py:26
  15.6 1.5 %collective-permute-start.3 = (bf16[256,1024]{1,0:T(8,128)(2,1)S(1)}, bf16[256,1024]{1,0:T(8,128)(2,1)S(1)}, u32[]{:S(2)}, u32[]{:S(2)}) collective-permute-start(bf16[256,1024]{1,0:T(8,128)(2,1)S(1)} %get-tuple-element.49.own.q2), channel_id=1, source_target_pairs={{0,4},{2,6},{4,0},{6,2},{8,12},{10,14},{12,8},{14,10},{16,20},{18,... | collective-permute-start | bytes 1572872 | tf_op jit(solution)/shard_map/ppermute | solution.py:30
  17.1 3.5 %collective-permute-start.1 = (bf16[128,2048]{1,0:T(8,128)(2,1)S(1)}, bf16[128,2048]{1,0:T(8,128)(2,1)S(1)}, u32[]{:S(2)}, u32[]{:S(2)}) collective-permute-start(bf16[128,2048]{1,0:T(8,128)(2,1)S(1)} %get-tuple-element.47), channel_id=1, source_target_pairs={{0,8},{2,10},{4,12},{6,14},{8,16},{10,18},{12,20},{14,22},{16,24},... | collective-permute-start | bytes 1572872 | tf_op jit(solution)/shard_map/ppermute | solution.py:26
  20.6 0.6 collective-permute-start.9
  21.2 0.8 shard_map.140.rest_1_.back
  22.0 27.4 %collective-permute-done.3.other = bf16[256,1024]{1,0:T(8,128)(2,1)S(1)} collective-permute-done((bf16[256,1024]{1,0:T(8,128)(2,1)S(1)}, bf16[256,1024]{1,0:T(8,128)(2,1)S(1)}, u32[]{:S(2)}, u32[]{:S(2)}) %collective-permute-start.3) | collective-permute-done | bytes 524320 | tf_op jit(solution)/shard_map/ppermute | solution.py:30
  49.4 1.0 shard_map.139
  50.5 0.0 collective-permute-done.1.far
  50.5 0.0 collective-permute-done.2.near
  50.5 4.6 %shard_map.141 = (bf16[256,128]{1,0:T(8,128)(2,1)S(1)}, bf16[128,1024]{1,0:T(8,128)(2,1)S(1)}, bf16[128,1024]{1,0:T(8,128)(2,1)S(1)}) custom-call(bf16[128,2048]{1,0:T(8,128)(2,1)S(1)} %collective-permute-done.1.far, bf16[256,2048]{1,0:T(8,128)(2,1)S(1)} %collective-permute-done.2.near, bf16[256,2048]{1,0:T(8,128)(2,1)S(1)} %get-tuple-element.48.own, ...), custom_call_target="tpu_custom_call" | custom-call | flops 110000000 | tf_op jit(solution)/shard_map/pallas_call | solution.py:90
  55.1 0.0 copy-start.21
  55.1 0.3 collective-permute-done.7.refs_0_
  55.5 0.1 collective-permute-start.8
  55.6 1.4 %collective-permute-start.6 = (bf16[384,1024]{1,0:T(8,128)(2,1)}, bf16[384,1024]{1,0:T(8,128)(2,1)}, u32[]{:S(2)}, u32[]{:S(2)}) collective-permute-start(bf16[384,1024]{1,0:T(8,128)(2,1)} %get-tuple-element.57), channel_id=1, source_target_pairs={{8,0},{10,2},{12,4},{14,6},{16,8},{18,10},{20,12},{22,14},{24,16},... | collective-permute-start | bytes 2359304 | tf_op jit(solution)/shard_map/ppermute | solution.py:26
  57.0 6.7 %collective-permute-start.5 = (bf16[384,1024]{1,0:T(8,128)(2,1)S(1)}, bf16[384,1024]{1,0:T(8,128)(2,1)}, u32[]{:S(2)}, u32[]{:S(2)}) collective-permute-start(bf16[384,1024]{1,0:T(8,128)(2,1)S(1)} %get-tuple-element.51.rest_0_), channel_id=1, source_target_pairs={{0,8},{2,10},{4,12},{6,14},{8,16},{10,18},{12,20},{14,22},{16,24},... | collective-permute-start | bytes 2359304 | tf_op jit(solution)/shard_map/ppermute | solution.py:26
  63.7 0.1 collective-permute-start.4
  63.8 0.1 copy.21.picks
  63.9 1.7 %collective-permute-done.4.got = bf16[128,1024]{1,0:T(8,128)(2,1)} collective-permute-done((bf16[128,1024]{1,0:T(8,128)(2,1)}, bf16[128,1024]{1,0:T(8,128)(2,1)}, u32[]{:S(2)}, u32[]{:S(2)}) %collective-permute-start.4) | collective-permute-done | bytes 262176 | tf_op jit(solution)/shard_map/ppermute | solution.py:30
  65.6 1.6 %copy-done.1 = bf16[1,2048,512]{2,1,0:T(8,128)(2,1)S(1)} copy-done((bf16[1,2048,512]{2,1,0:T(8,128)(2,1)S(1)}, bf16[1,2048,512]{2,1,0:T(8,128)(2,1)}, u32[]{:S(2)}) %copy-start.1) | copy-done | bytes 2097176
  67.2 3.1 %shard_map.142 = (f32[128,1024]{1,0:T(8,128)S(1)}, f32[128,1024]{1,0:T(8,128)S(1)}, bf16[128,512]{1,0:T(8,128)(2,1)S(1)}, f32[128,512]{1,0:T(8,128)S(1)}, f32[128,512]{1,0:T(8,128)S(1)}) custom-call(bf16[128,1024]{1,0:T(8,128)(2,1)S(1)} %get-tuple-element.52.keep.refs_1_, bf16[128,1024]{1,0:T(8,128)(2,1)} %collective-permute-done.4.got, ...), custom_call_target="tpu_custom_call" | custom-call | flops 110000000 | tf_op jit(solution)/shard_map/pallas_call | solution.py:90
  70.3 6.8 %collective-permute-done.9.refs_0_ = bf16[256,2048]{1,0:T(8,128)(2,1)} collective-permute-done((bf16[256,2048]{1,0:T(8,128)(2,1)}, bf16[256,2048]{1,0:T(8,128)(2,1)}, u32[]{:S(2)}, u32[]{:S(2)}) %collective-permute-start.9) | collective-permute-done | bytes 1048608 | tf_op jit(solution)/shard_map/ppermute | solution.py:42
  77.1 0.0 collective-permute-start.10
  77.1 2.1 %collective-permute-done.6.refs_2_.above = bf16[384,1024]{1,0:T(8,128)(2,1)} collective-permute-done((bf16[384,1024]{1,0:T(8,128)(2,1)}, bf16[384,1024]{1,0:T(8,128)(2,1)}, u32[]{:S(2)}, u32[]{:S(2)}) %collective-permute-start.6) | collective-permute-done | bytes 786464 | tf_op jit(solution)/shard_map/ppermute | solution.py:26
  79.3 0.9 collective-permute-done.5.refs_1_.below
  80.1 0.0 collective-permute-done.10.over_s
  80.1 0.0 collective-permute-done.8.inner_s
  80.1 1.0 copy-done.18
  81.2 5.6 %shard_map.146 = (bf16[128,1152]{1,0:T(8,128)(2,1)S(1)}, bf16[128,1152]{1,0:T(8,128)(2,1)S(1)}, bf16[128,512]{1,0:T(8,128)(2,1)S(1)}, f32[128,512]{1,0:T(8,128)S(1)}, f32[128,512]{1,0:T(8,128)S(1)}) custom-call(bf16[128,1024]{1,0:T(8,128)(2,1)S(1)} %get-tuple-element.52.keep.refs_1_, bf16[128,1024]{1,0:T(8,128)(2,1)} %collective-permute-done.4.got, ...), custom_call_target="tpu_custom_call" | custom-call | flops 4950000128 | tf_op jit(solution)/shard_map/pallas_call | solution.py:90
  86.8 0.0 collective-permute-start.11
  86.8 1.5 %shard_map.148 = (bf16[384,1024]{1,0:T(8,128)(2,1)S(1)}, bf16[384,1024]{1,0:T(8,128)(2,1)S(1)}) custom-call(bf16[256,1024]{1,0:T(8,128)(2,1)S(1)} %copy-done.20, bf16[384,1024]{1,0:T(8,128)(2,1)} %collective-permute-done.5.refs_1_.below, bf16[384,1024]{1,0:T(8,128)(2,1)} %collective-permute-done.6.refs_2_.above), custom_call_target="tpu_custom_call" | custom-call | flops 1100000000 | tf_op jit(solution)/shard_map/pallas_call | solution.py:90
  88.3 0.0 copy-start.13
  88.3 0.0 copy-start.15
  88.3 0.0 collective-permute-done.11.got
  88.4 0.1 shard_map.147
  88.5 1.4 %collective-permute-start.15 = (bf16[256,1152]{1,0:T(8,128)(2,1)S(1)}, bf16[256,1152]{1,0:T(8,128)(2,1)S(1)}, u32[]{:S(2)}, u32[]{:S(2)}) collective-permute-start(bf16[256,1152]{1,0:T(8,128)(2,1)S(1)} %get-tuple-element.64.rest_0_.co), channel_id=1, source_target_pairs={{4,0},{6,2},{8,4},{10,6},{12,8},{14,10},{16,12},{18,14},{20,16},{2... | collective-permute-start | bytes 1769480 | tf_op jit(solution)/shard_map/ppermute | solution.py:26
  89.9 4.6 %collective-permute-start.14 = (bf16[256,1152]{1,0:T(8,128)(2,1)S(1)}, bf16[256,1152]{1,0:T(8,128)(2,1)S(1)}, u32[]{:S(2)}, u32[]{:S(2)}) collective-permute-start(bf16[256,1152]{1,0:T(8,128)(2,1)S(1)} %get-tuple-element.64.rest_0_.co), channel_id=1, source_target_pairs={{0,4},{2,6},{4,8},{6,10},{8,12},{10,14},{12,16},{14,18},{16,20},{1... | collective-permute-start | bytes 1769480 | tf_op jit(solution)/shard_map/ppermute | solution.py:26
  94.5 4.5 %collective-permute-start.13 = (bf16[128,1152]{1,0:T(8,128)(2,1)S(1)}, bf16[128,1152]{1,0:T(8,128)(2,1)S(1)}, u32[]{:S(2)}, u32[]{:S(2)}) collective-permute-start(bf16[128,1152]{1,0:T(8,128)(2,1)S(1)} %get-tuple-element.69), channel_id=1, source_target_pairs={{0,8},{2,10},{4,12},{6,14},{8,16},{10,18},{12,20},{14,22},{16,24},... | collective-permute-start | bytes 884744 | tf_op jit(solution)/shard_map/ppermute | solution.py:26
  99.0 0.0 copy-start.4
  99.0 1.6 %collective-permute-start.16 = (bf16[128,1152]{1,0:T(8,128)(2,1)S(1)}, bf16[128,1152]{1,0:T(8,128)(2,1)S(1)}, u32[]{:S(2)}, u32[]{:S(2)}) collective-permute-start(bf16[128,1152]{1,0:T(8,128)(2,1)S(1)} %get-tuple-element.70), channel_id=1, source_target_pairs={{8,0},{10,2},{12,4},{14,6},{16,8},{18,10},{20,12},{22,14},{24,16},... | collective-permute-start | bytes 884744 | tf_op jit(solution)/shard_map/ppermute | solution.py:26
  100.7 5.2 %shard_map.150 = (bf16[8,2,512,128]{3,2,1,0:T(8,128)(2,1)S(1)}, bf16[8,2,128,512]{3,2,1,0:T(8,128)(2,1)S(1)}, bf16[256,1024]{1,0:T(8,128)(2,1)S(1)}, bf16[128,10...) custom-call(bf16[128,2048]{1,0:T(8,128)(2,1)S(1)} %copy-done.15, ...), custom_call_target="tpu_custom_call" | custom-call | flops 7699999744 | tf_op jit(solution)/shard_map/pallas_call | solution.py:90
  105.9 2.9 %shard_map.149.after = bf16[128,2048]{1,0:T(8,128)(2,1)} custom-call(bf16[128,1024]{1,0:T(8,128)(2,1)S(1)} %get-tuple-element.52.keep.refs_1_, bf16[128,1024]{1,0:T(8,128)(2,1)} %collective-permute-done.4.got, bf16[128,512]{1,0:T(8,128)(2,1)S(1)} %get-tuple-element.54.hidden_own, bf16[128,512]{1,0:T(8,128)(2,1)S(1)} %get-tuple-element.60.hidden, ...), custom_call_target="tpu_custom_call" | custom-call | flops 3300000000 | tf_op jit(solution)/shard_map/pallas_call | solution.py:90
  108.8 0.0 collective-permute-done.13.cfb
  108.8 4.6 %collective-permute-done.16.cfa = bf16[128,1152]{1,0:T(8,128)(2,1)S(1)} collective-permute-done((bf16[128,1152]{1,0:T(8,128)(2,1)S(1)}, bf16[128,1152]{1,0:T(8,128)(2,1)S(1)}, u32[]{:S(2)}, u32[]{:S(2)}) %collective-permute-start.16) | collective-permute-done | bytes 294944 | tf_op jit(solution)/shard_map/ppermute | solution.py:26
  113.4 0.0 collective-permute-done.15.cna
  113.4 5.3 %collective-permute-done.14.cnb = bf16[256,1152]{1,0:T(8,128)(2,1)S(1)} collective-permute-done((bf16[256,1152]{1,0:T(8,128)(2,1)S(1)}, bf16[256,1152]{1,0:T(8,128)(2,1)S(1)}, u32[]{:S(2)}, u32[]{:S(2)}) %collective-permute-start.14) | collective-permute-done | bytes 589856 | tf_op jit(solution)/shard_map/ppermute | solution.py:26
  118.7 1.0 copy-done.22
  119.8 10.5 %shard_map.151 = (bf16[128,2048]{1,0:T(8,128)(2,1)S(1)}, bf16[128,2048]{1,0:T(8,128)(2,1)S(1)}, bf16[128,1024]{1,0:T(8,128)(2,1)S(1)}, bf16[128,1024]{1,0:T(8,128)(2,1)S(1)}) custom-call(bf16[128,2048]{1,0:T(8,128)(2,1)S(1)} %copy-done.15, bf16[256,2048]{1,0:T(8,128)(2,1)S(1)} %copy-done.8, bf16[256,2048]{1,0:T(8,128)(2,1)S(1)} %copy-done.6, ...), custom_call_target="tpu_custom_call" | custom-call | flops 17600000000 | tf_op jit(solution)/shard_map/pallas_call | solution.py:90
  130.3 0.1 collective-permute-start.18
  130.4 0.5 collective-permute-start.17
  130.9 0.1 collective-permute-start.12
  131.0 0.9 collective-permute-done.18.got
  131.9 4.3 %shard_map.153 = bf16[128,2048]{1,0:T(8,128)(2,1)} custom-call(bf16[128,1024]{1,0:T(8,128)(2,1)S(1)} %get-tuple-element.81.keep, bf16[128,1024]{1,0:T(8,128)(2,1)S(1)} %collective-permute-done.18.got, f32[128,512]{1,0:T(8,128)S(1)} %get-tuple-element.83.slope_up_own, f32[128,512]{1,0:T(8,128)S(1)} %get-tuple-element.84.active_own, ...), custom_call_target="tpu_custom_call" | custom-call | flops 4950000128 | tf_op jit(solution)/shard_map/pallas_call | solution.py:90
  136.2 0.0 collective-permute-done.12.q_got
  136.2 0.0 collective-permute-done.17.got
  136.2 1.3 shard_map.152
  (44 shorter events, 0.1 us)
Async XLA Ops:
  0.6 10.6 %copy-start.9 = (bf16[1,128,2048]{2,1,0:T(8,128)(2,1)S(1)}, bf16[1,128,2048]{2,1,0:T(8,128)(2,1)}, u32[]{:S(2)}) copy-start(bf16[1,128,2048]{2,1,0:T(8,128)(2,1)} %query.3) | copy-start | bytes 1572868
  0.6 10.6 %copy-start.10 = (bf16[1,128,2048]{2,1,0:T(8,128)(2,1)S(1)}, bf16[1,128,2048]{2,1,0:T(8,128)(2,1)}, u32[]{:S(2)}) copy-start(bf16[1,128,2048]{2,1,0:T(8,128)(2,1)} %key.3) | copy-start | bytes 1572868
  0.7 10.6 %copy-start.11 = (bf16[1,128,2048]{2,1,0:T(8,128)(2,1)S(1)}, bf16[1,128,2048]{2,1,0:T(8,128)(2,1)}, u32[]{:S(2)}) copy-start(bf16[1,128,2048]{2,1,0:T(8,128)(2,1)} %value.3) | copy-start | bytes 1572868
  0.7 10.6 %copy-start.16 = (s32[1,1,3]{2,1,0:T(1,128)S(1)}, s32[1,1,3]{2,1,0:T(1,128)}, u32[]{:S(2)}) copy-start(s32[1,1,3]{2,1,0:T(1,128)} %mask.3) | copy-start | bytes 40
  5.7 15.5 %copy-start.3 = (bf16[1,512,2048]{2,1,0:T(8,128)(2,1)S(1)}, bf16[1,512,2048]{2,1,0:T(8,128)(2,1)}, u32[]{:S(2)}) copy-start(bf16[1,512,2048]{2,1,0:T(8,128)(2,1)} %param.19) | copy-start | bytes 6291460
  5.7 15.5 %copy-start.17 = (bf16[1,128,2048]{2,1,0:T(8,128)(2,1)S(1)}, bf16[1,128,2048]{2,1,0:T(8,128)(2,1)}, u32[]{:S(2)}) copy-start(bf16[1,128,2048]{2,1,0:T(8,128)(2,1)} %cot.3) | copy-start | bytes 1572868
  5.7 49.8 %collective-permute-start.7 = (bf16[2,1024,512]{2,1,0:T(8,128)(2,1)}, bf16[2,1024,512]{2,1,0:T(8,128)(2,1)}, u32[]{:S(2)}, u32[]{:S(2)}) collective-permute-start(bf16[2,1024,512]{2,1,0:T(8,128)(2,1)} %get-tuple-element.58), channel_id=1, source_target_pairs={{0,1},{1,0},{2,3},{3,2},{4,5},{5,4},{6,7},{7,6},{8,9},{9,8},{10,11... | collective-permute-start | bytes 6291464 | tf_op jit(solution)/shard_map/ppermute | solution.py:42
  8.7 2.5 %collective-permute-start = (bf16[128,3200]{1,0:T(8,128)(2,1)}, bf16[128,3200]{1,0:T(8,128)(2,1)S(1)}, u32[]{:S(2)}, u32[]{:S(2)}) collective-permute-start(bf16[128,3200]{1,0:T(8,128)(2,1)} %get-tuple-element.46), channel_id=1, source_target_pairs={{0,2},{2,0},{4,6},{6,4},{8,10},{10,8},{12,14},{14,12},{16,18},{18,... | collective-permute-start | bytes 2457608 | tf_op jit(solution)/shard_map/ppermute | solution.py:30
  12.0 38.4 %copy-start.5 = (bf16[256,2048]{1,0:T(8,128)(2,1)}, bf16[256,2048]{1,0:T(8,128)(2,1)S(1)}, u32[]{:S(2)}) copy-start(bf16[256,2048]{1,0:T(8,128)(2,1)S(1)} %get-tuple-element.48.own) | copy-start | bytes 3145732
  12.1 38.4 %copy-start.12 = (bf16[256,1024]{1,0:T(8,128)(2,1)}, bf16[256,1024]{1,0:T(8,128)(2,1)S(1)}, u32[]{:S(2)}) copy-start(bf16[256,1024]{1,0:T(8,128)(2,1)S(1)} %get-tuple-element.49.own.q2) | copy-start | bytes 1572868
  12.1 38.4 %collective-permute-start.2 = (bf16[256,2048]{1,0:T(8,128)(2,1)S(1)}, bf16[256,2048]{1,0:T(8,128)(2,1)S(1)}, u32[]{:S(2)}, u32[]{:S(2)}) collective-permute-start(bf16[256,2048]{1,0:T(8,128)(2,1)S(1)} %get-tuple-element.48.own), channel_id=1, source_target_pairs={{0,4},{2,6},{4,8},{6,10},{8,12},{10,14},{12,16},{14,18},{16,20},{1... | collective-permute-start | bytes 3145736 | tf_op jit(solution)/shard_map/ppermute | solution.py:26
  15.6 33.9 %collective-permute-start.3 = (bf16[256,1024]{1,0:T(8,128)(2,1)S(1)}, bf16[256,1024]{1,0:T(8,128)(2,1)S(1)}, u32[]{:S(2)}, u32[]{:S(2)}) collective-permute-start(bf16[256,1024]{1,0:T(8,128)(2,1)S(1)} %get-tuple-element.49.own.q2), channel_id=1, source_target_pairs={{0,4},{2,6},{4,0},{6,2},{8,12},{10,14},{12,8},{14,10},{16,20},{18,... | collective-permute-start | bytes 1572872 | tf_op jit(solution)/shard_map/ppermute | solution.py:30
  17.1 33.4 %collective-permute-start.1 = (bf16[128,2048]{1,0:T(8,128)(2,1)S(1)}, bf16[128,2048]{1,0:T(8,128)(2,1)S(1)}, u32[]{:S(2)}, u32[]{:S(2)}) collective-permute-start(bf16[128,2048]{1,0:T(8,128)(2,1)S(1)} %get-tuple-element.47), channel_id=1, source_target_pairs={{0,8},{2,10},{4,12},{6,14},{8,16},{10,18},{12,20},{14,22},{16,24},... | collective-permute-start | bytes 1572872 | tf_op jit(solution)/shard_map/ppermute | solution.py:26
  20.6 56.5 %collective-permute-start.9 = (bf16[256,2048]{1,0:T(8,128)(2,1)}, bf16[256,2048]{1,0:T(8,128)(2,1)}, u32[]{:S(2)}, u32[]{:S(2)}) collective-permute-start(bf16[256,2048]{1,0:T(8,128)(2,1)} %get-tuple-element.59), channel_id=1, source_target_pairs={{0,1},{1,0},{2,3},{3,2},{4,5},{5,4},{6,7},{7,6},{8,9},{9,8},{10,11... | collective-permute-start | bytes 3145736 | tf_op jit(solution)/shard_map/ppermute | solution.py:42
  49.4 5.7 %copy-start.19 = (bf16[256,1024]{1,0:T(8,128)(2,1)}, bf16[256,1024]{1,0:T(8,128)(2,1)S(1)}, u32[]{:S(2)}) copy-start(bf16[256,1024]{1,0:T(8,128)(2,1)S(1)} %collective-permute-done.3.other) | copy-start | bytes 1572868
  50.5 4.6 %copy-start.14 = (bf16[128,2048]{1,0:T(8,128)(2,1)}, bf16[128,2048]{1,0:T(8,128)(2,1)S(1)}, u32[]{:S(2)}) copy-start(bf16[128,2048]{1,0:T(8,128)(2,1)S(1)} %collective-permute-done.1.far) | copy-start | bytes 1572868
  50.5 4.6 %copy-start.7 = (bf16[256,2048]{1,0:T(8,128)(2,1)}, bf16[256,2048]{1,0:T(8,128)(2,1)S(1)}, u32[]{:S(2)}) copy-start(bf16[256,2048]{1,0:T(8,128)(2,1)S(1)} %collective-permute-done.2.near) | copy-start | bytes 3145732
  55.1 8.6 %copy-start.21 = (bf16[128,1024]{1,0:T(8,128)(2,1)}, bf16[128,1024]{1,0:T(8,128)(2,1)S(1)}, u32[]{:S(2)}) copy-start(bf16[128,1024]{1,0:T(8,128)(2,1)S(1)} %get-tuple-element.53) | copy-start | bytes 786436
  55.5 8.3 %copy-start.24 = (s32[1,128,1]{1,2,0:T(1,128)S(1)}, s32[1,128,1]{1,2,0:T(1,128)}, u32[]{:S(2)}) copy-start(s32[1,128,1]{1,2,0:T(1,128)} %param.14) | copy-start | bytes 1540
  55.5 8.3 %copy-start.23 = (f32[1,128,1]{1,2,0:T(1,128)S(1)}, f32[1,128,1]{1,2,0:T(1,128)}, u32[]{:S(2)}) copy-start(f32[1,128,1]{1,2,0:T(1,128)} %param.15) | copy-start | bytes 1540
  55.5 10.1 %copy-start = (bf16[1,2048,512]{2,1,0:T(8,128)(2,1)S(1)}, bf16[1,2048,512]{2,1,0:T(8,128)(2,1)}, u32[]{:S(2)}) copy-start(bf16[1,2048,512]{2,1,0:T(8,128)(2,1)} %param.17) | copy-start | bytes 6291460
  55.5 24.7 %collective-permute-start.8 = (bf16[2,1024,512]{2,1,0:T(8,128)(2,1)}, bf16[2,1024,512]{2,1,0:T(8,128)(2,1)}, u32[]{:S(2)}, u32[]{:S(2)}) collective-permute-start(bf16[2,1024,512]{2,1,0:T(8,128)(2,1)} %shard_map.144.inner), channel_id=1, source_target_pairs={{0,2},{2,0},{4,6},{6,4},{8,10},{10,8},{12,14},{14,12},{16,18},{18,... | collective-permute-start | bytes 6291464 | tf_op jit(solution)/shard_map/ppermute | solution.py:30
  55.6 23.7 %collective-permute-start.6 = (bf16[384,1024]{1,0:T(8,128)(2,1)}, bf16[384,1024]{1,0:T(8,128)(2,1)}, u32[]{:S(2)}, u32[]{:S(2)}) collective-permute-start(bf16[384,1024]{1,0:T(8,128)(2,1)} %get-tuple-element.57), channel_id=1, source_target_pairs={{8,0},{10,2},{12,4},{14,6},{16,8},{18,10},{20,12},{22,14},{24,16},... | collective-permute-start | bytes 2359304 | tf_op jit(solution)/shard_map/ppermute | solution.py:26
  57.0 23.1 %collective-permute-start.5 = (bf16[384,1024]{1,0:T(8,128)(2,1)S(1)}, bf16[384,1024]{1,0:T(8,128)(2,1)}, u32[]{:S(2)}, u32[]{:S(2)}) collective-permute-start(bf16[384,1024]{1,0:T(8,128)(2,1)S(1)} %get-tuple-element.51.rest_0_), channel_id=1, source_target_pairs={{0,8},{2,10},{4,12},{6,14},{8,16},{10,18},{12,20},{14,22},{16,24},... | collective-permute-start | bytes 2359304 | tf_op jit(solution)/shard_map/ppermute | solution.py:26
  63.7 1.9 %collective-permute-start.4 = (bf16[128,1024]{1,0:T(8,128)(2,1)}, bf16[128,1024]{1,0:T(8,128)(2,1)}, u32[]{:S(2)}, u32[]{:S(2)}) collective-permute-start(bf16[128,1024]{1,0:T(8,128)(2,1)} %copy-done.21), channel_id=1, source_target_pairs={{0,2},{2,0},{4,6},{6,4},{8,10},{10,8},{12,14},{14,12},{16,18},{18,... | collective-permute-start | bytes 786440 | tf_op jit(solution)/shard_map/ppermute | solution.py:30
  65.6 1.6 %copy-start.1 = (bf16[1,2048,512]{2,1,0:T(8,128)(2,1)S(1)}, bf16[1,2048,512]{2,1,0:T(8,128)(2,1)}, u32[]{:S(2)}) copy-start(bf16[1,2048,512]{2,1,0:T(8,128)(2,1)} %param.18) | copy-start | bytes 6291460
  77.1 3.0 %collective-permute-start.10 = (bf16[256,2048]{1,0:T(8,128)(2,1)}, bf16[256,2048]{1,0:T(8,128)(2,1)S(1)}, u32[]{:S(2)}, u32[]{:S(2)}) collective-permute-start(bf16[256,2048]{1,0:T(8,128)(2,1)} %shard_map.145.over), channel_id=1, source_target_pairs={{0,2},{2,0},{4,6},{6,4},{8,10},{10,8},{12,14},{14,12},{16,18},{18,... | collective-permute-start | bytes 3145736 | tf_op jit(solution)/shard_map/ppermute | solution.py:30
  80.1 1.0 copy-start.18
  80.1 6.7 %copy-start.20 = (bf16[256,1024]{1,0:T(8,128)(2,1)S(1)}, bf16[256,1024]{1,0:T(8,128)(2,1)}, u32[]{:S(2)}) copy-start(bf16[256,1024]{1,0:T(8,128)(2,1)} %copy-done.19) | copy-start | bytes 1572868
  86.8 1.6 %collective-permute-start.11 = (bf16[128,1152]{1,0:T(8,128)(2,1)S(1)}, bf16[128,1152]{1,0:T(8,128)(2,1)S(1)}, u32[]{:S(2)}, u32[]{:S(2)}) collective-permute-start(bf16[128,1152]{1,0:T(8,128)(2,1)S(1)} %get-tuple-element.62), channel_id=1, source_target_pairs={{0,2},{2,0},{4,6},{6,4},{8,10},{10,8},{12,14},{14,12},{16,18},{18,... | collective-permute-start | bytes 884744 | tf_op jit(solution)/shard_map/ppermute | solution.py:30
  88.3 12.3 %copy-start.6 = (bf16[256,2048]{1,0:T(8,128)(2,1)S(1)}, bf16[256,2048]{1,0:T(8,128)(2,1)}, u32[]{:S(2)}) copy-start(bf16[256,2048]{1,0:T(8,128)(2,1)} %copy-done.5) | copy-start | bytes 3145732
  88.3 12.3 %copy-start.8 = (bf16[256,2048]{1,0:T(8,128)(2,1)S(1)}, bf16[256,2048]{1,0:T(8,128)(2,1)}, u32[]{:S(2)}) copy-start(bf16[256,2048]{1,0:T(8,128)(2,1)} %copy-done.7) | copy-start | bytes 3145732
  88.3 12.3 %copy-start.13 = (bf16[256,1024]{1,0:T(8,128)(2,1)S(1)}, bf16[256,1024]{1,0:T(8,128)(2,1)}, u32[]{:S(2)}) copy-start(bf16[256,1024]{1,0:T(8,128)(2,1)} %copy-done.12) | copy-start | bytes 1572868
  88.3 12.3 %copy-start.15 = (bf16[128,2048]{1,0:T(8,128)(2,1)S(1)}, bf16[128,2048]{1,0:T(8,128)(2,1)}, u32[]{:S(2)}) copy-start(bf16[128,2048]{1,0:T(8,128)(2,1)} %copy-done.14) | copy-start | bytes 1572868
  88.5 24.9 %collective-permute-start.15 = (bf16[256,1152]{1,0:T(8,128)(2,1)S(1)}, bf16[256,1152]{1,0:T(8,128)(2,1)S(1)}, u32[]{:S(2)}, u32[]{:S(2)}) collective-permute-start(bf16[256,1152]{1,0:T(8,128)(2,1)S(1)} %get-tuple-element.64.rest_0_.co), channel_id=1, source_target_pairs={{4,0},{6,2},{8,4},{10,6},{12,8},{14,10},{16,12},{18,14},{20,16},{2... | collective-permute-start | bytes 1769480 | tf_op jit(solution)/shard_map/ppermute | solution.py:26
  89.9 28.8 %collective-permute-start.14 = (bf16[256,1152]{1,0:T(8,128)(2,1)S(1)}, bf16[256,1152]{1,0:T(8,128)(2,1)S(1)}, u32[]{:S(2)}, u32[]{:S(2)}) collective-permute-start(bf16[256,1152]{1,0:T(8,128)(2,1)S(1)} %get-tuple-element.64.rest_0_.co), channel_id=1, source_target_pairs={{0,4},{2,6},{4,8},{6,10},{8,12},{10,14},{12,16},{14,18},{16,20},{1... | collective-permute-start | bytes 1769480 | tf_op jit(solution)/shard_map/ppermute | solution.py:26
  94.5 14.3 %collective-permute-start.13 = (bf16[128,1152]{1,0:T(8,128)(2,1)S(1)}, bf16[128,1152]{1,0:T(8,128)(2,1)S(1)}, u32[]{:S(2)}, u32[]{:S(2)}) collective-permute-start(bf16[128,1152]{1,0:T(8,128)(2,1)S(1)} %get-tuple-element.69), channel_id=1, source_target_pairs={{0,8},{2,10},{4,12},{6,14},{8,16},{10,18},{12,20},{14,22},{16,24},... | collective-permute-start | bytes 884744 | tf_op jit(solution)/shard_map/ppermute | solution.py:26
  99.0 6.9 %copy-start.4 = (bf16[1,512,2048]{2,1,0:T(8,128)(2,1)S(1)}, bf16[1,512,2048]{2,1,0:T(8,128)(2,1)}, u32[]{:S(2)}) copy-start(bf16[1,512,2048]{2,1,0:T(8,128)(2,1)} %param.19) | copy-start | bytes 6291460
  99.0 14.4 %collective-permute-start.16 = (bf16[128,1152]{1,0:T(8,128)(2,1)S(1)}, bf16[128,1152]{1,0:T(8,128)(2,1)S(1)}, u32[]{:S(2)}, u32[]{:S(2)}) collective-permute-start(bf16[128,1152]{1,0:T(8,128)(2,1)S(1)} %get-tuple-element.70), channel_id=1, source_target_pairs={{8,0},{10,2},{12,4},{14,6},{16,8},{18,10},{20,12},{22,14},{24,16},... | collective-permute-start | bytes 884744 | tf_op jit(solution)/shard_map/ppermute | solution.py:26
  118.7 1.0 copy-start.22
  119.8 12.1 %copy-start.2 = (bf16[1,2048,512]{2,1,0:T(8,128)(2,1)S(1)}, bf16[1,2048,512]{2,1,0:T(8,128)(2,1)}, u32[]{:S(2)}) copy-start(bf16[1,2048,512]{2,1,0:T(8,128)(2,1)} %param.18) | copy-start | bytes 6291460
  130.3 1.6 %collective-permute-start.18 = (bf16[128,1024]{1,0:T(8,128)(2,1)S(1)}, bf16[128,1024]{1,0:T(8,128)(2,1)S(1)}, u32[]{:S(2)}, u32[]{:S(2)}) collective-permute-start(bf16[128,1024]{1,0:T(8,128)(2,1)S(1)} %get-tuple-element.82), channel_id=1, source_target_pairs={{0,2},{2,0},{4,6},{6,4},{8,10},{10,8},{12,14},{14,12},{16,18},{18,... | collective-permute-start | bytes 786440 | tf_op jit(solution)/shard_map/ppermute | solution.py:30
  130.4 5.8 %collective-permute-start.17 = (bf16[128,2048]{1,0:T(8,128)(2,1)S(1)}, bf16[128,2048]{1,0:T(8,128)(2,1)S(1)}, u32[]{:S(2)}, u32[]{:S(2)}) collective-permute-start(bf16[128,2048]{1,0:T(8,128)(2,1)S(1)} %get-tuple-element.77), channel_id=1, source_target_pairs={{0,2},{2,0},{4,6},{6,4},{8,10},{10,8},{12,14},{14,12},{16,18},{18,... | collective-permute-start | bytes 1572872 | tf_op jit(solution)/shard_map/ppermute | solution.py:30
  130.9 5.3 %collective-permute-start.12 = (bf16[128,1024]{1,0:T(8,128)(2,1)S(1)}, bf16[128,1024]{1,0:T(8,128)(2,1)S(1)}, u32[]{:S(2)}, u32[]{:S(2)}) collective-permute-start(bf16[128,1024]{1,0:T(8,128)(2,1)S(1)} %get-tuple-element.67), channel_id=1, source_target_pairs={{0,2},{2,0},{4,6},{6,4},{8,10},{10,8},{12,14},{14,12},{16,18},{18,... | collective-permute-start | bytes 786440 | tf_op jit(solution)/shard_map/ppermute | solution.py:30

commit v5 on v4

--- a/solution.py
+++ b/solution.py
@@ -219,24 +219,21 @@
     copy.wait()
 
 
-def cut_kernel(
-    mask, gate, up, down, query, key, value, inner, down_half, sent, parts, down_parts, blocks, seen, sems, seen_sem
-):
-    def moves(matrix, buffers, out):
-        pieces, size = buffers.shape[:2]
-        start = this_core() * pieces * size
-        return [
-            (matrix.at[pl.ds(start + n * size, size)], buffers.at[n], out.at[pl.ds(n * size, size)])
-            for n in range(pieces)
-        ]
-
-    through(
-        split_moves(query, key, value, blocks, sent)
-        + moves(gate, parts.at[0], inner.at[0])
-        + moves(up, parts.at[1], inner.at[1])
-        + moves(down, down_parts, down_half),
-        sems,
-    )
+def half_moves(matrix, buffers, out):
+    pieces, size = buffers.shape[:2]
+    start = this_core() * pieces * size
+    return [
+        (matrix.at[pl.ds(start + n * size, size)], buffers.at[n], out.at[pl.ds(n * size, size)]) for n in range(pieces)
+    ]
+
+
+def inner_kernel(gate, up, inner, parts, sems):
+    through([move for n, x in enumerate((gate, up)) for move in half_moves(x, parts.at[n], inner.at[n])], sems)
+
+
+def cut_kernel(mask, down, query, key, value, after, down_half, sent, down_parts, blocks, seen, sems, seen_sem):
+    moves = split_moves(query, key, value, blocks, sent) + half_moves(down, down_parts, down_half)
+    through(moves, sems)
     send_seen(mask, seen, sent, seen_sem)
 
 
@@ -559,7 +556,8 @@
 
 
 def layer_kernel(keep, got, hidden_own, hidden, picks, down, over, over_s, *rest):
-    out = rest[-1]
+    out, done = rest[-2:]
+    done[...] = jnp.zeros_like(done)
     core = this_core()
     rows_in = in_order(core, keep[...], got[...]).astype(F32)
     summed = nn(hidden_own[...], down[...]) + down_of_other(hidden[...], core, over, over_s)
@@ -596,20 +594,27 @@
         rows, wide = upstream.shape[1:]
         units = w_gate.shape[1]
         pieces = 4
-        inner, down_half, self.mates = call(
+        inner = call(
+            inner_kernel,
+            like(2, wide // 2, units),
+            hbm(w_gate, w_up),
+            [pltpu.VMEM((2, pieces, wide // 2 // pieces, units), BF), pltpu.SemaphoreType.DMA((2, 2 * pieces))],
+            limit=60,
+            spaces=HBM,
+        )
+        down_half, self.mates = call(
             cut_kernel,
-            (like(2, wide // 2, units), like(units // 2, wide), like(rows, 3 * wide // 2 + SIDE)),
-            [(mask, SMEM)] + hbm(w_gate, w_up, w_down, *own_rows),
+            (like(units // 2, wide), like(rows, 3 * wide // 2 + SIDE)),
+            [(mask, SMEM)] + hbm(w_down, *own_rows) + anywhere(inner),
             [
-                pltpu.VMEM((2, pieces, wide // 2 // pieces, units), BF),
                 pltpu.VMEM((pieces, units // 2 // pieces, wide), BF),
                 pltpu.VMEM((3, rows, wide // 2), BF),
                 pltpu.VMEM((SIDE, rows), BF),
-                pltpu.SemaphoreType.DMA((2, 3 * pieces + 3)),
+                pltpu.SemaphoreType.DMA((2, pieces + 3)),
                 pltpu.SemaphoreType.DMA(()),
             ],
             limit=60,
-            spaces=(HBM, HBM, HBM),
+            spaces=(HBM, HBM),
         )
         self.inner, self.over = crossed(inner), crossed(down_half)
         self.whole = (w_gate, w_up, w_down)
@@ -633,7 +638,7 @@
             time=0.1,
         )
         inner_o, over = tied(self.inner, keep), tied(self.over, sum_keep)
-        sum_got = tied(sum_got, *after, time=6)
+        sum_got = tied(sum_got, *after, time=14)
         self.down = (w_down, over, swapped(over))
         self.inner = (inner_o, swapped(inner_o))
         cot_keep, cot_send, hidden, *slopes = call(
@@ -647,7 +652,7 @@
         def layer(*after):
             return call(
                 layer_kernel,
-                like(rows, wide),
+                (like(rows, wide), like(8, SIDE, kind=F32)),
                 vmem(keep, got, hidden_own, hidden, self.picks, *self.down) + anywhere(*after),
                 time=3,
             )
@@ -786,7 +791,7 @@
         cot_keep, cot_send = call(
             kernel, (half, half), vmem(attn_cot, keep, got)
         )
-        return cot_keep, cot_send, lambda *after: layer_out
+        return cot_keep, cot_send, lambda *after: (layer_out, layer_out)
 
     def tangent(self, keep, got):
         rows = in_order(self.core, keep, got)
@@ -850,7 +855,7 @@
     )
     cfb, cnb, cna, cfa = neighbours(co, co_even, co_odd)
 
-    layer_out = layer(co, q_before)
+    layer_out, layer_done = layer(co, q_before)
     sums = like((WIN + 1) * rows, width, kind=F32)
     probs, probs_low, grads_q, q_keep, q_send, key_sums, value_sums = call(
         functools.partial(own_grads_kernel, size),
@@ -870,7 +875,7 @@
         (kv_half, kv_half, half, half),
         vmem(far, near, own, q2, q_before, q_after, cfb, cnb, cna, cfa)
         + vmem(probs, probs_low, grads_q, key_sums, value_sums)
-        + anywhere(layer_out),
+        + anywhere(layer_done),
         [pltpu.VMEM((6, heads, rows), F32)] * 2,
         time=16,
     )

time: 139 us -> 134 us (0.964)
  waiting for transfers between devices: 52.7 us -> 49.5 us
    ppermute x2, waiting for transfers between devices: 7.18 us -> 0.01 us  [crossed(): return lax.ppermute(x, 'exp', [(0, 1), (1, 0)])]
    ppermute x9, waiting for transfers between devices: 32.6 us -> 38.3 us  [swapped(): lax.ppermute(x, 'ctx', [(i, i ^ bit) for i in range(lax.axis_size('ctx'))])]
    ppermute x8, waiting for transfers between devices: 12.9 us -> 11.1 us  [moved(): return lax.ppermute(x, 'ctx', pairs)]
    pallas_call x17 -> x18, Pallas kernels: 46.6 us -> 47.9 us  [call(): pl.pallas_call(kernel, out_shape=outs, in_specs=[space for _, space in ar...]
    unnamed x50 -> x48, local copies, waits for them, and re-layouts: 3.77 us -> 2.52 us
  transfers between devices with their start and end apart: 19 -> 19, of which waited for: 10 -> 8; matrix products, arithmetic and copies ran while one was open for 0% -> 0% of each run, Pallas kernels for 18% -> 21%
where the time goes in v5:
time: 134 us
  waiting for transfers between devices  49.5 us (37%)
  Pallas kernels  47.9 us (36%)
  starting transfers between devices  32.8 us (24%)
  local copies, waits for them, and re-layouts  2.64 us (2%)
    pallas_call x18, Pallas kernels, call(): pl.pallas_call(kernel, out_shape=outs, in_specs=[space for _, space in ar...  47.9 us
    ppermute x9, waiting for transfers between devices, swapped(): lax.ppermute(x, 'ctx', [(i, i ^ bit) for i in range(lax.axis_size('ctx'))])  38.3 us
    ppermute x8, starting transfers between devices, moved(): return lax.ppermute(x, 'ctx', pairs)  26 us
    ppermute x8, waiting for transfers between devices, moved(): return lax.ppermute(x, 'ctx', pairs)  11.1 us
    ppermute x2, starting transfers between devices, crossed(): return lax.ppermute(x, 'exp', [(0, 1), (1, 0)])  3.6 us
    ppermute x9, starting transfers between devices, swapped(): lax.ppermute(x, 'ctx', [(i, i ^ bit) for i in range(lax.axis_size('ctx'))])  3.14 us
  transfers between devices with their start and end apart: 19, of which 8 were waited for; matrix products, arithmetic and copies ran while one was open for 0% of the time, Pallas kernels for 21%

profile of v5, /device:TPU:0, one launch (start us, length us, event | category | flops | bytes accessed | tf_op | source)
XLA Modules:
  0.0 133.9 jit_solution(13466496382042223939)
XLA Ops:
  0.6 2.5 %shard_map.137.after = bf16[2,1024,512]{2,1,0:T(8,128)(2,1)} custom-call(bf16[2048,512]{1,0:T(8,128)(2,1)} %bitcast.12, bf16[2048,512]{1,0:T(8,128)(2,1)} %bitcast.15), custom_call_target="tpu_custom_call" | custom-call | flops 1100000000 | tf_op jit(solution)/shard_map/pallas_call | solution.py:90
  3.1 3.0 %collective-permute-start.7 = (bf16[2,1024,512]{2,1,0:T(8,128)(2,1)}, bf16[2,1024,512]{2,1,0:T(8,128)(2,1)}, u32[]{:S(2)}, u32[]{:S(2)}) collective-permute-start(bf16[2,1024,512]{2,1,0:T(8,128)(2,1)} %shard_map.137.after), channel_id=1, source_target_pairs={{0,1},{1,0},{2,3},{3,2},{4,5},{5,4},{6,7},{7,6},{8,9},{9,8},{10,11... | collective-permute-start | bytes 6291464 | tf_op jit(solution)/shard_map/ppermute | solution.py:42
  6.1 3.8 %shard_map.138 = (bf16[256,2048]{1,0:T(8,128)(2,1)}, bf16[128,3200]{1,0:T(8,128)(2,1)}) custom-call(s32[1,1,3]{2,1,0:T(1,128)} %mask.3, bf16[512,2048]{1,0:T(8,128)(2,1)} %bitcast.18, bf16[1,128,2048]{2,1,0:T(8,128)(2,1)} %query.3, bf16[1,128,2048]{2,1,0:T(8,128)(2,1)} %key.3, bf16[1,128,2048]{2,1,0:T(8,128)(2,1)} %value.3, ...), custom_call_target="tpu_custom_call" | custom-call | flops 1100000000 | tf_op jit(solution)/shard_map/pallas_call | solution.py:90
  9.9 0.1 collective-permute-start
  10.0 2.5 %collective-permute-done.got = bf16[128,3200]{1,0:T(8,128)(2,1)S(1)} collective-permute-done((bf16[128,3200]{1,0:T(8,128)(2,1)}, bf16[128,3200]{1,0:T(8,128)(2,1)S(1)}, u32[]{:S(2)}, u32[]{:S(2)}) %collective-permute-start) | collective-permute-done | bytes 819232 | tf_op jit(solution)/shard_map/ppermute | solution.py:30
  12.5 0.8 shard_map.139
  13.3 0.0 copy-start.12
  13.3 0.0 copy-start.3
  13.4 0.0 copy-start.17
  13.4 3.8 %collective-permute-start.2 = (bf16[256,2048]{1,0:T(8,128)(2,1)S(1)}, bf16[256,2048]{1,0:T(8,128)(2,1)S(1)}, u32[]{:S(2)}, u32[]{:S(2)}) collective-permute-start(bf16[256,2048]{1,0:T(8,128)(2,1)S(1)} %get-tuple-element.49.own), channel_id=1, source_target_pairs={{0,4},{2,6},{4,8},{6,10},{8,12},{10,14},{12,16},{14,18},{16,20},{1... | collective-permute-start | bytes 3145736 | tf_op jit(solution)/shard_map/ppermute | solution.py:26
  17.1 1.5 %collective-permute-start.3 = (bf16[256,1024]{1,0:T(8,128)(2,1)S(1)}, bf16[256,1024]{1,0:T(8,128)(2,1)S(1)}, u32[]{:S(2)}, u32[]{:S(2)}) collective-permute-start(bf16[256,1024]{1,0:T(8,128)(2,1)S(1)} %get-tuple-element.50.own.q2), channel_id=1, source_target_pairs={{0,4},{2,6},{4,0},{6,2},{8,12},{10,14},{12,8},{14,10},{16,20},{18,... | collective-permute-start | bytes 1572872 | tf_op jit(solution)/shard_map/ppermute | solution.py:30
  18.7 3.5 %collective-permute-start.1 = (bf16[128,2048]{1,0:T(8,128)(2,1)S(1)}, bf16[128,2048]{1,0:T(8,128)(2,1)S(1)}, u32[]{:S(2)}, u32[]{:S(2)}) collective-permute-start(bf16[128,2048]{1,0:T(8,128)(2,1)S(1)} %get-tuple-element.48), channel_id=1, source_target_pairs={{0,8},{2,10},{4,12},{6,14},{8,16},{10,18},{12,20},{14,22},{16,24},... | collective-permute-start | bytes 1572872 | tf_op jit(solution)/shard_map/ppermute | solution.py:26
  22.2 0.6 collective-permute-start.9
  22.8 28.2 %collective-permute-done.3.other = bf16[256,1024]{1,0:T(8,128)(2,1)S(1)} collective-permute-done((bf16[256,1024]{1,0:T(8,128)(2,1)S(1)}, bf16[256,1024]{1,0:T(8,128)(2,1)S(1)}, u32[]{:S(2)}, u32[]{:S(2)}) %collective-permute-start.3) | collective-permute-done | bytes 524320 | tf_op jit(solution)/shard_map/ppermute | solution.py:30
  51.0 1.0 shard_map.140
  52.0 1.3 collective-permute-start.6
  53.3 0.0 collective-permute-done.1.far
  53.3 0.0 copy-start.14
  53.4 6.9 %collective-permute-start.5 = (bf16[384,1024]{1,0:T(8,128)(2,1)S(1)}, bf16[384,1024]{1,0:T(8,128)(2,1)}, u32[]{:S(2)}, u32[]{:S(2)}) collective-permute-start(bf16[384,1024]{1,0:T(8,128)(2,1)S(1)} %get-tuple-element.52.rest_0_), channel_id=1, source_target_pairs={{0,8},{2,10},{4,12},{6,14},{8,16},{10,18},{12,20},{14,22},{16,24},... | collective-permute-start | bytes 2359304 | tf_op jit(solution)/shard_map/ppermute | solution.py:26
  60.2 0.8 shard_map.141.rest_1_.back
  61.1 0.0 collective-permute-done.2.near
  61.1 4.6 %shard_map.142 = (bf16[256,128]{1,0:T(8,128)(2,1)S(1)}, bf16[128,1024]{1,0:T(8,128)(2,1)S(1)}, bf16[128,1024]{1,0:T(8,128)(2,1)S(1)}) custom-call(bf16[128,2048]{1,0:T(8,128)(2,1)S(1)} %collective-permute-done.1.far, bf16[256,2048]{1,0:T(8,128)(2,1)S(1)} %collective-permute-done.2.near, bf16[256,2048]{1,0:T(8,128)(2,1)S(1)} %get-tuple-element.49.own, ...), custom_call_target="tpu_custom_call" | custom-call | flops 110000000 | tf_op jit(solution)/shard_map/pallas_call | solution.py:90
  65.7 0.0 copy-start.21
  65.7 0.0 collective-permute-done.7.refs_0_
  65.8 0.7 copy-done.21
  66.4 0.0 collective-permute-start.8
  66.5 0.5 collective-permute-start.4
  67.0 0.1 copy-done.23
  67.1 0.0 copy-done.22
  67.1 0.1 copy.21.picks
  67.2 4.1 %collective-permute-done.4.got = bf16[128,1024]{1,0:T(8,128)(2,1)} collective-permute-done((bf16[128,1024]{1,0:T(8,128)(2,1)}, bf16[128,1024]{1,0:T(8,128)(2,1)}, u32[]{:S(2)}, u32[]{:S(2)}) %collective-permute-start.4) | collective-permute-done | bytes 262176 | tf_op jit(solution)/shard_map/ppermute | solution.py:30
  71.3 1.6 %copy-done.1 = bf16[1,2048,512]{2,1,0:T(8,128)(2,1)S(1)} copy-done((bf16[1,2048,512]{2,1,0:T(8,128)(2,1)S(1)}, bf16[1,2048,512]{2,1,0:T(8,128)(2,1)}, u32[]{:S(2)}) %copy-start.1) | copy-done | bytes 2097176
  72.9 3.1 %shard_map.143 = (f32[128,1024]{1,0:T(8,128)S(1)}, f32[128,1024]{1,0:T(8,128)S(1)}, bf16[128,512]{1,0:T(8,128)(2,1)S(1)}, f32[128,512]{1,0:T(8,128)S(1)}, f32[128,512]{1,0:T(8,128)S(1)}) custom-call(bf16[128,1024]{1,0:T(8,128)(2,1)S(1)} %get-tuple-element.53.keep.refs_1_, bf16[128,1024]{1,0:T(8,128)(2,1)} %collective-permute-done.4.got, ...), custom_call_target="tpu_custom_call" | custom-call | flops 110000000 | tf_op jit(solution)/shard_map/pallas_call | solution.py:90
  76.0 0.0 collective-permute-done.9.refs_0_
  76.0 0.2 collective-permute-start.10
  76.2 0.0 collective-permute-done.6.refs_2_.above
  76.2 0.2 collective-permute-done.5.refs_1_.below
  76.4 2.5 %collective-permute-done.10.over_s = bf16[256,2048]{1,0:T(8,128)(2,1)S(1)} collective-permute-done((bf16[256,2048]{1,0:T(8,128)(2,1)}, bf16[256,2048]{1,0:T(8,128)(2,1)S(1)}, u32[]{:S(2)}, u32[]{:S(2)}) %collective-permute-start.10) | collective-permute-done | bytes 1048608 | tf_op jit(solution)/shard_map/ppermute | solution.py:30
  78.9 0.0 collective-permute-done.8.inner_s
  79.0 5.6 %shard_map.147 = (bf16[128,1152]{1,0:T(8,128)(2,1)S(1)}, bf16[128,1152]{1,0:T(8,128)(2,1)S(1)}, bf16[128,512]{1,0:T(8,128)(2,1)S(1)}, f32[128,512]{1,0:T(8,128)S(1)}, f32[128,512]{1,0:T(8,128)S(1)}) custom-call(bf16[128,1024]{1,0:T(8,128)(2,1)S(1)} %get-tuple-element.53.keep.refs_1_, bf16[128,1024]{1,0:T(8,128)(2,1)} %collective-permute-done.4.got, ...), custom_call_target="tpu_custom_call" | custom-call | flops 4950000128 | tf_op jit(solution)/shard_map/pallas_call | solution.py:90
  84.6 0.2 collective-permute-start.11
  84.7 1.5 %shard_map.149 = (bf16[384,1024]{1,0:T(8,128)(2,1)S(1)}, bf16[384,1024]{1,0:T(8,128)(2,1)S(1)}) custom-call(bf16[256,1024]{1,0:T(8,128)(2,1)S(1)} %copy-done.20, bf16[384,1024]{1,0:T(8,128)(2,1)} %collective-permute-done.5.refs_1_.below, bf16[384,1024]{1,0:T(8,128)(2,1)} %collective-permute-done.6.refs_2_.above), custom_call_target="tpu_custom_call" | custom-call | flops 1100000000 | tf_op jit(solution)/shard_map/pallas_call | solution.py:90
  86.2 0.0 copy-start.13
  86.3 0.0 copy-start.15
  86.3 0.1 shard_map.148
  86.4 1.4 %collective-permute-start.15 = (bf16[256,1152]{1,0:T(8,128)(2,1)S(1)}, bf16[256,1152]{1,0:T(8,128)(2,1)S(1)}, u32[]{:S(2)}, u32[]{:S(2)}) collective-permute-start(bf16[256,1152]{1,0:T(8,128)(2,1)S(1)} %get-tuple-element.64.rest_0_.co), channel_id=1, source_target_pairs={{4,0},{6,2},{8,4},{10,6},{12,8},{14,10},{16,12},{18,14},{20,16},{2... | collective-permute-start | bytes 1769480 | tf_op jit(solution)/shard_map/ppermute | solution.py:26
  87.8 4.6 %collective-permute-start.14 = (bf16[256,1152]{1,0:T(8,128)(2,1)S(1)}, bf16[256,1152]{1,0:T(8,128)(2,1)S(1)}, u32[]{:S(2)}, u32[]{:S(2)}) collective-permute-start(bf16[256,1152]{1,0:T(8,128)(2,1)S(1)} %get-tuple-element.64.rest_0_.co), channel_id=1, source_target_pairs={{0,4},{2,6},{4,8},{6,10},{8,12},{10,14},{12,16},{14,18},{16,20},{1... | collective-permute-start | bytes 1769480 | tf_op jit(solution)/shard_map/ppermute | solution.py:26
  92.4 3.0 %collective-permute-start.13 = (bf16[128,1152]{1,0:T(8,128)(2,1)S(1)}, bf16[128,1152]{1,0:T(8,128)(2,1)S(1)}, u32[]{:S(2)}, u32[]{:S(2)}) collective-permute-start(bf16[128,1152]{1,0:T(8,128)(2,1)S(1)} %get-tuple-element.70), channel_id=1, source_target_pairs={{0,8},{2,10},{4,12},{6,14},{8,16},{10,18},{12,20},{14,22},{16,24},... | collective-permute-start | bytes 884744 | tf_op jit(solution)/shard_map/ppermute | solution.py:26
  95.5 0.0 copy-start.4
  95.5 1.6 %collective-permute-start.16 = (bf16[128,1152]{1,0:T(8,128)(2,1)S(1)}, bf16[128,1152]{1,0:T(8,128)(2,1)S(1)}, u32[]{:S(2)}, u32[]{:S(2)}) collective-permute-start(bf16[128,1152]{1,0:T(8,128)(2,1)S(1)} %get-tuple-element.71), channel_id=1, source_target_pairs={{8,0},{10,2},{12,4},{14,6},{16,8},{18,10},{20,12},{22,14},{24,16},... | collective-permute-start | bytes 884744 | tf_op jit(solution)/shard_map/ppermute | solution.py:26
  97.1 5.1 %shard_map.151 = (bf16[8,2,512,128]{3,2,1,0:T(8,128)(2,1)S(1)}, bf16[8,2,128,512]{3,2,1,0:T(8,128)(2,1)S(1)}, bf16[256,1024]{1,0:T(8,128)(2,1)S(1)}, bf16[128,10...) custom-call(bf16[128,2048]{1,0:T(8,128)(2,1)S(1)} %copy-done.15, ...), custom_call_target="tpu_custom_call" | custom-call | flops 7699999744 | tf_op jit(solution)/shard_map/pallas_call | solution.py:90
  102.3 2.9 %shard_map.150 = (bf16[128,2048]{1,0:T(8,128)(2,1)}, f32[8,128]{1,0:T(8,128)S(1)}) custom-call(bf16[128,1024]{1,0:T(8,128)(2,1)S(1)} %get-tuple-element.53.keep.refs_1_, bf16[128,1024]{1,0:T(8,128)(2,1)} %collective-permute-done.4.got, bf16[128,512]{1,0:T(8,128)(2,1)S(1)} %get-tuple-element.55.hidden_own, bf16[128,512]{1,0:T(8,128)(2,1)S(1)} %get-tuple-element.60.hidden, ...), custom_call_target="tpu_custom_call" | custom-call | flops 3300000000 | tf_op jit(solution)/shard_map/pallas_call | solution.py:90
  105.2 0.0 collective-permute-done.13.cfb
  105.2 5.7 %collective-permute-done.16.cfa = bf16[128,1152]{1,0:T(8,128)(2,1)S(1)} collective-permute-done((bf16[128,1152]{1,0:T(8,128)(2,1)S(1)}, bf16[128,1152]{1,0:T(8,128)(2,1)S(1)}, u32[]{:S(2)}, u32[]{:S(2)}) %collective-permute-start.16) | collective-permute-done | bytes 294944 | tf_op jit(solution)/shard_map/ppermute | solution.py:26
  110.9 0.0 collective-permute-done.15.cna
  110.9 5.3 %collective-permute-done.14.cnb = bf16[256,1152]{1,0:T(8,128)(2,1)S(1)} collective-permute-done((bf16[256,1152]{1,0:T(8,128)(2,1)S(1)}, bf16[256,1152]{1,0:T(8,128)(2,1)S(1)}, u32[]{:S(2)}, u32[]{:S(2)}) %collective-permute-start.14) | collective-permute-done | bytes 589856 | tf_op jit(solution)/shard_map/ppermute | solution.py:26
  116.1 10.5 %shard_map.152 = (bf16[128,2048]{1,0:T(8,128)(2,1)S(1)}, bf16[128,2048]{1,0:T(8,128)(2,1)S(1)}, bf16[128,1024]{1,0:T(8,128)(2,1)S(1)}, bf16[128,1024]{1,0:T(8,128)(2,1)S(1)}) custom-call(bf16[128,2048]{1,0:T(8,128)(2,1)S(1)} %copy-done.15, bf16[256,2048]{1,0:T(8,128)(2,1)S(1)} %copy-done.8, bf16[256,2048]{1,0:T(8,128)(2,1)S(1)} %copy-done.6, ...), custom_call_target="tpu_custom_call" | custom-call | flops 17600000000 | tf_op jit(solution)/shard_map/pallas_call | solution.py:90
  126.7 0.1 collective-permute-start.18
  126.8 0.5 collective-permute-start.17
  127.2 0.1 collective-permute-start.12
  127.3 0.9 collective-permute-done.18.got
  128.3 4.3 %shard_map.154 = bf16[128,2048]{1,0:T(8,128)(2,1)} custom-call(bf16[128,1024]{1,0:T(8,128)(2,1)S(1)} %get-tuple-element.83.keep, bf16[128,1024]{1,0:T(8,128)(2,1)S(1)} %collective-permute-done.18.got, f32[128,512]{1,0:T(8,128)S(1)} %get-tuple-element.85.slope_up_own, f32[128,512]{1,0:T(8,128)S(1)} %get-tuple-element.86.active_own, ...), custom_call_target="tpu_custom_call" | custom-call | flops 4950000128 | tf_op jit(solution)/shard_map/pallas_call | solution.py:90
  132.6 0.0 collective-permute-done.12.q_got
  132.6 1.3 shard_map.153
  (43 shorter events, 0.1 us)
Async XLA Ops:
  3.1 62.6 %collective-permute-start.7 = (bf16[2,1024,512]{2,1,0:T(8,128)(2,1)}, bf16[2,1024,512]{2,1,0:T(8,128)(2,1)}, u32[]{:S(2)}, u32[]{:S(2)}) collective-permute-start(bf16[2,1024,512]{2,1,0:T(8,128)(2,1)} %shard_map.137.after), channel_id=1, source_target_pairs={{0,1},{1,0},{2,3},{3,2},{4,5},{5,4},{6,7},{7,6},{8,9},{9,8},{10,11... | collective-permute-start | bytes 6291464 | tf_op jit(solution)/shard_map/ppermute | solution.py:42
  6.1 6.4 %copy-start.9 = (bf16[1,128,2048]{2,1,0:T(8,128)(2,1)S(1)}, bf16[1,128,2048]{2,1,0:T(8,128)(2,1)}, u32[]{:S(2)}) copy-start(bf16[1,128,2048]{2,1,0:T(8,128)(2,1)} %query.3) | copy-start | bytes 1572868
  6.1 6.4 %copy-start.10 = (bf16[1,128,2048]{2,1,0:T(8,128)(2,1)S(1)}, bf16[1,128,2048]{2,1,0:T(8,128)(2,1)}, u32[]{:S(2)}) copy-start(bf16[1,128,2048]{2,1,0:T(8,128)(2,1)} %key.3) | copy-start | bytes 1572868
  6.1 6.4 %copy-start.11 = (bf16[1,128,2048]{2,1,0:T(8,128)(2,1)S(1)}, bf16[1,128,2048]{2,1,0:T(8,128)(2,1)}, u32[]{:S(2)}) copy-start(bf16[1,128,2048]{2,1,0:T(8,128)(2,1)} %value.3) | copy-start | bytes 1572868
  6.1 6.4 %copy-start.16 = (s32[1,1,3]{2,1,0:T(1,128)S(1)}, s32[1,1,3]{2,1,0:T(1,128)}, u32[]{:S(2)}) copy-start(s32[1,1,3]{2,1,0:T(1,128)} %mask.3) | copy-start | bytes 40
  9.9 2.6 %collective-permute-start = (bf16[128,3200]{1,0:T(8,128)(2,1)}, bf16[128,3200]{1,0:T(8,128)(2,1)S(1)}, u32[]{:S(2)}, u32[]{:S(2)}) collective-permute-start(bf16[128,3200]{1,0:T(8,128)(2,1)} %get-tuple-element.47), channel_id=1, source_target_pairs={{0,2},{2,0},{4,6},{6,4},{8,10},{10,8},{12,14},{14,12},{16,18},{18,... | collective-permute-start | bytes 2457608 | tf_op jit(solution)/shard_map/ppermute | solution.py:30
  13.3 47.8 %copy-start.5 = (bf16[256,2048]{1,0:T(8,128)(2,1)}, bf16[256,2048]{1,0:T(8,128)(2,1)S(1)}, u32[]{:S(2)}) copy-start(bf16[256,2048]{1,0:T(8,128)(2,1)S(1)} %get-tuple-element.49.own) | copy-start | bytes 3145732
  13.3 47.8 %copy-start.12 = (bf16[256,1024]{1,0:T(8,128)(2,1)}, bf16[256,1024]{1,0:T(8,128)(2,1)S(1)}, u32[]{:S(2)}) copy-start(bf16[256,1024]{1,0:T(8,128)(2,1)S(1)} %get-tuple-element.50.own.q2) | copy-start | bytes 1572868
  13.3 46.9 %copy-start.3 = (bf16[1,512,2048]{2,1,0:T(8,128)(2,1)S(1)}, bf16[1,512,2048]{2,1,0:T(8,128)(2,1)}, u32[]{:S(2)}) copy-start(bf16[1,512,2048]{2,1,0:T(8,128)(2,1)} %param.19) | copy-start | bytes 6291460
  13.4 46.9 %copy-start.17 = (bf16[1,128,2048]{2,1,0:T(8,128)(2,1)S(1)}, bf16[1,128,2048]{2,1,0:T(8,128)(2,1)}, u32[]{:S(2)}) copy-start(bf16[1,128,2048]{2,1,0:T(8,128)(2,1)} %cot.3) | copy-start | bytes 1572868
  13.4 47.7 %collective-permute-start.2 = (bf16[256,2048]{1,0:T(8,128)(2,1)S(1)}, bf16[256,2048]{1,0:T(8,128)(2,1)S(1)}, u32[]{:S(2)}, u32[]{:S(2)}) collective-permute-start(bf16[256,2048]{1,0:T(8,128)(2,1)S(1)} %get-tuple-element.49.own), channel_id=1, source_target_pairs={{0,4},{2,6},{4,8},{6,10},{8,12},{10,14},{12,16},{14,18},{16,20},{1... | collective-permute-start | bytes 3145736 | tf_op jit(solution)/shard_map/ppermute | solution.py:26
  17.1 33.9 %collective-permute-start.3 = (bf16[256,1024]{1,0:T(8,128)(2,1)S(1)}, bf16[256,1024]{1,0:T(8,128)(2,1)S(1)}, u32[]{:S(2)}, u32[]{:S(2)}) collective-permute-start(bf16[256,1024]{1,0:T(8,128)(2,1)S(1)} %get-tuple-element.50.own.q2), channel_id=1, source_target_pairs={{0,4},{2,6},{4,0},{6,2},{8,12},{10,14},{12,8},{14,10},{16,20},{18,... | collective-permute-start | bytes 1572872 | tf_op jit(solution)/shard_map/ppermute | solution.py:30
  18.7 34.7 %collective-permute-start.1 = (bf16[128,2048]{1,0:T(8,128)(2,1)S(1)}, bf16[128,2048]{1,0:T(8,128)(2,1)S(1)}, u32[]{:S(2)}, u32[]{:S(2)}) collective-permute-start(bf16[128,2048]{1,0:T(8,128)(2,1)S(1)} %get-tuple-element.48), channel_id=1, source_target_pairs={{0,8},{2,10},{4,12},{6,14},{8,16},{10,18},{12,20},{14,22},{16,24},... | collective-permute-start | bytes 1572872 | tf_op jit(solution)/shard_map/ppermute | solution.py:26
  22.2 53.8 %collective-permute-start.9 = (bf16[256,2048]{1,0:T(8,128)(2,1)}, bf16[256,2048]{1,0:T(8,128)(2,1)}, u32[]{:S(2)}, u32[]{:S(2)}) collective-permute-start(bf16[256,2048]{1,0:T(8,128)(2,1)} %get-tuple-element.59), channel_id=1, source_target_pairs={{0,1},{1,0},{2,3},{3,2},{4,5},{5,4},{6,7},{7,6},{8,9},{9,8},{10,11... | collective-permute-start | bytes 3145736 | tf_op jit(solution)/shard_map/ppermute | solution.py:42
  51.0 10.1 %copy-start.19 = (bf16[256,1024]{1,0:T(8,128)(2,1)}, bf16[256,1024]{1,0:T(8,128)(2,1)S(1)}, u32[]{:S(2)}) copy-start(bf16[256,1024]{1,0:T(8,128)(2,1)S(1)} %collective-permute-done.3.other) | copy-start | bytes 1572868
  52.0 24.2 %collective-permute-start.6 = (bf16[384,1024]{1,0:T(8,128)(2,1)}, bf16[384,1024]{1,0:T(8,128)(2,1)}, u32[]{:S(2)}, u32[]{:S(2)}) collective-permute-start(bf16[384,1024]{1,0:T(8,128)(2,1)} %get-tuple-element.58), channel_id=1, source_target_pairs={{8,0},{10,2},{12,4},{14,6},{16,8},{18,10},{20,12},{22,14},{24,16},... | collective-permute-start | bytes 2359304 | tf_op jit(solution)/shard_map/ppermute | solution.py:26
  53.3 7.8 %copy-start.14 = (bf16[128,2048]{1,0:T(8,128)(2,1)}, bf16[128,2048]{1,0:T(8,128)(2,1)S(1)}, u32[]{:S(2)}) copy-start(bf16[128,2048]{1,0:T(8,128)(2,1)S(1)} %collective-permute-done.1.far) | copy-start | bytes 1572868
  53.4 23.0 %collective-permute-start.5 = (bf16[384,1024]{1,0:T(8,128)(2,1)S(1)}, bf16[384,1024]{1,0:T(8,128)(2,1)}, u32[]{:S(2)}, u32[]{:S(2)}) collective-permute-start(bf16[384,1024]{1,0:T(8,128)(2,1)S(1)} %get-tuple-element.52.rest_0_), channel_id=1, source_target_pairs={{0,8},{2,10},{4,12},{6,14},{8,16},{10,18},{12,20},{14,22},{16,24},... | collective-permute-start | bytes 2359304 | tf_op jit(solution)/shard_map/ppermute | solution.py:26
  61.1 4.6 %copy-start.7 = (bf16[256,2048]{1,0:T(8,128)(2,1)}, bf16[256,2048]{1,0:T(8,128)(2,1)S(1)}, u32[]{:S(2)}) copy-start(bf16[256,2048]{1,0:T(8,128)(2,1)S(1)} %collective-permute-done.2.near) | copy-start | bytes 3145732
  65.7 0.7 copy-start.21
  66.4 0.7 copy-start.23
  66.4 0.7 copy-start.22
  66.4 4.9 %copy-start = (bf16[1,2048,512]{2,1,0:T(8,128)(2,1)S(1)}, bf16[1,2048,512]{2,1,0:T(8,128)(2,1)}, u32[]{:S(2)}) copy-start(bf16[1,2048,512]{2,1,0:T(8,128)(2,1)} %param.17) | copy-start | bytes 6291460
  66.4 12.5 %collective-permute-start.8 = (bf16[2,1024,512]{2,1,0:T(8,128)(2,1)}, bf16[2,1024,512]{2,1,0:T(8,128)(2,1)}, u32[]{:S(2)}, u32[]{:S(2)}) collective-permute-start(bf16[2,1024,512]{2,1,0:T(8,128)(2,1)} %shard_map.145.inner), channel_id=1, source_target_pairs={{0,2},{2,0},{4,6},{6,4},{8,10},{10,8},{12,14},{14,12},{16,18},{18,... | collective-permute-start | bytes 6291464 | tf_op jit(solution)/shard_map/ppermute | solution.py:30
  66.5 4.9 %collective-permute-start.4 = (bf16[128,1024]{1,0:T(8,128)(2,1)}, bf16[128,1024]{1,0:T(8,128)(2,1)}, u32[]{:S(2)}, u32[]{:S(2)}) collective-permute-start(bf16[128,1024]{1,0:T(8,128)(2,1)} %copy-done.21), channel_id=1, source_target_pairs={{0,2},{2,0},{4,6},{6,4},{8,10},{10,8},{12,14},{14,12},{16,18},{18,... | collective-permute-start | bytes 786440 | tf_op jit(solution)/shard_map/ppermute | solution.py:30
  71.3 1.6 %copy-start.1 = (bf16[1,2048,512]{2,1,0:T(8,128)(2,1)S(1)}, bf16[1,2048,512]{2,1,0:T(8,128)(2,1)}, u32[]{:S(2)}) copy-start(bf16[1,2048,512]{2,1,0:T(8,128)(2,1)} %param.18) | copy-start | bytes 6291460
  76.0 2.9 %collective-permute-start.10 = (bf16[256,2048]{1,0:T(8,128)(2,1)}, bf16[256,2048]{1,0:T(8,128)(2,1)S(1)}, u32[]{:S(2)}, u32[]{:S(2)}) collective-permute-start(bf16[256,2048]{1,0:T(8,128)(2,1)} %shard_map.146.over), channel_id=1, source_target_pairs={{0,2},{2,0},{4,6},{6,4},{8,10},{10,8},{12,14},{14,12},{16,18},{18,... | collective-permute-start | bytes 3145736 | tf_op jit(solution)/shard_map/ppermute | solution.py:30
  76.4 2.6 %copy-start.18 = (bf16[1,128,2048]{2,1,0:T(8,128)(2,1)S(1)}, bf16[1,128,2048]{2,1,0:T(8,128)(2,1)}, u32[]{:S(2)}) copy-start(bf16[1,128,2048]{2,1,0:T(8,128)(2,1)} %cot.3) | copy-start | bytes 1572868
  76.4 8.3 %copy-start.20 = (bf16[256,1024]{1,0:T(8,128)(2,1)S(1)}, bf16[256,1024]{1,0:T(8,128)(2,1)}, u32[]{:S(2)}) copy-start(bf16[256,1024]{1,0:T(8,128)(2,1)} %copy-done.19) | copy-start | bytes 1572868
  84.6 1.7 %collective-permute-start.11 = (bf16[128,1152]{1,0:T(8,128)(2,1)S(1)}, bf16[128,1152]{1,0:T(8,128)(2,1)S(1)}, u32[]{:S(2)}, u32[]{:S(2)}) collective-permute-start(bf16[128,1152]{1,0:T(8,128)(2,1)S(1)} %get-tuple-element.62), channel_id=1, source_target_pairs={{0,2},{2,0},{4,6},{6,4},{8,10},{10,8},{12,14},{14,12},{16,18},{18,... | collective-permute-start | bytes 884744 | tf_op jit(solution)/shard_map/ppermute | solution.py:30
  86.2 10.9 %copy-start.6 = (bf16[256,2048]{1,0:T(8,128)(2,1)S(1)}, bf16[256,2048]{1,0:T(8,128)(2,1)}, u32[]{:S(2)}) copy-start(bf16[256,2048]{1,0:T(8,128)(2,1)} %copy-done.5) | copy-start | bytes 3145732
  86.2 10.9 %copy-start.8 = (bf16[256,2048]{1,0:T(8,128)(2,1)S(1)}, bf16[256,2048]{1,0:T(8,128)(2,1)}, u32[]{:S(2)}) copy-start(bf16[256,2048]{1,0:T(8,128)(2,1)} %copy-done.7) | copy-start | bytes 3145732
  86.2 10.9 %copy-start.13 = (bf16[256,1024]{1,0:T(8,128)(2,1)S(1)}, bf16[256,1024]{1,0:T(8,128)(2,1)}, u32[]{:S(2)}) copy-start(bf16[256,1024]{1,0:T(8,128)(2,1)} %copy-done.12) | copy-start | bytes 1572868
  86.3 10.8 %copy-start.15 = (bf16[128,2048]{1,0:T(8,128)(2,1)S(1)}, bf16[128,2048]{1,0:T(8,128)(2,1)}, u32[]{:S(2)}) copy-start(bf16[128,2048]{1,0:T(8,128)(2,1)} %copy-done.14) | copy-start | bytes 1572868
  86.4 24.5 %collective-permute-start.15 = (bf16[256,1152]{1,0:T(8,128)(2,1)S(1)}, bf16[256,1152]{1,0:T(8,128)(2,1)S(1)}, u32[]{:S(2)}, u32[]{:S(2)}) collective-permute-start(bf16[256,1152]{1,0:T(8,128)(2,1)S(1)} %get-tuple-element.64.rest_0_.co), channel_id=1, source_target_pairs={{4,0},{6,2},{8,4},{10,6},{12,8},{14,10},{16,12},{18,14},{20,16},{2... | collective-permute-start | bytes 1769480 | tf_op jit(solution)/shard_map/ppermute | solution.py:26
  87.8 28.3 %collective-permute-start.14 = (bf16[256,1152]{1,0:T(8,128)(2,1)S(1)}, bf16[256,1152]{1,0:T(8,128)(2,1)S(1)}, u32[]{:S(2)}, u32[]{:S(2)}) collective-permute-start(bf16[256,1152]{1,0:T(8,128)(2,1)S(1)} %get-tuple-element.64.rest_0_.co), channel_id=1, source_target_pairs={{0,4},{2,6},{4,8},{6,10},{8,12},{10,14},{12,16},{14,18},{16,20},{1... | collective-permute-start | bytes 1769480 | tf_op jit(solution)/shard_map/ppermute | solution.py:26
  92.4 12.7 %collective-permute-start.13 = (bf16[128,1152]{1,0:T(8,128)(2,1)S(1)}, bf16[128,1152]{1,0:T(8,128)(2,1)S(1)}, u32[]{:S(2)}, u32[]{:S(2)}) collective-permute-start(bf16[128,1152]{1,0:T(8,128)(2,1)S(1)} %get-tuple-element.70), channel_id=1, source_target_pairs={{0,8},{2,10},{4,12},{6,14},{8,16},{10,18},{12,20},{14,22},{16,24},... | collective-permute-start | bytes 884744 | tf_op jit(solution)/shard_map/ppermute | solution.py:26
  95.5 6.8 %copy-start.4 = (bf16[1,512,2048]{2,1,0:T(8,128)(2,1)S(1)}, bf16[1,512,2048]{2,1,0:T(8,128)(2,1)}, u32[]{:S(2)}) copy-start(bf16[1,512,2048]{2,1,0:T(8,128)(2,1)} %param.19) | copy-start | bytes 6291460
  95.5 15.4 %collective-permute-start.16 = (bf16[128,1152]{1,0:T(8,128)(2,1)S(1)}, bf16[128,1152]{1,0:T(8,128)(2,1)S(1)}, u32[]{:S(2)}, u32[]{:S(2)}) collective-permute-start(bf16[128,1152]{1,0:T(8,128)(2,1)S(1)} %get-tuple-element.71), channel_id=1, source_target_pairs={{8,0},{10,2},{12,4},{14,6},{16,8},{18,10},{20,12},{22,14},{24,16},... | collective-permute-start | bytes 884744 | tf_op jit(solution)/shard_map/ppermute | solution.py:26
  116.1 12.1 %copy-start.2 = (bf16[1,2048,512]{2,1,0:T(8,128)(2,1)S(1)}, bf16[1,2048,512]{2,1,0:T(8,128)(2,1)}, u32[]{:S(2)}) copy-start(bf16[1,2048,512]{2,1,0:T(8,128)(2,1)} %param.18) | copy-start | bytes 6291460
  126.7 1.6 %collective-permute-start.18 = (bf16[128,1024]{1,0:T(8,128)(2,1)S(1)}, bf16[128,1024]{1,0:T(8,128)(2,1)S(1)}, u32[]{:S(2)}, u32[]{:S(2)}) collective-permute-start(bf16[128,1024]{1,0:T(8,128)(2,1)S(1)} %get-tuple-element.84), channel_id=1, source_target_pairs={{0,2},{2,0},{4,6},{6,4},{8,10},{10,8},{12,14},{14,12},{16,18},{18,... | collective-permute-start | bytes 786440 | tf_op jit(solution)/shard_map/ppermute | solution.py:30
  126.8 5.8 %collective-permute-start.17 = (bf16[128,2048]{1,0:T(8,128)(2,1)S(1)}, bf16[128,2048]{1,0:T(8,128)(2,1)S(1)}, u32[]{:S(2)}, u32[]{:S(2)}) collective-permute-start(bf16[128,2048]{1,0:T(8,128)(2,1)S(1)} %get-tuple-element.79), channel_id=1, source_target_pairs={{0,2},{2,0},{4,6},{6,4},{8,10},{10,8},{12,14},{14,12},{16,18},{18,... | collective-permute-start | bytes 1572872 | tf_op jit(solution)/shard_map/ppermute | solution.py:30
  127.2 5.4 %collective-permute-start.12 = (bf16[128,1024]{1,0:T(8,128)(2,1)S(1)}, bf16[128,1024]{1,0:T(8,128)(2,1)S(1)}, u32[]{:S(2)}, u32[]{:S(2)}) collective-permute-start(bf16[128,1024]{1,0:T(8,128)(2,1)S(1)} %get-tuple-element.68), channel_id=1, source_target_pairs={{0,2},{2,0},{4,6},{6,4},{8,10},{10,8},{12,14},{14,12},{16,18},{18,... | collective-permute-start | bytes 786440 | tf_op jit(solution)/shard_map/ppermute | solution.py:30

commit v6 on v5

--- a/solution.py
+++ b/solution.py
@@ -564,24 +564,25 @@
     out[...] = (rows_in + summed.astype(BF).astype(F32) * picks[:, 2:3]).astype(BF)
 
 
+def load_kernel(*refs):
+    count = (len(refs) - 3) // 2
+    sources, outs, done, sems = refs[:count], refs[count + 1 : 2 * count + 1], refs[-2], refs[-1]
+    copies = fetch([pltpu.make_async_copy(a, b, sems.at[n]) for n, (a, b) in enumerate(zip(sources, outs))])
+    done[...] = jnp.zeros_like(done)
+    ready(copies)
+
+
 def tangent_kernel(
     keep, got, slope_up_own, active_own, slope_up, active, picks, gate, up, inner, inner_s, down, over, over_s, out,
-    inners, overs, sems,
 ):
     core = this_core()
-    gate_o, gate_s, up_o, up_s, over, over_s = stream(
-        [(ref.at[n], inners.at[m, n]) for n in range(2) for m, ref in enumerate((inner, inner_s))]
-        + [(over, overs.at[0]), (over_s, overs.at[1])],
-        sems,
-    )
     rows_keep, rows_got = keep[...], got[...]
     rows_in = in_order(core, rows_keep, rows_got)
     hidden = slope_up_own[...] * nn(rows_in, gate[...]) + active_own[...] * nn(rows_in, up[...])
     summed = nn(hidden.astype(BF), down[...])
-    gate_tan = nn(rows_keep, gate_o()) + nn(rows_got, gate_s())
-    up_tan = nn(rows_keep, up_o()) + nn(rows_got, up_s())
+    gate_tan, up_tan = (nn(rows_keep, inner[n]) + nn(rows_got, inner_s[n]) for n in range(2))
     hidden = slope_up[...] * gate_tan + active[...] * up_tan
-    summed = summed + down_of_other(hidden.astype(BF), core, over(), over_s())
+    summed = summed + down_of_other(hidden.astype(BF), core, over, over_s)
     out[...] = (rows_in.astype(F32) + summed.astype(BF).astype(F32) * picks[:, 2:3]).astype(BF)
 
 
@@ -659,21 +660,24 @@
 
         return cot_keep, cot_send, layer
 
+    def prefetch(self, after):
+        arrays = (*self.inner, *self.down[1:])
+        *loaded, done = call(
+            load_kernel,
+            (*(like(*x.shape) for x in arrays), like(8, SIDE, kind=F32)),
+            hbm(*arrays) + anywhere(after),
+            [pltpu.SemaphoreType.DMA((len(arrays),))],
+            time=2,
+        )
+        self.inner, self.down = tuple(loaded[:2]), (self.down[0], *loaded[2:])
+        return done
+
     def tangent(self, keep, got):
         return call(
             tangent_kernel,
             like(self.rows, self.wide),
-            vmem(keep, got, *self.slopes, self.picks, *self.whole[:2])
-            + anywhere(*self.inner)
-            + vmem(self.down[0])
-            + anywhere(*self.down[1:]),
-            [
-                pltpu.VMEM((2, 2, self.wide // 2, self.units), BF),
-                pltpu.VMEM((2, self.units // 2, self.wide), BF),
-                pltpu.SemaphoreType.DMA((6,)),
-            ],
+            vmem(keep, got, *self.slopes, self.picks, *self.whole[:2], *self.inner, *self.down),
             time=4.5,
-            limit=16,
         )
 
 
@@ -793,6 +797,9 @@
         )
         return cot_keep, cot_send, lambda *after: (layer_out, layer_out)
 
+    def prefetch(self, after):
+        return after
+
     def tangent(self, keep, got):
         rows = in_order(self.core, keep, got)
         got_rows = self.sent(rows).reshape(-1, rows.shape[1])
@@ -856,6 +863,7 @@
     cfb, cnb, cna, cfa = neighbours(co, co_even, co_odd)
 
     layer_out, layer_done = layer(co, q_before)
+    layer_done = experts.prefetch(layer_done)
     sums = like((WIN + 1) * rows, width, kind=F32)
     probs, probs_low, grads_q, q_keep, q_send, key_sums, value_sums = call(
         functools.partial(own_grads_kernel, size),

time: 134 us -> 133 us (level)
  waiting for transfers between devices: 49.5 us -> 46.9 us
    ppermute x8, waiting for transfers between devices: 11.1 us -> 8.54 us  [moved(): return lax.ppermute(x, 'ctx', pairs)]
    pallas_call x18 -> x19, Pallas kernels: 47.9 us -> 49 us  [call(): pl.pallas_call(kernel, out_shape=outs, in_specs=[space for _, space in ar...]
  transfers between devices with their start and end apart: 19 -> 19, of which waited for: 8 -> 8; matrix products, arithmetic and copies ran while one was open for 0% -> 0% of each run, Pallas kernels for 21% -> 22%
where the time goes in v6:
time: 133 us; the launch traced here: 132 us
  Pallas kernels  49 us (37%)
  waiting for transfers between devices  46.9 us (35%)
  starting transfers between devices  32.8 us (25%)
  local copies, waits for them, and re-layouts  2.64 us (2%)
    pallas_call x19, Pallas kernels, call(): pl.pallas_call(kernel, out_shape=outs, in_specs=[space for _, space in ar...  49 us
    ppermute x9, waiting for transfers between devices, swapped(): lax.ppermute(x, 'ctx', [(i, i ^ bit) for i in range(lax.axis_size('ctx'))])  38.3 us
    ppermute x8, starting transfers between devices, moved(): return lax.ppermute(x, 'ctx', pairs)  26.1 us
    ppermute x8, waiting for transfers between devices, moved(): return lax.ppermute(x, 'ctx', pairs)  8.54 us
    ppermute x2, starting transfers between devices, crossed(): return lax.ppermute(x, 'exp', [(0, 1), (1, 0)])  3.6 us
    ppermute x9, starting transfers between devices, swapped(): lax.ppermute(x, 'ctx', [(i, i ^ bit) for i in range(lax.axis_size('ctx'))])  3.12 us
  transfers between devices with their start and end apart: 19, of which 8 were waited for; matrix products, arithmetic and copies ran while one was open for 0% of the time, Pallas kernels for 22%

profile of v6, /device:TPU:0, one launch (start us, length us, event | category | flops | bytes accessed | tf_op | source)
XLA Modules:
  0.0 132.4 jit_solution(13478406852235523273)
XLA Ops:
  0.6 2.5 %shard_map.137.after = bf16[2,1024,512]{2,1,0:T(8,128)(2,1)} custom-call(bf16[2048,512]{1,0:T(8,128)(2,1)} %bitcast.12, bf16[2048,512]{1,0:T(8,128)(2,1)} %bitcast.15), custom_call_target="tpu_custom_call" | custom-call | flops 1100000000 | tf_op jit(solution)/shard_map/pallas_call | solution.py:90
  3.1 3.0 %collective-permute-start.7 = (bf16[2,1024,512]{2,1,0:T(8,128)(2,1)}, bf16[2,1024,512]{2,1,0:T(8,128)(2,1)}, u32[]{:S(2)}, u32[]{:S(2)}) collective-permute-start(bf16[2,1024,512]{2,1,0:T(8,128)(2,1)} %shard_map.137.after), channel_id=1, source_target_pairs={{0,1},{1,0},{2,3},{3,2},{4,5},{5,4},{6,7},{7,6},{8,9},{9,8},{10,11... | collective-permute-start | bytes 6291464 | tf_op jit(solution)/shard_map/ppermute | solution.py:42
  6.1 3.8 %shard_map.138 = (bf16[256,2048]{1,0:T(8,128)(2,1)}, bf16[128,3200]{1,0:T(8,128)(2,1)}) custom-call(s32[1,1,3]{2,1,0:T(1,128)} %mask.3, bf16[512,2048]{1,0:T(8,128)(2,1)} %bitcast.18, bf16[1,128,2048]{2,1,0:T(8,128)(2,1)} %query.3, bf16[1,128,2048]{2,1,0:T(8,128)(2,1)} %key.3, bf16[1,128,2048]{2,1,0:T(8,128)(2,1)} %value.3, ...), custom_call_target="tpu_custom_call" | custom-call | flops 1100000000 | tf_op jit(solution)/shard_map/pallas_call | solution.py:90
  9.9 0.1 collective-permute-start
  10.0 2.5 %collective-permute-done.got = bf16[128,3200]{1,0:T(8,128)(2,1)S(1)} collective-permute-done((bf16[128,3200]{1,0:T(8,128)(2,1)}, bf16[128,3200]{1,0:T(8,128)(2,1)S(1)}, u32[]{:S(2)}, u32[]{:S(2)}) %collective-permute-start) | collective-permute-done | bytes 819232 | tf_op jit(solution)/shard_map/ppermute | solution.py:30
  12.5 0.8 shard_map.139
  13.3 0.0 copy-start.12
  13.3 0.0 copy-start.3
  13.3 0.0 copy-start.17
  13.4 3.8 %collective-permute-start.2 = (bf16[256,2048]{1,0:T(8,128)(2,1)S(1)}, bf16[256,2048]{1,0:T(8,128)(2,1)S(1)}, u32[]{:S(2)}, u32[]{:S(2)}) collective-permute-start(bf16[256,2048]{1,0:T(8,128)(2,1)S(1)} %get-tuple-element.54.own), channel_id=1, source_target_pairs={{0,4},{2,6},{4,8},{6,10},{8,12},{10,14},{12,16},{14,18},{16,20},{1... | collective-permute-start | bytes 3145736 | tf_op jit(solution)/shard_map/ppermute | solution.py:26
  17.1 1.5 %collective-permute-start.3 = (bf16[256,1024]{1,0:T(8,128)(2,1)S(1)}, bf16[256,1024]{1,0:T(8,128)(2,1)S(1)}, u32[]{:S(2)}, u32[]{:S(2)}) collective-permute-start(bf16[256,1024]{1,0:T(8,128)(2,1)S(1)} %get-tuple-element.55.own.q2), channel_id=1, source_target_pairs={{0,4},{2,6},{4,0},{6,2},{8,12},{10,14},{12,8},{14,10},{16,20},{18,... | collective-permute-start | bytes 1572872 | tf_op jit(solution)/shard_map/ppermute | solution.py:30
  18.6 3.5 %collective-permute-start.1 = (bf16[128,2048]{1,0:T(8,128)(2,1)S(1)}, bf16[128,2048]{1,0:T(8,128)(2,1)S(1)}, u32[]{:S(2)}, u32[]{:S(2)}) collective-permute-start(bf16[128,2048]{1,0:T(8,128)(2,1)S(1)} %get-tuple-element.53), channel_id=1, source_target_pairs={{0,8},{2,10},{4,12},{6,14},{8,16},{10,18},{12,20},{14,22},{16,24},... | collective-permute-start | bytes 1572872 | tf_op jit(solution)/shard_map/ppermute | solution.py:26
  22.1 0.6 collective-permute-start.9
  22.7 28.2 %collective-permute-done.3.other = bf16[256,1024]{1,0:T(8,128)(2,1)S(1)} collective-permute-done((bf16[256,1024]{1,0:T(8,128)(2,1)S(1)}, bf16[256,1024]{1,0:T(8,128)(2,1)S(1)}, u32[]{:S(2)}, u32[]{:S(2)}) %collective-permute-start.3) | collective-permute-done | bytes 524320 | tf_op jit(solution)/shard_map/ppermute | solution.py:30
  51.0 1.1 shard_map.140
  52.0 1.3 collective-permute-start.6
  53.3 0.0 collective-permute-done.1.far
  53.3 0.0 copy-start.14
  53.3 6.9 %collective-permute-start.5 = (bf16[384,1024]{1,0:T(8,128)(2,1)S(1)}, bf16[384,1024]{1,0:T(8,128)(2,1)}, u32[]{:S(2)}, u32[]{:S(2)}) collective-permute-start(bf16[384,1024]{1,0:T(8,128)(2,1)S(1)} %get-tuple-element.57.rest_0_), channel_id=1, source_target_pairs={{0,8},{2,10},{4,12},{6,14},{8,16},{10,18},{12,20},{14,22},{16,24},... | collective-permute-start | bytes 2359304 | tf_op jit(solution)/shard_map/ppermute | solution.py:26
  60.2 0.8 shard_map.141.rest_1_.back
  61.1 0.0 collective-permute-done.2.near
  61.1 4.6 %shard_map.142 = (bf16[256,128]{1,0:T(8,128)(2,1)S(1)}, bf16[128,1024]{1,0:T(8,128)(2,1)S(1)}, bf16[128,1024]{1,0:T(8,128)(2,1)S(1)}) custom-call(bf16[128,2048]{1,0:T(8,128)(2,1)S(1)} %collective-permute-done.1.far, bf16[256,2048]{1,0:T(8,128)(2,1)S(1)} %collective-permute-done.2.near, bf16[256,2048]{1,0:T(8,128)(2,1)S(1)} %get-tuple-element.54.own, ...), custom_call_target="tpu_custom_call" | custom-call | flops 110000000 | tf_op jit(solution)/shard_map/pallas_call | solution.py:90
  65.7 0.0 copy-start.21
  65.7 0.0 collective-permute-done.7.refs_0_
  65.7 0.7 copy-done.21
  66.4 0.0 collective-permute-start.8
  66.5 0.5 collective-permute-start.4
  66.9 0.1 copy-done.23
  67.1 0.0 copy-done.22
  67.1 0.1 copy.21.picks
  67.2 4.1 %collective-permute-done.4.got = bf16[128,1024]{1,0:T(8,128)(2,1)} collective-permute-done((bf16[128,1024]{1,0:T(8,128)(2,1)}, bf16[128,1024]{1,0:T(8,128)(2,1)}, u32[]{:S(2)}, u32[]{:S(2)}) %collective-permute-start.4) | collective-permute-done | bytes 262176 | tf_op jit(solution)/shard_map/ppermute | solution.py:30
  71.3 1.6 %copy-done.1 = bf16[1,2048,512]{2,1,0:T(8,128)(2,1)S(1)} copy-done((bf16[1,2048,512]{2,1,0:T(8,128)(2,1)S(1)}, bf16[1,2048,512]{2,1,0:T(8,128)(2,1)}, u32[]{:S(2)}) %copy-start.1) | copy-done | bytes 2097176
  72.9 3.1 %shard_map.143 = (f32[128,1024]{1,0:T(8,128)S(1)}, f32[128,1024]{1,0:T(8,128)S(1)}, bf16[128,512]{1,0:T(8,128)(2,1)S(1)}, f32[128,512]{1,0:T(8,128)S(1)}, f32[128,512]{1,0:T(8,128)S(1)}) custom-call(bf16[128,1024]{1,0:T(8,128)(2,1)S(1)} %get-tuple-element.58.keep.refs_1_, bf16[128,1024]{1,0:T(8,128)(2,1)} %collective-permute-done.4.got, ...), custom_call_target="tpu_custom_call" | custom-call | flops 110000000 | tf_op jit(solution)/shard_map/pallas_call | solution.py:90
  76.0 0.0 collective-permute-done.9.refs_0_
  76.0 0.2 collective-permute-start.10
  76.2 0.2 collective-permute-done.5.refs_1_.below
  76.4 2.5 %collective-permute-done.10.over_s.refs_3_ = bf16[256,2048]{1,0:T(8,128)(2,1)S(1)} collective-permute-done((bf16[256,2048]{1,0:T(8,128)(2,1)}, bf16[256,2048]{1,0:T(8,128)(2,1)S(1)}, u32[]{:S(2)}, u32[]{:S(2)}) %collective-permute-start.10) | collective-permute-done | bytes 1048608 | tf_op jit(solution)/shard_map/ppermute | solution.py:30
  78.9 0.0 collective-permute-done.8.inner_s.refs_1_
  78.9 5.6 %shard_map.147 = (bf16[128,1152]{1,0:T(8,128)(2,1)S(1)}, bf16[128,1152]{1,0:T(8,128)(2,1)S(1)}, bf16[128,512]{1,0:T(8,128)(2,1)S(1)}, f32[128,512]{1,0:T(8,128)S(1)}, f32[128,512]{1,0:T(8,128)S(1)}) custom-call(bf16[128,1024]{1,0:T(8,128)(2,1)S(1)} %get-tuple-element.58.keep.refs_1_, bf16[128,1024]{1,0:T(8,128)(2,1)} %collective-permute-done.4.got, ...), custom_call_target="tpu_custom_call" | custom-call | flops 4950000128 | tf_op jit(solution)/shard_map/pallas_call | solution.py:90
  84.5 0.2 collective-permute-start.11
  84.7 1.5 %shard_map.149 = (bf16[384,1024]{1,0:T(8,128)(2,1)S(1)}, bf16[384,1024]{1,0:T(8,128)(2,1)S(1)}) custom-call(bf16[256,1024]{1,0:T(8,128)(2,1)S(1)} %copy-done.20, bf16[384,1024]{1,0:T(8,128)(2,1)} %collective-permute-done.5.refs_1_.below, bf16[384,1024]{1,0:T(8,128)(2,1)} %collective-permute-done.6.refs_2_.above), custom_call_target="tpu_custom_call" | custom-call | flops 1100000000 | tf_op jit(solution)/shard_map/pallas_call | solution.py:90
  86.2 0.0 copy-start.13
  86.2 0.0 copy-start.15
  86.2 0.0 collective-permute-done.11.got
  86.2 0.1 shard_map.148
  86.4 1.4 %collective-permute-start.15 = (bf16[256,1152]{1,0:T(8,128)(2,1)S(1)}, bf16[256,1152]{1,0:T(8,128)(2,1)S(1)}, u32[]{:S(2)}, u32[]{:S(2)}) collective-permute-start(bf16[256,1152]{1,0:T(8,128)(2,1)S(1)} %get-tuple-element.69.rest_0_.co), channel_id=1, source_target_pairs={{4,0},{6,2},{8,4},{10,6},{12,8},{14,10},{16,12},{18,14},{20,16},{2... | collective-permute-start | bytes 1769480 | tf_op jit(solution)/shard_map/ppermute | solution.py:26
  87.8 4.6 %collective-permute-start.14 = (bf16[256,1152]{1,0:T(8,128)(2,1)S(1)}, bf16[256,1152]{1,0:T(8,128)(2,1)S(1)}, u32[]{:S(2)}, u32[]{:S(2)}) collective-permute-start(bf16[256,1152]{1,0:T(8,128)(2,1)S(1)} %get-tuple-element.69.rest_0_.co), channel_id=1, source_target_pairs={{0,4},{2,6},{4,8},{6,10},{8,12},{10,14},{12,16},{14,18},{16,20},{1... | collective-permute-start | bytes 1769480 | tf_op jit(solution)/shard_map/ppermute | solution.py:26
  92.4 3.0 %collective-permute-start.13 = (bf16[128,1152]{1,0:T(8,128)(2,1)S(1)}, bf16[128,1152]{1,0:T(8,128)(2,1)S(1)}, u32[]{:S(2)}, u32[]{:S(2)}) collective-permute-start(bf16[128,1152]{1,0:T(8,128)(2,1)S(1)} %get-tuple-element.75), channel_id=1, source_target_pairs={{0,8},{2,10},{4,12},{6,14},{8,16},{10,18},{12,20},{14,22},{16,24},... | collective-permute-start | bytes 884744 | tf_op jit(solution)/shard_map/ppermute | solution.py:26
  95.4 0.0 copy-start.4
  95.5 1.6 %collective-permute-start.16 = (bf16[128,1152]{1,0:T(8,128)(2,1)S(1)}, bf16[128,1152]{1,0:T(8,128)(2,1)S(1)}, u32[]{:S(2)}, u32[]{:S(2)}) collective-permute-start(bf16[128,1152]{1,0:T(8,128)(2,1)S(1)} %get-tuple-element.76), channel_id=1, source_target_pairs={{8,0},{10,2},{12,4},{14,6},{16,8},{18,10},{20,12},{22,14},{24,16},... | collective-permute-start | bytes 884744 | tf_op jit(solution)/shard_map/ppermute | solution.py:26
  97.1 5.2 %shard_map.151 = (bf16[8,2,512,128]{3,2,1,0:T(8,128)(2,1)S(1)}, bf16[8,2,128,512]{3,2,1,0:T(8,128)(2,1)S(1)}, bf16[256,1024]{1,0:T(8,128)(2,1)S(1)}, bf16[128,10...) custom-call(bf16[128,2048]{1,0:T(8,128)(2,1)S(1)} %copy-done.15, ...), custom_call_target="tpu_custom_call" | custom-call | flops 7699999744 | tf_op jit(solution)/shard_map/pallas_call | solution.py:90
  102.3 2.9 %shard_map.150 = (bf16[128,2048]{1,0:T(8,128)(2,1)}, f32[8,128]{1,0:T(8,128)S(1)}) custom-call(bf16[128,1024]{1,0:T(8,128)(2,1)S(1)} %get-tuple-element.58.keep.refs_1_, bf16[128,1024]{1,0:T(8,128)(2,1)} %collective-permute-done.4.got, bf16[128,512]{1,0:T(8,128)(2,1)S(1)} %get-tuple-element.60.hidden_own, bf16[128,512]{1,0:T(8,128)(2,1)S(1)} %get-tuple-element.65.hidden, ...), custom_call_target="tpu_custom_call" | custom-call | flops 3300000000 | tf_op jit(solution)/shard_map/pallas_call | solution.py:90
  105.2 2.5 %shard_map.152 = (bf16[2,1024,512]{2,1,0:T(8,128)(2,1)S(1)}, bf16[2,1024,512]{2,1,0:T(8,128)(2,1)S(1)}, bf16[256,2048]{1,0:T(8,128)(2,1)S(1)}, bf16[256,2048]{1,0:T(8,128)(2,1)S(1)}, f32[8,128]{1,0:T(8,128)S(1)}) custom-call(bf16[2,1024,512]{2,1,0:T(8,128)(2,1)} %shard_map.145.inner.refs_0_, bf16[2,1024,512]{2,1,0:T(8,128)(2,1)} %collective-permute-done.8.inner_s.refs_1_, ...), custom_call_target="tpu_custom_call" | custom-call | flops 2200000000 | tf_op jit(solution)/shard_map/pallas_call | solution.py:90
  107.8 0.0 collective-permute-done.13.cfb
  107.8 3.1 %collective-permute-done.16.cfa = bf16[128,1152]{1,0:T(8,128)(2,1)S(1)} collective-permute-done((bf16[128,1152]{1,0:T(8,128)(2,1)S(1)}, bf16[128,1152]{1,0:T(8,128)(2,1)S(1)}, u32[]{:S(2)}, u32[]{:S(2)}) %collective-permute-start.16) | collective-permute-done | bytes 294944 | tf_op jit(solution)/shard_map/ppermute | solution.py:26
  110.8 0.0 collective-permute-done.15.cna
  110.9 5.3 %collective-permute-done.14.cnb = bf16[256,1152]{1,0:T(8,128)(2,1)S(1)} collective-permute-done((bf16[256,1152]{1,0:T(8,128)(2,1)S(1)}, bf16[256,1152]{1,0:T(8,128)(2,1)S(1)}, u32[]{:S(2)}, u32[]{:S(2)}) %collective-permute-start.14) | collective-permute-done | bytes 589856 | tf_op jit(solution)/shard_map/ppermute | solution.py:26
  116.1 10.5 %shard_map.153 = (bf16[128,2048]{1,0:T(8,128)(2,1)S(1)}, bf16[128,2048]{1,0:T(8,128)(2,1)S(1)}, bf16[128,1024]{1,0:T(8,128)(2,1)S(1)}, bf16[128,1024]{1,0:T(8,128)(2,1)S(1)}) custom-call(bf16[128,2048]{1,0:T(8,128)(2,1)S(1)} %copy-done.15, bf16[256,2048]{1,0:T(8,128)(2,1)S(1)} %copy-done.8, bf16[256,2048]{1,0:T(8,128)(2,1)S(1)} %copy-done.6, ...), custom_call_target="tpu_custom_call" | custom-call | flops 17600000000 | tf_op jit(solution)/shard_map/pallas_call | solution.py:90
  126.7 0.1 collective-permute-start.18
  126.8 0.5 collective-permute-start.17
  127.2 0.1 collective-permute-start.12
  127.3 0.9 collective-permute-done.18.got
  128.3 2.8 %shard_map.155 = bf16[128,2048]{1,0:T(8,128)(2,1)} custom-call(bf16[128,1024]{1,0:T(8,128)(2,1)S(1)} %get-tuple-element.89.keep, bf16[128,1024]{1,0:T(8,128)(2,1)S(1)} %collective-permute-done.18.got, f32[128,512]{1,0:T(8,128)S(1)} %get-tuple-element.91.slope_up_own, f32[128,512]{1,0:T(8,128)S(1)} %get-tuple-element.92.active_own, ...), custom_call_target="tpu_custom_call" | custom-call | flops 4950000128 | tf_op jit(solution)/shard_map/pallas_call | solution.py:90
  131.1 1.3 shard_map.154
  (44 shorter events, 0.1 us)
Async XLA Ops:
  3.1 62.6 %collective-permute-start.7 = (bf16[2,1024,512]{2,1,0:T(8,128)(2,1)}, bf16[2,1024,512]{2,1,0:T(8,128)(2,1)}, u32[]{:S(2)}, u32[]{:S(2)}) collective-permute-start(bf16[2,1024,512]{2,1,0:T(8,128)(2,1)} %shard_map.137.after), channel_id=1, source_target_pairs={{0,1},{1,0},{2,3},{3,2},{4,5},{5,4},{6,7},{7,6},{8,9},{9,8},{10,11... | collective-permute-start | bytes 6291464 | tf_op jit(solution)/shard_map/ppermute | solution.py:42
  6.1 6.4 %copy-start.9 = (bf16[1,128,2048]{2,1,0:T(8,128)(2,1)S(1)}, bf16[1,128,2048]{2,1,0:T(8,128)(2,1)}, u32[]{:S(2)}) copy-start(bf16[1,128,2048]{2,1,0:T(8,128)(2,1)} %query.3) | copy-start | bytes 1572868
  6.1 6.4 %copy-start.10 = (bf16[1,128,2048]{2,1,0:T(8,128)(2,1)S(1)}, bf16[1,128,2048]{2,1,0:T(8,128)(2,1)}, u32[]{:S(2)}) copy-start(bf16[1,128,2048]{2,1,0:T(8,128)(2,1)} %key.3) | copy-start | bytes 1572868
  6.1 6.4 %copy-start.11 = (bf16[1,128,2048]{2,1,0:T(8,128)(2,1)S(1)}, bf16[1,128,2048]{2,1,0:T(8,128)(2,1)}, u32[]{:S(2)}) copy-start(bf16[1,128,2048]{2,1,0:T(8,128)(2,1)} %value.3) | copy-start | bytes 1572868
  6.1 6.4 %copy-start.16 = (s32[1,1,3]{2,1,0:T(1,128)S(1)}, s32[1,1,3]{2,1,0:T(1,128)}, u32[]{:S(2)}) copy-start(s32[1,1,3]{2,1,0:T(1,128)} %mask.3) | copy-start | bytes 40
  9.9 2.6 %collective-permute-start = (bf16[128,3200]{1,0:T(8,128)(2,1)}, bf16[128,3200]{1,0:T(8,128)(2,1)S(1)}, u32[]{:S(2)}, u32[]{:S(2)}) collective-permute-start(bf16[128,3200]{1,0:T(8,128)(2,1)} %get-tuple-element.52), channel_id=1, source_target_pairs={{0,2},{2,0},{4,6},{6,4},{8,10},{10,8},{12,14},{14,12},{16,18},{18,... | collective-permute-start | bytes 2457608 | tf_op jit(solution)/shard_map/ppermute | solution.py:30
  13.3 47.8 %copy-start.5 = (bf16[256,2048]{1,0:T(8,128)(2,1)}, bf16[256,2048]{1,0:T(8,128)(2,1)S(1)}, u32[]{:S(2)}) copy-start(bf16[256,2048]{1,0:T(8,128)(2,1)S(1)} %get-tuple-element.54.own) | copy-start | bytes 3145732
  13.3 47.8 %copy-start.12 = (bf16[256,1024]{1,0:T(8,128)(2,1)}, bf16[256,1024]{1,0:T(8,128)(2,1)S(1)}, u32[]{:S(2)}) copy-start(bf16[256,1024]{1,0:T(8,128)(2,1)S(1)} %get-tuple-element.55.own.q2) | copy-start | bytes 1572868
  13.3 46.9 %copy-start.3 = (bf16[1,512,2048]{2,1,0:T(8,128)(2,1)S(1)}, bf16[1,512,2048]{2,1,0:T(8,128)(2,1)}, u32[]{:S(2)}) copy-start(bf16[1,512,2048]{2,1,0:T(8,128)(2,1)} %param.19) | copy-start | bytes 6291460
  13.3 46.9 %copy-start.17 = (bf16[1,128,2048]{2,1,0:T(8,128)(2,1)S(1)}, bf16[1,128,2048]{2,1,0:T(8,128)(2,1)}, u32[]{:S(2)}) copy-start(bf16[1,128,2048]{2,1,0:T(8,128)(2,1)} %cot.3) | copy-start | bytes 1572868
  13.4 47.7 %collective-permute-start.2 = (bf16[256,2048]{1,0:T(8,128)(2,1)S(1)}, bf16[256,2048]{1,0:T(8,128)(2,1)S(1)}, u32[]{:S(2)}, u32[]{:S(2)}) collective-permute-start(bf16[256,2048]{1,0:T(8,128)(2,1)S(1)} %get-tuple-element.54.own), channel_id=1, source_target_pairs={{0,4},{2,6},{4,8},{6,10},{8,12},{10,14},{12,16},{14,18},{16,20},{1... | collective-permute-start | bytes 3145736 | tf_op jit(solution)/shard_map/ppermute | solution.py:26
  17.1 33.9 %collective-permute-start.3 = (bf16[256,1024]{1,0:T(8,128)(2,1)S(1)}, bf16[256,1024]{1,0:T(8,128)(2,1)S(1)}, u32[]{:S(2)}, u32[]{:S(2)}) collective-permute-start(bf16[256,1024]{1,0:T(8,128)(2,1)S(1)} %get-tuple-element.55.own.q2), channel_id=1, source_target_pairs={{0,4},{2,6},{4,0},{6,2},{8,12},{10,14},{12,8},{14,10},{16,20},{18,... | collective-permute-start | bytes 1572872 | tf_op jit(solution)/shard_map/ppermute | solution.py:30
  18.6 34.7 %collective-permute-start.1 = (bf16[128,2048]{1,0:T(8,128)(2,1)S(1)}, bf16[128,2048]{1,0:T(8,128)(2,1)S(1)}, u32[]{:S(2)}, u32[]{:S(2)}) collective-permute-start(bf16[128,2048]{1,0:T(8,128)(2,1)S(1)} %get-tuple-element.53), channel_id=1, source_target_pairs={{0,8},{2,10},{4,12},{6,14},{8,16},{10,18},{12,20},{14,22},{16,24},... | collective-permute-start | bytes 1572872 | tf_op jit(solution)/shard_map/ppermute | solution.py:26
  22.1 53.8 %collective-permute-start.9 = (bf16[256,2048]{1,0:T(8,128)(2,1)}, bf16[256,2048]{1,0:T(8,128)(2,1)}, u32[]{:S(2)}, u32[]{:S(2)}) collective-permute-start(bf16[256,2048]{1,0:T(8,128)(2,1)} %get-tuple-element.64), channel_id=1, source_target_pairs={{0,1},{1,0},{2,3},{3,2},{4,5},{5,4},{6,7},{7,6},{8,9},{9,8},{10,11... | collective-permute-start | bytes 3145736 | tf_op jit(solution)/shard_map/ppermute | solution.py:42
  51.0 10.1 %copy-start.19 = (bf16[256,1024]{1,0:T(8,128)(2,1)}, bf16[256,1024]{1,0:T(8,128)(2,1)S(1)}, u32[]{:S(2)}) copy-start(bf16[256,1024]{1,0:T(8,128)(2,1)S(1)} %collective-permute-done.3.other) | copy-start | bytes 1572868
  52.0 24.2 %collective-permute-start.6 = (bf16[384,1024]{1,0:T(8,128)(2,1)}, bf16[384,1024]{1,0:T(8,128)(2,1)}, u32[]{:S(2)}, u32[]{:S(2)}) collective-permute-start(bf16[384,1024]{1,0:T(8,128)(2,1)} %get-tuple-element.63), channel_id=1, source_target_pairs={{8,0},{10,2},{12,4},{14,6},{16,8},{18,10},{20,12},{22,14},{24,16},... | collective-permute-start | bytes 2359304 | tf_op jit(solution)/shard_map/ppermute | solution.py:26
  53.3 7.8 %copy-start.14 = (bf16[128,2048]{1,0:T(8,128)(2,1)}, bf16[128,2048]{1,0:T(8,128)(2,1)S(1)}, u32[]{:S(2)}) copy-start(bf16[128,2048]{1,0:T(8,128)(2,1)S(1)} %collective-permute-done.1.far) | copy-start | bytes 1572868
  53.3 23.0 %collective-permute-start.5 = (bf16[384,1024]{1,0:T(8,128)(2,1)S(1)}, bf16[384,1024]{1,0:T(8,128)(2,1)}, u32[]{:S(2)}, u32[]{:S(2)}) collective-permute-start(bf16[384,1024]{1,0:T(8,128)(2,1)S(1)} %get-tuple-element.57.rest_0_), channel_id=1, source_target_pairs={{0,8},{2,10},{4,12},{6,14},{8,16},{10,18},{12,20},{14,22},{16,24},... | collective-permute-start | bytes 2359304 | tf_op jit(solution)/shard_map/ppermute | solution.py:26
  61.1 4.6 %copy-start.7 = (bf16[256,2048]{1,0:T(8,128)(2,1)}, bf16[256,2048]{1,0:T(8,128)(2,1)S(1)}, u32[]{:S(2)}) copy-start(bf16[256,2048]{1,0:T(8,128)(2,1)S(1)} %collective-permute-done.2.near) | copy-start | bytes 3145732
  65.7 0.7 copy-start.21
  66.4 0.7 copy-start.23
  66.4 0.7 copy-start.22
  66.4 4.9 %copy-start = (bf16[1,2048,512]{2,1,0:T(8,128)(2,1)S(1)}, bf16[1,2048,512]{2,1,0:T(8,128)(2,1)}, u32[]{:S(2)}) copy-start(bf16[1,2048,512]{2,1,0:T(8,128)(2,1)} %param.17) | copy-start | bytes 6291460
  66.4 12.5 %collective-permute-start.8 = (bf16[2,1024,512]{2,1,0:T(8,128)(2,1)}, bf16[2,1024,512]{2,1,0:T(8,128)(2,1)}, u32[]{:S(2)}, u32[]{:S(2)}) collective-permute-start(bf16[2,1024,512]{2,1,0:T(8,128)(2,1)} %shard_map.145.inner.refs_0_), channel_id=1, source_target_pairs={{0,2},{2,0},{4,6},{6,4},{8,10},{10,8},{12,14},{14,12},{16,18},{18,... | collective-permute-start | bytes 6291464 | tf_op jit(solution)/shard_map/ppermute | solution.py:30
  66.5 4.9 %collective-permute-start.4 = (bf16[128,1024]{1,0:T(8,128)(2,1)}, bf16[128,1024]{1,0:T(8,128)(2,1)}, u32[]{:S(2)}, u32[]{:S(2)}) collective-permute-start(bf16[128,1024]{1,0:T(8,128)(2,1)} %copy-done.21), channel_id=1, source_target_pairs={{0,2},{2,0},{4,6},{6,4},{8,10},{10,8},{12,14},{14,12},{16,18},{18,... | collective-permute-start | bytes 786440 | tf_op jit(solution)/shard_map/ppermute | solution.py:30
  71.3 1.6 %copy-start.1 = (bf16[1,2048,512]{2,1,0:T(8,128)(2,1)S(1)}, bf16[1,2048,512]{2,1,0:T(8,128)(2,1)}, u32[]{:S(2)}) copy-start(bf16[1,2048,512]{2,1,0:T(8,128)(2,1)} %param.18) | copy-start | bytes 6291460
  76.0 2.9 %collective-permute-start.10 = (bf16[256,2048]{1,0:T(8,128)(2,1)}, bf16[256,2048]{1,0:T(8,128)(2,1)S(1)}, u32[]{:S(2)}, u32[]{:S(2)}) collective-permute-start(bf16[256,2048]{1,0:T(8,128)(2,1)} %shard_map.146.over.refs_2_), channel_id=1, source_target_pairs={{0,2},{2,0},{4,6},{6,4},{8,10},{10,8},{12,14},{14,12},{16,18},{18,... | collective-permute-start | bytes 3145736 | tf_op jit(solution)/shard_map/ppermute | solution.py:30
  76.4 2.5 %copy-start.18 = (bf16[1,128,2048]{2,1,0:T(8,128)(2,1)S(1)}, bf16[1,128,2048]{2,1,0:T(8,128)(2,1)}, u32[]{:S(2)}) copy-start(bf16[1,128,2048]{2,1,0:T(8,128)(2,1)} %cot.3) | copy-start | bytes 1572868
  76.4 8.3 %copy-start.20 = (bf16[256,1024]{1,0:T(8,128)(2,1)S(1)}, bf16[256,1024]{1,0:T(8,128)(2,1)}, u32[]{:S(2)}) copy-start(bf16[256,1024]{1,0:T(8,128)(2,1)} %copy-done.19) | copy-start | bytes 1572868
  84.5 1.7 %collective-permute-start.11 = (bf16[128,1152]{1,0:T(8,128)(2,1)S(1)}, bf16[128,1152]{1,0:T(8,128)(2,1)S(1)}, u32[]{:S(2)}, u32[]{:S(2)}) collective-permute-start(bf16[128,1152]{1,0:T(8,128)(2,1)S(1)} %get-tuple-element.67), channel_id=1, source_target_pairs={{0,2},{2,0},{4,6},{6,4},{8,10},{10,8},{12,14},{14,12},{16,18},{18,... | collective-permute-start | bytes 884744 | tf_op jit(solution)/shard_map/ppermute | solution.py:30
  86.2 10.9 %copy-start.6 = (bf16[256,2048]{1,0:T(8,128)(2,1)S(1)}, bf16[256,2048]{1,0:T(8,128)(2,1)}, u32[]{:S(2)}) copy-start(bf16[256,2048]{1,0:T(8,128)(2,1)} %copy-done.5) | copy-start | bytes 3145732
  86.2 10.9 %copy-start.8 = (bf16[256,2048]{1,0:T(8,128)(2,1)S(1)}, bf16[256,2048]{1,0:T(8,128)(2,1)}, u32[]{:S(2)}) copy-start(bf16[256,2048]{1,0:T(8,128)(2,1)} %copy-done.7) | copy-start | bytes 3145732
  86.2 10.9 %copy-start.13 = (bf16[256,1024]{1,0:T(8,128)(2,1)S(1)}, bf16[256,1024]{1,0:T(8,128)(2,1)}, u32[]{:S(2)}) copy-start(bf16[256,1024]{1,0:T(8,128)(2,1)} %copy-done.12) | copy-start | bytes 1572868
  86.2 10.9 %copy-start.15 = (bf16[128,2048]{1,0:T(8,128)(2,1)S(1)}, bf16[128,2048]{1,0:T(8,128)(2,1)}, u32[]{:S(2)}) copy-start(bf16[128,2048]{1,0:T(8,128)(2,1)} %copy-done.14) | copy-start | bytes 1572868
  86.4 24.5 %collective-permute-start.15 = (bf16[256,1152]{1,0:T(8,128)(2,1)S(1)}, bf16[256,1152]{1,0:T(8,128)(2,1)S(1)}, u32[]{:S(2)}, u32[]{:S(2)}) collective-permute-start(bf16[256,1152]{1,0:T(8,128)(2,1)S(1)} %get-tuple-element.69.rest_0_.co), channel_id=1, source_target_pairs={{4,0},{6,2},{8,4},{10,6},{12,8},{14,10},{16,12},{18,14},{20,16},{2... | collective-permute-start | bytes 1769480 | tf_op jit(solution)/shard_map/ppermute | solution.py:26
  87.8 28.3 %collective-permute-start.14 = (bf16[256,1152]{1,0:T(8,128)(2,1)S(1)}, bf16[256,1152]{1,0:T(8,128)(2,1)S(1)}, u32[]{:S(2)}, u32[]{:S(2)}) collective-permute-start(bf16[256,1152]{1,0:T(8,128)(2,1)S(1)} %get-tuple-element.69.rest_0_.co), channel_id=1, source_target_pairs={{0,4},{2,6},{4,8},{6,10},{8,12},{10,14},{12,16},{14,18},{16,20},{1... | collective-permute-start | bytes 1769480 | tf_op jit(solution)/shard_map/ppermute | solution.py:26
  92.4 15.4 %collective-permute-start.13 = (bf16[128,1152]{1,0:T(8,128)(2,1)S(1)}, bf16[128,1152]{1,0:T(8,128)(2,1)S(1)}, u32[]{:S(2)}, u32[]{:S(2)}) collective-permute-start(bf16[128,1152]{1,0:T(8,128)(2,1)S(1)} %get-tuple-element.75), channel_id=1, source_target_pairs={{0,8},{2,10},{4,12},{6,14},{8,16},{10,18},{12,20},{14,22},{16,24},... | collective-permute-start | bytes 884744 | tf_op jit(solution)/shard_map/ppermute | solution.py:26
  95.4 6.9 %copy-start.4 = (bf16[1,512,2048]{2,1,0:T(8,128)(2,1)S(1)}, bf16[1,512,2048]{2,1,0:T(8,128)(2,1)}, u32[]{:S(2)}) copy-start(bf16[1,512,2048]{2,1,0:T(8,128)(2,1)} %param.19) | copy-start | bytes 6291460
  95.5 15.4 %collective-permute-start.16 = (bf16[128,1152]{1,0:T(8,128)(2,1)S(1)}, bf16[128,1152]{1,0:T(8,128)(2,1)S(1)}, u32[]{:S(2)}, u32[]{:S(2)}) collective-permute-start(bf16[128,1152]{1,0:T(8,128)(2,1)S(1)} %get-tuple-element.76), channel_id=1, source_target_pairs={{8,0},{10,2},{12,4},{14,6},{16,8},{18,10},{20,12},{22,14},{24,16},... | collective-permute-start | bytes 884744 | tf_op jit(solution)/shard_map/ppermute | solution.py:26
  116.1 12.2 %copy-start.2 = (bf16[1,2048,512]{2,1,0:T(8,128)(2,1)S(1)}, bf16[1,2048,512]{2,1,0:T(8,128)(2,1)}, u32[]{:S(2)}) copy-start(bf16[1,2048,512]{2,1,0:T(8,128)(2,1)} %param.18) | copy-start | bytes 6291460
  126.7 1.6 %collective-permute-start.18 = (bf16[128,1024]{1,0:T(8,128)(2,1)S(1)}, bf16[128,1024]{1,0:T(8,128)(2,1)S(1)}, u32[]{:S(2)}, u32[]{:S(2)}) collective-permute-start(bf16[128,1024]{1,0:T(8,128)(2,1)S(1)} %get-tuple-element.90), channel_id=1, source_target_pairs={{0,2},{2,0},{4,6},{6,4},{8,10},{10,8},{12,14},{14,12},{16,18},{18,... | collective-permute-start | bytes 786440 | tf_op jit(solution)/shard_map/ppermute | solution.py:30
  126.8 4.4 %collective-permute-start.17 = (bf16[128,2048]{1,0:T(8,128)(2,1)S(1)}, bf16[128,2048]{1,0:T(8,128)(2,1)S(1)}, u32[]{:S(2)}, u32[]{:S(2)}) collective-permute-start(bf16[128,2048]{1,0:T(8,128)(2,1)S(1)} %get-tuple-element.85), channel_id=1, source_target_pairs={{0,2},{2,0},{4,6},{6,4},{8,10},{10,8},{12,14},{14,12},{16,18},{18,... | collective-permute-start | bytes 1572872 | tf_op jit(solution)/shard_map/ppermute | solution.py:30
  127.2 3.9 %collective-permute-start.12 = (bf16[128,1024]{1,0:T(8,128)(2,1)S(1)}, bf16[128,1024]{1,0:T(8,128)(2,1)S(1)}, u32[]{:S(2)}, u32[]{:S(2)}) collective-permute-start(bf16[128,1024]{1,0:T(8,128)(2,1)S(1)} %get-tuple-element.73), channel_id=1, source_target_pairs={{0,2},{2,0},{4,6},{6,4},{8,10},{10,8},{12,14},{14,12},{16,18},{18,... | collective-permute-start | bytes 786440 | tf_op jit(solution)/shard_map/ppermute | solution.py:30

commit v7 on v6

--- a/solution.py
+++ b/solution.py
@@ -282,7 +282,7 @@
     core = this_core()
     window = window_refs(far, near, own, rows)
     causal = causal_of(rows)
-    seen = [flags[block * rows : block * rows + LEVEL, :].astype(F32) for block in range(PAIR)]
+    seen = [flags[block * rows : (block + 1) * rows, :].astype(F32)[:LEVEL] for block in range(PAIR)]
 
     def one(head):
         here = pl.ds(pl.multiple_of(head * size, size), size)

time: 133 us -> 133 us (level)
  no operation moved by 1% of the time
where the time goes in v7:
time: 133 us; the launch traced here: 132 us
  Pallas kernels  49 us (37%)
  waiting for transfers between devices  46.9 us (35%)
  starting transfers between devices  32.8 us (25%)
  local copies, waits for them, and re-layouts  2.64 us (2%)
    pallas_call x19, Pallas kernels, call(): pl.pallas_call(kernel, out_shape=outs, in_specs=[space for _, space in ar...  49 us
    ppermute x9, waiting for transfers between devices, swapped(): lax.ppermute(x, 'ctx', [(i, i ^ bit) for i in range(lax.axis_size('ctx'))])  38.3 us
    ppermute x8, starting transfers between devices, moved(): return lax.ppermute(x, 'ctx', pairs)  26.1 us
    ppermute x8, waiting for transfers between devices, moved(): return lax.ppermute(x, 'ctx', pairs)  8.54 us
    ppermute x2, starting transfers between devices, crossed(): return lax.ppermute(x, 'exp', [(0, 1), (1, 0)])  3.6 us
    ppermute x9, starting transfers between devices, swapped(): lax.ppermute(x, 'ctx', [(i, i ^ bit) for i in range(lax.axis_size('ctx'))])  3.12 us
  transfers between devices with their start and end apart: 19, of which 8 were waited for; matrix products, arithmetic and copies ran while one was open for 0% of the time, Pallas kernels for 22%

profile of v7, /device:TPU:0, one launch (start us, length us, event | category | flops | bytes accessed | tf_op | source)
XLA Modules:
  0.0 132.4 jit_solution(13478406852235523273)
XLA Ops:
  0.6 2.5 %shard_map.137.after = bf16[2,1024,512]{2,1,0:T(8,128)(2,1)} custom-call(bf16[2048,512]{1,0:T(8,128)(2,1)} %bitcast.12, bf16[2048,512]{1,0:T(8,128)(2,1)} %bitcast.15), custom_call_target="tpu_custom_call" | custom-call | flops 1100000000 | tf_op jit(solution)/shard_map/pallas_call | solution.py:90
  3.1 3.0 %collective-permute-start.7 = (bf16[2,1024,512]{2,1,0:T(8,128)(2,1)}, bf16[2,1024,512]{2,1,0:T(8,128)(2,1)}, u32[]{:S(2)}, u32[]{:S(2)}) collective-permute-start(bf16[2,1024,512]{2,1,0:T(8,128)(2,1)} %shard_map.137.after), channel_id=1, source_target_pairs={{0,1},{1,0},{2,3},{3,2},{4,5},{5,4},{6,7},{7,6},{8,9},{9,8},{10,11... | collective-permute-start | bytes 6291464 | tf_op jit(solution)/shard_map/ppermute | solution.py:42
  6.1 3.8 %shard_map.138 = (bf16[256,2048]{1,0:T(8,128)(2,1)}, bf16[128,3200]{1,0:T(8,128)(2,1)}) custom-call(s32[1,1,3]{2,1,0:T(1,128)} %mask.3, bf16[512,2048]{1,0:T(8,128)(2,1)} %bitcast.18, bf16[1,128,2048]{2,1,0:T(8,128)(2,1)} %query.3, bf16[1,128,2048]{2,1,0:T(8,128)(2,1)} %key.3, bf16[1,128,2048]{2,1,0:T(8,128)(2,1)} %value.3, ...), custom_call_target="tpu_custom_call" | custom-call | flops 1100000000 | tf_op jit(solution)/shard_map/pallas_call | solution.py:90
  9.9 0.1 collective-permute-start
  10.0 2.5 %collective-permute-done.got = bf16[128,3200]{1,0:T(8,128)(2,1)S(1)} collective-permute-done((bf16[128,3200]{1,0:T(8,128)(2,1)}, bf16[128,3200]{1,0:T(8,128)(2,1)S(1)}, u32[]{:S(2)}, u32[]{:S(2)}) %collective-permute-start) | collective-permute-done | bytes 819232 | tf_op jit(solution)/shard_map/ppermute | solution.py:30
  12.5 0.8 shard_map.139
  13.3 0.0 copy-start.12
  13.3 0.0 copy-start.3
  13.3 0.0 copy-start.17
  13.4 3.8 %collective-permute-start.2 = (bf16[256,2048]{1,0:T(8,128)(2,1)S(1)}, bf16[256,2048]{1,0:T(8,128)(2,1)S(1)}, u32[]{:S(2)}, u32[]{:S(2)}) collective-permute-start(bf16[256,2048]{1,0:T(8,128)(2,1)S(1)} %get-tuple-element.54.own), channel_id=1, source_target_pairs={{0,4},{2,6},{4,8},{6,10},{8,12},{10,14},{12,16},{14,18},{16,20},{1... | collective-permute-start | bytes 3145736 | tf_op jit(solution)/shard_map/ppermute | solution.py:26
  17.1 1.5 %collective-permute-start.3 = (bf16[256,1024]{1,0:T(8,128)(2,1)S(1)}, bf16[256,1024]{1,0:T(8,128)(2,1)S(1)}, u32[]{:S(2)}, u32[]{:S(2)}) collective-permute-start(bf16[256,1024]{1,0:T(8,128)(2,1)S(1)} %get-tuple-element.55.own.q2), channel_id=1, source_target_pairs={{0,4},{2,6},{4,0},{6,2},{8,12},{10,14},{12,8},{14,10},{16,20},{18,... | collective-permute-start | bytes 1572872 | tf_op jit(solution)/shard_map/ppermute | solution.py:30
  18.6 3.5 %collective-permute-start.1 = (bf16[128,2048]{1,0:T(8,128)(2,1)S(1)}, bf16[128,2048]{1,0:T(8,128)(2,1)S(1)}, u32[]{:S(2)}, u32[]{:S(2)}) collective-permute-start(bf16[128,2048]{1,0:T(8,128)(2,1)S(1)} %get-tuple-element.53), channel_id=1, source_target_pairs={{0,8},{2,10},{4,12},{6,14},{8,16},{10,18},{12,20},{14,22},{16,24},... | collective-permute-start | bytes 1572872 | tf_op jit(solution)/shard_map/ppermute | solution.py:26
  22.1 0.6 collective-permute-start.9
  22.7 28.2 %collective-permute-done.3.other = bf16[256,1024]{1,0:T(8,128)(2,1)S(1)} collective-permute-done((bf16[256,1024]{1,0:T(8,128)(2,1)S(1)}, bf16[256,1024]{1,0:T(8,128)(2,1)S(1)}, u32[]{:S(2)}, u32[]{:S(2)}) %collective-permute-start.3) | collective-permute-done | bytes 524320 | tf_op jit(solution)/shard_map/ppermute | solution.py:30
  51.0 1.1 shard_map.140
  52.0 1.3 collective-permute-start.6
  53.3 0.0 collective-permute-done.1.far
  53.3 0.0 copy-start.14
  53.3 6.9 %collective-permute-start.5 = (bf16[384,1024]{1,0:T(8,128)(2,1)S(1)}, bf16[384,1024]{1,0:T(8,128)(2,1)}, u32[]{:S(2)}, u32[]{:S(2)}) collective-permute-start(bf16[384,1024]{1,0:T(8,128)(2,1)S(1)} %get-tuple-element.57.rest_0_), channel_id=1, source_target_pairs={{0,8},{2,10},{4,12},{6,14},{8,16},{10,18},{12,20},{14,22},{16,24},... | collective-permute-start | bytes 2359304 | tf_op jit(solution)/shard_map/ppermute | solution.py:26
  60.2 0.8 shard_map.141.rest_1_.back
  61.1 0.0 collective-permute-done.2.near
  61.1 4.6 %shard_map.142 = (bf16[256,128]{1,0:T(8,128)(2,1)S(1)}, bf16[128,1024]{1,0:T(8,128)(2,1)S(1)}, bf16[128,1024]{1,0:T(8,128)(2,1)S(1)}) custom-call(bf16[128,2048]{1,0:T(8,128)(2,1)S(1)} %collective-permute-done.1.far, bf16[256,2048]{1,0:T(8,128)(2,1)S(1)} %collective-permute-done.2.near, bf16[256,2048]{1,0:T(8,128)(2,1)S(1)} %get-tuple-element.54.own, ...), custom_call_target="tpu_custom_call" | custom-call | flops 110000000 | tf_op jit(solution)/shard_map/pallas_call | solution.py:90
  65.7 0.0 copy-start.21
  65.7 0.0 collective-permute-done.7.refs_0_
  65.7 0.7 copy-done.21
  66.4 0.0 collective-permute-start.8
  66.5 0.5 collective-permute-start.4
  66.9 0.1 copy-done.23
  67.1 0.0 copy-done.22
  67.1 0.1 copy.21.picks
  67.2 4.1 %collective-permute-done.4.got = bf16[128,1024]{1,0:T(8,128)(2,1)} collective-permute-done((bf16[128,1024]{1,0:T(8,128)(2,1)}, bf16[128,1024]{1,0:T(8,128)(2,1)}, u32[]{:S(2)}, u32[]{:S(2)}) %collective-permute-start.4) | collective-permute-done | bytes 262176 | tf_op jit(solution)/shard_map/ppermute | solution.py:30
  71.3 1.6 %copy-done.1 = bf16[1,2048,512]{2,1,0:T(8,128)(2,1)S(1)} copy-done((bf16[1,2048,512]{2,1,0:T(8,128)(2,1)S(1)}, bf16[1,2048,512]{2,1,0:T(8,128)(2,1)}, u32[]{:S(2)}) %copy-start.1) | copy-done | bytes 2097176
  72.9 3.1 %shard_map.143 = (f32[128,1024]{1,0:T(8,128)S(1)}, f32[128,1024]{1,0:T(8,128)S(1)}, bf16[128,512]{1,0:T(8,128)(2,1)S(1)}, f32[128,512]{1,0:T(8,128)S(1)}, f32[128,512]{1,0:T(8,128)S(1)}) custom-call(bf16[128,1024]{1,0:T(8,128)(2,1)S(1)} %get-tuple-element.58.keep.refs_1_, bf16[128,1024]{1,0:T(8,128)(2,1)} %collective-permute-done.4.got, ...), custom_call_target="tpu_custom_call" | custom-call | flops 110000000 | tf_op jit(solution)/shard_map/pallas_call | solution.py:90
  76.0 0.0 collective-permute-done.9.refs_0_
  76.0 0.2 collective-permute-start.10
  76.2 0.2 collective-permute-done.5.refs_1_.below
  76.4 2.5 %collective-permute-done.10.over_s.refs_3_ = bf16[256,2048]{1,0:T(8,128)(2,1)S(1)} collective-permute-done((bf16[256,2048]{1,0:T(8,128)(2,1)}, bf16[256,2048]{1,0:T(8,128)(2,1)S(1)}, u32[]{:S(2)}, u32[]{:S(2)}) %collective-permute-start.10) | collective-permute-done | bytes 1048608 | tf_op jit(solution)/shard_map/ppermute | solution.py:30
  78.9 0.0 collective-permute-done.8.inner_s.refs_1_
  78.9 5.6 %shard_map.147 = (bf16[128,1152]{1,0:T(8,128)(2,1)S(1)}, bf16[128,1152]{1,0:T(8,128)(2,1)S(1)}, bf16[128,512]{1,0:T(8,128)(2,1)S(1)}, f32[128,512]{1,0:T(8,128)S(1)}, f32[128,512]{1,0:T(8,128)S(1)}) custom-call(bf16[128,1024]{1,0:T(8,128)(2,1)S(1)} %get-tuple-element.58.keep.refs_1_, bf16[128,1024]{1,0:T(8,128)(2,1)} %collective-permute-done.4.got, ...), custom_call_target="tpu_custom_call" | custom-call | flops 4950000128 | tf_op jit(solution)/shard_map/pallas_call | solution.py:90
  84.5 0.2 collective-permute-start.11
  84.7 1.5 %shard_map.149 = (bf16[384,1024]{1,0:T(8,128)(2,1)S(1)}, bf16[384,1024]{1,0:T(8,128)(2,1)S(1)}) custom-call(bf16[256,1024]{1,0:T(8,128)(2,1)S(1)} %copy-done.20, bf16[384,1024]{1,0:T(8,128)(2,1)} %collective-permute-done.5.refs_1_.below, bf16[384,1024]{1,0:T(8,128)(2,1)} %collective-permute-done.6.refs_2_.above), custom_call_target="tpu_custom_call" | custom-call | flops 1100000000 | tf_op jit(solution)/shard_map/pallas_call | solution.py:90
  86.2 0.0 copy-start.13
  86.2 0.0 copy-start.15
  86.2 0.0 collective-permute-done.11.got
  86.2 0.1 shard_map.148
  86.4 1.4 %collective-permute-start.15 = (bf16[256,1152]{1,0:T(8,128)(2,1)S(1)}, bf16[256,1152]{1,0:T(8,128)(2,1)S(1)}, u32[]{:S(2)}, u32[]{:S(2)}) collective-permute-start(bf16[256,1152]{1,0:T(8,128)(2,1)S(1)} %get-tuple-element.69.rest_0_.co), channel_id=1, source_target_pairs={{4,0},{6,2},{8,4},{10,6},{12,8},{14,10},{16,12},{18,14},{20,16},{2... | collective-permute-start | bytes 1769480 | tf_op jit(solution)/shard_map/ppermute | solution.py:26
  87.8 4.6 %collective-permute-start.14 = (bf16[256,1152]{1,0:T(8,128)(2,1)S(1)}, bf16[256,1152]{1,0:T(8,128)(2,1)S(1)}, u32[]{:S(2)}, u32[]{:S(2)}) collective-permute-start(bf16[256,1152]{1,0:T(8,128)(2,1)S(1)} %get-tuple-element.69.rest_0_.co), channel_id=1, source_target_pairs={{0,4},{2,6},{4,8},{6,10},{8,12},{10,14},{12,16},{14,18},{16,20},{1... | collective-permute-start | bytes 1769480 | tf_op jit(solution)/shard_map/ppermute | solution.py:26
  92.4 3.0 %collective-permute-start.13 = (bf16[128,1152]{1,0:T(8,128)(2,1)S(1)}, bf16[128,1152]{1,0:T(8,128)(2,1)S(1)}, u32[]{:S(2)}, u32[]{:S(2)}) collective-permute-start(bf16[128,1152]{1,0:T(8,128)(2,1)S(1)} %get-tuple-element.75), channel_id=1, source_target_pairs={{0,8},{2,10},{4,12},{6,14},{8,16},{10,18},{12,20},{14,22},{16,24},... | collective-permute-start | bytes 884744 | tf_op jit(solution)/shard_map/ppermute | solution.py:26
  95.4 0.0 copy-start.4
  95.5 1.6 %collective-permute-start.16 = (bf16[128,1152]{1,0:T(8,128)(2,1)S(1)}, bf16[128,1152]{1,0:T(8,128)(2,1)S(1)}, u32[]{:S(2)}, u32[]{:S(2)}) collective-permute-start(bf16[128,1152]{1,0:T(8,128)(2,1)S(1)} %get-tuple-element.76), channel_id=1, source_target_pairs={{8,0},{10,2},{12,4},{14,6},{16,8},{18,10},{20,12},{22,14},{24,16},... | collective-permute-start | bytes 884744 | tf_op jit(solution)/shard_map/ppermute | solution.py:26
  97.1 5.2 %shard_map.151 = (bf16[8,2,512,128]{3,2,1,0:T(8,128)(2,1)S(1)}, bf16[8,2,128,512]{3,2,1,0:T(8,128)(2,1)S(1)}, bf16[256,1024]{1,0:T(8,128)(2,1)S(1)}, bf16[128,10...) custom-call(bf16[128,2048]{1,0:T(8,128)(2,1)S(1)} %copy-done.15, ...), custom_call_target="tpu_custom_call" | custom-call | flops 7699999744 | tf_op jit(solution)/shard_map/pallas_call | solution.py:90
  102.3 2.9 %shard_map.150 = (bf16[128,2048]{1,0:T(8,128)(2,1)}, f32[8,128]{1,0:T(8,128)S(1)}) custom-call(bf16[128,1024]{1,0:T(8,128)(2,1)S(1)} %get-tuple-element.58.keep.refs_1_, bf16[128,1024]{1,0:T(8,128)(2,1)} %collective-permute-done.4.got, bf16[128,512]{1,0:T(8,128)(2,1)S(1)} %get-tuple-element.60.hidden_own, bf16[128,512]{1,0:T(8,128)(2,1)S(1)} %get-tuple-element.65.hidden, ...), custom_call_target="tpu_custom_call" | custom-call | flops 3300000000 | tf_op jit(solution)/shard_map/pallas_call | solution.py:90
  105.2 2.5 %shard_map.152 = (bf16[2,1024,512]{2,1,0:T(8,128)(2,1)S(1)}, bf16[2,1024,512]{2,1,0:T(8,128)(2,1)S(1)}, bf16[256,2048]{1,0:T(8,128)(2,1)S(1)}, bf16[256,2048]{1,0:T(8,128)(2,1)S(1)}, f32[8,128]{1,0:T(8,128)S(1)}) custom-call(bf16[2,1024,512]{2,1,0:T(8,128)(2,1)} %shard_map.145.inner.refs_0_, bf16[2,1024,512]{2,1,0:T(8,128)(2,1)} %collective-permute-done.8.inner_s.refs_1_, ...), custom_call_target="tpu_custom_call" | custom-call | flops 2200000000 | tf_op jit(solution)/shard_map/pallas_call | solution.py:90
  107.8 0.0 collective-permute-done.13.cfb
  107.8 3.1 %collective-permute-done.16.cfa = bf16[128,1152]{1,0:T(8,128)(2,1)S(1)} collective-permute-done((bf16[128,1152]{1,0:T(8,128)(2,1)S(1)}, bf16[128,1152]{1,0:T(8,128)(2,1)S(1)}, u32[]{:S(2)}, u32[]{:S(2)}) %collective-permute-start.16) | collective-permute-done | bytes 294944 | tf_op jit(solution)/shard_map/ppermute | solution.py:26
  110.8 0.0 collective-permute-done.15.cna
  110.9 5.3 %collective-permute-done.14.cnb = bf16[256,1152]{1,0:T(8,128)(2,1)S(1)} collective-permute-done((bf16[256,1152]{1,0:T(8,128)(2,1)S(1)}, bf16[256,1152]{1,0:T(8,128)(2,1)S(1)}, u32[]{:S(2)}, u32[]{:S(2)}) %collective-permute-start.14) | collective-permute-done | bytes 589856 | tf_op jit(solution)/shard_map/ppermute | solution.py:26
  116.1 10.5 %shard_map.153 = (bf16[128,2048]{1,0:T(8,128)(2,1)S(1)}, bf16[128,2048]{1,0:T(8,128)(2,1)S(1)}, bf16[128,1024]{1,0:T(8,128)(2,1)S(1)}, bf16[128,1024]{1,0:T(8,128)(2,1)S(1)}) custom-call(bf16[128,2048]{1,0:T(8,128)(2,1)S(1)} %copy-done.15, bf16[256,2048]{1,0:T(8,128)(2,1)S(1)} %copy-done.8, bf16[256,2048]{1,0:T(8,128)(2,1)S(1)} %copy-done.6, ...), custom_call_target="tpu_custom_call" | custom-call | flops 17600000000 | tf_op jit(solution)/shard_map/pallas_call | solution.py:90
  126.7 0.1 collective-permute-start.18
  126.8 0.5 collective-permute-start.17
  127.2 0.1 collective-permute-start.12
  127.3 0.9 collective-permute-done.18.got
  128.3 2.8 %shard_map.155 = bf16[128,2048]{1,0:T(8,128)(2,1)} custom-call(bf16[128,1024]{1,0:T(8,128)(2,1)S(1)} %get-tuple-element.89.keep, bf16[128,1024]{1,0:T(8,128)(2,1)S(1)} %collective-permute-done.18.got, f32[128,512]{1,0:T(8,128)S(1)} %get-tuple-element.91.slope_up_own, f32[128,512]{1,0:T(8,128)S(1)} %get-tuple-element.92.active_own, ...), custom_call_target="tpu_custom_call" | custom-call | flops 4950000128 | tf_op jit(solution)/shard_map/pallas_call | solution.py:90
  131.1 1.3 shard_map.154
  (44 shorter events, 0.1 us)
Async XLA Ops:
  3.1 62.6 %collective-permute-start.7 = (bf16[2,1024,512]{2,1,0:T(8,128)(2,1)}, bf16[2,1024,512]{2,1,0:T(8,128)(2,1)}, u32[]{:S(2)}, u32[]{:S(2)}) collective-permute-start(bf16[2,1024,512]{2,1,0:T(8,128)(2,1)} %shard_map.137.after), channel_id=1, source_target_pairs={{0,1},{1,0},{2,3},{3,2},{4,5},{5,4},{6,7},{7,6},{8,9},{9,8},{10,11... | collective-permute-start | bytes 6291464 | tf_op jit(solution)/shard_map/ppermute | solution.py:42
  6.1 6.4 %copy-start.9 = (bf16[1,128,2048]{2,1,0:T(8,128)(2,1)S(1)}, bf16[1,128,2048]{2,1,0:T(8,128)(2,1)}, u32[]{:S(2)}) copy-start(bf16[1,128,2048]{2,1,0:T(8,128)(2,1)} %query.3) | copy-start | bytes 1572868
  6.1 6.4 %copy-start.10 = (bf16[1,128,2048]{2,1,0:T(8,128)(2,1)S(1)}, bf16[1,128,2048]{2,1,0:T(8,128)(2,1)}, u32[]{:S(2)}) copy-start(bf16[1,128,2048]{2,1,0:T(8,128)(2,1)} %key.3) | copy-start | bytes 1572868
  6.1 6.4 %copy-start.11 = (bf16[1,128,2048]{2,1,0:T(8,128)(2,1)S(1)}, bf16[1,128,2048]{2,1,0:T(8,128)(2,1)}, u32[]{:S(2)}) copy-start(bf16[1,128,2048]{2,1,0:T(8,128)(2,1)} %value.3) | copy-start | bytes 1572868
  6.1 6.4 %copy-start.16 = (s32[1,1,3]{2,1,0:T(1,128)S(1)}, s32[1,1,3]{2,1,0:T(1,128)}, u32[]{:S(2)}) copy-start(s32[1,1,3]{2,1,0:T(1,128)} %mask.3) | copy-start | bytes 40
  9.9 2.6 %collective-permute-start = (bf16[128,3200]{1,0:T(8,128)(2,1)}, bf16[128,3200]{1,0:T(8,128)(2,1)S(1)}, u32[]{:S(2)}, u32[]{:S(2)}) collective-permute-start(bf16[128,3200]{1,0:T(8,128)(2,1)} %get-tuple-element.52), channel_id=1, source_target_pairs={{0,2},{2,0},{4,6},{6,4},{8,10},{10,8},{12,14},{14,12},{16,18},{18,... | collective-permute-start | bytes 2457608 | tf_op jit(solution)/shard_map/ppermute | solution.py:30
  13.3 47.8 %copy-start.5 = (bf16[256,2048]{1,0:T(8,128)(2,1)}, bf16[256,2048]{1,0:T(8,128)(2,1)S(1)}, u32[]{:S(2)}) copy-start(bf16[256,2048]{1,0:T(8,128)(2,1)S(1)} %get-tuple-element.54.own) | copy-start | bytes 3145732
  13.3 47.8 %copy-start.12 = (bf16[256,1024]{1,0:T(8,128)(2,1)}, bf16[256,1024]{1,0:T(8,128)(2,1)S(1)}, u32[]{:S(2)}) copy-start(bf16[256,1024]{1,0:T(8,128)(2,1)S(1)} %get-tuple-element.55.own.q2) | copy-start | bytes 1572868
  13.3 46.9 %copy-start.3 = (bf16[1,512,2048]{2,1,0:T(8,128)(2,1)S(1)}, bf16[1,512,2048]{2,1,0:T(8,128)(2,1)}, u32[]{:S(2)}) copy-start(bf16[1,512,2048]{2,1,0:T(8,128)(2,1)} %param.19) | copy-start | bytes 6291460
  13.3 46.9 %copy-start.17 = (bf16[1,128,2048]{2,1,0:T(8,128)(2,1)S(1)}, bf16[1,128,2048]{2,1,0:T(8,128)(2,1)}, u32[]{:S(2)}) copy-start(bf16[1,128,2048]{2,1,0:T(8,128)(2,1)} %cot.3) | copy-start | bytes 1572868
  13.4 47.7 %collective-permute-start.2 = (bf16[256,2048]{1,0:T(8,128)(2,1)S(1)}, bf16[256,2048]{1,0:T(8,128)(2,1)S(1)}, u32[]{:S(2)}, u32[]{:S(2)}) collective-permute-start(bf16[256,2048]{1,0:T(8,128)(2,1)S(1)} %get-tuple-element.54.own), channel_id=1, source_target_pairs={{0,4},{2,6},{4,8},{6,10},{8,12},{10,14},{12,16},{14,18},{16,20},{1... | collective-permute-start | bytes 3145736 | tf_op jit(solution)/shard_map/ppermute | solution.py:26
  17.1 33.9 %collective-permute-start.3 = (bf16[256,1024]{1,0:T(8,128)(2,1)S(1)}, bf16[256,1024]{1,0:T(8,128)(2,1)S(1)}, u32[]{:S(2)}, u32[]{:S(2)}) collective-permute-start(bf16[256,1024]{1,0:T(8,128)(2,1)S(1)} %get-tuple-element.55.own.q2), channel_id=1, source_target_pairs={{0,4},{2,6},{4,0},{6,2},{8,12},{10,14},{12,8},{14,10},{16,20},{18,... | collective-permute-start | bytes 1572872 | tf_op jit(solution)/shard_map/ppermute | solution.py:30
  18.6 34.7 %collective-permute-start.1 = (bf16[128,2048]{1,0:T(8,128)(2,1)S(1)}, bf16[128,2048]{1,0:T(8,128)(2,1)S(1)}, u32[]{:S(2)}, u32[]{:S(2)}) collective-permute-start(bf16[128,2048]{1,0:T(8,128)(2,1)S(1)} %get-tuple-element.53), channel_id=1, source_target_pairs={{0,8},{2,10},{4,12},{6,14},{8,16},{10,18},{12,20},{14,22},{16,24},... | collective-permute-start | bytes 1572872 | tf_op jit(solution)/shard_map/ppermute | solution.py:26
  22.1 53.8 %collective-permute-start.9 = (bf16[256,2048]{1,0:T(8,128)(2,1)}, bf16[256,2048]{1,0:T(8,128)(2,1)}, u32[]{:S(2)}, u32[]{:S(2)}) collective-permute-start(bf16[256,2048]{1,0:T(8,128)(2,1)} %get-tuple-element.64), channel_id=1, source_target_pairs={{0,1},{1,0},{2,3},{3,2},{4,5},{5,4},{6,7},{7,6},{8,9},{9,8},{10,11... | collective-permute-start | bytes 3145736 | tf_op jit(solution)/shard_map/ppermute | solution.py:42
  51.0 10.1 %copy-start.19 = (bf16[256,1024]{1,0:T(8,128)(2,1)}, bf16[256,1024]{1,0:T(8,128)(2,1)S(1)}, u32[]{:S(2)}) copy-start(bf16[256,1024]{1,0:T(8,128)(2,1)S(1)} %collective-permute-done.3.other) | copy-start | bytes 1572868
  52.0 24.2 %collective-permute-start.6 = (bf16[384,1024]{1,0:T(8,128)(2,1)}, bf16[384,1024]{1,0:T(8,128)(2,1)}, u32[]{:S(2)}, u32[]{:S(2)}) collective-permute-start(bf16[384,1024]{1,0:T(8,128)(2,1)} %get-tuple-element.63), channel_id=1, source_target_pairs={{8,0},{10,2},{12,4},{14,6},{16,8},{18,10},{20,12},{22,14},{24,16},... | collective-permute-start | bytes 2359304 | tf_op jit(solution)/shard_map/ppermute | solution.py:26
  53.3 7.8 %copy-start.14 = (bf16[128,2048]{1,0:T(8,128)(2,1)}, bf16[128,2048]{1,0:T(8,128)(2,1)S(1)}, u32[]{:S(2)}) copy-start(bf16[128,2048]{1,0:T(8,128)(2,1)S(1)} %collective-permute-done.1.far) | copy-start | bytes 1572868
  53.3 23.0 %collective-permute-start.5 = (bf16[384,1024]{1,0:T(8,128)(2,1)S(1)}, bf16[384,1024]{1,0:T(8,128)(2,1)}, u32[]{:S(2)}, u32[]{:S(2)}) collective-permute-start(bf16[384,1024]{1,0:T(8,128)(2,1)S(1)} %get-tuple-element.57.rest_0_), channel_id=1, source_target_pairs={{0,8},{2,10},{4,12},{6,14},{8,16},{10,18},{12,20},{14,22},{16,24},... | collective-permute-start | bytes 2359304 | tf_op jit(solution)/shard_map/ppermute | solution.py:26
  61.1 4.6 %copy-start.7 = (bf16[256,2048]{1,0:T(8,128)(2,1)}, bf16[256,2048]{1,0:T(8,128)(2,1)S(1)}, u32[]{:S(2)}) copy-start(bf16[256,2048]{1,0:T(8,128)(2,1)S(1)} %collective-permute-done.2.near) | copy-start | bytes 3145732
  65.7 0.7 copy-start.21
  66.4 0.7 copy-start.23
  66.4 0.7 copy-start.22
  66.4 4.9 %copy-start = (bf16[1,2048,512]{2,1,0:T(8,128)(2,1)S(1)}, bf16[1,2048,512]{2,1,0:T(8,128)(2,1)}, u32[]{:S(2)}) copy-start(bf16[1,2048,512]{2,1,0:T(8,128)(2,1)} %param.17) | copy-start | bytes 6291460
  66.4 12.5 %collective-permute-start.8 = (bf16[2,1024,512]{2,1,0:T(8,128)(2,1)}, bf16[2,1024,512]{2,1,0:T(8,128)(2,1)}, u32[]{:S(2)}, u32[]{:S(2)}) collective-permute-start(bf16[2,1024,512]{2,1,0:T(8,128)(2,1)} %shard_map.145.inner.refs_0_), channel_id=1, source_target_pairs={{0,2},{2,0},{4,6},{6,4},{8,10},{10,8},{12,14},{14,12},{16,18},{18,... | collective-permute-start | bytes 6291464 | tf_op jit(solution)/shard_map/ppermute | solution.py:30
  66.5 4.9 %collective-permute-start.4 = (bf16[128,1024]{1,0:T(8,128)(2,1)}, bf16[128,1024]{1,0:T(8,128)(2,1)}, u32[]{:S(2)}, u32[]{:S(2)}) collective-permute-start(bf16[128,1024]{1,0:T(8,128)(2,1)} %copy-done.21), channel_id=1, source_target_pairs={{0,2},{2,0},{4,6},{6,4},{8,10},{10,8},{12,14},{14,12},{16,18},{18,... | collective-permute-start | bytes 786440 | tf_op jit(solution)/shard_map/ppermute | solution.py:30
  71.3 1.6 %copy-start.1 = (bf16[1,2048,512]{2,1,0:T(8,128)(2,1)S(1)}, bf16[1,2048,512]{2,1,0:T(8,128)(2,1)}, u32[]{:S(2)}) copy-start(bf16[1,2048,512]{2,1,0:T(8,128)(2,1)} %param.18) | copy-start | bytes 6291460
  76.0 2.9 %collective-permute-start.10 = (bf16[256,2048]{1,0:T(8,128)(2,1)}, bf16[256,2048]{1,0:T(8,128)(2,1)S(1)}, u32[]{:S(2)}, u32[]{:S(2)}) collective-permute-start(bf16[256,2048]{1,0:T(8,128)(2,1)} %shard_map.146.over.refs_2_), channel_id=1, source_target_pairs={{0,2},{2,0},{4,6},{6,4},{8,10},{10,8},{12,14},{14,12},{16,18},{18,... | collective-permute-start | bytes 3145736 | tf_op jit(solution)/shard_map/ppermute | solution.py:30
  76.4 2.5 %copy-start.18 = (bf16[1,128,2048]{2,1,0:T(8,128)(2,1)S(1)}, bf16[1,128,2048]{2,1,0:T(8,128)(2,1)}, u32[]{:S(2)}) copy-start(bf16[1,128,2048]{2,1,0:T(8,128)(2,1)} %cot.3) | copy-start | bytes 1572868
  76.4 8.3 %copy-start.20 = (bf16[256,1024]{1,0:T(8,128)(2,1)S(1)}, bf16[256,1024]{1,0:T(8,128)(2,1)}, u32[]{:S(2)}) copy-start(bf16[256,1024]{1,0:T(8,128)(2,1)} %copy-done.19) | copy-start | bytes 1572868
  84.5 1.7 %collective-permute-start.11 = (bf16[128,1152]{1,0:T(8,128)(2,1)S(1)}, bf16[128,1152]{1,0:T(8,128)(2,1)S(1)}, u32[]{:S(2)}, u32[]{:S(2)}) collective-permute-start(bf16[128,1152]{1,0:T(8,128)(2,1)S(1)} %get-tuple-element.67), channel_id=1, source_target_pairs={{0,2},{2,0},{4,6},{6,4},{8,10},{10,8},{12,14},{14,12},{16,18},{18,... | collective-permute-start | bytes 884744 | tf_op jit(solution)/shard_map/ppermute | solution.py:30
  86.2 10.9 %copy-start.6 = (bf16[256,2048]{1,0:T(8,128)(2,1)S(1)}, bf16[256,2048]{1,0:T(8,128)(2,1)}, u32[]{:S(2)}) copy-start(bf16[256,2048]{1,0:T(8,128)(2,1)} %copy-done.5) | copy-start | bytes 3145732
  86.2 10.9 %copy-start.8 = (bf16[256,2048]{1,0:T(8,128)(2,1)S(1)}, bf16[256,2048]{1,0:T(8,128)(2,1)}, u32[]{:S(2)}) copy-start(bf16[256,2048]{1,0:T(8,128)(2,1)} %copy-done.7) | copy-start | bytes 3145732
  86.2 10.9 %copy-start.13 = (bf16[256,1024]{1,0:T(8,128)(2,1)S(1)}, bf16[256,1024]{1,0:T(8,128)(2,1)}, u32[]{:S(2)}) copy-start(bf16[256,1024]{1,0:T(8,128)(2,1)} %copy-done.12) | copy-start | bytes 1572868
  86.2 10.9 %copy-start.15 = (bf16[128,2048]{1,0:T(8,128)(2,1)S(1)}, bf16[128,2048]{1,0:T(8,128)(2,1)}, u32[]{:S(2)}) copy-start(bf16[128,2048]{1,0:T(8,128)(2,1)} %copy-done.14) | copy-start | bytes 1572868
  86.4 24.5 %collective-permute-start.15 = (bf16[256,1152]{1,0:T(8,128)(2,1)S(1)}, bf16[256,1152]{1,0:T(8,128)(2,1)S(1)}, u32[]{:S(2)}, u32[]{:S(2)}) collective-permute-start(bf16[256,1152]{1,0:T(8,128)(2,1)S(1)} %get-tuple-element.69.rest_0_.co), channel_id=1, source_target_pairs={{4,0},{6,2},{8,4},{10,6},{12,8},{14,10},{16,12},{18,14},{20,16},{2... | collective-permute-start | bytes 1769480 | tf_op jit(solution)/shard_map/ppermute | solution.py:26
  87.8 28.3 %collective-permute-start.14 = (bf16[256,1152]{1,0:T(8,128)(2,1)S(1)}, bf16[256,1152]{1,0:T(8,128)(2,1)S(1)}, u32[]{:S(2)}, u32[]{:S(2)}) collective-permute-start(bf16[256,1152]{1,0:T(8,128)(2,1)S(1)} %get-tuple-element.69.rest_0_.co), channel_id=1, source_target_pairs={{0,4},{2,6},{4,8},{6,10},{8,12},{10,14},{12,16},{14,18},{16,20},{1... | collective-permute-start | bytes 1769480 | tf_op jit(solution)/shard_map/ppermute | solution.py:26
  92.4 15.4 %collective-permute-start.13 = (bf16[128,1152]{1,0:T(8,128)(2,1)S(1)}, bf16[128,1152]{1,0:T(8,128)(2,1)S(1)}, u32[]{:S(2)}, u32[]{:S(2)}) collective-permute-start(bf16[128,1152]{1,0:T(8,128)(2,1)S(1)} %get-tuple-element.75), channel_id=1, source_target_pairs={{0,8},{2,10},{4,12},{6,14},{8,16},{10,18},{12,20},{14,22},{16,24},... | collective-permute-start | bytes 884744 | tf_op jit(solution)/shard_map/ppermute | solution.py:26
  95.4 6.9 %copy-start.4 = (bf16[1,512,2048]{2,1,0:T(8,128)(2,1)S(1)}, bf16[1,512,2048]{2,1,0:T(8,128)(2,1)}, u32[]{:S(2)}) copy-start(bf16[1,512,2048]{2,1,0:T(8,128)(2,1)} %param.19) | copy-start | bytes 6291460
  95.5 15.4 %collective-permute-start.16 = (bf16[128,1152]{1,0:T(8,128)(2,1)S(1)}, bf16[128,1152]{1,0:T(8,128)(2,1)S(1)}, u32[]{:S(2)}, u32[]{:S(2)}) collective-permute-start(bf16[128,1152]{1,0:T(8,128)(2,1)S(1)} %get-tuple-element.76), channel_id=1, source_target_pairs={{8,0},{10,2},{12,4},{14,6},{16,8},{18,10},{20,12},{22,14},{24,16},... | collective-permute-start | bytes 884744 | tf_op jit(solution)/shard_map/ppermute | solution.py:26
  116.1 12.2 %copy-start.2 = (bf16[1,2048,512]{2,1,0:T(8,128)(2,1)S(1)}, bf16[1,2048,512]{2,1,0:T(8,128)(2,1)}, u32[]{:S(2)}) copy-start(bf16[1,2048,512]{2,1,0:T(8,128)(2,1)} %param.18) | copy-start | bytes 6291460
  126.7 1.6 %collective-permute-start.18 = (bf16[128,1024]{1,0:T(8,128)(2,1)S(1)}, bf16[128,1024]{1,0:T(8,128)(2,1)S(1)}, u32[]{:S(2)}, u32[]{:S(2)}) collective-permute-start(bf16[128,1024]{1,0:T(8,128)(2,1)S(1)} %get-tuple-element.90), channel_id=1, source_target_pairs={{0,2},{2,0},{4,6},{6,4},{8,10},{10,8},{12,14},{14,12},{16,18},{18,... | collective-permute-start | bytes 786440 | tf_op jit(solution)/shard_map/ppermute | solution.py:30
  126.8 4.4 %collective-permute-start.17 = (bf16[128,2048]{1,0:T(8,128)(2,1)S(1)}, bf16[128,2048]{1,0:T(8,128)(2,1)S(1)}, u32[]{:S(2)}, u32[]{:S(2)}) collective-permute-start(bf16[128,2048]{1,0:T(8,128)(2,1)S(1)} %get-tuple-element.85), channel_id=1, source_target_pairs={{0,2},{2,0},{4,6},{6,4},{8,10},{10,8},{12,14},{14,12},{16,18},{18,... | collective-permute-start | bytes 1572872 | tf_op jit(solution)/shard_map/ppermute | solution.py:30
  127.2 3.9 %collective-permute-start.12 = (bf16[128,1024]{1,0:T(8,128)(2,1)S(1)}, bf16[128,1024]{1,0:T(8,128)(2,1)S(1)}, u32[]{:S(2)}, u32[]{:S(2)}) collective-permute-start(bf16[128,1024]{1,0:T(8,128)(2,1)S(1)} %get-tuple-element.73), channel_id=1, source_target_pairs={{0,2},{2,0},{4,6},{6,4},{8,10},{10,8},{12,14},{14,12},{16,18},{18,... | collective-permute-start | bytes 786440 | tf_op jit(solution)/shard_map/ppermute | solution.py:30
